TPU v7x, 512 devices: a whole 4x8x8 slice. The times are simulated.
512 devices in a mesh: row: 64 (over y_lo, z, x), col: 8 (over y_hi, core).
Axes of the slice: x: 4, y: 8 (y_hi: 4, y_lo: 2; y = y_hi * 2 + y_lo), z: 8, core: 2. Of those that a mesh axis runs over, the one named last changes fastest.
Arguments:
- x_scaled: float32 [4096, 12288], P('row', 'col'), may hold values from -4 to 4
Outputs:
- update: float32 [4096, 12288], P('row', 'col')
All inputs are finite; a program needn't handle non-finite values.
Results may differ from a plain program's by a relative error of at most 0.0041.
Values may be sent and summed in bfloat16 or wider, within the bound.
No kernel may reach another device: no remote copies, remote signals or barrier semaphores. Data moves between devices by JAX's collectives and lax.ppermute only.
A program may use at most 64 MiB of HBM per device.

v0:
```python
import jax
import jax.numpy as jnp
from jax import lax
from jax.sharding import PartitionSpec as P

N = 12288


coef_linear = 3.4445
coef_cubic = -4.775
coef_quintic = 2.0315


def cross_block(own, piece):
    return lax.dot_general(own, piece, (((1,), (1,)), ((), ())), preferred_element_type=jnp.float32)


def per_device(x_scaled):
    xb = x_scaled.astype(jnp.bfloat16)
    stacked = lax.all_gather(xb, "row", axis=0, tiled=True)
    partial_value = cross_block(xb, stacked)
    gram = lax.psum(partial_value, "col") / N
    proj = jnp.dot(
        gram, stacked, precision=lax.Precision.HIGHEST, preferred_element_type=jnp.float32
    )
    square_part = lax.dot_general(
        proj,
        stacked,
        (((1,), (1,)), ((), ())),
        precision=lax.Precision.HIGHEST,
        preferred_element_type=jnp.float32,
    )
    square = lax.psum(square_part, "col") / N
    poly = (coef_cubic * gram + coef_quintic * square).astype(jnp.bfloat16)
    return coef_linear * x_scaled + jnp.dot(poly, stacked, preferred_element_type=jnp.float32)


def solution(mesh):
    return jax.shard_map(
        per_device,
        mesh=mesh,
        in_specs=(P("row", "col"),),
        out_specs=P("row", "col"),
        check_vma=False,
    )
```

profile of v0, /device:TPU:1, one launch (start us, length us, event | category | flops | bytes accessed | tf_op | source)
XLA Modules:
  0.0 551.7 jit_solution(12780926225224754788)
XLA Ops:
  6.5 0.0 all-gather.2.cloned.1.call-start
  6.5 1.7 convert_element_type.6
  8.2 0.0 all-gather.2.cloned.1.call-update
  8.3 0.0 all-reduce.3.cloned.1.call-start
  8.3 293.7 %all-gather.2.cloned.1.call-done = bf16[4096,1536]{1,0:T(8,128)(2,1)} async-done(((bf16[64,1536]{1,0:T(8,128)(2,1)}), bf16[4096,1536]{1,0:T(8,128)(2,1)}) %all-gather.2.cloned.1.call-update) | async-done | bytes 12582928 | tf_op jit(solution)/shard_map/all_gather | solution.py:20
  302.0 9.6 %fusion.8 = f32[64,4096]{1,0:T(8,128)} fusion(bf16[64,1536]{1,0:T(8,128)(2,1)} %convert_element_type.6, bf16[4096,1536]{1,0:T(8,128)(2,1)} %all-gather.2.cloned.1.call-done), kind=kOutput, calls=%fused_computation.10 | convolution fusion | flops 805306368 | bytes 13828096 | tf_op jit(solution)/shard_map/dot_general | solution.py:15
  311.5 0.0 all-reduce.3.cloned.1.call-update
  311.5 0.0 all-reduce.5.cloned.1.call-start
  311.6 119.0 %all-reduce.3.cloned.1.call-done = f32[64,4096]{1,0:T(8,128)} async-done(((f32[64,4096]{1,0:T(8,128)}), f32[64,4096]{1,0:T(8,128)}) %all-reduce.3.cloned.1.call-update) | async-done | bytes 1048592 | tf_op jit(solution)/shard_map/psum | solution.py:22
  430.6 9.8 %fusion = f32[64,1536]{1,0:T(8,128)S(1)} fusion(bf16[4096,1536]{1,0:T(8,128)(2,1)} %all-gather.2.cloned.1.call-done, f32[64,4096]{1,0:T(8,128)} %all-reduce.3.cloned.1.call-done), kind=kOutput, calls=%fused_computation.2 | convolution fusion | flops 4832100352 | bytes 14024704 | tf_op jit(solution)/shard_map/dot_general | solution.py:23
  440.5 0.0 copy-start
  440.5 0.0 copy-start.1
  440.5 15.4 %fusion.9 = f32[64,4096]{1,0:T(8,128)} fusion(f32[64,1536]{1,0:T(8,128)S(1)} %fusion, bf16[4096,1536]{1,0:T(8,128)(2,1)} %all-gather.2.cloned.1.call-done), kind=kOutput, calls=%fused_computation.11 | convolution fusion | flops 4831838208 | bytes 14024704 | tf_op jit(solution)/shard_map/dot_general | solution.py:26
  455.9 0.0 all-reduce.5.cloned.1.call-update
  455.9 81.3 %all-reduce.5.cloned.1.call-done = f32[64,4096]{1,0:T(8,128)} async-done(((f32[64,4096]{1,0:T(8,128)}), f32[64,4096]{1,0:T(8,128)}) %all-reduce.5.cloned.1.call-update) | async-done | bytes 1048592 | tf_op jit(solution)/shard_map/psum | solution.py:33
  537.2 0.0 copy-done
  537.2 0.0 copy-done.1
  537.2 8.0 %convolution_add_fusion = f32[64,1536]{1,0:T(8,128)} fusion(bf16[4096,1536]{1,0:T(8,128)(2,1)} %all-gather.2.cloned.1.call-done, f32[64,4096]{1,0:T(8,128)} %all-reduce.5.cloned.1.call-done, f32[64,4096]{1,0:T(8,128)S(1)} %copy-done, f32[64,1536]{1,0:T(8,128)S(1)} %copy-done.1), kind=kOutput, calls=%fused_computation | convolution fusion | flops 806551552 | bytes 15466496 | tf_op jit(solution)/shard_map/dot_general | solution.py:35
Async XLA Ops:
  6.5 295.4 %all-gather.2.cloned.1.call-start = ((), (), s32[]{:S(2)}) async-start(), calls=%async_computation | async-start | bytes 12779520 | tf_op jit(solution)/shard_map/all_gather | solution.py:20
  8.3 422.4 %all-reduce.3.cloned.1.call-start = ((), (), s32[]{:S(2)}) async-start(), calls=%async_computation.1 | async-start | bytes 2097152 | tf_op jit(solution)/shard_map/psum | solution.py:22
  311.5 225.7 %all-reduce.5.cloned.1.call-start = ((), (), s32[]{:S(2)}) async-start(), calls=%async_computation.2 | async-start | bytes 2097152 | tf_op jit(solution)/shard_map/psum | solution.py:33
  440.5 96.8 %copy-start = (f32[64,4096]{1,0:T(8,128)S(1)}, f32[64,4096]{1,0:T(8,128)}, u32[]{:S(2)}) copy-start(f32[64,4096]{1,0:T(8,128)} %all-reduce.3.cloned.1.call-done) | copy-start | bytes 3145732
  440.5 96.8 %copy-start.1 = (f32[64,1536]{1,0:T(8,128)S(1)}, f32[64,1536]{1,0:T(8,128)}, u32[]{:S(2)}) copy-start(f32[64,1536]{1,0:T(8,128)} %param.1) | copy-start | bytes 1179652
Sparse Core Ops, SparseCore 0:
  9.4 292.4 all-gather.1
  311.7 118.9 all-reduce.2
  456.1 81.1 all-reduce.4
where the time goes:
time: 552 us
  waiting for transfers between devices  494 us (89%)
  matrix products  42.8 us (8%)
  between operations  13.1 us (2%)
    all_gather x1, waiting for transfers between devices, per_device(): stacked = lax.all_gather(xb, 'row', axis=0, tiled=True)  294 us
    psum x1, waiting for transfers between devices, per_device(): gram = lax.psum(partial_value, 'col') / N  119 us
    psum x1, waiting for transfers between devices, per_device(): square = lax.psum(square_part, 'col') / N  81.3 us
    dot_general x1, matrix products, per_device(): lax.dot_general(proj, stacked, (((1,), (1,)), ((), ())), precision=lax.Pr...  15.4 us
  transfers between devices with their start and end apart: 3, of which 3 were waited for; matrix products, arithmetic and copies ran while one was open for 0% of the time, Pallas kernels for 0%

commit v1 on v0

v1 whole, which is shorter than its diff:
```python
import jax
import jax.numpy as jnp
from jax import lax
from jax.sharding import Mesh, PartitionSpec as P

N = 12288

coef_linear = 3.4445
coef_cubic = -4.775
coef_quintic = 2.0315

LO = ("y_lo", "x")
COL = ("y_hi", "core")
ROW = ("y_lo", "z", "x")
EVERY = ("y_lo", "z", "x", "y_hi", "core")


def dot_nt(a, b):
    return lax.dot_general(a, b, (((1,), (1,)), ((), ())), preferred_element_type=jnp.float32)


def swap_lo_col():
    pairs = []
    for y_lo in range(2):
        for z in range(8):
            for x in range(4):
                for c in range(8):
                    to_y, to_x = divmod(c, 4)
                    source = ((y_lo * 8 + z) * 4 + x) * 8 + c
                    target = ((to_y * 8 + z) * 4 + to_x) * 8 + y_lo * 4 + x
                    pairs.append((source, target))
    return pairs


def spread(block, axis):
    return lax.all_to_all(jnp.broadcast_to(block[None], (8,) + block.shape), axis, 0, 0)


def sum_pieces(pieces, axis):
    me = lax.axis_index(axis)
    arrived = lax.all_to_all(pieces.astype(jnp.bfloat16), axis, 0, 0)
    own = lax.dynamic_index_in_dim(pieces, me, 0, keepdims=False)
    other = jnp.where(jnp.arange(8)[:, None, None] == me, 0.0, arrived.astype(jnp.float32))
    return own + other.sum(0)


def per_device(x_scaled):
    rows, cols = x_scaled.shape
    xb = x_scaled.astype(jnp.bfloat16)
    by_hi = lax.all_gather(xb, "z", axis=0, tiled=True)
    by_lo = spread(xb, LO).reshape(8 * rows, cols)

    tile = dot_nt(by_lo, by_hi) * (1.0 / N)
    gram = sum_pieces(tile.reshape(8, rows, 8 * rows), COL)

    rounded = gram.astype(jnp.bfloat16)
    left = lax.all_gather(rounded, COL, axis=0, tiled=True)
    right = spread(rounded, "z").reshape(8 * rows, 8 * rows)
    square = sum_pieces(dot_nt(left, right).reshape(8, rows, 8 * rows), LO)
    square = lax.ppermute(square, EVERY, swap_lo_col())

    poly = (coef_cubic * gram + coef_quintic * square).astype(jnp.bfloat16)
    poly = lax.all_gather(poly, COL, axis=0, tiled=True)
    product = jnp.dot(poly, by_hi, preferred_element_type=jnp.float32)
    return coef_linear * x_scaled + sum_pieces(product.reshape(8, rows, cols), LO)


def solution(mesh):
    fine = Mesh(mesh.devices.reshape(2, 8, 4, 4, 2), EVERY)
    return jax.shard_map(
        per_device,
        mesh=fine,
        in_specs=(P(ROW, COL),),
        out_specs=P(ROW, COL),
        check_vma=False,
    )
```

time: 552 us -> 188 us (0.34)
  waiting for transfers between devices: 494 us -> 64.3 us
  blocking collectives: 0 us -> 63.8 us
  matrix products: 42.8 us -> 5.02 us
  starting transfers between devices: 0.09 us -> 31.3 us
    all_gather x1, waiting for transfers between devices: 294 us -> 37.7 us  [per_device(): by_hi = lax.all_gather(xb, 'z', axis=0, tiled=True)]
    psum x2 -> x0, waiting for transfers between devices: 200 us -> none  [the longest x1 119 us: per_device(): gram = lax.psum(partial_value, 'col') / N]
    dot_general x4 -> x3, matrix products: 42.8 us -> 5.02 us  [the longest x2 4.04 us: dot_nt(): lax.dot_general(a, b, (((1,), (1,)), ((), ())), preferred_element_type=jn...]
    all_gather x0 -> x2, blocking collectives: none -> 37.7 us  [the longest x1 20.5 us: per_device(): poly = lax.all_gather(poly, COL, axis=0, tiled=True)]
    all_to_all x0 -> x4, starting transfers between devices: none -> 27.2 us  [the longest x2 17.4 us: sum_pieces(): arrived = lax.all_to_all(pieces.astype(jnp.bfloat16), axis, 0, 0)]
    all_to_all x0 -> x1, blocking collectives: none -> 26.1 us  [sum_pieces(): arrived = lax.all_to_all(pieces.astype(jnp.bfloat16), axis, 0, 0)]
    all_to_all x0 -> x4, waiting for transfers between devices: none -> 24 us  [the longest x2 24 us: sum_pieces(): arrived = lax.all_to_all(pieces.astype(jnp.bfloat16), axis, 0, 0)]
  transfers between devices with their start and end apart: 3 -> 6, of which waited for: 3 -> 4; matrix products, arithmetic and copies ran while one was open for 0% -> 1% of each run, Pallas kernels for 0% -> 0%
where the time goes in v1:
time: 188 us; the launch traced here: 187 us
  waiting for transfers between devices  64.3 us (34%)
  blocking collectives  63.8 us (34%)
  starting transfers between devices  31.3 us (17%)
  between operations  13.5 us (7%)
  other arithmetic  5.29 us (3%)
  matrix products  5.02 us (3%)
  local copies, waits for them, and re-layouts  3.68 us (2%)
    all_gather x1, waiting for transfers between devices, per_device(): by_hi = lax.all_gather(xb, 'z', axis=0, tiled=True)  37.7 us
    all_to_all x1, blocking collectives, sum_pieces(): arrived = lax.all_to_all(pieces.astype(jnp.bfloat16), axis, 0, 0)  26.1 us
    all_to_all x2, waiting for transfers between devices, sum_pieces(): arrived = lax.all_to_all(pieces.astype(jnp.bfloat16), axis, 0, 0)  24 us
    all_gather x1, blocking collectives, per_device(): poly = lax.all_gather(poly, COL, axis=0, tiled=True)  20.5 us
    all_to_all x2, starting transfers between devices, sum_pieces(): arrived = lax.all_to_all(pieces.astype(jnp.bfloat16), axis, 0, 0)  17.4 us
    all_gather x1, blocking collectives, per_device(): left = lax.all_gather(rounded, COL, axis=0, tiled=True)  17.2 us
    all_to_all x2, starting transfers between devices, spread(): lax.all_to_all(jnp.broadcast_to(block[None], (8,) + block.shape), axis, 0...  9.77 us
    ppermute x1, starting transfers between devices, per_device(): square = lax.ppermute(square, EVERY, swap_lo_col())  4.12 us
  transfers between devices with their start and end apart: 6, of which 4 were waited for; matrix products, arithmetic and copies ran while one was open for 1% of the time, Pallas kernels for 0%

profile of v1, /device:TPU:1, one launch (start us, length us, event | category | flops | bytes accessed | tf_op | source)
XLA Modules:
  0.0 186.9 jit_solution(2606072771283207567)
XLA Ops:
  6.5 0.0 all-gather.2.cloned.1.call-start
  6.5 1.7 convert_element_type.30
  8.2 0.0 all-gather.2.cloned.1.call-update
  8.3 2.2 %broadcast_in_dim.47 = bf16[8,64,1536]{2,1,0:T(8,128)(2,1)} broadcast(bf16[64,1536]{1,0:T(8,128)(2,1)} %convert_element_type.30), dimensions={1,2} | broadcast | bytes 1769472 | tf_op jit(solution)/shard_map/broadcast_in_dim | solution.py:36
  10.5 5.9 %all-to-all-start = ((bf16[8,64,1536]{2,1,0:T(8,128)(2,1)}), bf16[8,64,1536]{2,1,0:T(8,128)(2,1)S(1)}, u32[]{:S(2)}, u32[]{:S(2)}) async-start(bf16[8,64,1536]{2,1,0:T(8,128)(2,1)} %broadcast_in_dim.47), calls=%async_computation | async-start | bytes 3145728 | tf_op jit(solution)/shard_map/all_to_all | solution.py:36
  16.3 37.7 %all-gather.2.cloned.1.call-done = bf16[512,1536]{1,0:T(8,128)(2,1)} async-done(((bf16[64,1536]{1,0:T(8,128)(2,1)}), bf16[512,1536]{1,0:T(8,128)(2,1)}) %all-gather.2.cloned.1.call-update) | async-done | bytes 1572880 | tf_op jit(solution)/shard_map/all_gather | solution.py:50
  54.0 0.0 all-to-all-done
  54.0 2.4 %convolution_multiply_fusion = f32[512,512]{1,0:T(8,128)S(1)} fusion(bf16[512,1536]{1,0:T(8,128)(2,1)S(1)} %bitcast.41, bf16[512,1536]{1,0:T(8,128)(2,1)} %all-gather.2.cloned.1.call-done), kind=kOutput, calls=%fused_computation.1 | convolution fusion | flops 805568512 | bytes 4194304 | tf_op jit(solution)/shard_map/dot_general | solution.py:19
  56.4 0.9 convert_element_type.31
  57.3 11.8 %all-to-all-start.1 = ((bf16[8,64,512]{2,1,0:T(8,128)(2,1)}), bf16[8,64,512]{2,1,0:T(8,128)(2,1)S(1)}, u32[]{:S(2)}, u32[]{:S(2)}) async-start(bf16[8,64,512]{2,1,0:T(8,128)(2,1)} %convert_element_type.31), calls=%async_computation.1 | async-start | bytes 1048576 | tf_op jit(solution)/shard_map/all_to_all | solution.py:41
  69.1 15.6 %all-to-all-done.1 = bf16[8,64,512]{2,1,0:T(8,128)(2,1)S(1)} async-done(((bf16[8,64,512]{2,1,0:T(8,128)(2,1)}), bf16[8,64,512]{2,1,0:T(8,128)(2,1)S(1)}, u32[]{:S(2)}, u32[]{:S(2)}) %all-to-all-start.1) | async-done | bytes 524320 | tf_op jit(solution)/shard_map/all_to_all | solution.py:41
  84.7 0.2 select_reduce_fusion.2
  84.9 0.8 broadcast_in_dim.51
  85.8 3.9 %all-to-all-start.2 = ((bf16[8,64,512]{2,1,0:T(8,128)(2,1)}), bf16[8,64,512]{2,1,0:T(8,128)(2,1)S(1)}, u32[]{:S(2)}, u32[]{:S(2)}) async-start(bf16[8,64,512]{2,1,0:T(8,128)(2,1)} %broadcast_in_dim.51), calls=%async_computation.2 | async-start | bytes 1048576 | tf_op jit(solution)/shard_map/all_to_all | solution.py:36
  89.7 17.2 %all_gather.10 = bf16[512,512]{1,0:T(8,128)(2,1)S(1)} all-gather(bf16[64,512]{1,0:T(8,128)(2,1)S(1)} %fusion.3), channel_id=1, replica_groups=mesh['y_lo'=2,'z'=8,'x'=4,'y_hi'=4,'core'=2] {'y_hi','core'}, dimensions={0}, use_global_device_ids=true | all-gather | bytes 589824 | tf_op jit(solution)/shard_map/all_gather | solution.py:57
  106.9 0.0 all-to-all-done.2
  106.9 1.6 fusion.4
  108.5 0.0 copy-start.1
  108.5 5.6 %all-to-all-start.3 = ((bf16[8,64,512]{2,1,0:T(8,128)(2,1)}), bf16[8,64,512]{2,1,0:T(8,128)(2,1)S(1)}, u32[]{:S(2)}, u32[]{:S(2)}) async-start(bf16[8,64,512]{2,1,0:T(8,128)(2,1)} %get-tuple-element.5), calls=%async_computation.3 | async-start | bytes 1048576 | tf_op jit(solution)/shard_map/all_to_all | solution.py:41
  114.1 8.4 %all-to-all-done.3 = bf16[8,64,512]{2,1,0:T(8,128)(2,1)S(1)} async-done(((bf16[8,64,512]{2,1,0:T(8,128)(2,1)}), bf16[8,64,512]{2,1,0:T(8,128)(2,1)S(1)}, u32[]{:S(2)}, u32[]{:S(2)}) %all-to-all-start.3) | async-done | bytes 524320 | tf_op jit(solution)/shard_map/all_to_all | solution.py:41
  122.5 0.2 select_reduce_fusion.1
  122.7 0.9 bitcast_add_fusion.1
  123.6 4.1 %collective-permute-start = (f32[64,512]{1,0:T(8,128)S(1)}, f32[64,512]{1,0:T(8,128)S(1)}, u32[]{:S(2)}, u32[]{:S(2)}) collective-permute-start(f32[64,512]{1,0:T(8,128)S(1)} %bitcast_add_fusion.1), channel_id=1, source_target_pairs={{0,0},{1,8},{2,16},{3,24},{4,256},{5,264},{6,272},{7,280},{8,1},{9... | collective-permute-start | bytes 393224 | tf_op jit(solution)/shard_map/ppermute | solution.py:60
  127.7 2.6 %collective-permute-done = f32[64,512]{1,0:T(8,128)S(1)} collective-permute-done((f32[64,512]{1,0:T(8,128)S(1)}, f32[64,512]{1,0:T(8,128)S(1)}, u32[]{:S(2)}, u32[]{:S(2)}) %collective-permute-start) | collective-permute-done | bytes 131104 | tf_op jit(solution)/shard_map/ppermute | solution.py:60
  130.4 20.5 %all_gather.11 = bf16[512,512]{1,0:T(8,128)(2,1)S(1)} all-gather(bf16[64,512]{1,0:T(8,128)(2,1)S(1)} %add_convert_fusion), channel_id=1, replica_groups=mesh['y_lo'=2,'z'=8,'x'=4,'y_hi'=4,'core'=2] {'y_hi','core'}, dimensions={0}, use_global_device_ids=true | all-gather | bytes 589824 | tf_op jit(solution)/shard_map/all_gather | solution.py:63
  151.0 0.0 copy-done.1
  151.0 1.0 fusion.5
  151.9 0.2 convert_element_type.38
  152.1 26.1 %all_to_all.25 = bf16[8,64,1536]{2,1,0:T(8,128)(2,1)S(1)} all-to-all(bf16[8,64,1536]{2,1,0:T(8,128)(2,1)S(1)} %convert_element_type.38), channel_id=1, replica_groups=mesh['y_lo'=2,'z'=8,'x'=4,'y_hi'=4,'core'=2] {'y_lo','x'}, dimensions={0} | all-to-all | bytes 3145728 | tf_op jit(solution)/shard_map/all_to_all | solution.py:41
  178.3 0.0 copy-start
  178.3 0.4 select_reduce_fusion
  178.6 0.6 copy-done
  179.2 0.8 fusion
  (5 shorter events, 0.1 us)
Async XLA Ops:
  6.5 47.5 %all-gather.2.cloned.1.call-start = ((), (), s32[]{:S(2)}) async-start(), calls=%async_computation.5 | async-start | bytes 1769472 | tf_op jit(solution)/shard_map/all_gather | solution.py:50
  10.5 43.5 %all-to-all-start = ((bf16[8,64,1536]{2,1,0:T(8,128)(2,1)}), bf16[8,64,1536]{2,1,0:T(8,128)(2,1)S(1)}, u32[]{:S(2)}, u32[]{:S(2)}) async-start(bf16[8,64,1536]{2,1,0:T(8,128)(2,1)} %broadcast_in_dim.47), calls=%async_computation | async-start | bytes 3145728 | tf_op jit(solution)/shard_map/all_to_all | solution.py:36
  57.3 27.4 %all-to-all-start.1 = ((bf16[8,64,512]{2,1,0:T(8,128)(2,1)}), bf16[8,64,512]{2,1,0:T(8,128)(2,1)S(1)}, u32[]{:S(2)}, u32[]{:S(2)}) async-start(bf16[8,64,512]{2,1,0:T(8,128)(2,1)} %convert_element_type.31), calls=%async_computation.1 | async-start | bytes 1048576 | tf_op jit(solution)/shard_map/all_to_all | solution.py:41
  85.8 21.1 %all-to-all-start.2 = ((bf16[8,64,512]{2,1,0:T(8,128)(2,1)}), bf16[8,64,512]{2,1,0:T(8,128)(2,1)S(1)}, u32[]{:S(2)}, u32[]{:S(2)}) async-start(bf16[8,64,512]{2,1,0:T(8,128)(2,1)} %broadcast_in_dim.51), calls=%async_computation.2 | async-start | bytes 1048576 | tf_op jit(solution)/shard_map/all_to_all | solution.py:36
  108.5 42.4 %copy-start.1 = (bf16[512,1536]{1,0:T(8,128)(2,1)S(1)}, bf16[512,1536]{1,0:T(8,128)(2,1)}, u32[]{:S(2)}) copy-start(bf16[512,1536]{1,0:T(8,128)(2,1)} %all-gather.2.cloned.1.call-done) | copy-start | bytes 4718596
  108.5 14.0 %all-to-all-start.3 = ((bf16[8,64,512]{2,1,0:T(8,128)(2,1)}), bf16[8,64,512]{2,1,0:T(8,128)(2,1)S(1)}, u32[]{:S(2)}, u32[]{:S(2)}) async-start(bf16[8,64,512]{2,1,0:T(8,128)(2,1)} %get-tuple-element.5), calls=%async_computation.3 | async-start | bytes 1048576 | tf_op jit(solution)/shard_map/all_to_all | solution.py:41
  123.6 6.8 %collective-permute-start = (f32[64,512]{1,0:T(8,128)S(1)}, f32[64,512]{1,0:T(8,128)S(1)}, u32[]{:S(2)}, u32[]{:S(2)}) collective-permute-start(f32[64,512]{1,0:T(8,128)S(1)} %bitcast_add_fusion.1), channel_id=1, source_target_pairs={{0,0},{1,8},{2,16},{3,24},{4,256},{5,264},{6,272},{7,280},{8,1},{9... | collective-permute-start | bytes 393224 | tf_op jit(solution)/shard_map/ppermute | solution.py:60
  178.3 1.0 copy-start
Sparse Core Ops, SparseCore 0:
  9.4 44.5 all-gather.1

commit v2 on v1

--- a/solution.py
+++ b/solution.py
@@ -47,10 +47,11 @@
 def per_device(x_scaled):
     rows, cols = x_scaled.shape
     xb = x_scaled.astype(jnp.bfloat16)
-    by_hi = lax.all_gather(xb, "z", axis=0, tiled=True)
-    by_lo = spread(xb, LO).reshape(8 * rows, cols)
+    by_hi = spread(xb, "z").reshape(8 * rows, cols)
+    pair = lax.all_gather(xb, "y_lo", axis=0)
+    by_lo = [lax.all_gather(pair[y], "x", axis=0, tiled=True) for y in range(2)]
 
-    tile = dot_nt(by_lo, by_hi) * (1.0 / N)
+    tile = jnp.concatenate([dot_nt(part, by_hi) for part in by_lo]) * (1.0 / N)
     gram = sum_pieces(tile.reshape(8, rows, 8 * rows), COL)
 
     rounded = gram.astype(jnp.bfloat16)

time: 188 us -> 175 us (0.931)
  blocking collectives: 63.8 us -> 95.2 us
  waiting for transfers between devices: 64.3 us -> 34.6 us
  between operations: 13.5 us -> 0.1 us
    all_gather x1 -> x0, waiting for transfers between devices: 37.7 us -> none  [per_device(): by_hi = lax.all_gather(xb, 'z', axis=0, tiled=True)]
    all_gather x0 -> x3, blocking collectives: none -> 30 us  [the longest x2 23.9 us: per_device(): by_lo = [lax.all_gather(pair[y], 'x', axis=0, tiled=True) for y in range(2)]]
    all_to_all x2, waiting for transfers between devices: 0.01 us -> 8.19 us  [spread(): lax.all_to_all(jnp.broadcast_to(block[None], (8,) + block.shape), axis, 0...]
    all_to_all x2, starting transfers between devices: 9.77 us -> 14.4 us  [spread(): lax.all_to_all(jnp.broadcast_to(block[None], (8,) + block.shape), axis, 0...]
    all_to_all x2, starting transfers between devices: 17.4 us -> 13.8 us  [sum_pieces(): arrived = lax.all_to_all(pieces.astype(jnp.bfloat16), axis, 0, 0)]
    dot_general x2 -> x3, matrix products: 4.04 us -> 3.82 us  [dot_nt(): lax.dot_general(a, b, (((1,), (1,)), ((), ())), preferred_element_type=jn...]
  transfers between devices with their start and end apart: 6 -> 5, of which waited for: 4 -> 4; matrix products, arithmetic and copies ran while one was open for 1% -> 0% of each run, Pallas kernels for 0% -> 0%
where the time goes in v2:
time: 175 us; the launch traced here: 174 us
  blocking collectives  95.2 us (54%)
  waiting for transfers between devices  34.6 us (20%)
  starting transfers between devices  32.2 us (18%)
  matrix products  4.8 us (3%)
  other arithmetic  4.55 us (3%)
  local copies, waits for them, and re-layouts  2.78 us (2%)
    all_to_all x1, blocking collectives, sum_pieces(): arrived = lax.all_to_all(pieces.astype(jnp.bfloat16), axis, 0, 0)  26 us
    all_gather x2, blocking collectives, per_device(): by_lo = [lax.all_gather(pair[y], 'x', axis=0, tiled=True) for y in range(2)]  23.9 us
    all_to_all x2, waiting for transfers between devices, sum_pieces(): arrived = lax.all_to_all(pieces.astype(jnp.bfloat16), axis, 0, 0)  23.8 us
    all_gather x1, blocking collectives, per_device(): poly = lax.all_gather(poly, COL, axis=0, tiled=True)  20.8 us
    all_gather x1, blocking collectives, per_device(): left = lax.all_gather(rounded, COL, axis=0, tiled=True)  18.3 us
    all_to_all x2, starting transfers between devices, spread(): lax.all_to_all(jnp.broadcast_to(block[None], (8,) + block.shape), axis, 0...  14.4 us
    all_to_all x2, starting transfers between devices, sum_pieces(): arrived = lax.all_to_all(pieces.astype(jnp.bfloat16), axis, 0, 0)  13.8 us
    all_to_all x2, waiting for transfers between devices, spread(): lax.all_to_all(jnp.broadcast_to(block[None], (8,) + block.shape), axis, 0...  8.19 us
  transfers between devices with their start and end apart: 5, of which 4 were waited for; matrix products, arithmetic and copies ran while one was open for 0% of the time, Pallas kernels for 0%

profile of v2, /device:TPU:1, one launch (start us, length us, event | category | flops | bytes accessed | tf_op | source)
XLA Modules:
  0.0 174.2 jit_solution(7944038400864970602)
XLA Ops:
  0.0 1.0 convert_element_type.30
  1.0 1.3 broadcast_in_dim.47
  2.3 10.9 %all-to-all-start = ((bf16[8,64,1536]{2,1,0:T(8,128)(2,1)}), bf16[8,64,1536]{2,1,0:T(8,128)(2,1)S(1)}, u32[]{:S(2)}, u32[]{:S(2)}) async-start(bf16[8,64,1536]{2,1,0:T(8,128)(2,1)} %broadcast_in_dim.47), calls=%async_computation | async-start | bytes 3145728 | tf_op jit(solution)/shard_map/all_to_all | solution.py:36
  13.2 6.1 %all-gather = bf16[128,1536]{1,0:T(8,128)(2,1)S(1)} all-gather(bf16[64,1536]{1,0:T(8,128)(2,1)S(1)} %convert_element_type.30), channel_id=2, replica_groups=mesh['y_lo'=2,'z'=8,'x'=4,'y_hi'=4,'core'=2] {'y_lo'}, dimensions={0}, use_global_device_ids=true | all-gather | bytes 589824 | tf_op jit(solution)/shard_map/all_gather | solution.py:51
  19.3 12.6 %all-gather.3 = bf16[256,1536]{1,0:T(8,128)(2,1)S(1)} all-gather(bf16[64,1536]{1,0:T(8,128)(2,1)S(1)} %get-tuple-element.5), channel_id=5, replica_groups=mesh['y_lo'=2,'z'=8,'x'=4,'y_hi'=4,'core'=2] {'x'}, dimensions={0}, use_global_device_ids=true | all-gather | bytes 983040 | tf_op jit(solution)/shard_map/all_gather | solution.py:52
  32.0 11.3 %all-gather.4 = bf16[256,1536]{1,0:T(8,128)(2,1)S(1)} all-gather(bf16[64,1536]{1,0:T(8,128)(2,1)S(1)} %get-tuple-element.6), channel_id=6, replica_groups=mesh['y_lo'=2,'z'=8,'x'=4,'y_hi'=4,'core'=2] {'x'}, dimensions={0}, use_global_device_ids=true | all-gather | bytes 983040 | tf_op jit(solution)/shard_map/all_gather | solution.py:52
  43.3 8.2 %all-to-all-done = bf16[8,64,1536]{2,1,0:T(8,128)(2,1)S(1)} async-done(((bf16[8,64,1536]{2,1,0:T(8,128)(2,1)}), bf16[8,64,1536]{2,1,0:T(8,128)(2,1)S(1)}, u32[]{:S(2)}, u32[]{:S(2)}) %all-to-all-start) | async-done | bytes 1572896 | tf_op jit(solution)/shard_map/all_to_all | solution.py:36
  51.4 0.6 fusion.8
  52.1 0.6 fusion.7
  52.7 0.1 maximum_multiply_fusion
  52.8 0.9 convert_element_type.31
  53.6 9.8 %all-to-all-start.1 = ((bf16[8,64,512]{2,1,0:T(8,128)(2,1)}), bf16[8,64,512]{2,1,0:T(8,128)(2,1)S(1)}, u32[]{:S(2)}, u32[]{:S(2)}) async-start(bf16[8,64,512]{2,1,0:T(8,128)(2,1)} %convert_element_type.31), calls=%async_computation.1 | async-start | bytes 1048576 | tf_op jit(solution)/shard_map/all_to_all | solution.py:41
  63.4 15.4 %all-to-all-done.1 = bf16[8,64,512]{2,1,0:T(8,128)(2,1)S(1)} async-done(((bf16[8,64,512]{2,1,0:T(8,128)(2,1)}), bf16[8,64,512]{2,1,0:T(8,128)(2,1)S(1)}, u32[]{:S(2)}, u32[]{:S(2)}) %all-to-all-start.1) | async-done | bytes 524320 | tf_op jit(solution)/shard_map/all_to_all | solution.py:41
  78.8 0.2 select_reduce_fusion.2
  79.0 0.8 broadcast_in_dim.51
  79.8 3.5 %all-to-all-start.2 = ((bf16[8,64,512]{2,1,0:T(8,128)(2,1)}), bf16[8,64,512]{2,1,0:T(8,128)(2,1)S(1)}, u32[]{:S(2)}, u32[]{:S(2)}) async-start(bf16[8,64,512]{2,1,0:T(8,128)(2,1)} %broadcast_in_dim.51), calls=%async_computation.2 | async-start | bytes 1048576 | tf_op jit(solution)/shard_map/all_to_all | solution.py:36
  83.4 18.3 %all_gather.22 = bf16[512,512]{1,0:T(8,128)(2,1)} all-gather(bf16[64,512]{1,0:T(8,128)(2,1)S(1)} %fusion.3), channel_id=1, replica_groups=mesh['y_lo'=2,'z'=8,'x'=4,'y_hi'=4,'core'=2] {'y_hi','core'}, dimensions={0}, use_global_device_ids=true | all-gather | bytes 589824 | tf_op jit(solution)/shard_map/all_gather | solution.py:58
  101.7 0.0 all-to-all-done.2
  101.7 2.6 %fusion.5 = (bf16[8,64,512]{2,1,0:T(8,128)(2,1)}, f32[8,64,512]{2,1,0:T(8,128)}) fusion(bf16[8,64,512]{2,1,0:T(8,128)(2,1)} %bitcast.45, bf16[512,512,1]{1,0,2:T(8,128)(2,1)S(1)} %bitcast.44), kind=kOutput, calls=%fused_computation.16 | convolution fusion | flops 268697600 | bytes 2621440 | tf_op jit(solution)/shard_map/dot_general | solution.py:19
  104.3 4.0 %all-to-all-start.3 = ((bf16[8,64,512]{2,1,0:T(8,128)(2,1)}), bf16[8,64,512]{2,1,0:T(8,128)(2,1)S(1)}, u32[]{:S(2)}, u32[]{:S(2)}) async-start(bf16[8,64,512]{2,1,0:T(8,128)(2,1)} %get-tuple-element.7), calls=%async_computation.3 | async-start | bytes 1048576 | tf_op jit(solution)/shard_map/all_to_all | solution.py:41
  108.3 8.4 %all-to-all-done.3 = bf16[8,64,512]{2,1,0:T(8,128)(2,1)S(1)} async-done(((bf16[8,64,512]{2,1,0:T(8,128)(2,1)}), bf16[8,64,512]{2,1,0:T(8,128)(2,1)S(1)}, u32[]{:S(2)}, u32[]{:S(2)}) %all-to-all-start.3) | async-done | bytes 524320 | tf_op jit(solution)/shard_map/all_to_all | solution.py:41
  116.7 0.2 select_reduce_fusion.1
  116.9 0.9 bitcast_add_fusion.1
  117.8 4.1 %collective-permute-start = (f32[64,512]{1,0:T(8,128)S(1)}, f32[64,512]{1,0:T(8,128)S(1)}, u32[]{:S(2)}, u32[]{:S(2)}) collective-permute-start(f32[64,512]{1,0:T(8,128)S(1)} %bitcast_add_fusion.1), channel_id=1, source_target_pairs={{0,0},{1,8},{2,16},{3,24},{4,256},{5,264},{6,272},{7,280},{8,1},{9... | collective-permute-start | bytes 393224 | tf_op jit(solution)/shard_map/ppermute | solution.py:61
  122.0 2.6 %collective-permute-done = f32[64,512]{1,0:T(8,128)S(1)} collective-permute-done((f32[64,512]{1,0:T(8,128)S(1)}, f32[64,512]{1,0:T(8,128)S(1)}, u32[]{:S(2)}, u32[]{:S(2)}) %collective-permute-start) | collective-permute-done | bytes 131104 | tf_op jit(solution)/shard_map/ppermute | solution.py:61
  124.6 20.8 %all_gather.23 = bf16[512,512]{1,0:T(8,128)(2,1)S(1)} all-gather(bf16[64,512]{1,0:T(8,128)(2,1)S(1)} %add_convert_fusion), channel_id=1, replica_groups=mesh['y_lo'=2,'z'=8,'x'=4,'y_hi'=4,'core'=2] {'y_hi','core'}, dimensions={0}, use_global_device_ids=true | all-gather | bytes 589824 | tf_op jit(solution)/shard_map/all_gather | solution.py:64
  145.4 1.0 fusion.6
  146.4 26.0 %all_to_all.25 = bf16[8,64,1536]{2,1,0:T(8,128)(2,1)S(1)} all-to-all(bf16[8,64,1536]{2,1,0:T(8,128)(2,1)S(1)} %get-tuple-element.9), channel_id=1, replica_groups=mesh['y_lo'=2,'z'=8,'x'=4,'y_hi'=4,'core'=2] {'y_lo','x'}, dimensions={0} | all-to-all | bytes 3145728 | tf_op jit(solution)/shard_map/all_to_all | solution.py:41
  172.4 0.0 copy-start
  172.4 0.4 select_reduce_fusion
  172.8 0.6 copy-done
  173.4 0.8 fusion
  (6 shorter events, 0.1 us)
Async XLA Ops:
  2.3 49.1 %all-to-all-start = ((bf16[8,64,1536]{2,1,0:T(8,128)(2,1)}), bf16[8,64,1536]{2,1,0:T(8,128)(2,1)S(1)}, u32[]{:S(2)}, u32[]{:S(2)}) async-start(bf16[8,64,1536]{2,1,0:T(8,128)(2,1)} %broadcast_in_dim.47), calls=%async_computation | async-start | bytes 3145728 | tf_op jit(solution)/shard_map/all_to_all | solution.py:36
  53.6 25.1 %all-to-all-start.1 = ((bf16[8,64,512]{2,1,0:T(8,128)(2,1)}), bf16[8,64,512]{2,1,0:T(8,128)(2,1)S(1)}, u32[]{:S(2)}, u32[]{:S(2)}) async-start(bf16[8,64,512]{2,1,0:T(8,128)(2,1)} %convert_element_type.31), calls=%async_computation.1 | async-start | bytes 1048576 | tf_op jit(solution)/shard_map/all_to_all | solution.py:41
  79.8 21.9 %all-to-all-start.2 = ((bf16[8,64,512]{2,1,0:T(8,128)(2,1)}), bf16[8,64,512]{2,1,0:T(8,128)(2,1)S(1)}, u32[]{:S(2)}, u32[]{:S(2)}) async-start(bf16[8,64,512]{2,1,0:T(8,128)(2,1)} %broadcast_in_dim.51), calls=%async_computation.2 | async-start | bytes 1048576 | tf_op jit(solution)/shard_map/all_to_all | solution.py:36
  104.3 12.4 %all-to-all-start.3 = ((bf16[8,64,512]{2,1,0:T(8,128)(2,1)}), bf16[8,64,512]{2,1,0:T(8,128)(2,1)S(1)}, u32[]{:S(2)}, u32[]{:S(2)}) async-start(bf16[8,64,512]{2,1,0:T(8,128)(2,1)} %get-tuple-element.7), calls=%async_computation.3 | async-start | bytes 1048576 | tf_op jit(solution)/shard_map/all_to_all | solution.py:41
  117.8 6.8 %collective-permute-start = (f32[64,512]{1,0:T(8,128)S(1)}, f32[64,512]{1,0:T(8,128)S(1)}, u32[]{:S(2)}, u32[]{:S(2)}) collective-permute-start(f32[64,512]{1,0:T(8,128)S(1)} %bitcast_add_fusion.1), channel_id=1, source_target_pairs={{0,0},{1,8},{2,16},{3,24},{4,256},{5,264},{6,272},{7,280},{8,1},{9... | collective-permute-start | bytes 393224 | tf_op jit(solution)/shard_map/ppermute | solution.py:61
  172.4 1.0 copy-start

commit v3 on v2

--- a/solution.py
+++ b/solution.py
@@ -10,7 +10,7 @@
 coef_quintic = 2.0315
 
 LO = ("y_lo", "x")
-COL = ("y_hi", "core")
+COL = ("core", "y_hi")
 ROW = ("y_lo", "z", "x")
 EVERY = ("y_lo", "z", "x", "y_hi", "core")
 
@@ -24,11 +24,11 @@
     for y_lo in range(2):
         for z in range(8):
             for x in range(4):
-                for c in range(8):
-                    to_y, to_x = divmod(c, 4)
-                    source = ((y_lo * 8 + z) * 4 + x) * 8 + c
-                    target = ((to_y * 8 + z) * 4 + to_x) * 8 + y_lo * 4 + x
-                    pairs.append((source, target))
+                for y_hi in range(4):
+                    for core in range(2):
+                        source = (((y_lo * 8 + z) * 4 + x) * 4 + y_hi) * 2 + core
+                        target = (((core * 8 + z) * 4 + y_hi) * 4 + x) * 2 + y_lo
+                        pairs.append((source, target))
     return pairs
 
 
@@ -37,10 +37,10 @@
 
 
 def sum_pieces(pieces, axis):
-    me = lax.axis_index(axis)
+    me, count = lax.axis_index(axis), pieces.shape[0]
     arrived = lax.all_to_all(pieces.astype(jnp.bfloat16), axis, 0, 0)
     own = lax.dynamic_index_in_dim(pieces, me, 0, keepdims=False)
-    other = jnp.where(jnp.arange(8)[:, None, None] == me, 0.0, arrived.astype(jnp.float32))
+    other = jnp.where(jnp.arange(count)[:, None, None] == me, 0.0, arrived.astype(jnp.float32))
     return own + other.sum(0)
 
 
@@ -51,8 +51,11 @@
     pair = lax.all_gather(xb, "y_lo", axis=0)
     by_lo = [lax.all_gather(pair[y], "x", axis=0, tiled=True) for y in range(2)]
 
-    tile = jnp.concatenate([dot_nt(part, by_hi) for part in by_lo]) * (1.0 / N)
-    gram = sum_pieces(tile.reshape(8, rows, 8 * rows), COL)
+    core = lax.axis_index("core")
+    away = dot_nt(jnp.where(core == 0, by_lo[1], by_lo[0]), by_hi) * (1.0 / N)
+    home = dot_nt(jnp.where(core == 0, by_lo[0], by_lo[1]), by_hi) * (1.0 / N)
+    home = home + lax.ppermute(away, "core", [(0, 1), (1, 0)])
+    gram = sum_pieces(home.reshape(4, rows, 8 * rows), "y_hi")
 
     rounded = gram.astype(jnp.bfloat16)
     left = lax.all_gather(rounded, COL, axis=0, tiled=True)
@@ -71,7 +74,7 @@
     return jax.shard_map(
         per_device,
         mesh=fine,
-        in_specs=(P(ROW, COL),),
-        out_specs=P(ROW, COL),
+        in_specs=(P(ROW, ("y_hi", "core")),),
+        out_specs=P(ROW, ("y_hi", "core")),
         check_vma=False,
     )

time: 175 us -> 199 us (1.14)
  blocking collectives: 95.2 us -> 122 us
  waiting for transfers between devices: 34.6 us -> 28.2 us
  starting transfers between devices: 32.2 us -> 36.4 us
    all_gather x1, blocking collectives: 20.8 us -> 38.4 us  [per_device(): poly = lax.all_gather(poly, COL, axis=0, tiled=True)]
    all_gather x1, blocking collectives: 18.3 us -> 30.4 us  [per_device(): left = lax.all_gather(rounded, COL, axis=0, tiled=True)]
    all_to_all x2, waiting for transfers between devices: 23.8 us -> 16.3 us  [sum_pieces(): arrived = lax.all_to_all(pieces.astype(jnp.bfloat16), axis, 0, 0)]
    ppermute x0 -> x1, starting transfers between devices: none -> 5.78 us  [per_device(): home = home + lax.ppermute(away, 'core', [(0, 1), (1, 0)])]
    all_to_all x1, blocking collectives: 26 us -> 23 us  [sum_pieces(): arrived = lax.all_to_all(pieces.astype(jnp.bfloat16), axis, 0, 0)]
    all_to_all x2, starting transfers between devices: 13.8 us -> 10.8 us  [sum_pieces(): arrived = lax.all_to_all(pieces.astype(jnp.bfloat16), axis, 0, 0)]
  transfers between devices with their start and end apart: 5 -> 6, of which waited for: 4 -> 5; matrix products, arithmetic and copies ran while one was open for 0% -> 0% of each run, Pallas kernels for 0% -> 0%
where the time goes in v3:
time: 199 us; the launch traced here: 198 us
  blocking collectives  122 us (61%)
  starting transfers between devices  36.4 us (18%)
  waiting for transfers between devices  28.2 us (14%)
  other arithmetic  4.26 us (2%)
  matrix products  3.82 us (2%)
  local copies, waits for them, and re-layouts  2.77 us (1%)
    all_gather x1, blocking collectives, per_device(): poly = lax.all_gather(poly, COL, axis=0, tiled=True)  38.4 us
    all_gather x1, blocking collectives, per_device(): left = lax.all_gather(rounded, COL, axis=0, tiled=True)  30.4 us
    all_gather x2, blocking collectives, per_device(): by_lo = [lax.all_gather(pair[y], 'x', axis=0, tiled=True) for y in range(2)]  24.4 us
    all_to_all x1, blocking collectives, sum_pieces(): arrived = lax.all_to_all(pieces.astype(jnp.bfloat16), axis, 0, 0)  23 us
    all_to_all x2, waiting for transfers between devices, sum_pieces(): arrived = lax.all_to_all(pieces.astype(jnp.bfloat16), axis, 0, 0)  16.3 us
    all_to_all x2, starting transfers between devices, spread(): lax.all_to_all(jnp.broadcast_to(block[None], (8,) + block.shape), axis, 0...  14.4 us
    all_to_all x2, starting transfers between devices, sum_pieces(): arrived = lax.all_to_all(pieces.astype(jnp.bfloat16), axis, 0, 0)  10.8 us
    all_to_all x2, waiting for transfers between devices, spread(): lax.all_to_all(jnp.broadcast_to(block[None], (8,) + block.shape), axis, 0...  7.77 us
  transfers between devices with their start and end apart: 6, of which 5 were waited for; matrix products, arithmetic and copies ran while one was open for 0% of the time, Pallas kernels for 0%

profile of v3, /device:TPU:1, one launch (start us, length us, event | category | flops | bytes accessed | tf_op | source)
XLA Modules:
  0.0 197.9 jit_solution(15135418079491890573)
XLA Ops:
  0.0 1.0 convert_element_type.30
  1.0 1.3 broadcast_in_dim.53
  2.3 10.9 %all-to-all-start = ((bf16[8,64,1536]{2,1,0:T(8,128)(2,1)}), bf16[8,64,1536]{2,1,0:T(8,128)(2,1)S(1)}, u32[]{:S(2)}, u32[]{:S(2)}) async-start(bf16[8,64,1536]{2,1,0:T(8,128)(2,1)} %broadcast_in_dim.53), calls=%async_computation | async-start | bytes 3145728 | tf_op jit(solution)/shard_map/all_to_all | solution.py:36
  13.2 6.1 %all-gather = bf16[128,1536]{1,0:T(8,128)(2,1)S(1)} all-gather(bf16[64,1536]{1,0:T(8,128)(2,1)S(1)} %convert_element_type.30), channel_id=2, replica_groups=mesh['y_lo'=2,'z'=8,'x'=4,'y_hi'=4,'core'=2] {'y_lo'}, dimensions={0}, use_global_device_ids=true | all-gather | bytes 589824 | tf_op jit(solution)/shard_map/all_gather | solution.py:51
  19.3 12.6 %all-gather.3 = bf16[256,1536]{1,0:T(8,128)(2,1)S(1)} all-gather(bf16[64,1536]{1,0:T(8,128)(2,1)S(1)} %get-tuple-element.5), channel_id=5, replica_groups=mesh['y_lo'=2,'z'=8,'x'=4,'y_hi'=4,'core'=2] {'x'}, dimensions={0}, use_global_device_ids=true | all-gather | bytes 983040 | tf_op jit(solution)/shard_map/all_gather | solution.py:52
  31.9 11.7 %all-gather.4 = bf16[256,1536]{1,0:T(8,128)(2,1)} all-gather(bf16[64,1536]{1,0:T(8,128)(2,1)S(1)} %get-tuple-element.6), channel_id=6, replica_groups=mesh['y_lo'=2,'z'=8,'x'=4,'y_hi'=4,'core'=2] {'x'}, dimensions={0}, use_global_device_ids=true | all-gather | bytes 983040 | tf_op jit(solution)/shard_map/all_gather | solution.py:52
  43.7 7.8 %all-to-all-done = bf16[8,64,1536]{2,1,0:T(8,128)(2,1)S(1)} async-done(((bf16[8,64,1536]{2,1,0:T(8,128)(2,1)}), bf16[8,64,1536]{2,1,0:T(8,128)(2,1)S(1)}, u32[]{:S(2)}, u32[]{:S(2)}) %all-to-all-start) | async-done | bytes 1572896 | tf_op jit(solution)/shard_map/all_to_all | solution.py:36
  51.4 0.0 copy-start
  51.4 0.6 convolution_multiply_fusion
  52.0 5.8 %collective-permute-start = (f32[256,512]{1,0:T(8,128)S(1)}, f32[256,512]{1,0:T(8,128)S(1)}, u32[]{:S(2)}, u32[]{:S(2)}) collective-permute-start(f32[256,512]{1,0:T(8,128)S(1)} %convolution_multiply_fusion), channel_id=1, source_target_pairs={{0,1},{1,0},{2,3},{3,2},{4,5},{5,4},{6,7},{7,6},{8,9},{9,8},{10,11... | collective-permute-start | bytes 1572872 | tf_op jit(solution)/shard_map/ppermute | solution.py:57
  57.8 1.5 collective-permute-done
  59.3 0.0 copy-done
  59.3 0.6 fusion
  60.0 0.7 convert_element_type.31
  60.7 6.8 %all-to-all-start.1 = ((bf16[4,64,512]{2,1,0:T(8,128)(2,1)}), bf16[4,64,512]{2,1,0:T(8,128)(2,1)S(1)}, u32[]{:S(2)}, u32[]{:S(2)}) async-start(bf16[4,64,512]{2,1,0:T(8,128)(2,1)} %convert_element_type.31), calls=%async_computation.1 | async-start | bytes 524288 | tf_op jit(solution)/shard_map/all_to_all | solution.py:41
  67.5 8.6 %all-to-all-done.1 = bf16[4,64,512]{2,1,0:T(8,128)(2,1)S(1)} async-done(((bf16[4,64,512]{2,1,0:T(8,128)(2,1)}), bf16[4,64,512]{2,1,0:T(8,128)(2,1)S(1)}, u32[]{:S(2)}, u32[]{:S(2)}) %all-to-all-start.1) | async-done | bytes 262176 | tf_op jit(solution)/shard_map/all_to_all | solution.py:41
  76.1 0.1 select_reduce_fusion.2
  76.3 0.8 broadcast_in_dim.57
  77.1 3.5 %all-to-all-start.2 = ((bf16[8,64,512]{2,1,0:T(8,128)(2,1)}), bf16[8,64,512]{2,1,0:T(8,128)(2,1)S(1)}, u32[]{:S(2)}, u32[]{:S(2)}) async-start(bf16[8,64,512]{2,1,0:T(8,128)(2,1)} %broadcast_in_dim.57), calls=%async_computation.2 | async-start | bytes 1048576 | tf_op jit(solution)/shard_map/all_to_all | solution.py:36
  80.6 30.4 %all_gather.22 = bf16[512,512]{1,0:T(8,128)(2,1)S(1)} all-gather(bf16[64,512]{1,0:T(8,128)(2,1)S(1)} %fusion.8), channel_id=1, replica_groups=mesh['y_lo'=2,'z'=8,'x'=4,'y_hi'=4,'core'=2] {'core','y_hi'}, dimensions={0}, use_global_device_ids=true | all-gather | bytes 589824 | tf_op jit(solution)/shard_map/all_gather | solution.py:61
  111.1 0.0 all-to-all-done.2
  111.1 1.6 fusion.10
  112.7 4.0 %all-to-all-start.3 = ((bf16[8,64,512]{2,1,0:T(8,128)(2,1)}), bf16[8,64,512]{2,1,0:T(8,128)(2,1)S(1)}, u32[]{:S(2)}, u32[]{:S(2)}) async-start(bf16[8,64,512]{2,1,0:T(8,128)(2,1)} %get-tuple-element.7), calls=%async_computation.3 | async-start | bytes 1048576 | tf_op jit(solution)/shard_map/all_to_all | solution.py:41
  116.7 7.7 %all-to-all-done.3 = bf16[8,64,512]{2,1,0:T(8,128)(2,1)S(1)} async-done(((bf16[8,64,512]{2,1,0:T(8,128)(2,1)}), bf16[8,64,512]{2,1,0:T(8,128)(2,1)S(1)}, u32[]{:S(2)}, u32[]{:S(2)}) %all-to-all-start.3) | async-done | bytes 524320 | tf_op jit(solution)/shard_map/all_to_all | solution.py:41
  124.4 0.2 select_reduce_fusion.1
  124.6 0.9 bitcast_add_fusion.1
  125.5 5.4 %collective-permute-start.1 = (f32[64,512]{1,0:T(8,128)S(1)}, f32[64,512]{1,0:T(8,128)S(1)}, u32[]{:S(2)}, u32[]{:S(2)}) collective-permute-start(f32[64,512]{1,0:T(8,128)S(1)} %bitcast_add_fusion.1), channel_id=1, source_target_pairs={{0,0},{1,256},{2,8},{3,264},{4,16},{5,272},{6,24},{7,280},{8,2},{9... | collective-permute-start | bytes 393224 | tf_op jit(solution)/shard_map/ppermute | solution.py:64
  130.9 2.6 %collective-permute-done.1 = f32[64,512]{1,0:T(8,128)S(1)} collective-permute-done((f32[64,512]{1,0:T(8,128)S(1)}, f32[64,512]{1,0:T(8,128)S(1)}, u32[]{:S(2)}, u32[]{:S(2)}) %collective-permute-start.1) | collective-permute-done | bytes 131104 | tf_op jit(solution)/shard_map/ppermute | solution.py:64
  133.6 38.4 %all_gather.23 = bf16[512,512]{1,0:T(8,128)(2,1)S(1)} all-gather(bf16[64,512]{1,0:T(8,128)(2,1)S(1)} %add_convert_fusion), channel_id=1, replica_groups=mesh['y_lo'=2,'z'=8,'x'=4,'y_hi'=4,'core'=2] {'core','y_hi'}, dimensions={0}, use_global_device_ids=true | all-gather | bytes 589824 | tf_op jit(solution)/shard_map/all_gather | solution.py:67
  172.0 1.0 fusion.11
  173.0 23.0 %all_to_all.25 = bf16[8,64,1536]{2,1,0:T(8,128)(2,1)S(1)} all-to-all(bf16[8,64,1536]{2,1,0:T(8,128)(2,1)S(1)} %get-tuple-element.9), channel_id=1, replica_groups=mesh['y_lo'=2,'z'=8,'x'=4,'y_hi'=4,'core'=2] {'y_lo','x'}, dimensions={0} | all-to-all | bytes 3145728 | tf_op jit(solution)/shard_map/all_to_all | solution.py:41
  196.0 0.0 copy-start.1
  196.0 0.4 select_reduce_fusion
  196.4 0.6 copy-done.1
  197.0 0.8 fusion.5
  (6 shorter events, 0.1 us)
Async XLA Ops:
  2.3 49.1 %all-to-all-start = ((bf16[8,64,1536]{2,1,0:T(8,128)(2,1)}), bf16[8,64,1536]{2,1,0:T(8,128)(2,1)S(1)}, u32[]{:S(2)}, u32[]{:S(2)}) async-start(bf16[8,64,1536]{2,1,0:T(8,128)(2,1)} %broadcast_in_dim.53), calls=%async_computation | async-start | bytes 3145728 | tf_op jit(solution)/shard_map/all_to_all | solution.py:36
  51.4 7.9 %copy-start = (bf16[256,1536]{1,0:T(8,128)(2,1)S(1)}, bf16[256,1536]{1,0:T(8,128)(2,1)}, u32[]{:S(2)}) copy-start(bf16[256,1536]{1,0:T(8,128)(2,1)} %all-gather.4) | copy-start | bytes 2359300
  52.0 7.3 %collective-permute-start = (f32[256,512]{1,0:T(8,128)S(1)}, f32[256,512]{1,0:T(8,128)S(1)}, u32[]{:S(2)}, u32[]{:S(2)}) collective-permute-start(f32[256,512]{1,0:T(8,128)S(1)} %convolution_multiply_fusion), channel_id=1, source_target_pairs={{0,1},{1,0},{2,3},{3,2},{4,5},{5,4},{6,7},{7,6},{8,9},{9,8},{10,11... | collective-permute-start | bytes 1572872 | tf_op jit(solution)/shard_map/ppermute | solution.py:57
  60.7 15.4 %all-to-all-start.1 = ((bf16[4,64,512]{2,1,0:T(8,128)(2,1)}), bf16[4,64,512]{2,1,0:T(8,128)(2,1)S(1)}, u32[]{:S(2)}, u32[]{:S(2)}) async-start(bf16[4,64,512]{2,1,0:T(8,128)(2,1)} %convert_element_type.31), calls=%async_computation.1 | async-start | bytes 524288 | tf_op jit(solution)/shard_map/all_to_all | solution.py:41
  77.1 34.0 %all-to-all-start.2 = ((bf16[8,64,512]{2,1,0:T(8,128)(2,1)}), bf16[8,64,512]{2,1,0:T(8,128)(2,1)S(1)}, u32[]{:S(2)}, u32[]{:S(2)}) async-start(bf16[8,64,512]{2,1,0:T(8,128)(2,1)} %broadcast_in_dim.57), calls=%async_computation.2 | async-start | bytes 1048576 | tf_op jit(solution)/shard_map/all_to_all | solution.py:36
  112.7 11.7 %all-to-all-start.3 = ((bf16[8,64,512]{2,1,0:T(8,128)(2,1)}), bf16[8,64,512]{2,1,0:T(8,128)(2,1)S(1)}, u32[]{:S(2)}, u32[]{:S(2)}) async-start(bf16[8,64,512]{2,1,0:T(8,128)(2,1)} %get-tuple-element.7), calls=%async_computation.3 | async-start | bytes 1048576 | tf_op jit(solution)/shard_map/all_to_all | solution.py:41
  125.5 8.1 %collective-permute-start.1 = (f32[64,512]{1,0:T(8,128)S(1)}, f32[64,512]{1,0:T(8,128)S(1)}, u32[]{:S(2)}, u32[]{:S(2)}) collective-permute-start(f32[64,512]{1,0:T(8,128)S(1)} %bitcast_add_fusion.1), channel_id=1, source_target_pairs={{0,0},{1,256},{2,8},{3,264},{4,16},{5,272},{6,24},{7,280},{8,2},{9... | collective-permute-start | bytes 393224 | tf_op jit(solution)/shard_map/ppermute | solution.py:64
  196.0 1.0 copy-start.1

commit v4 on v3

--- a/solution.py
+++ b/solution.py
@@ -9,8 +9,8 @@
 coef_cubic = -4.775
 coef_quintic = 2.0315
 
-LO = ("y_lo", "x")
-COL = ("core", "y_hi")
+LO = ("x", "y_lo")
+COL = ("y_hi", "core")
 ROW = ("y_lo", "z", "x")
 EVERY = ("y_lo", "z", "x", "y_hi", "core")
 
@@ -74,7 +74,7 @@
     return jax.shard_map(
         per_device,
         mesh=fine,
-        in_specs=(P(ROW, ("y_hi", "core")),),
-        out_specs=P(ROW, ("y_hi", "core")),
+        in_specs=(P(ROW, COL),),
+        out_specs=P(ROW, COL),
         check_vma=False,
     )

time: 199 us -> 175 us (0.88)
  blocking collectives: 122 us -> 98.4 us
    all_gather x1, blocking collectives: 38.4 us -> 24.7 us  [per_device(): poly = lax.all_gather(poly, COL, axis=0, tiled=True)]
    all_gather x1, blocking collectives: 30.4 us -> 18.4 us  [per_device(): left = lax.all_gather(rounded, COL, axis=0, tiled=True)]
where the time goes in v4:
time: 175 us; the launch traced here: 174 us
  blocking collectives  98.4 us (56%)
  starting transfers between devices  35 us (20%)
  waiting for transfers between devices  29.9 us (17%)
  other arithmetic  4.26 us (2%)
  matrix products  3.81 us (2%)
  local copies, waits for them, and re-layouts  2.77 us (2%)
    all_to_all x1, blocking collectives, sum_pieces(): arrived = lax.all_to_all(pieces.astype(jnp.bfloat16), axis, 0, 0)  24.9 us
    all_gather x1, blocking collectives, per_device(): poly = lax.all_gather(poly, COL, axis=0, tiled=True)  24.7 us
    all_gather x2, blocking collectives, per_device(): by_lo = [lax.all_gather(pair[y], 'x', axis=0, tiled=True) for y in range(2)]  24.4 us
    all_gather x1, blocking collectives, per_device(): left = lax.all_gather(rounded, COL, axis=0, tiled=True)  18.4 us
    all_to_all x2, waiting for transfers between devices, sum_pieces(): arrived = lax.all_to_all(pieces.astype(jnp.bfloat16), axis, 0, 0)  17.9 us
    all_to_all x2, starting transfers between devices, spread(): lax.all_to_all(jnp.broadcast_to(block[None], (8,) + block.shape), axis, 0...  14.4 us
    all_to_all x2, starting transfers between devices, sum_pieces(): arrived = lax.all_to_all(pieces.astype(jnp.bfloat16), axis, 0, 0)  10.8 us
    all_to_all x2, waiting for transfers between devices, spread(): lax.all_to_all(jnp.broadcast_to(block[None], (8,) + block.shape), axis, 0...  7.77 us
  transfers between devices with their start and end apart: 6, of which 5 were waited for; matrix products, arithmetic and copies ran while one was open for 0% of the time, Pallas kernels for 0%

profile of v4, /device:TPU:1, one launch (start us, length us, event | category | flops | bytes accessed | tf_op | source)
XLA Modules:
  0.0 174.2 jit_solution(16787879764926988999)
XLA Ops:
  0.0 1.0 convert_element_type.30
  1.0 1.3 broadcast_in_dim.53
  2.3 10.9 %all-to-all-start = ((bf16[8,64,1536]{2,1,0:T(8,128)(2,1)}), bf16[8,64,1536]{2,1,0:T(8,128)(2,1)S(1)}, u32[]{:S(2)}, u32[]{:S(2)}) async-start(bf16[8,64,1536]{2,1,0:T(8,128)(2,1)} %broadcast_in_dim.53), calls=%async_computation | async-start | bytes 3145728 | tf_op jit(solution)/shard_map/all_to_all | solution.py:36
  13.2 6.1 %all-gather = bf16[128,1536]{1,0:T(8,128)(2,1)S(1)} all-gather(bf16[64,1536]{1,0:T(8,128)(2,1)S(1)} %convert_element_type.30), channel_id=2, replica_groups=mesh['y_lo'=2,'z'=8,'x'=4,'y_hi'=4,'core'=2] {'y_lo'}, dimensions={0}, use_global_device_ids=true | all-gather | bytes 589824 | tf_op jit(solution)/shard_map/all_gather | solution.py:51
  19.3 12.6 %all-gather.3 = bf16[256,1536]{1,0:T(8,128)(2,1)S(1)} all-gather(bf16[64,1536]{1,0:T(8,128)(2,1)S(1)} %get-tuple-element.5), channel_id=5, replica_groups=mesh['y_lo'=2,'z'=8,'x'=4,'y_hi'=4,'core'=2] {'x'}, dimensions={0}, use_global_device_ids=true | all-gather | bytes 983040 | tf_op jit(solution)/shard_map/all_gather | solution.py:52
  31.9 11.7 %all-gather.4 = bf16[256,1536]{1,0:T(8,128)(2,1)} all-gather(bf16[64,1536]{1,0:T(8,128)(2,1)S(1)} %get-tuple-element.6), channel_id=6, replica_groups=mesh['y_lo'=2,'z'=8,'x'=4,'y_hi'=4,'core'=2] {'x'}, dimensions={0}, use_global_device_ids=true | all-gather | bytes 983040 | tf_op jit(solution)/shard_map/all_gather | solution.py:52
  43.7 7.8 %all-to-all-done = bf16[8,64,1536]{2,1,0:T(8,128)(2,1)S(1)} async-done(((bf16[8,64,1536]{2,1,0:T(8,128)(2,1)}), bf16[8,64,1536]{2,1,0:T(8,128)(2,1)S(1)}, u32[]{:S(2)}, u32[]{:S(2)}) %all-to-all-start) | async-done | bytes 1572896 | tf_op jit(solution)/shard_map/all_to_all | solution.py:36
  51.4 0.0 copy-start
  51.4 0.6 convolution_multiply_fusion
  52.0 5.8 %collective-permute-start = (f32[256,512]{1,0:T(8,128)S(1)}, f32[256,512]{1,0:T(8,128)S(1)}, u32[]{:S(2)}, u32[]{:S(2)}) collective-permute-start(f32[256,512]{1,0:T(8,128)S(1)} %convolution_multiply_fusion), channel_id=1, source_target_pairs={{0,1},{1,0},{2,3},{3,2},{4,5},{5,4},{6,7},{7,6},{8,9},{9,8},{10,11... | collective-permute-start | bytes 1572872 | tf_op jit(solution)/shard_map/ppermute | solution.py:57
  57.8 1.5 collective-permute-done
  59.3 0.0 copy-done
  59.3 0.6 fusion
  60.0 0.7 convert_element_type.31
  60.7 6.8 %all-to-all-start.1 = ((bf16[4,64,512]{2,1,0:T(8,128)(2,1)}), bf16[4,64,512]{2,1,0:T(8,128)(2,1)S(1)}, u32[]{:S(2)}, u32[]{:S(2)}) async-start(bf16[4,64,512]{2,1,0:T(8,128)(2,1)} %convert_element_type.31), calls=%async_computation.1 | async-start | bytes 524288 | tf_op jit(solution)/shard_map/all_to_all | solution.py:41
  67.5 8.6 %all-to-all-done.1 = bf16[4,64,512]{2,1,0:T(8,128)(2,1)S(1)} async-done(((bf16[4,64,512]{2,1,0:T(8,128)(2,1)}), bf16[4,64,512]{2,1,0:T(8,128)(2,1)S(1)}, u32[]{:S(2)}, u32[]{:S(2)}) %all-to-all-start.1) | async-done | bytes 262176 | tf_op jit(solution)/shard_map/all_to_all | solution.py:41
  76.1 0.1 select_reduce_fusion.2
  76.3 0.8 broadcast_in_dim.57
  77.1 3.5 %all-to-all-start.2 = ((bf16[8,64,512]{2,1,0:T(8,128)(2,1)}), bf16[8,64,512]{2,1,0:T(8,128)(2,1)S(1)}, u32[]{:S(2)}, u32[]{:S(2)}) async-start(bf16[8,64,512]{2,1,0:T(8,128)(2,1)} %broadcast_in_dim.57), calls=%async_computation.2 | async-start | bytes 1048576 | tf_op jit(solution)/shard_map/all_to_all | solution.py:36
  80.6 18.4 %all_gather.22 = bf16[512,512]{1,0:T(8,128)(2,1)S(1)} all-gather(bf16[64,512]{1,0:T(8,128)(2,1)S(1)} %fusion.8), channel_id=1, replica_groups=mesh['y_lo'=2,'z'=8,'x'=4,'y_hi'=4,'core'=2] {'y_hi','core'}, dimensions={0}, use_global_device_ids=true | all-gather | bytes 589824 | tf_op jit(solution)/shard_map/all_gather | solution.py:61
  99.0 0.0 all-to-all-done.2
  99.0 1.6 fusion.10
  100.7 4.0 %all-to-all-start.3 = ((bf16[8,64,512]{2,1,0:T(8,128)(2,1)}), bf16[8,64,512]{2,1,0:T(8,128)(2,1)S(1)}, u32[]{:S(2)}, u32[]{:S(2)}) async-start(bf16[8,64,512]{2,1,0:T(8,128)(2,1)} %get-tuple-element.7), calls=%async_computation.3 | async-start | bytes 1048576 | tf_op jit(solution)/shard_map/all_to_all | solution.py:41
  104.7 9.3 %all-to-all-done.3 = bf16[8,64,512]{2,1,0:T(8,128)(2,1)S(1)} async-done(((bf16[8,64,512]{2,1,0:T(8,128)(2,1)}), bf16[8,64,512]{2,1,0:T(8,128)(2,1)S(1)}, u32[]{:S(2)}, u32[]{:S(2)}) %all-to-all-start.3) | async-done | bytes 524320 | tf_op jit(solution)/shard_map/all_to_all | solution.py:41
  114.0 0.2 select_reduce_fusion.1
  114.2 0.9 bitcast_add_fusion.1
  115.1 4.1 %collective-permute-start.1 = (f32[64,512]{1,0:T(8,128)S(1)}, f32[64,512]{1,0:T(8,128)S(1)}, u32[]{:S(2)}, u32[]{:S(2)}) collective-permute-start(f32[64,512]{1,0:T(8,128)S(1)} %bitcast_add_fusion.1), channel_id=1, source_target_pairs={{0,0},{1,256},{2,8},{3,264},{4,16},{5,272},{6,24},{7,280},{8,2},{9... | collective-permute-start | bytes 393224 | tf_op jit(solution)/shard_map/ppermute | solution.py:64
  119.2 2.6 %collective-permute-done.1 = f32[64,512]{1,0:T(8,128)S(1)} collective-permute-done((f32[64,512]{1,0:T(8,128)S(1)}, f32[64,512]{1,0:T(8,128)S(1)}, u32[]{:S(2)}, u32[]{:S(2)}) %collective-permute-start.1) | collective-permute-done | bytes 131104 | tf_op jit(solution)/shard_map/ppermute | solution.py:64
  121.9 24.7 %all_gather.23 = bf16[512,512]{1,0:T(8,128)(2,1)S(1)} all-gather(bf16[64,512]{1,0:T(8,128)(2,1)S(1)} %add_convert_fusion), channel_id=1, replica_groups=mesh['y_lo'=2,'z'=8,'x'=4,'y_hi'=4,'core'=2] {'y_hi','core'}, dimensions={0}, use_global_device_ids=true | all-gather | bytes 589824 | tf_op jit(solution)/shard_map/all_gather | solution.py:67
  146.5 1.0 fusion.11
  147.5 24.9 %all_to_all.25 = bf16[8,64,1536]{2,1,0:T(8,128)(2,1)S(1)} all-to-all(bf16[8,64,1536]{2,1,0:T(8,128)(2,1)S(1)} %get-tuple-element.9), channel_id=1, replica_groups=mesh['y_lo'=2,'z'=8,'x'=4,'y_hi'=4,'core'=2] {'x','y_lo'}, dimensions={0} | all-to-all | bytes 3145728 | tf_op jit(solution)/shard_map/all_to_all | solution.py:41
  172.4 0.0 copy-start.1
  172.4 0.4 select_reduce_fusion
  172.8 0.6 copy-done.1
  173.4 0.8 fusion.5
  (6 shorter events, 0.1 us)
Async XLA Ops:
  2.3 49.1 %all-to-all-start = ((bf16[8,64,1536]{2,1,0:T(8,128)(2,1)}), bf16[8,64,1536]{2,1,0:T(8,128)(2,1)S(1)}, u32[]{:S(2)}, u32[]{:S(2)}) async-start(bf16[8,64,1536]{2,1,0:T(8,128)(2,1)} %broadcast_in_dim.53), calls=%async_computation | async-start | bytes 3145728 | tf_op jit(solution)/shard_map/all_to_all | solution.py:36
  51.4 7.9 %copy-start = (bf16[256,1536]{1,0:T(8,128)(2,1)S(1)}, bf16[256,1536]{1,0:T(8,128)(2,1)}, u32[]{:S(2)}) copy-start(bf16[256,1536]{1,0:T(8,128)(2,1)} %all-gather.4) | copy-start | bytes 2359300
  52.0 7.3 %collective-permute-start = (f32[256,512]{1,0:T(8,128)S(1)}, f32[256,512]{1,0:T(8,128)S(1)}, u32[]{:S(2)}, u32[]{:S(2)}) collective-permute-start(f32[256,512]{1,0:T(8,128)S(1)} %convolution_multiply_fusion), channel_id=1, source_target_pairs={{0,1},{1,0},{2,3},{3,2},{4,5},{5,4},{6,7},{7,6},{8,9},{9,8},{10,11... | collective-permute-start | bytes 1572872 | tf_op jit(solution)/shard_map/ppermute | solution.py:57
  60.7 15.4 %all-to-all-start.1 = ((bf16[4,64,512]{2,1,0:T(8,128)(2,1)}), bf16[4,64,512]{2,1,0:T(8,128)(2,1)S(1)}, u32[]{:S(2)}, u32[]{:S(2)}) async-start(bf16[4,64,512]{2,1,0:T(8,128)(2,1)} %convert_element_type.31), calls=%async_computation.1 | async-start | bytes 524288 | tf_op jit(solution)/shard_map/all_to_all | solution.py:41
  77.1 21.9 %all-to-all-start.2 = ((bf16[8,64,512]{2,1,0:T(8,128)(2,1)}), bf16[8,64,512]{2,1,0:T(8,128)(2,1)S(1)}, u32[]{:S(2)}, u32[]{:S(2)}) async-start(bf16[8,64,512]{2,1,0:T(8,128)(2,1)} %broadcast_in_dim.57), calls=%async_computation.2 | async-start | bytes 1048576 | tf_op jit(solution)/shard_map/all_to_all | solution.py:36
  100.7 13.4 %all-to-all-start.3 = ((bf16[8,64,512]{2,1,0:T(8,128)(2,1)}), bf16[8,64,512]{2,1,0:T(8,128)(2,1)S(1)}, u32[]{:S(2)}, u32[]{:S(2)}) async-start(bf16[8,64,512]{2,1,0:T(8,128)(2,1)} %get-tuple-element.7), calls=%async_computation.3 | async-start | bytes 1048576 | tf_op jit(solution)/shard_map/all_to_all | solution.py:41
  115.1 6.7 %collective-permute-start.1 = (f32[64,512]{1,0:T(8,128)S(1)}, f32[64,512]{1,0:T(8,128)S(1)}, u32[]{:S(2)}, u32[]{:S(2)}) collective-permute-start(f32[64,512]{1,0:T(8,128)S(1)} %bitcast_add_fusion.1), channel_id=1, source_target_pairs={{0,0},{1,256},{2,8},{3,264},{4,16},{5,272},{6,24},{7,280},{8,2},{9... | collective-permute-start | bytes 393224 | tf_op jit(solution)/shard_map/ppermute | solution.py:64
  172.4 1.0 copy-start.1

commit v5 on v4

--- a/solution.py
+++ b/solution.py
@@ -19,17 +19,30 @@
     return lax.dot_general(a, b, (((1,), (1,)), ((), ())), preferred_element_type=jnp.float32)
 
 
-def swap_lo_col():
+def pairs_to(place):
     pairs = []
     for y_lo in range(2):
         for z in range(8):
             for x in range(4):
                 for y_hi in range(4):
                     for core in range(2):
+                        to_lo, to_x, to_hi, to_core = place(y_lo, x, y_hi, core)
                         source = (((y_lo * 8 + z) * 4 + x) * 4 + y_hi) * 2 + core
-                        target = (((core * 8 + z) * 4 + y_hi) * 4 + x) * 2 + y_lo
+                        target = (((to_lo * 8 + z) * 4 + to_x) * 4 + to_hi) * 2 + to_core
                         pairs.append((source, target))
     return pairs
+
+
+def swap_lo_col(block):
+    return lax.ppermute(block, EVERY, pairs_to(lambda y_lo, x, y_hi, core: (core, y_hi, x, y_lo)))
+
+
+def swap_y_lo_core(block):
+    return lax.ppermute(block, EVERY, pairs_to(lambda y_lo, x, y_hi, core: (core, x, y_hi, y_lo)))
+
+
+def from_x(block, step):
+    return lax.ppermute(block, "x", [(i, (i - step) % 4) for i in range(4)])
 
 
 def spread(block, axis):
@@ -57,16 +70,35 @@
     home = home + lax.ppermute(away, "core", [(0, 1), (1, 0)])
     gram = sum_pieces(home.reshape(4, rows, 8 * rows), "y_hi")
 
+    depth = by_hi.shape[0]
+    ahead, behind = from_x(by_hi, 1), from_x(by_hi, -1)
+    across = from_x(ahead[: depth // 2], 1), from_x(behind[depth // 2 :], -1)
+
     rounded = gram.astype(jnp.bfloat16)
     left = lax.all_gather(rounded, COL, axis=0, tiled=True)
     right = spread(rounded, "z").reshape(8 * rows, 8 * rows)
+    gram = swap_lo_col(gram)
     square = sum_pieces(dot_nt(left, right).reshape(8, rows, 8 * rows), LO)
-    square = lax.ppermute(square, EVERY, swap_lo_col())
 
-    poly = (coef_cubic * gram + coef_quintic * square).astype(jnp.bfloat16)
-    poly = lax.all_gather(poly, COL, axis=0, tiled=True)
-    product = jnp.dot(poly, by_hi, preferred_element_type=jnp.float32)
-    return coef_linear * x_scaled + sum_pieces(product.reshape(8, rows, cols), LO)
+    poly = swap_y_lo_core((coef_cubic * gram + coef_quintic * square).astype(jnp.bfloat16))
+    poly = lax.all_gather(poly, COL, axis=0).reshape(4, 2, rows, depth)
+    x_at, y_at = lax.axis_index("x"), lax.axis_index("y_lo")
+
+    def product(y):
+        def at(step):
+            return lax.dynamic_slice(poly, ((x_at + step) % 4, y, 0, 0), (1, 1, rows, depth))[0, 0]
+
+        def times(a, b):
+            return jnp.dot(a, b, preferred_element_type=jnp.float32)
+
+        far = at(2)
+        return (
+            times(at(0), by_hi) + times(at(1), ahead) + times(at(3), behind)
+            + times(far[:, : depth // 2], across[0]) + times(far[:, depth // 2 :], across[1])
+        )
+
+    away = lax.ppermute(product(1 - y_at).astype(jnp.bfloat16), "y_lo", [(0, 1), (1, 0)])
+    return coef_linear * x_scaled + product(y_at) + away.astype(jnp.float32)
 
 
 def solution(mesh):

time: 175 us -> 178 us (1.017)
  blocking collectives: 98.4 us -> 67.7 us
  starting transfers between devices: 35 us -> 58.7 us
  matrix products: 3.81 us -> 11 us
    all_to_all x1 -> x0, blocking collectives: 24.9 us -> none  [sum_pieces(): arrived = lax.all_to_all(pieces.astype(jnp.bfloat16), axis, 0, 0)]
    ppermute x1 -> x7, starting transfers between devices: 4.05 us -> 27 us  [the longest x4 13.2 us: from_x(): return lax.ppermute(block, 'x', [(i, (i - step) % 4) for i in range(4)])]
    all_gather x1, blocking collectives: 24.7 us -> 17.7 us  [per_device(): poly = lax.all_gather(poly, COL, axis=0).reshape(4, 2, rows, depth)]
    dot_general x1 -> x10, matrix products: 0.98 us -> 6.95 us  [times(): return jnp.dot(a, b, preferred_element_type=jnp.float32)]
    all_to_all x2, waiting for transfers between devices: 17.9 us -> 15.2 us  [sum_pieces(): arrived = lax.all_to_all(pieces.astype(jnp.bfloat16), axis, 0, 0)]
    ppermute x1 -> x7, waiting for transfers between devices: 2.64 us -> 5 us  [the longest x1 4.48 us: per_device(): lax.ppermute(product(1 - y_at).astype(jnp.bfloat16), 'y_lo', [(0, 1), (1,...]
  transfers between devices with their start and end apart: 6 -> 12, of which waited for: 5 -> 6; matrix products, arithmetic and copies ran while one was open for 0% -> 5% of each run, Pallas kernels for 0% -> 0%
where the time goes in v5:
time: 178 us; the launch traced here: 176 us
  blocking collectives  67.7 us (38%)
  starting transfers between devices  58.7 us (33%)
  waiting for transfers between devices  29.4 us (17%)
  matrix products  11 us (6%)
  other arithmetic  5.08 us (3%)
  local copies, waits for them, and re-layouts  3.45 us (2%)
    all_gather x2, blocking collectives, per_device(): by_lo = [lax.all_gather(pair[y], 'x', axis=0, tiled=True) for y in range(2)]  24.4 us
    all_gather x1, blocking collectives, per_device(): left = lax.all_gather(rounded, COL, axis=0, tiled=True)  19.5 us
    all_gather x1, blocking collectives, per_device(): poly = lax.all_gather(poly, COL, axis=0).reshape(4, 2, rows, depth)  17.7 us
    all_to_all x2, waiting for transfers between devices, sum_pieces(): arrived = lax.all_to_all(pieces.astype(jnp.bfloat16), axis, 0, 0)  15.2 us
    all_to_all x2, starting transfers between devices, spread(): lax.all_to_all(jnp.broadcast_to(block[None], (8,) + block.shape), axis, 0...  15 us
    ppermute x4, starting transfers between devices, from_x(): return lax.ppermute(block, 'x', [(i, (i - step) % 4) for i in range(4)])  13.2 us
    all_to_all x2, starting transfers between devices, sum_pieces(): arrived = lax.all_to_all(pieces.astype(jnp.bfloat16), axis, 0, 0)  11 us
    all_to_all x2, waiting for transfers between devices, spread(): lax.all_to_all(jnp.broadcast_to(block[None], (8,) + block.shape), axis, 0...  7.77 us
  transfers between devices with their start and end apart: 12, of which 6 were waited for; matrix products, arithmetic and copies ran while one was open for 5% of the time, Pallas kernels for 0%

profile of v5, /device:TPU:1, one launch (start us, length us, event | category | flops | bytes accessed | tf_op | source)
XLA Modules:
  0.0 175.7 jit_solution(10568149184267237155)
XLA Ops:
  0.0 1.0 convert_element_type.30
  1.0 1.3 broadcast_in_dim.40
  2.3 10.9 %all-to-all-start = ((bf16[8,64,1536]{2,1,0:T(8,128)(2,1)}), bf16[8,64,1536]{2,1,0:T(8,128)(2,1)S(1)}, u32[]{:S(2)}, u32[]{:S(2)}) async-start(bf16[8,64,1536]{2,1,0:T(8,128)(2,1)} %broadcast_in_dim.40), calls=%async_computation | async-start | bytes 3145728 | tf_op jit(solution)/shard_map/all_to_all | solution.py:49
  13.2 6.1 %all-gather = bf16[128,1536]{1,0:T(8,128)(2,1)S(1)} all-gather(bf16[64,1536]{1,0:T(8,128)(2,1)S(1)} %convert_element_type.30), channel_id=2, replica_groups=mesh['y_lo'=2,'z'=8,'x'=4,'y_hi'=4,'core'=2] {'y_lo'}, dimensions={0}, use_global_device_ids=true | all-gather | bytes 589824 | tf_op jit(solution)/shard_map/all_gather | solution.py:64
  19.3 12.6 %all-gather.4 = bf16[256,1536]{1,0:T(8,128)(2,1)S(1)} all-gather(bf16[64,1536]{1,0:T(8,128)(2,1)S(1)} %get-tuple-element.9), channel_id=6, replica_groups=mesh['y_lo'=2,'z'=8,'x'=4,'y_hi'=4,'core'=2] {'x'}, dimensions={0}, use_global_device_ids=true | all-gather | bytes 983040 | tf_op jit(solution)/shard_map/all_gather | solution.py:65
  32.0 11.7 %all-gather.5 = bf16[256,1536]{1,0:T(8,128)(2,1)} all-gather(bf16[64,1536]{1,0:T(8,128)(2,1)S(1)} %get-tuple-element.10), channel_id=7, replica_groups=mesh['y_lo'=2,'z'=8,'x'=4,'y_hi'=4,'core'=2] {'x'}, dimensions={0}, use_global_device_ids=true | all-gather | bytes 983040 | tf_op jit(solution)/shard_map/all_gather | solution.py:65
  43.7 7.8 %all-to-all-done = bf16[8,64,1536]{2,1,0:T(8,128)(2,1)S(1)} async-done(((bf16[8,64,1536]{2,1,0:T(8,128)(2,1)}), bf16[8,64,1536]{2,1,0:T(8,128)(2,1)S(1)}, u32[]{:S(2)}, u32[]{:S(2)}) %all-to-all-start) | async-done | bytes 1572896 | tf_op jit(solution)/shard_map/all_to_all | solution.py:49
  51.5 0.6 convolution_multiply_fusion
  52.1 5.8 %collective-permute-start = (f32[256,512]{1,0:T(8,128)S(1)}, f32[256,512]{1,0:T(8,128)S(1)}, u32[]{:S(2)}, u32[]{:S(2)}) collective-permute-start(f32[256,512]{1,0:T(8,128)S(1)} %convolution_multiply_fusion), channel_id=1, source_target_pairs={{0,1},{1,0},{2,3},{3,2},{4,5},{5,4},{6,7},{7,6},{8,9},{9,8},{10,11... | collective-permute-start | bytes 1572872 | tf_op jit(solution)/shard_map/ppermute | solution.py:70
  57.8 1.5 collective-permute-done
  59.4 0.6 fusion.7
  60.0 0.8 convert_element_type.31
  60.8 6.8 %all-to-all-start.1 = ((bf16[4,64,512]{2,1,0:T(8,128)(2,1)}), bf16[4,64,512]{2,1,0:T(8,128)(2,1)S(1)}, u32[]{:S(2)}, u32[]{:S(2)}) async-start(bf16[4,64,512]{2,1,0:T(8,128)(2,1)} %convert_element_type.31), calls=%async_computation.1 | async-start | bytes 524288 | tf_op jit(solution)/shard_map/all_to_all | solution.py:54
  67.6 8.6 %all-to-all-done.1 = bf16[4,64,512]{2,1,0:T(8,128)(2,1)S(1)} async-done(((bf16[4,64,512]{2,1,0:T(8,128)(2,1)}), bf16[4,64,512]{2,1,0:T(8,128)(2,1)S(1)}, u32[]{:S(2)}, u32[]{:S(2)}) %all-to-all-start.1) | async-done | bytes 262176 | tf_op jit(solution)/shard_map/all_to_all | solution.py:54
  76.2 0.1 select_reduce_fusion.1
  76.4 0.9 broadcast_in_dim.44
  77.2 4.1 %all-to-all-start.2 = ((bf16[8,64,512]{2,1,0:T(8,128)(2,1)}), bf16[8,64,512]{2,1,0:T(8,128)(2,1)}, u32[]{:S(2)}, u32[]{:S(2)}) async-start(bf16[8,64,512]{2,1,0:T(8,128)(2,1)} %broadcast_in_dim.44), calls=%async_computation.2 | async-start | bytes 1048576 | tf_op jit(solution)/shard_map/all_to_all | solution.py:49
  81.4 3.1 %collective-permute-start.4 = (bf16[512,1536]{1,0:T(8,128)(2,1)S(1)}, bf16[512,1536]{1,0:T(8,128)(2,1)}, u32[]{:S(2)}, u32[]{:S(2)}) collective-permute-start(bf16[512,1536]{1,0:T(8,128)(2,1)S(1)} %bitcast.64), channel_id=1, source_target_pairs={{0,8},{8,16},{16,24},{24,0},{1,9},{9,17},{17,25},{25,1},{2,10},{10... | collective-permute-start | bytes 4718600 | tf_op jit(solution)/shard_map/ppermute | solution.py:45
  84.5 3.4 %collective-permute-start.3 = (bf16[512,1536]{1,0:T(8,128)(2,1)S(1)}, bf16[512,1536]{1,0:T(8,128)(2,1)S(1)}, u32[]{:S(2)}, u32[]{:S(2)}) collective-permute-start(bf16[512,1536]{1,0:T(8,128)(2,1)S(1)} %bitcast.65), channel_id=1, source_target_pairs={{0,24},{8,0},{16,8},{24,16},{1,25},{9,1},{17,9},{25,17},{2,26},{10... | collective-permute-start | bytes 4718600 | tf_op jit(solution)/shard_map/ppermute | solution.py:45
  87.9 0.9 fusion.45
  88.8 19.5 %all_gather.25 = bf16[512,512]{1,0:T(8,128)(2,1)} all-gather(bf16[64,512]{1,0:T(8,128)(2,1)S(1)} %get-tuple-element.5), channel_id=1, replica_groups=mesh['y_lo'=2,'z'=8,'x'=4,'y_hi'=4,'core'=2] {'y_hi','core'}, dimensions={0}, use_global_device_ids=true | all-gather | bytes 589824 | tf_op jit(solution)/shard_map/all_gather | solution.py:78
  108.4 0.0 all-to-all-done.2
  108.4 2.8 %fusion.47 = (bf16[8,64,512]{2,1,0:T(8,128)(2,1)}, f32[8,64,512]{2,1,0:T(8,128)}) fusion(bf16[8,64,512]{2,1,0:T(8,128)(2,1)} %bitcast.78, bf16[512,512,1]{1,0,2:T(8,128)(2,1)} %bitcast.7), kind=kOutput, calls=%fused_computation.62 | convolution fusion | flops 268697600 | bytes 2621440 | tf_op jit(solution)/shard_map/dot_general | solution.py:19
  111.2 4.1 %all-to-all-start.3 = ((bf16[8,64,512]{2,1,0:T(8,128)(2,1)}), bf16[8,64,512]{2,1,0:T(8,128)(2,1)}, u32[]{:S(2)}, u32[]{:S(2)}) async-start(bf16[8,64,512]{2,1,0:T(8,128)(2,1)} %get-tuple-element.11), calls=%async_computation.3 | async-start | bytes 1048576 | tf_op jit(solution)/shard_map/all_to_all | solution.py:54
  115.4 3.5 %collective-permute-start.1 = (f32[64,512]{1,0:T(8,128)S(1)}, f32[64,512]{1,0:T(8,128)S(1)}, u32[]{:S(2)}, u32[]{:S(2)}) collective-permute-start(f32[64,512]{1,0:T(8,128)S(1)} %get-tuple-element.6), channel_id=1, source_target_pairs={{0,0},{1,256},{2,8},{3,264},{4,16},{5,272},{6,24},{7,280},{8,2},{9... | collective-permute-start | bytes 393224 | tf_op jit(solution)/shard_map/ppermute | solution.py:37
  118.9 6.6 %all-to-all-done.3 = bf16[8,64,512]{2,1,0:T(8,128)(2,1)} async-done(((bf16[8,64,512]{2,1,0:T(8,128)(2,1)}), bf16[8,64,512]{2,1,0:T(8,128)(2,1)}, u32[]{:S(2)}, u32[]{:S(2)}) %all-to-all-start.3) | async-done | bytes 524320 | tf_op jit(solution)/shard_map/all_to_all | solution.py:54
  125.5 1.2 select_reduce_fusion
  126.7 0.5 collective-permute-done.1
  127.2 0.9 fusion.14
  128.2 6.8 %collective-permute-start.2 = (bf16[64,512]{1,0:T(8,128)(2,1)S(1)}, bf16[64,512]{1,0:T(8,128)(2,1)S(1)}, u32[]{:S(2)}, u32[]{:S(2)}) collective-permute-start(bf16[64,512]{1,0:T(8,128)(2,1)S(1)} %fusion.14), channel_id=1, source_target_pairs={{0,0},{1,256},{2,2},{3,258},{4,4},{5,260},{6,6},{7,262},{8,8},{9,2... | collective-permute-start | bytes 196616 | tf_op jit(solution)/shard_map/ppermute | solution.py:41
  135.1 1.2 slice.39
  136.3 3.4 %collective-permute-start.6 = (bf16[256,1536]{1,0:T(8,128)(2,1)S(1)}, bf16[256,1536]{1,0:T(8,128)(2,1)S(1)}, u32[]{:S(2)}, u32[]{:S(2)}) collective-permute-start(bf16[256,1536]{1,0:T(8,128)(2,1)S(1)} %slice.39), channel_id=1, source_target_pairs={{0,8},{8,16},{16,24},{24,0},{1,9},{9,17},{17,25},{25,1},{2,10},{10... | collective-permute-start | bytes 2359304 | tf_op jit(solution)/shard_map/ppermute | solution.py:45
  139.7 0.1 slice.37
  139.8 3.3 %collective-permute-start.5 = (bf16[256,1536]{1,0:T(8,128)(2,1)S(1)}, bf16[256,1536]{1,0:T(8,128)(2,1)S(1)}, u32[]{:S(2)}, u32[]{:S(2)}) collective-permute-start(bf16[256,1536]{1,0:T(8,128)(2,1)S(1)} %slice.37), channel_id=1, source_target_pairs={{0,24},{8,0},{16,8},{24,16},{1,25},{9,1},{17,9},{25,17},{2,26},{10... | collective-permute-start | bytes 2359304 | tf_op jit(solution)/shard_map/ppermute | solution.py:45
  143.1 17.7 %all-gather.3 = bf16[512,512]{1,0:T(8,128)(2,1)S(1)} all-gather(bf16[64,512]{1,0:T(8,128)(2,1)S(1)} %collective-permute-done.2), channel_id=5, replica_groups=mesh['y_lo'=2,'z'=8,'x'=4,'y_hi'=4,'core'=2] {'y_hi','core'}, dimensions={0}, use_global_device_ids=true | all-gather | bytes 589824 | tf_op jit(solution)/shard_map/all_gather | solution.py:84
  160.8 0.4 fusion.18
  161.2 0.4 fusion.22
  161.6 0.2 fusion.31
  161.9 0.4 convolution_add_fusion.1
  162.3 0.4 convolution_add_fusion.3
  162.7 0.2 fusion.33
  162.9 1.8 %fusion.6 = bf16[64,1536]{1,0:T(8,128)(2,1)S(1)} fusion(f32[64,1536]{1,0:T(8,128)S(1)} %fusion.31, f32[64,1536]{1,0:T(8,128)S(1)} %fusion.33, f32[64,1536]{1,0:T(8,128)S(1)} %convolution_add_fusion.1, bf16[512,1536]{1,0:T(8,128)(2,1)} %collective-permute-done.4, bf16[4,2,64,512]{3,2,1,0:T(8,128)(2,1)S(1)} %bitcast.76, s32[]{:T(128)S(6)} %select_n.96, ...), kind=kOutput, calls=%fused_computation.10 | convolution fusion | flops 101056512 | bytes 3014664 | tf_op jit(solution)/shard_map/dot_general | solution.py:92
  164.7 0.0 copy-start.2
  164.7 3.4 %collective-permute-start.7 = (bf16[64,1536]{1,0:T(8,128)(2,1)S(1)}, bf16[64,1536]{1,0:T(8,128)(2,1)S(1)}, u32[]{:S(2)}, u32[]{:S(2)}) collective-permute-start(bf16[64,1536]{1,0:T(8,128)(2,1)S(1)} %fusion.6), channel_id=1, source_target_pairs={{0,256},{256,0},{1,257},{257,1},{2,258},{258,2},{3,259},{259,3},{4... | collective-permute-start | bytes 589832 | tf_op jit(solution)/shard_map/ppermute | solution.py:100
  168.1 0.2 fusion.35
  168.4 0.3 fusion.37
  168.6 4.5 %collective-permute-done.7 = bf16[64,1536]{1,0:T(8,128)(2,1)S(1)} collective-permute-done((bf16[64,1536]{1,0:T(8,128)(2,1)S(1)}, bf16[64,1536]{1,0:T(8,128)(2,1)S(1)}, u32[]{:S(2)}, u32[]{:S(2)}) %collective-permute-start.7) | collective-permute-done | bytes 196640 | tf_op jit(solution)/shard_map/ppermute | solution.py:100
  173.1 2.6 %fusion.3 = f32[64,1536]{1,0:T(8,128)} fusion(f32[64,1536]{1,0:T(8,128)S(1)} %fusion.35, f32[64,1536]{1,0:T(8,128)S(1)} %fusion.37, f32[64,1536]{1,0:T(8,128)S(1)} %convolution_add_fusion.3, bf16[512,1536]{1,0:T(8,128)(2,1)} %collective-permute-done.4, bf16[64,1536]{1,0:T(8,128)(2,1)S(1)} %collective-permute-done.7, f32[64,1536]{1,0:T(8,128)S(1)} %copy-done.2, ...), kind=kOutput, calls=%fused_computation.7 | convolution fusion | flops 101351424 | bytes 3801096 | tf_op jit(solution)/shard_map/dot_general | solution.py:92
  (15 shorter events, 0.1 us)
Async XLA Ops:
  2.3 49.1 %all-to-all-start = ((bf16[8,64,1536]{2,1,0:T(8,128)(2,1)}), bf16[8,64,1536]{2,1,0:T(8,128)(2,1)S(1)}, u32[]{:S(2)}, u32[]{:S(2)}) async-start(bf16[8,64,1536]{2,1,0:T(8,128)(2,1)} %broadcast_in_dim.40), calls=%async_computation | async-start | bytes 3145728 | tf_op jit(solution)/shard_map/all_to_all | solution.py:49
  51.5 7.9 %copy-start.1 = (bf16[256,1536]{1,0:T(8,128)(2,1)S(1)}, bf16[256,1536]{1,0:T(8,128)(2,1)}, u32[]{:S(2)}) copy-start(bf16[256,1536]{1,0:T(8,128)(2,1)} %all-gather.5) | copy-start | bytes 2359300
  52.1 7.3 %collective-permute-start = (f32[256,512]{1,0:T(8,128)S(1)}, f32[256,512]{1,0:T(8,128)S(1)}, u32[]{:S(2)}, u32[]{:S(2)}) collective-permute-start(f32[256,512]{1,0:T(8,128)S(1)} %convolution_multiply_fusion), channel_id=1, source_target_pairs={{0,1},{1,0},{2,3},{3,2},{4,5},{5,4},{6,7},{7,6},{8,9},{9,8},{10,11... | collective-permute-start | bytes 1572872 | tf_op jit(solution)/shard_map/ppermute | solution.py:70
  60.0 17.3 %copy-start = (f32[256,512]{1,0:T(8,128)}, f32[256,512]{1,0:T(8,128)S(1)}, u32[]{:S(2)}) copy-start(f32[256,512]{1,0:T(8,128)S(1)} %fusion.7) | copy-start | bytes 1572868
  60.8 15.4 %all-to-all-start.1 = ((bf16[4,64,512]{2,1,0:T(8,128)(2,1)}), bf16[4,64,512]{2,1,0:T(8,128)(2,1)S(1)}, u32[]{:S(2)}, u32[]{:S(2)}) async-start(bf16[4,64,512]{2,1,0:T(8,128)(2,1)} %convert_element_type.31), calls=%async_computation.1 | async-start | bytes 524288 | tf_op jit(solution)/shard_map/all_to_all | solution.py:54
  77.2 31.1 %all-to-all-start.2 = ((bf16[8,64,512]{2,1,0:T(8,128)(2,1)}), bf16[8,64,512]{2,1,0:T(8,128)(2,1)}, u32[]{:S(2)}, u32[]{:S(2)}) async-start(bf16[8,64,512]{2,1,0:T(8,128)(2,1)} %broadcast_in_dim.44), calls=%async_computation.2 | async-start | bytes 1048576 | tf_op jit(solution)/shard_map/all_to_all | solution.py:49
  81.4 53.7 %collective-permute-start.4 = (bf16[512,1536]{1,0:T(8,128)(2,1)S(1)}, bf16[512,1536]{1,0:T(8,128)(2,1)}, u32[]{:S(2)}, u32[]{:S(2)}) collective-permute-start(bf16[512,1536]{1,0:T(8,128)(2,1)S(1)} %bitcast.64), channel_id=1, source_target_pairs={{0,8},{8,16},{16,24},{24,0},{1,9},{9,17},{17,25},{25,1},{2,10},{10... | collective-permute-start | bytes 4718600 | tf_op jit(solution)/shard_map/ppermute | solution.py:45
  84.5 55.2 %collective-permute-start.3 = (bf16[512,1536]{1,0:T(8,128)(2,1)S(1)}, bf16[512,1536]{1,0:T(8,128)(2,1)S(1)}, u32[]{:S(2)}, u32[]{:S(2)}) collective-permute-start(bf16[512,1536]{1,0:T(8,128)(2,1)S(1)} %bitcast.65), channel_id=1, source_target_pairs={{0,24},{8,0},{16,8},{24,16},{1,25},{9,1},{17,9},{25,17},{2,26},{10... | collective-permute-start | bytes 4718600 | tf_op jit(solution)/shard_map/ppermute | solution.py:45
  111.2 14.3 %all-to-all-start.3 = ((bf16[8,64,512]{2,1,0:T(8,128)(2,1)}), bf16[8,64,512]{2,1,0:T(8,128)(2,1)}, u32[]{:S(2)}, u32[]{:S(2)}) async-start(bf16[8,64,512]{2,1,0:T(8,128)(2,1)} %get-tuple-element.11), calls=%async_computation.3 | async-start | bytes 1048576 | tf_op jit(solution)/shard_map/all_to_all | solution.py:54
  115.4 11.9 %collective-permute-start.1 = (f32[64,512]{1,0:T(8,128)S(1)}, f32[64,512]{1,0:T(8,128)S(1)}, u32[]{:S(2)}, u32[]{:S(2)}) collective-permute-start(f32[64,512]{1,0:T(8,128)S(1)} %get-tuple-element.6), channel_id=1, source_target_pairs={{0,0},{1,256},{2,8},{3,264},{4,16},{5,272},{6,24},{7,280},{8,2},{9... | collective-permute-start | bytes 393224 | tf_op jit(solution)/shard_map/ppermute | solution.py:37
  128.2 14.9 %collective-permute-start.2 = (bf16[64,512]{1,0:T(8,128)(2,1)S(1)}, bf16[64,512]{1,0:T(8,128)(2,1)S(1)}, u32[]{:S(2)}, u32[]{:S(2)}) collective-permute-start(bf16[64,512]{1,0:T(8,128)(2,1)S(1)} %fusion.14), channel_id=1, source_target_pairs={{0,0},{1,256},{2,2},{3,258},{4,4},{5,260},{6,6},{7,262},{8,8},{9,2... | collective-permute-start | bytes 196616 | tf_op jit(solution)/shard_map/ppermute | solution.py:41
  136.3 25.3 %collective-permute-start.6 = (bf16[256,1536]{1,0:T(8,128)(2,1)S(1)}, bf16[256,1536]{1,0:T(8,128)(2,1)S(1)}, u32[]{:S(2)}, u32[]{:S(2)}) collective-permute-start(bf16[256,1536]{1,0:T(8,128)(2,1)S(1)} %slice.39), channel_id=1, source_target_pairs={{0,8},{8,16},{16,24},{24,0},{1,9},{9,17},{17,25},{25,1},{2,10},{10... | collective-permute-start | bytes 2359304 | tf_op jit(solution)/shard_map/ppermute | solution.py:45
  139.8 22.9 %collective-permute-start.5 = (bf16[256,1536]{1,0:T(8,128)(2,1)S(1)}, bf16[256,1536]{1,0:T(8,128)(2,1)S(1)}, u32[]{:S(2)}, u32[]{:S(2)}) collective-permute-start(bf16[256,1536]{1,0:T(8,128)(2,1)S(1)} %slice.37), channel_id=1, source_target_pairs={{0,24},{8,0},{16,8},{24,16},{1,25},{9,1},{17,9},{25,17},{2,26},{10... | collective-permute-start | bytes 2359304 | tf_op jit(solution)/shard_map/ppermute | solution.py:45
  164.7 8.4 %copy-start.2 = (f32[64,1536]{1,0:T(8,128)S(1)}, f32[64,1536]{1,0:T(8,128)}, u32[]{:S(2)}) copy-start(f32[64,1536]{1,0:T(8,128)} %param.1) | copy-start | bytes 1179652
  164.7 8.4 %collective-permute-start.7 = (bf16[64,1536]{1,0:T(8,128)(2,1)S(1)}, bf16[64,1536]{1,0:T(8,128)(2,1)S(1)}, u32[]{:S(2)}, u32[]{:S(2)}) collective-permute-start(bf16[64,1536]{1,0:T(8,128)(2,1)S(1)} %fusion.6), channel_id=1, source_target_pairs={{0,256},{256,0},{1,257},{257,1},{2,258},{258,2},{3,259},{259,3},{4... | collective-permute-start | bytes 589832 | tf_op jit(solution)/shard_map/ppermute | solution.py:100

commit v6 on v4

--- a/solution.py
+++ b/solution.py
@@ -12,24 +12,16 @@
 LO = ("x", "y_lo")
 COL = ("y_hi", "core")
 ROW = ("y_lo", "z", "x")
-EVERY = ("y_lo", "z", "x", "y_hi", "core")
+MESH = ("y_lo", "z", "x", "y_hi", "core")
 
 
 def dot_nt(a, b):
     return lax.dot_general(a, b, (((1,), (1,)), ((), ())), preferred_element_type=jnp.float32)
 
 
-def swap_lo_col():
-    pairs = []
-    for y_lo in range(2):
-        for z in range(8):
-            for x in range(4):
-                for y_hi in range(4):
-                    for core in range(2):
-                        source = (((y_lo * 8 + z) * 4 + x) * 4 + y_hi) * 2 + core
-                        target = (((core * 8 + z) * 4 + y_hi) * 4 + x) * 2 + y_lo
-                        pairs.append((source, target))
-    return pairs
+def swap_x_y_hi(block):
+    pairs = [((x * 4 + y) * 2 + k, (y * 4 + x) * 2 + k) for x in range(4) for y in range(4) for k in range(2)]
+    return lax.ppermute(block, ("x", "y_hi", "core"), pairs)
 
 
 def spread(block, axis):
@@ -58,10 +50,16 @@
     gram = sum_pieces(home.reshape(4, rows, 8 * rows), "y_hi")
 
     rounded = gram.astype(jnp.bfloat16)
-    left = lax.all_gather(rounded, COL, axis=0, tiled=True)
     right = spread(rounded, "z").reshape(8 * rows, 8 * rows)
-    square = sum_pieces(dot_nt(left, right).reshape(8, rows, 8 * rows), LO)
-    square = lax.ppermute(square, EVERY, swap_lo_col())
+    right_other = lax.ppermute(right, "core", [(0, 1), (1, 0)])
+    left = lax.all_gather(swap_x_y_hi(rounded), "y_lo", axis=0)
+    left = lax.all_gather(left, "x", axis=0).reshape(4, 2, rows, 8 * rows)
+    own = jnp.where(core == 0, left[:, 0], left[:, 1]).reshape(4 * rows, 8 * rows)
+    other = jnp.where(core == 0, left[:, 1], left[:, 0]).reshape(4 * rows, 8 * rows)
+    square = jnp.dot(own, right, preferred_element_type=jnp.float32) + jnp.dot(
+        other, right_other, preferred_element_type=jnp.float32
+    )
+    square = sum_pieces(square.reshape(4, rows, 8 * rows), "y_hi")
 
     poly = (coef_cubic * gram + coef_quintic * square).astype(jnp.bfloat16)
     poly = lax.all_gather(poly, COL, axis=0, tiled=True)
@@ -70,7 +68,7 @@
 
 
 def solution(mesh):
-    fine = Mesh(mesh.devices.reshape(2, 8, 4, 4, 2), EVERY)
+    fine = Mesh(mesh.devices.reshape(2, 8, 4, 4, 2), MESH)
     return jax.shard_map(
         per_device,
         mesh=fine,

time: 175 us -> 177 us (1.011)
  blocking collectives: 98.4 us -> 78.5 us
  waiting for transfers between devices: 29.9 us -> 49.1 us
  starting transfers between devices: 35 us -> 36.9 us
    all_to_all x1, blocking collectives: 24.9 us -> 11.3 us  [sum_pieces(): arrived = lax.all_to_all(pieces.astype(jnp.bfloat16), axis, 0, 0)]
    all_to_all x2, waiting for transfers between devices: 17.9 us -> 29.8 us  [sum_pieces(): arrived = lax.all_to_all(pieces.astype(jnp.bfloat16), axis, 0, 0)]
    all_to_all x2, waiting for transfers between devices: 7.77 us -> 17.8 us  [spread(): lax.all_to_all(jnp.broadcast_to(block[None], (8,) + block.shape), axis, 0...]
    all_gather x1, blocking collectives: 24.7 us -> 20.2 us  [per_device(): poly = lax.all_gather(poly, COL, axis=0, tiled=True)]
    ppermute x1 -> x2, waiting for transfers between devices: 2.64 us -> 0.01 us  [the longest x1 0.01 us: swap_x_y_hi(): return lax.ppermute(block, ('x', 'y_hi', 'core'), pairs)]
    ppermute x1 -> x2, starting transfers between devices: 4.05 us -> 6.39 us  [the longest x1 5.73 us: per_device(): right_other = lax.ppermute(right, 'core', [(0, 1), (1, 0)])]
    dot_general x1, matrix products: 0.98 us -> 3.13 us  [per_device(): product = jnp.dot(poly, by_hi, preferred_element_type=jnp.float32)]
    all_gather x1 -> x2, blocking collectives: 18.4 us -> 16.5 us  [the longest x1 12.7 us: per_device(): left = lax.all_gather(left, 'x', axis=0).reshape(4, 2, rows, 8 * rows)]
  transfers between devices with their start and end apart: 6 -> 7, of which waited for: 5 -> 5; matrix products, arithmetic and copies ran while one was open for 0% -> 0% of each run, Pallas kernels for 0% -> 0%
where the time goes in v6:
time: 177 us; the launch traced here: 176 us
  blocking collectives  78.5 us (44%)
  waiting for transfers between devices  49.1 us (28%)
  starting transfers between devices  36.9 us (21%)
  matrix products  4.94 us (3%)
  other arithmetic  4.37 us (2%)
  local copies, waits for them, and re-layouts  2.14 us (1%)
    all_to_all x2, waiting for transfers between devices, sum_pieces(): arrived = lax.all_to_all(pieces.astype(jnp.bfloat16), axis, 0, 0)  29.8 us
    all_gather x2, blocking collectives, per_device(): by_lo = [lax.all_gather(pair[y], 'x', axis=0, tiled=True) for y in range(2)]  24.4 us
    all_gather x1, blocking collectives, per_device(): poly = lax.all_gather(poly, COL, axis=0, tiled=True)  20.2 us
    all_to_all x2, waiting for transfers between devices, spread(): lax.all_to_all(jnp.broadcast_to(block[None], (8,) + block.shape), axis, 0...  17.8 us
    all_to_all x2, starting transfers between devices, spread(): lax.all_to_all(jnp.broadcast_to(block[None], (8,) + block.shape), axis, 0...  14.4 us
    all_gather x1, blocking collectives, per_device(): left = lax.all_gather(left, 'x', axis=0).reshape(4, 2, rows, 8 * rows)  12.7 us
    all_to_all x1, blocking collectives, sum_pieces(): arrived = lax.all_to_all(pieces.astype(jnp.bfloat16), axis, 0, 0)  11.3 us
    all_to_all x2, starting transfers between devices, sum_pieces(): arrived = lax.all_to_all(pieces.astype(jnp.bfloat16), axis, 0, 0)  10.4 us
  transfers between devices with their start and end apart: 7, of which 5 were waited for; matrix products, arithmetic and copies ran while one was open for 0% of the time, Pallas kernels for 0%

profile of v6, /device:TPU:1, one launch (start us, length us, event | category | flops | bytes accessed | tf_op | source)
XLA Modules:
  0.0 176.1 jit_solution(9487639255534806780)
XLA Ops:
  0.0 1.0 convert_element_type.30
  1.0 1.3 broadcast_in_dim.45
  2.3 10.9 %all-to-all-start = ((bf16[8,64,1536]{2,1,0:T(8,128)(2,1)}), bf16[8,64,1536]{2,1,0:T(8,128)(2,1)S(1)}, u32[]{:S(2)}, u32[]{:S(2)}) async-start(bf16[8,64,1536]{2,1,0:T(8,128)(2,1)} %broadcast_in_dim.45), calls=%async_computation | async-start | bytes 3145728 | tf_op jit(solution)/shard_map/all_to_all | solution.py:28
  13.2 6.1 %all-gather = bf16[128,1536]{1,0:T(8,128)(2,1)S(1)} all-gather(bf16[64,1536]{1,0:T(8,128)(2,1)S(1)} %convert_element_type.30), channel_id=2, replica_groups=mesh['y_lo'=2,'z'=8,'x'=4,'y_hi'=4,'core'=2] {'y_lo'}, dimensions={0}, use_global_device_ids=true | all-gather | bytes 589824 | tf_op jit(solution)/shard_map/all_gather | solution.py:43
  19.3 12.6 %all-gather.5 = bf16[256,1536]{1,0:T(8,128)(2,1)S(1)} all-gather(bf16[64,1536]{1,0:T(8,128)(2,1)S(1)} %get-tuple-element.7), channel_id=7, replica_groups=mesh['y_lo'=2,'z'=8,'x'=4,'y_hi'=4,'core'=2] {'x'}, dimensions={0}, use_global_device_ids=true | all-gather | bytes 983040 | tf_op jit(solution)/shard_map/all_gather | solution.py:44
  31.9 11.7 %all-gather.6 = bf16[256,1536]{1,0:T(8,128)(2,1)} all-gather(bf16[64,1536]{1,0:T(8,128)(2,1)S(1)} %get-tuple-element.8), channel_id=8, replica_groups=mesh['y_lo'=2,'z'=8,'x'=4,'y_hi'=4,'core'=2] {'x'}, dimensions={0}, use_global_device_ids=true | all-gather | bytes 983040 | tf_op jit(solution)/shard_map/all_gather | solution.py:44
  43.7 7.8 %all-to-all-done = bf16[8,64,1536]{2,1,0:T(8,128)(2,1)S(1)} async-done(((bf16[8,64,1536]{2,1,0:T(8,128)(2,1)}), bf16[8,64,1536]{2,1,0:T(8,128)(2,1)S(1)}, u32[]{:S(2)}, u32[]{:S(2)}) %all-to-all-start) | async-done | bytes 1572896 | tf_op jit(solution)/shard_map/all_to_all | solution.py:28
  51.4 0.0 copy-start
  51.4 0.6 convolution_multiply_fusion
  52.0 5.8 %collective-permute-start = (f32[256,512]{1,0:T(8,128)S(1)}, f32[256,512]{1,0:T(8,128)S(1)}, u32[]{:S(2)}, u32[]{:S(2)}) collective-permute-start(f32[256,512]{1,0:T(8,128)S(1)} %convolution_multiply_fusion), channel_id=1, source_target_pairs={{0,1},{1,0},{2,3},{3,2},{4,5},{5,4},{6,7},{7,6},{8,9},{9,8},{10,11... | collective-permute-start | bytes 1572872 | tf_op jit(solution)/shard_map/ppermute | solution.py:49
  57.8 1.5 collective-permute-done
  59.3 0.0 copy-done
  59.3 0.6 fusion
  59.9 0.7 convert_element_type.31
  60.7 6.8 %all-to-all-start.1 = ((bf16[4,64,512]{2,1,0:T(8,128)(2,1)}), bf16[4,64,512]{2,1,0:T(8,128)(2,1)S(1)}, u32[]{:S(2)}, u32[]{:S(2)}) async-start(bf16[4,64,512]{2,1,0:T(8,128)(2,1)} %convert_element_type.31), calls=%async_computation.1 | async-start | bytes 524288 | tf_op jit(solution)/shard_map/all_to_all | solution.py:33
  67.5 8.6 %all-to-all-done.1 = bf16[4,64,512]{2,1,0:T(8,128)(2,1)S(1)} async-done(((bf16[4,64,512]{2,1,0:T(8,128)(2,1)}), bf16[4,64,512]{2,1,0:T(8,128)(2,1)S(1)}, u32[]{:S(2)}, u32[]{:S(2)}) %all-to-all-start.1) | async-done | bytes 262176 | tf_op jit(solution)/shard_map/all_to_all | solution.py:33
  76.1 0.1 select_reduce_fusion.2
  76.3 0.8 broadcast_in_dim.49
  77.1 3.5 %all-to-all-start.2 = ((bf16[8,64,512]{2,1,0:T(8,128)(2,1)}), bf16[8,64,512]{2,1,0:T(8,128)(2,1)S(1)}, u32[]{:S(2)}, u32[]{:S(2)}) async-start(bf16[8,64,512]{2,1,0:T(8,128)(2,1)} %broadcast_in_dim.49), calls=%async_computation.2 | async-start | bytes 1048576 | tf_op jit(solution)/shard_map/all_to_all | solution.py:28
  80.6 0.7 collective-permute-start.1
  81.3 0.0 collective-permute-done.1
  81.3 3.8 %all-gather.3 = bf16[128,512]{1,0:T(8,128)(2,1)S(1)} all-gather(bf16[64,512]{1,0:T(8,128)(2,1)S(1)} %collective-permute-done.1), channel_id=5, replica_groups=mesh['y_lo'=2,'z'=8,'x'=4,'y_hi'=4,'core'=2] {'y_lo'}, dimensions={0}, use_global_device_ids=true | all-gather | bytes 196608 | tf_op jit(solution)/shard_map/all_gather | solution.py:55
  85.1 10.0 %all-to-all-done.2 = bf16[8,64,512]{2,1,0:T(8,128)(2,1)S(1)} async-done(((bf16[8,64,512]{2,1,0:T(8,128)(2,1)}), bf16[8,64,512]{2,1,0:T(8,128)(2,1)S(1)}, u32[]{:S(2)}, u32[]{:S(2)}) %all-to-all-start.2) | async-done | bytes 524320 | tf_op jit(solution)/shard_map/all_to_all | solution.py:28
  95.1 5.7 %collective-permute-start.2 = (bf16[512,512]{1,0:T(8,128)(2,1)S(1)}, bf16[512,512]{1,0:T(8,128)(2,1)S(1)}, u32[]{:S(2)}, u32[]{:S(2)}) collective-permute-start(bf16[512,512]{1,0:T(8,128)(2,1)S(1)} %bitcast.54), channel_id=1, source_target_pairs={{0,1},{1,0},{2,3},{3,2},{4,5},{5,4},{6,7},{7,6},{8,9},{9,8},{10,11... | collective-permute-start | bytes 1572872 | tf_op jit(solution)/shard_map/ppermute | solution.py:54
  100.9 12.7 %all-gather.4 = bf16[8,64,512]{2,1,0:T(8,128)(2,1)S(1)} all-gather(bf16[2,64,512]{2,1,0:T(8,128)(2,1)S(1)} %bitcast.60), channel_id=6, replica_groups=mesh['y_lo'=2,'z'=8,'x'=4,'y_hi'=4,'core'=2] {'x'}, dimensions={0}, use_global_device_ids=true | all-gather | bytes 655360 | tf_op jit(solution)/shard_map/all_gather | solution.py:56
  113.6 0.3 fusion.14
  113.9 0.0 collective-permute-done.2
  113.9 0.3 convolution_add_fusion
  114.3 11.3 %all_to_all.25 = bf16[4,64,512]{2,1,0:T(8,128)(2,1)S(1)} all-to-all(bf16[4,64,512]{2,1,0:T(8,128)(2,1)S(1)} %convert_element_type.35), channel_id=1, replica_groups=mesh['y_lo'=2,'z'=8,'x'=4,'y_hi'=4,'core'=2] {'y_hi'}, dimensions={0} | all-to-all | bytes 524288 | tf_op jit(solution)/shard_map/all_to_all | solution.py:33
  125.6 0.1 select_reduce_fusion.1
  125.7 0.1 fusion.8
  125.8 20.2 %all_gather.35 = bf16[512,512]{1,0:T(8,128)(2,1)S(1)} all-gather(bf16[64,512]{1,0:T(8,128)(2,1)S(1)} %fusion.8), channel_id=1, replica_groups=mesh['y_lo'=2,'z'=8,'x'=4,'y_hi'=4,'core'=2] {'y_hi','core'}, dimensions={0}, use_global_device_ids=true | all-gather | bytes 589824 | tf_op jit(solution)/shard_map/all_gather | solution.py:65
  145.9 3.1 %fusion.13 = (bf16[8,64,1536]{2,1,0:T(8,128)(2,1)}, f32[8,64,1536]{2,1,0:T(8,128)}) fusion(bf16[8,64,512]{2,1,0:T(8,128)(2,1)S(1)} %bitcast.57, bf16[512,1536,1]{1,0,2:T(8,128)(2,1)S(1)} %bitcast.47), kind=kOutput, calls=%fused_computation.27 | convolution fusion | flops 806092800 | bytes 6815744 | tf_op jit(solution)/shard_map/dot_general | solution.py:66
  149.1 3.6 %all-to-all-start.4 = ((bf16[8,64,1536]{2,1,0:T(8,128)(2,1)}), bf16[8,64,1536]{2,1,0:T(8,128)(2,1)S(1)}, u32[]{:S(2)}, u32[]{:S(2)}) async-start(bf16[8,64,1536]{2,1,0:T(8,128)(2,1)} %get-tuple-element.9), calls=%async_computation.4 | async-start | bytes 3145728 | tf_op jit(solution)/shard_map/all_to_all | solution.py:33
  152.7 0.0 copy-start.1
  152.7 21.2 %all-to-all-done.4 = bf16[8,64,1536]{2,1,0:T(8,128)(2,1)S(1)} async-done(((bf16[8,64,1536]{2,1,0:T(8,128)(2,1)}), bf16[8,64,1536]{2,1,0:T(8,128)(2,1)S(1)}, u32[]{:S(2)}, u32[]{:S(2)}) %all-to-all-start.4) | async-done | bytes 1572896 | tf_op jit(solution)/shard_map/all_to_all | solution.py:33
  173.9 0.4 select_reduce_fusion
  174.3 0.0 copy-done.1
  174.3 1.8 %fusion.5 = f32[64,1536]{1,0:T(8,128)} fusion(f32[64,1536]{1,0:T(8,128)S(1)} %select_reduce_fusion, f32[8,64,1536]{2,1,0:T(8,128)} %get-tuple-element.10, s32[]{:T(128)S(6)} %select_n.63, f32[64,1536]{1,0:T(8,128)S(1)} %copy-done.1), kind=kLoop, calls=%fused_computation.12 | loop fusion | flops 294912 | bytes 1572868 | tf_op jit(solution)/shard_map/add | solution.py:67
  (7 shorter events, 0.2 us)
Async XLA Ops:
  2.3 49.1 %all-to-all-start = ((bf16[8,64,1536]{2,1,0:T(8,128)(2,1)}), bf16[8,64,1536]{2,1,0:T(8,128)(2,1)S(1)}, u32[]{:S(2)}, u32[]{:S(2)}) async-start(bf16[8,64,1536]{2,1,0:T(8,128)(2,1)} %broadcast_in_dim.45), calls=%async_computation | async-start | bytes 3145728 | tf_op jit(solution)/shard_map/all_to_all | solution.py:28
  51.4 7.9 %copy-start = (bf16[256,1536]{1,0:T(8,128)(2,1)S(1)}, bf16[256,1536]{1,0:T(8,128)(2,1)}, u32[]{:S(2)}) copy-start(bf16[256,1536]{1,0:T(8,128)(2,1)} %all-gather.6) | copy-start | bytes 2359300
  52.0 7.3 %collective-permute-start = (f32[256,512]{1,0:T(8,128)S(1)}, f32[256,512]{1,0:T(8,128)S(1)}, u32[]{:S(2)}, u32[]{:S(2)}) collective-permute-start(f32[256,512]{1,0:T(8,128)S(1)} %convolution_multiply_fusion), channel_id=1, source_target_pairs={{0,1},{1,0},{2,3},{3,2},{4,5},{5,4},{6,7},{7,6},{8,9},{9,8},{10,11... | collective-permute-start | bytes 1572872 | tf_op jit(solution)/shard_map/ppermute | solution.py:49
  60.7 15.4 %all-to-all-start.1 = ((bf16[4,64,512]{2,1,0:T(8,128)(2,1)}), bf16[4,64,512]{2,1,0:T(8,128)(2,1)S(1)}, u32[]{:S(2)}, u32[]{:S(2)}) async-start(bf16[4,64,512]{2,1,0:T(8,128)(2,1)} %convert_element_type.31), calls=%async_computation.1 | async-start | bytes 524288 | tf_op jit(solution)/shard_map/all_to_all | solution.py:33
  77.1 18.0 %all-to-all-start.2 = ((bf16[8,64,512]{2,1,0:T(8,128)(2,1)}), bf16[8,64,512]{2,1,0:T(8,128)(2,1)S(1)}, u32[]{:S(2)}, u32[]{:S(2)}) async-start(bf16[8,64,512]{2,1,0:T(8,128)(2,1)} %broadcast_in_dim.49), calls=%async_computation.2 | async-start | bytes 1048576 | tf_op jit(solution)/shard_map/all_to_all | solution.py:28
  80.6 0.7 collective-permute-start.1
  95.1 18.8 %collective-permute-start.2 = (bf16[512,512]{1,0:T(8,128)(2,1)S(1)}, bf16[512,512]{1,0:T(8,128)(2,1)S(1)}, u32[]{:S(2)}, u32[]{:S(2)}) collective-permute-start(bf16[512,512]{1,0:T(8,128)(2,1)S(1)} %bitcast.54), channel_id=1, source_target_pairs={{0,1},{1,0},{2,3},{3,2},{4,5},{5,4},{6,7},{7,6},{8,9},{9,8},{10,11... | collective-permute-start | bytes 1572872 | tf_op jit(solution)/shard_map/ppermute | solution.py:54
  149.1 24.8 %all-to-all-start.4 = ((bf16[8,64,1536]{2,1,0:T(8,128)(2,1)}), bf16[8,64,1536]{2,1,0:T(8,128)(2,1)S(1)}, u32[]{:S(2)}, u32[]{:S(2)}) async-start(bf16[8,64,1536]{2,1,0:T(8,128)(2,1)} %get-tuple-element.9), calls=%async_computation.4 | async-start | bytes 3145728 | tf_op jit(solution)/shard_map/all_to_all | solution.py:33
  152.7 21.6 %copy-start.1 = (f32[64,1536]{1,0:T(8,128)S(1)}, f32[64,1536]{1,0:T(8,128)}, u32[]{:S(2)}) copy-start(f32[64,1536]{1,0:T(8,128)} %param.1) | copy-start | bytes 1179652

commit v7 on v6

--- a/solution.py
+++ b/solution.py
@@ -15,6 +15,10 @@
 MESH = ("y_lo", "z", "x", "y_hi", "core")
 
 
+def rest_of(x):
+    return x - lax.reduce_precision(x, exponent_bits=8, mantissa_bits=7)
+
+
 def dot_nt(a, b):
     return lax.dot_general(a, b, (((1,), (1,)), ((), ())), preferred_element_type=jnp.float32)
 
@@ -28,12 +32,20 @@
     return lax.all_to_all(jnp.broadcast_to(block[None], (8,) + block.shape), axis, 0, 0)
 
 
-def sum_pieces(pieces, axis):
-    me, count = lax.axis_index(axis), pieces.shape[0]
-    arrived = lax.all_to_all(pieces.astype(jnp.bfloat16), axis, 0, 0)
+def sum_others(arrived, me):
+    total = 0.0
+    for i in range(arrived.shape[0]):
+        total = total + jnp.where(i == me, 0.0, arrived[i].astype(jnp.float32))
+    return total
+
+
+def sum_pieces(pieces, rides, axis):
+    me = lax.axis_index(axis)
+    count, rows, cols = pieces.shape
+    sent = jnp.concatenate([pieces, jnp.broadcast_to(rides[:, None], (count, 16, cols))], axis=1)
+    arrived = lax.all_to_all(sent.astype(jnp.bfloat16), axis, 0, 0)
     own = lax.dynamic_index_in_dim(pieces, me, 0, keepdims=False)
-    other = jnp.where(jnp.arange(count)[:, None, None] == me, 0.0, arrived.astype(jnp.float32))
-    return own + other.sum(0)
+    return own + sum_others(arrived[:, :rows], me), arrived[:, rows].astype(jnp.float32)
 
 
 def per_device(x_scaled):
@@ -47,7 +59,17 @@
     away = dot_nt(jnp.where(core == 0, by_lo[1], by_lo[0]), by_hi) * (1.0 / N)
     home = dot_nt(jnp.where(core == 0, by_lo[0], by_lo[1]), by_hi) * (1.0 / N)
     home = home + lax.ppermute(away, "core", [(0, 1), (1, 0)])
-    gram = sum_pieces(home.reshape(4, rows, 8 * rows), "y_hi")
+    home = home.reshape(4, rows, 8 * rows)
+
+    x_at, y_lo_at, y_hi_at = (lax.axis_index(name) for name in ("x", "y_lo", "y_hi"))
+    across = lax.broadcasted_iota(jnp.int32, (rows, 8 * rows), 1)
+    down = lax.broadcasted_iota(jnp.int32, (rows, 8 * rows), 0)
+    on_diagonal = across == lax.axis_index("z") * rows + down
+    piece = lax.dynamic_index_in_dim(home, x_at, 0, keepdims=False)
+    rest = jnp.where(on_diagonal, rest_of(piece), 0.0).sum(0)
+    rides = jnp.where((jnp.arange(4)[:, None] == x_at) & (core == y_lo_at), rest[None], 0.0)
+    gram, rides = sum_pieces(home, rides, "y_hi")
+    gram = gram + jnp.where(on_diagonal, sum_others(rides, y_hi_at)[None], 0.0)
 
     rounded = gram.astype(jnp.bfloat16)
     right = spread(rounded, "z").reshape(8 * rows, 8 * rows)
@@ -59,12 +81,22 @@
     square = jnp.dot(own, right, preferred_element_type=jnp.float32) + jnp.dot(
         other, right_other, preferred_element_type=jnp.float32
     )
-    square = sum_pieces(square.reshape(4, rows, 8 * rows), "y_hi")
+    at_home = lax.dynamic_slice(left, (y_hi_at, core, 0, 0), (1, 1, rows, 8 * rows))[0, 0]
+    diagonal_down = jnp.where(on_diagonal, at_home.astype(jnp.float32), 0.0).sum(1, keepdims=True)
+    same = jnp.where(core == y_lo_at, right, right_other).astype(jnp.float32)
+    diagonal_across = (same * jnp.eye(8 * rows, dtype=jnp.float32)).sum(0)
+    rides = jnp.broadcast_to(jnp.where(y_hi_at == x_at, diagonal_across, 0.0)[None], (4, 8 * rows))
+    square, rides = sum_pieces(square.reshape(4, rows, 8 * rows), rides, "y_hi")
+    square = square + rest_of(gram) * (diagonal_down + rides.sum(0)[None])
 
     poly = (coef_cubic * gram + coef_quintic * square).astype(jnp.bfloat16)
     poly = lax.all_gather(poly, COL, axis=0, tiled=True)
-    product = jnp.dot(poly, by_hi, preferred_element_type=jnp.float32)
-    return coef_linear * x_scaled + sum_pieces(product.reshape(8, rows, cols), LO)
+    me = lax.axis_index(LO)
+    product = jnp.dot(poly, by_hi, preferred_element_type=jnp.float32).astype(jnp.bfloat16)
+    arrived = lax.all_to_all(product.reshape(8, rows, cols), LO, 0, 0)
+    mine = lax.dynamic_slice_in_dim(poly, me * rows, rows)
+    own = jnp.dot(mine, by_hi, preferred_element_type=jnp.float32)
+    return coef_linear * x_scaled + own + sum_others(arrived, me)
 
 
 def solution(mesh):

time: 177 us -> 181 us (1.023)
  blocking collectives: 78.5 us -> 65.3 us
  waiting for transfers between devices: 49.1 us -> 60.1 us
  matrix products: 4.94 us -> 7.96 us
  starting transfers between devices: 36.9 us -> 39.8 us
    all_to_all x1 -> x0, blocking collectives: 11.3 us -> none  [sum_pieces(): arrived = lax.all_to_all(pieces.astype(jnp.bfloat16), axis, 0, 0)]
    all_to_all x2 -> x3, waiting for transfers between devices: 29.8 us -> 39.5 us  [the longest x1 21 us: per_device(): arrived = lax.all_to_all(product.reshape(8, rows, cols), LO, 0, 0)]
    all_to_all x2 -> x3, starting transfers between devices: 10.4 us -> 15.2 us  [the longest x2 10.3 us: sum_pieces(): arrived = lax.all_to_all(sent.astype(jnp.bfloat16), axis, 0, 0)]
    dot_general x2, matrix products: 1.21 us -> 3.06 us  [dot_nt(): lax.dot_general(a, b, (((1,), (1,)), ((), ())), preferred_element_type=jn...]
    add x1 -> x2, other arithmetic: 1.83 us -> 0.01 us  [the longest x1 0.01 us: sum_others(): total = total + jnp.where(i == me, 0.0, arrived[i].astype(jnp.float32))]
    dot_general x1 -> x2, matrix products: 3.13 us -> 4.31 us  [the longest x1 2.16 us: per_device(): own = jnp.dot(mine, by_hi, preferred_element_type=jnp.float32)]
  transfers between devices with their start and end apart: 7 -> 8, of which waited for: 5 -> 6; matrix products, arithmetic and copies ran while one was open for 0% -> 0% of each run, Pallas kernels for 0% -> 0%
where the time goes in v7:
time: 181 us
  blocking collectives  65.3 us (36%)
  waiting for transfers between devices  60.1 us (33%)
  starting transfers between devices  39.8 us (22%)
  matrix products  7.96 us (4%)
  other arithmetic  4.32 us (2%)
  local copies, waits for them, and re-layouts  2.98 us (2%)
    all_gather x2, blocking collectives, per_device(): by_lo = [lax.all_gather(pair[y], 'x', axis=0, tiled=True) for y in range(2)]  23.9 us
    all_to_all x1, waiting for transfers between devices, per_device(): arrived = lax.all_to_all(product.reshape(8, rows, cols), LO, 0, 0)  21 us
    all_gather x1, blocking collectives, per_device(): poly = lax.all_gather(poly, COL, axis=0, tiled=True)  19.2 us
    all_to_all x2, waiting for transfers between devices, spread(): lax.all_to_all(jnp.broadcast_to(block[None], (8,) + block.shape), axis, 0...  18.8 us
    all_to_all x2, waiting for transfers between devices, sum_pieces(): arrived = lax.all_to_all(sent.astype(jnp.bfloat16), axis, 0, 0)  18.5 us
    all_to_all x2, starting transfers between devices, spread(): lax.all_to_all(jnp.broadcast_to(block[None], (8,) + block.shape), axis, 0...  14.4 us
    all_gather x1, blocking collectives, per_device(): left = lax.all_gather(left, 'x', axis=0).reshape(4, 2, rows, 8 * rows)  12.3 us
    all_to_all x2, starting transfers between devices, sum_pieces(): arrived = lax.all_to_all(sent.astype(jnp.bfloat16), axis, 0, 0)  10.3 us
  transfers between devices with their start and end apart: 8, of which 6 were waited for; matrix products, arithmetic and copies ran while one was open for 0% of the time, Pallas kernels for 0%

profile of v7, /device:TPU:1, one launch (start us, length us, event | category | flops | bytes accessed | tf_op | source)
XLA Modules:
  0.0 180.7 jit_solution(7253854556095075383)
XLA Ops:
  0.0 1.0 convert_element_type.103
  1.0 1.3 broadcast_in_dim.98
  2.3 10.9 %all-to-all-start = ((bf16[8,64,1536]{2,1,0:T(8,128)(2,1)}), bf16[8,64,1536]{2,1,0:T(8,128)(2,1)S(1)}, u32[]{:S(2)}, u32[]{:S(2)}) async-start(bf16[8,64,1536]{2,1,0:T(8,128)(2,1)} %broadcast_in_dim.98), calls=%async_computation | async-start | bytes 3145728 | tf_op jit(solution)/shard_map/all_to_all | solution.py:32
  13.2 6.1 %all-gather = bf16[128,1536]{1,0:T(8,128)(2,1)S(1)} all-gather(bf16[64,1536]{1,0:T(8,128)(2,1)S(1)} %convert_element_type.103), channel_id=2, replica_groups=mesh['y_lo'=2,'z'=8,'x'=4,'y_hi'=4,'core'=2] {'y_lo'}, dimensions={0}, use_global_device_ids=true | all-gather | bytes 589824 | tf_op jit(solution)/shard_map/all_gather | solution.py:55
  19.3 12.6 %all-gather.5 = bf16[256,1536]{1,0:T(8,128)(2,1)S(1)} all-gather(bf16[64,1536]{1,0:T(8,128)(2,1)S(1)} %get-tuple-element.9), channel_id=7, replica_groups=mesh['y_lo'=2,'z'=8,'x'=4,'y_hi'=4,'core'=2] {'x'}, dimensions={0}, use_global_device_ids=true | all-gather | bytes 983040 | tf_op jit(solution)/shard_map/all_gather | solution.py:56
  31.9 11.3 %all-gather.6 = bf16[256,1536]{1,0:T(8,128)(2,1)S(1)} all-gather(bf16[64,1536]{1,0:T(8,128)(2,1)S(1)} %get-tuple-element.10), channel_id=8, replica_groups=mesh['y_lo'=2,'z'=8,'x'=4,'y_hi'=4,'core'=2] {'x'}, dimensions={0}, use_global_device_ids=true | all-gather | bytes 983040 | tf_op jit(solution)/shard_map/all_gather | solution.py:56
  43.2 8.2 %all-to-all-done = bf16[8,64,1536]{2,1,0:T(8,128)(2,1)S(1)} async-done(((bf16[8,64,1536]{2,1,0:T(8,128)(2,1)}), bf16[8,64,1536]{2,1,0:T(8,128)(2,1)S(1)}, u32[]{:S(2)}, u32[]{:S(2)}) %all-to-all-start) | async-done | bytes 1572896 | tf_op jit(solution)/shard_map/all_to_all | solution.py:32
  51.4 1.4 convolution_multiply_fusion
  52.8 4.6 %collective-permute-start = (f32[256,512]{1,0:T(8,128)}, f32[256,512]{1,0:T(8,128)}, u32[]{:S(2)}, u32[]{:S(2)}) collective-permute-start(f32[256,512]{1,0:T(8,128)} %convolution_multiply_fusion), channel_id=1, source_target_pairs={{0,1},{1,0},{2,3},{3,2},{4,5},{5,4},{6,7},{7,6},{8,9},{9,8},{10,11... | collective-permute-start | bytes 1572872 | tf_op jit(solution)/shard_map/ppermute | solution.py:61
  57.4 1.8 %collective-permute-done = f32[256,512]{1,0:T(8,128)} collective-permute-done((f32[256,512]{1,0:T(8,128)}, f32[256,512]{1,0:T(8,128)}, u32[]{:S(2)}, u32[]{:S(2)}) %collective-permute-start) | collective-permute-done | bytes 524320 | tf_op jit(solution)/shard_map/ppermute | solution.py:61
  59.3 1.6 bitcast_convert_fusion
  60.9 0.0 copy-start
  60.9 0.8 copy-done
  61.7 0.1 fusion.7
  61.8 0.1 select_convert_fusion
  61.9 0.7 pad_maximum_fusion
  62.7 6.8 %all-to-all-start.1 = ((bf16[4,80,512]{2,1,0:T(8,128)(2,1)}), bf16[4,80,512]{2,1,0:T(8,128)(2,1)S(1)}, u32[]{:S(2)}, u32[]{:S(2)}) async-start(bf16[4,80,512]{2,1,0:T(8,128)(2,1)} %pad_maximum_fusion), calls=%async_computation.1 | async-start | bytes 655360 | tf_op jit(solution)/shard_map/all_to_all | solution.py:46
  69.5 10.4 %all-to-all-done.1 = bf16[4,80,512]{2,1,0:T(8,128)(2,1)S(1)} async-done(((bf16[4,80,512]{2,1,0:T(8,128)(2,1)}), bf16[4,80,512]{2,1,0:T(8,128)(2,1)S(1)}, u32[]{:S(2)}, u32[]{:S(2)}) %all-to-all-start.1) | async-done | bytes 327712 | tf_op jit(solution)/shard_map/all_to_all | solution.py:46
  79.8 1.0 fusion.15
  80.8 0.8 broadcast_in_dim.110
  81.7 3.5 %all-to-all-start.2 = ((bf16[8,64,512]{2,1,0:T(8,128)(2,1)}), bf16[8,64,512]{2,1,0:T(8,128)(2,1)S(1)}, u32[]{:S(2)}, u32[]{:S(2)}) async-start(bf16[8,64,512]{2,1,0:T(8,128)(2,1)} %broadcast_in_dim.110), calls=%async_computation.2 | async-start | bytes 1048576 | tf_op jit(solution)/shard_map/all_to_all | solution.py:32
  85.2 0.1 fusion.14
  85.3 0.7 collective-permute-start.1
  86.0 0.0 collective-permute-done.1
  86.0 3.8 %all-gather.3 = bf16[128,512]{1,0:T(8,128)(2,1)S(1)} all-gather(bf16[64,512]{1,0:T(8,128)(2,1)S(1)} %collective-permute-done.1), channel_id=5, replica_groups=mesh['y_lo'=2,'z'=8,'x'=4,'y_hi'=4,'core'=2] {'y_lo'}, dimensions={0}, use_global_device_ids=true | all-gather | bytes 196608 | tf_op jit(solution)/shard_map/all_gather | solution.py:77
  89.8 10.6 %all-to-all-done.2 = bf16[8,64,512]{2,1,0:T(8,128)(2,1)S(1)} async-done(((bf16[8,64,512]{2,1,0:T(8,128)(2,1)}), bf16[8,64,512]{2,1,0:T(8,128)(2,1)S(1)}, u32[]{:S(2)}, u32[]{:S(2)}) %all-to-all-start.2) | async-done | bytes 524320 | tf_op jit(solution)/shard_map/all_to_all | solution.py:32
  100.4 5.1 %collective-permute-start.2 = (bf16[512,512]{1,0:T(8,128)(2,1)S(1)}, bf16[512,512]{1,0:T(8,128)(2,1)S(1)}, u32[]{:S(2)}, u32[]{:S(2)}) collective-permute-start(bf16[512,512]{1,0:T(8,128)(2,1)S(1)} %bitcast.42), channel_id=1, source_target_pairs={{0,1},{1,0},{2,3},{3,2},{4,5},{5,4},{6,7},{7,6},{8,9},{9,8},{10,11... | collective-permute-start | bytes 1572872 | tf_op jit(solution)/shard_map/ppermute | solution.py:76
  105.5 12.3 %all-gather.4 = bf16[8,64,512]{2,1,0:T(8,128)(2,1)S(1)} all-gather(bf16[2,64,512]{2,1,0:T(8,128)(2,1)S(1)} %bitcast.53), channel_id=6, replica_groups=mesh['y_lo'=2,'z'=8,'x'=4,'y_hi'=4,'core'=2] {'x'}, dimensions={0}, use_global_device_ids=true | all-gather | bytes 655360 | tf_op jit(solution)/shard_map/all_gather | solution.py:78
  117.8 0.3 fusion.23
  118.1 0.0 collective-permute-done.2
  118.1 0.3 convolution_add_fusion.1
  118.5 0.1 select_reduce_fusion
  118.6 0.7 pad_maximum_fusion.1
  119.3 3.5 %all-to-all-start.3 = ((bf16[4,80,512]{2,1,0:T(8,128)(2,1)}), bf16[4,80,512]{2,1,0:T(8,128)(2,1)S(1)}, u32[]{:S(2)}, u32[]{:S(2)}) async-start(bf16[4,80,512]{2,1,0:T(8,128)(2,1)} %pad_maximum_fusion.1), calls=%async_computation.3 | async-start | bytes 655360 | tf_op jit(solution)/shard_map/all_to_all | solution.py:46
  122.8 0.2 fusion.13
  123.0 8.1 %all-to-all-done.3 = bf16[4,80,512]{2,1,0:T(8,128)(2,1)S(1)} async-done(((bf16[4,80,512]{2,1,0:T(8,128)(2,1)}), bf16[4,80,512]{2,1,0:T(8,128)(2,1)S(1)}, u32[]{:S(2)}, u32[]{:S(2)}) %all-to-all-start.3) | async-done | bytes 327712 | tf_op jit(solution)/shard_map/all_to_all | solution.py:46
  131.1 0.1 fusion.12
  131.3 19.2 %all_gather.35 = bf16[512,512]{1,0:T(8,128)(2,1)S(1)} all-gather(bf16[64,512]{1,0:T(8,128)(2,1)S(1)} %fusion.12), channel_id=1, replica_groups=mesh['y_lo'=2,'z'=8,'x'=4,'y_hi'=4,'core'=2] {'y_hi','core'}, dimensions={0}, use_global_device_ids=true | all-gather | bytes 589824 | tf_op jit(solution)/shard_map/all_gather | solution.py:93
  150.4 0.0 copy-start.1
  150.4 2.1 %convolution_convert_fusion = bf16[512,1536]{1,0:T(8,128)(2,1)} fusion(bf16[512,512]{1,0:T(8,128)(2,1)S(1)} %all_gather.35, bf16[512,1536]{1,0:T(8,128)(2,1)S(1)} %bitcast.40), kind=kOutput, calls=%fused_computation | convolution fusion | flops 806092800 | bytes 3670016 | tf_op jit(solution)/shard_map/dot_general | solution.py:95
  152.6 0.0 copy-done.1
  152.6 0.0 copy-start.2
  152.6 4.9 %all-to-all-start.4 = ((bf16[8,64,1536]{2,1,0:T(8,128)(2,1)}), bf16[8,64,1536]{2,1,0:T(8,128)(2,1)S(1)}, u32[]{:S(2)}, u32[]{:S(2)}) async-start(bf16[8,64,1536]{2,1,0:T(8,128)(2,1)} %bitcast.48), calls=%async_computation.4 | async-start | bytes 3145728 | tf_op jit(solution)/shard_map/all_to_all | solution.py:96
  157.5 21.0 %all-to-all-done.4 = bf16[8,64,1536]{2,1,0:T(8,128)(2,1)S(1)} async-done(((bf16[8,64,1536]{2,1,0:T(8,128)(2,1)}), bf16[8,64,1536]{2,1,0:T(8,128)(2,1)S(1)}, u32[]{:S(2)}, u32[]{:S(2)}) %all-to-all-start.4) | async-done | bytes 1572896 | tf_op jit(solution)/shard_map/all_to_all | solution.py:96
  178.6 0.0 copy-done.2
  178.6 2.2 %fusion = f32[64,1536]{1,0:T(8,128)} fusion(bf16[512,1536]{1,0:T(8,128)(2,1)S(1)} %bitcast.41, f32[64,1536]{1,0:T(8,128)S(1)} %copy-done.2, bf16[8,64,1536]{2,1,0:T(8,128)(2,1)S(1)} %all-to-all-done.4, pred[]{:T(512)S(6)} %eq.102, pred[]{:T(512)S(6)} %eq.101, pred[]{:T(512)S(6)} %eq.100, pred[]{:T(512)S(6)} %eq.99, pred[]{:T(512)S(6)} %eq.98, pred[]{:T(512)S(6)} %eq.97, ...), kind=kOutput, calls=%fused_computation.2 | convolution fusion | flops 103219200 | bytes 3997708 | tf_op jit(solution)/shard_map/dot_general | solution.py:98
  (11 shorter events, 0.2 us)
Async XLA Ops:
  2.3 49.1 %all-to-all-start = ((bf16[8,64,1536]{2,1,0:T(8,128)(2,1)}), bf16[8,64,1536]{2,1,0:T(8,128)(2,1)S(1)}, u32[]{:S(2)}, u32[]{:S(2)}) async-start(bf16[8,64,1536]{2,1,0:T(8,128)(2,1)} %broadcast_in_dim.98), calls=%async_computation | async-start | bytes 3145728 | tf_op jit(solution)/shard_map/all_to_all | solution.py:32
  52.8 6.4 %collective-permute-start = (f32[256,512]{1,0:T(8,128)}, f32[256,512]{1,0:T(8,128)}, u32[]{:S(2)}, u32[]{:S(2)}) collective-permute-start(f32[256,512]{1,0:T(8,128)} %convolution_multiply_fusion), channel_id=1, source_target_pairs={{0,1},{1,0},{2,3},{3,2},{4,5},{5,4},{6,7},{7,6},{8,9},{9,8},{10,11... | collective-permute-start | bytes 1572872 | tf_op jit(solution)/shard_map/ppermute | solution.py:61
  60.9 0.8 copy-start
  62.7 17.2 %all-to-all-start.1 = ((bf16[4,80,512]{2,1,0:T(8,128)(2,1)}), bf16[4,80,512]{2,1,0:T(8,128)(2,1)S(1)}, u32[]{:S(2)}, u32[]{:S(2)}) async-start(bf16[4,80,512]{2,1,0:T(8,128)(2,1)} %pad_maximum_fusion), calls=%async_computation.1 | async-start | bytes 655360 | tf_op jit(solution)/shard_map/all_to_all | solution.py:46
  81.7 18.7 %all-to-all-start.2 = ((bf16[8,64,512]{2,1,0:T(8,128)(2,1)}), bf16[8,64,512]{2,1,0:T(8,128)(2,1)S(1)}, u32[]{:S(2)}, u32[]{:S(2)}) async-start(bf16[8,64,512]{2,1,0:T(8,128)(2,1)} %broadcast_in_dim.110), calls=%async_computation.2 | async-start | bytes 1048576 | tf_op jit(solution)/shard_map/all_to_all | solution.py:32
  85.3 0.7 collective-permute-start.1
  100.4 17.7 %collective-permute-start.2 = (bf16[512,512]{1,0:T(8,128)(2,1)S(1)}, bf16[512,512]{1,0:T(8,128)(2,1)S(1)}, u32[]{:S(2)}, u32[]{:S(2)}) collective-permute-start(bf16[512,512]{1,0:T(8,128)(2,1)S(1)} %bitcast.42), channel_id=1, source_target_pairs={{0,1},{1,0},{2,3},{3,2},{4,5},{5,4},{6,7},{7,6},{8,9},{9,8},{10,11... | collective-permute-start | bytes 1572872 | tf_op jit(solution)/shard_map/ppermute | solution.py:76
  119.3 11.8 %all-to-all-start.3 = ((bf16[4,80,512]{2,1,0:T(8,128)(2,1)}), bf16[4,80,512]{2,1,0:T(8,128)(2,1)S(1)}, u32[]{:S(2)}, u32[]{:S(2)}) async-start(bf16[4,80,512]{2,1,0:T(8,128)(2,1)} %pad_maximum_fusion.1), calls=%async_computation.3 | async-start | bytes 655360 | tf_op jit(solution)/shard_map/all_to_all | solution.py:46
  150.4 2.1 %copy-start.1 = (bf16[512,512]{1,0:T(8,128)(2,1)}, bf16[512,512]{1,0:T(8,128)(2,1)S(1)}, u32[]{:S(2)}) copy-start(bf16[512,512]{1,0:T(8,128)(2,1)S(1)} %all_gather.35) | copy-start | bytes 1572868
  152.6 26.0 %copy-start.2 = (f32[64,1536]{1,0:T(8,128)S(1)}, f32[64,1536]{1,0:T(8,128)}, u32[]{:S(2)}) copy-start(f32[64,1536]{1,0:T(8,128)} %param.1) | copy-start | bytes 1179652
  152.6 26.0 %all-to-all-start.4 = ((bf16[8,64,1536]{2,1,0:T(8,128)(2,1)}), bf16[8,64,1536]{2,1,0:T(8,128)(2,1)S(1)}, u32[]{:S(2)}, u32[]{:S(2)}) async-start(bf16[8,64,1536]{2,1,0:T(8,128)(2,1)} %bitcast.48), calls=%async_computation.4 | async-start | bytes 3145728 | tf_op jit(solution)/shard_map/all_to_all | solution.py:96

commit v8 on v6

v8 whole, which is shorter than its diff:
```python
import jax
import jax.numpy as jnp
from jax import lax
from jax.sharding import Mesh, PartitionSpec as P

N = 12288

coef_linear = 3.4445
coef_cubic = -4.775
coef_quintic = 2.0315

LO = ("x", "y_lo")
COL = ("y_hi", "core")
ROW = ("y_lo", "z", "x")
MESH = ("y_lo", "z", "x", "y_hi", "core")


def rest_of(x):
    return x - lax.reduce_precision(x, exponent_bits=8, mantissa_bits=7)


def dot_nt(a, b):
    return lax.dot_general(a, b, (((1,), (1,)), ((), ())), preferred_element_type=jnp.float32)


def swap_x_y_hi(block):
    pairs = [((x * 4 + y) * 2 + k, (y * 4 + x) * 2 + k) for x in range(4) for y in range(4) for k in range(2)]
    return lax.ppermute(block, ("x", "y_hi", "core"), pairs)


def spread(block, axis):
    return lax.all_to_all(jnp.broadcast_to(block[None], (8,) + block.shape), axis, 0, 0)


def sum_others(arrived, me):
    total = 0.0
    for i in range(arrived.shape[0]):
        total = total + jnp.where(i == me, 0.0, arrived[i].astype(jnp.float32))
    return total


def sum_pieces(pieces, axis):
    me = lax.axis_index(axis)
    arrived = lax.all_to_all(pieces.astype(jnp.bfloat16), axis, 0, 0)
    return lax.dynamic_index_in_dim(pieces, me, 0, keepdims=False) + sum_others(arrived, me)


def per_device(x_scaled):
    rows, cols = x_scaled.shape
    xb = x_scaled.astype(jnp.bfloat16)
    by_hi = spread(xb, "z").reshape(8 * rows, cols)
    pair = lax.all_gather(xb, "y_lo", axis=0)
    by_lo = [lax.all_gather(pair[y], "x", axis=0, tiled=True) for y in range(2)]

    tile = jnp.concatenate([dot_nt(part, by_hi) for part in by_lo]) * (1.0 / N)
    gram = sum_pieces(tile.reshape(8, rows, 8 * rows), ("core", "y_hi"))

    rounded = gram.astype(jnp.bfloat16)
    right = spread(rounded, "z").reshape(8 * rows, 8 * rows)
    right_other = lax.ppermute(right, "core", [(0, 1), (1, 0)])
    left = lax.all_gather(swap_x_y_hi(rounded), "y_lo", axis=0)
    left = lax.all_gather(left, "x", axis=0).reshape(4, 2, rows, 8 * rows)
    core = lax.axis_index("core")
    own = jnp.where(core == 0, left[:, 0], left[:, 1]).reshape(4 * rows, 8 * rows)
    other = jnp.where(core == 0, left[:, 1], left[:, 0]).reshape(4 * rows, 8 * rows)
    square = jnp.dot(own, right, preferred_element_type=jnp.float32) + jnp.dot(
        other, right_other, preferred_element_type=jnp.float32
    )
    square = sum_pieces(square.reshape(4, rows, 8 * rows), "y_hi")

    at_home = lax.dynamic_slice(left, (lax.axis_index("y_hi"), core, 0, 0), (1, 1, rows, 8 * rows))[0, 0]
    column = lax.broadcasted_iota(jnp.int32, at_home.shape, 1) - lax.axis_index("z") * rows
    on_diagonal = column == lax.broadcasted_iota(jnp.int32, at_home.shape, 0)
    diagonal = jnp.where(on_diagonal, at_home.astype(jnp.float32), 0.0).sum(1, keepdims=True)
    square = square + rest_of(gram) * (2.0 * diagonal)

    poly = (coef_cubic * gram + coef_quintic * square).astype(jnp.bfloat16)
    poly = lax.all_gather(poly, COL, axis=0, tiled=True)
    me = lax.axis_index(LO)
    product = jnp.dot(poly, by_hi, preferred_element_type=jnp.float32).astype(jnp.bfloat16)
    arrived = lax.all_to_all(product.reshape(8, rows, cols), LO, 0, 0)
    mine = lax.dynamic_slice_in_dim(poly, me * rows, rows)
    own = jnp.dot(mine, by_hi, preferred_element_type=jnp.float32)
    return coef_linear * x_scaled + own + sum_others(arrived, me)


def solution(mesh):
    fine = Mesh(mesh.devices.reshape(2, 8, 4, 4, 2), MESH)
    return jax.shard_map(
        per_device,
        mesh=fine,
        in_specs=(P(ROW, COL),),
        out_specs=P(ROW, COL),
        check_vma=False,
    )
```

time: 177 us -> 177 us (level)
  waiting for transfers between devices: 49.1 us -> 66 us
  blocking collectives: 78.5 us -> 63.8 us
    all_to_all x0 -> x1, waiting for transfers between devices: none -> 21 us  [per_device(): arrived = lax.all_to_all(product.reshape(8, rows, cols), LO, 0, 0)]
    all_to_all x1 -> x0, blocking collectives: 11.3 us -> none  [sum_pieces(): arrived = lax.all_to_all(pieces.astype(jnp.bfloat16), axis, 0, 0)]
    all_to_all x2, waiting for transfers between devices: 29.8 us -> 23.7 us  [sum_pieces(): arrived = lax.all_to_all(pieces.astype(jnp.bfloat16), axis, 0, 0)]
    ppermute x1 -> x0, starting transfers between devices: 5.76 us -> none  [per_device(): home = home + lax.ppermute(away, 'core', [(0, 1), (1, 0)])]
    all_to_all x0 -> x1, starting transfers between devices: none -> 4.75 us  [per_device(): arrived = lax.all_to_all(product.reshape(8, rows, cols), LO, 0, 0)]
    all_to_all x2, waiting for transfers between devices: 17.8 us -> 21.3 us  [spread(): lax.all_to_all(jnp.broadcast_to(block[None], (8,) + block.shape), axis, 0...]
    ppermute x1, starting transfers between devices: 5.73 us -> 2.36 us  [per_device(): right_other = lax.ppermute(right, 'core', [(0, 1), (1, 0)])]
    all_to_all x2, starting transfers between devices: 10.4 us -> 13.2 us  [sum_pieces(): arrived = lax.all_to_all(pieces.astype(jnp.bfloat16), axis, 0, 0)]
where the time goes in v8:
time: 177 us
  waiting for transfers between devices  66 us (37%)
  blocking collectives  63.8 us (36%)
  starting transfers between devices  35.3 us (20%)
  matrix products  6.11 us (3%)
  other arithmetic  3.12 us (2%)
  local copies, waits for them, and re-layouts  2.17 us (1%)
    all_gather x2, blocking collectives, per_device(): by_lo = [lax.all_gather(pair[y], 'x', axis=0, tiled=True) for y in range(2)]  23.9 us
    all_to_all x2, waiting for transfers between devices, sum_pieces(): arrived = lax.all_to_all(pieces.astype(jnp.bfloat16), axis, 0, 0)  23.7 us
    all_to_all x2, waiting for transfers between devices, spread(): lax.all_to_all(jnp.broadcast_to(block[None], (8,) + block.shape), axis, 0...  21.3 us
    all_to_all x1, waiting for transfers between devices, per_device(): arrived = lax.all_to_all(product.reshape(8, rows, cols), LO, 0, 0)  21 us
    all_gather x1, blocking collectives, per_device(): poly = lax.all_gather(poly, COL, axis=0, tiled=True)  18.7 us
    all_to_all x2, starting transfers between devices, spread(): lax.all_to_all(jnp.broadcast_to(block[None], (8,) + block.shape), axis, 0...  14.4 us
    all_to_all x2, starting transfers between devices, sum_pieces(): arrived = lax.all_to_all(pieces.astype(jnp.bfloat16), axis, 0, 0)  13.2 us
    all_gather x1, blocking collectives, per_device(): left = lax.all_gather(left, 'x', axis=0).reshape(4, 2, rows, 8 * rows)  10.9 us
  transfers between devices with their start and end apart: 7, of which 5 were waited for; matrix products, arithmetic and copies ran while one was open for 0% of the time, Pallas kernels for 0%

profile of v8, /device:TPU:1, one launch (start us, length us, event | category | flops | bytes accessed | tf_op | source)
XLA Modules:
  0.0 176.6 jit_solution(15841846821765938098)
XLA Ops:
  0.0 1.0 convert_element_type.115
  1.0 1.3 broadcast_in_dim.45
  2.3 10.9 %all-to-all-start = ((bf16[8,64,1536]{2,1,0:T(8,128)(2,1)}), bf16[8,64,1536]{2,1,0:T(8,128)(2,1)S(1)}, u32[]{:S(2)}, u32[]{:S(2)}) async-start(bf16[8,64,1536]{2,1,0:T(8,128)(2,1)} %broadcast_in_dim.45), calls=%async_computation | async-start | bytes 3145728 | tf_op jit(solution)/shard_map/all_to_all | solution.py:32
  13.2 6.1 %all-gather = bf16[128,1536]{1,0:T(8,128)(2,1)S(1)} all-gather(bf16[64,1536]{1,0:T(8,128)(2,1)S(1)} %convert_element_type.115), channel_id=2, replica_groups=mesh['y_lo'=2,'z'=8,'x'=4,'y_hi'=4,'core'=2] {'y_lo'}, dimensions={0}, use_global_device_ids=true | all-gather | bytes 589824 | tf_op jit(solution)/shard_map/all_gather | solution.py:52
  19.3 12.6 %all-gather.5 = bf16[256,1536]{1,0:T(8,128)(2,1)S(1)} all-gather(bf16[64,1536]{1,0:T(8,128)(2,1)S(1)} %get-tuple-element.9), channel_id=7, replica_groups=mesh['y_lo'=2,'z'=8,'x'=4,'y_hi'=4,'core'=2] {'x'}, dimensions={0}, use_global_device_ids=true | all-gather | bytes 983040 | tf_op jit(solution)/shard_map/all_gather | solution.py:53
  32.0 11.3 %all-gather.6 = bf16[256,1536]{1,0:T(8,128)(2,1)S(1)} all-gather(bf16[64,1536]{1,0:T(8,128)(2,1)S(1)} %get-tuple-element.10), channel_id=8, replica_groups=mesh['y_lo'=2,'z'=8,'x'=4,'y_hi'=4,'core'=2] {'x'}, dimensions={0}, use_global_device_ids=true | all-gather | bytes 983040 | tf_op jit(solution)/shard_map/all_gather | solution.py:53
  43.3 8.2 %all-to-all-done = bf16[8,64,1536]{2,1,0:T(8,128)(2,1)S(1)} async-done(((bf16[8,64,1536]{2,1,0:T(8,128)(2,1)}), bf16[8,64,1536]{2,1,0:T(8,128)(2,1)S(1)}, u32[]{:S(2)}, u32[]{:S(2)}) %all-to-all-start) | async-done | bytes 1572896 | tf_op jit(solution)/shard_map/all_to_all | solution.py:32
  51.5 0.6 fusion.10
  52.1 0.6 fusion.11
  52.7 0.1 maximum_multiply_fusion
  52.8 0.9 convert_element_type.116
  53.6 9.8 %all-to-all-start.1 = ((bf16[8,64,512]{2,1,0:T(8,128)(2,1)}), bf16[8,64,512]{2,1,0:T(8,128)(2,1)S(1)}, u32[]{:S(2)}, u32[]{:S(2)}) async-start(bf16[8,64,512]{2,1,0:T(8,128)(2,1)} %convert_element_type.116), calls=%async_computation.1 | async-start | bytes 1048576 | tf_op jit(solution)/shard_map/all_to_all | solution.py:44
  63.4 15.9 %all-to-all-done.1 = bf16[8,64,512]{2,1,0:T(8,128)(2,1)S(1)} async-done(((bf16[8,64,512]{2,1,0:T(8,128)(2,1)}), bf16[8,64,512]{2,1,0:T(8,128)(2,1)S(1)}, u32[]{:S(2)}, u32[]{:S(2)}) %all-to-all-start.1) | async-done | bytes 524320 | tf_op jit(solution)/shard_map/all_to_all | solution.py:44
  79.3 0.1 convert_bitcast_fusion
  79.4 0.8 broadcast_in_dim.48
  80.2 3.5 %all-to-all-start.2 = ((bf16[8,64,512]{2,1,0:T(8,128)(2,1)}), bf16[8,64,512]{2,1,0:T(8,128)(2,1)S(1)}, u32[]{:S(2)}, u32[]{:S(2)}) async-start(bf16[8,64,512]{2,1,0:T(8,128)(2,1)} %broadcast_in_dim.48), calls=%async_computation.2 | async-start | bytes 1048576 | tf_op jit(solution)/shard_map/all_to_all | solution.py:32
  83.7 0.7 collective-permute-start
  84.4 0.0 collective-permute-done
  84.4 4.2 %all-gather.3 = bf16[128,512]{1,0:T(8,128)(2,1)S(1)} all-gather(bf16[64,512]{1,0:T(8,128)(2,1)S(1)} %collective-permute-done), channel_id=5, replica_groups=mesh['y_lo'=2,'z'=8,'x'=4,'y_hi'=4,'core'=2] {'y_lo'}, dimensions={0}, use_global_device_ids=true | all-gather | bytes 196608 | tf_op jit(solution)/shard_map/all_gather | solution.py:61
  88.6 13.1 %all-to-all-done.2 = bf16[8,64,512]{2,1,0:T(8,128)(2,1)S(1)} async-done(((bf16[8,64,512]{2,1,0:T(8,128)(2,1)}), bf16[8,64,512]{2,1,0:T(8,128)(2,1)S(1)}, u32[]{:S(2)}, u32[]{:S(2)}) %all-to-all-start.2) | async-done | bytes 524320 | tf_op jit(solution)/shard_map/all_to_all | solution.py:32
  101.7 2.4 %collective-permute-start.1 = (bf16[512,512]{1,0:T(8,128)(2,1)S(1)}, bf16[512,512]{1,0:T(8,128)(2,1)S(1)}, u32[]{:S(2)}, u32[]{:S(2)}) collective-permute-start(bf16[512,512]{1,0:T(8,128)(2,1)S(1)} %bitcast.45), channel_id=1, source_target_pairs={{0,1},{1,0},{2,3},{3,2},{4,5},{5,4},{6,7},{7,6},{8,9},{9,8},{10,11... | collective-permute-start | bytes 1572872 | tf_op jit(solution)/shard_map/ppermute | solution.py:60
  104.0 10.9 %all-gather.4 = bf16[8,64,512]{2,1,0:T(8,128)(2,1)S(1)} all-gather(bf16[2,64,512]{2,1,0:T(8,128)(2,1)S(1)} %bitcast.50), channel_id=6, replica_groups=mesh['y_lo'=2,'z'=8,'x'=4,'y_hi'=4,'core'=2] {'x'}, dimensions={0}, use_global_device_ids=true | all-gather | bytes 655360 | tf_op jit(solution)/shard_map/all_gather | solution.py:62
  115.0 0.3 fusion.12
  115.3 0.0 collective-permute-done.1
  115.3 0.3 convolution_add_fusion.1
  115.6 0.7 convert_element_type.127
  116.3 3.4 %all-to-all-start.3 = ((bf16[4,64,512]{2,1,0:T(8,128)(2,1)}), bf16[4,64,512]{2,1,0:T(8,128)(2,1)S(1)}, u32[]{:S(2)}, u32[]{:S(2)}) async-start(bf16[4,64,512]{2,1,0:T(8,128)(2,1)} %convert_element_type.127), calls=%async_computation.3 | async-start | bytes 524288 | tf_op jit(solution)/shard_map/all_to_all | solution.py:44
  119.8 0.1 fusion.6
  119.9 7.9 %all-to-all-done.3 = bf16[4,64,512]{2,1,0:T(8,128)(2,1)S(1)} async-done(((bf16[4,64,512]{2,1,0:T(8,128)(2,1)}), bf16[4,64,512]{2,1,0:T(8,128)(2,1)S(1)}, u32[]{:S(2)}, u32[]{:S(2)}) %all-to-all-start.3) | async-done | bytes 262176 | tf_op jit(solution)/shard_map/all_to_all | solution.py:44
  127.8 0.1 fusion.5
  127.9 18.7 %all_gather.35 = bf16[512,512]{1,0:T(8,128)(2,1)S(1)} all-gather(bf16[64,512]{1,0:T(8,128)(2,1)S(1)} %fusion.5), channel_id=1, replica_groups=mesh['y_lo'=2,'z'=8,'x'=4,'y_hi'=4,'core'=2] {'y_hi','core'}, dimensions={0}, use_global_device_ids=true | all-gather | bytes 589824 | tf_op jit(solution)/shard_map/all_gather | solution.py:78
  146.5 0.0 copy-start
  146.5 2.2 %convolution_convert_fusion = bf16[512,1536]{1,0:T(8,128)(2,1)} fusion(bf16[512,512]{1,0:T(8,128)(2,1)S(1)} %all_gather.35, bf16[512,1536]{1,0:T(8,128)(2,1)S(1)} %bitcast.37), kind=kOutput, calls=%fused_computation | convolution fusion | flops 806092800 | bytes 3670016 | tf_op jit(solution)/shard_map/dot_general | solution.py:80
  148.7 0.0 copy-done
  148.7 0.0 copy-start.1
  148.7 4.8 %all-to-all-start.4 = ((bf16[8,64,1536]{2,1,0:T(8,128)(2,1)}), bf16[8,64,1536]{2,1,0:T(8,128)(2,1)S(1)}, u32[]{:S(2)}, u32[]{:S(2)}) async-start(bf16[8,64,1536]{2,1,0:T(8,128)(2,1)} %bitcast.47), calls=%async_computation.4 | async-start | bytes 3145728 | tf_op jit(solution)/shard_map/all_to_all | solution.py:81
  153.4 21.0 %all-to-all-done.4 = bf16[8,64,1536]{2,1,0:T(8,128)(2,1)S(1)} async-done(((bf16[8,64,1536]{2,1,0:T(8,128)(2,1)}), bf16[8,64,1536]{2,1,0:T(8,128)(2,1)S(1)}, u32[]{:S(2)}, u32[]{:S(2)}) %all-to-all-start.4) | async-done | bytes 1572896 | tf_op jit(solution)/shard_map/all_to_all | solution.py:81
  174.5 0.0 copy-done.1
  174.5 2.2 %fusion = f32[64,1536]{1,0:T(8,128)} fusion(bf16[512,1536]{1,0:T(8,128)(2,1)S(1)} %bitcast.38, f32[64,1536]{1,0:T(8,128)S(1)} %copy-done.1, bf16[8,64,1536]{2,1,0:T(8,128)(2,1)S(1)} %all-to-all-done.4, pred[]{:T(512)S(6)} %eq.88, pred[]{:T(512)S(6)} %eq.87, pred[]{:T(512)S(6)} %eq.86, pred[]{:T(512)S(6)} %eq.85, pred[]{:T(512)S(6)} %eq.84, pred[]{:T(512)S(6)} %eq.83, ...), kind=kOutput, calls=%fused_computation.2 | convolution fusion | flops 103219200 | bytes 3997708 | tf_op jit(solution)/shard_map/dot_general | solution.py:83
  (5 shorter events, 0.1 us)
Async XLA Ops:
  2.3 49.1 %all-to-all-start = ((bf16[8,64,1536]{2,1,0:T(8,128)(2,1)}), bf16[8,64,1536]{2,1,0:T(8,128)(2,1)S(1)}, u32[]{:S(2)}, u32[]{:S(2)}) async-start(bf16[8,64,1536]{2,1,0:T(8,128)(2,1)} %broadcast_in_dim.45), calls=%async_computation | async-start | bytes 3145728 | tf_op jit(solution)/shard_map/all_to_all | solution.py:32
  53.6 25.6 %all-to-all-start.1 = ((bf16[8,64,512]{2,1,0:T(8,128)(2,1)}), bf16[8,64,512]{2,1,0:T(8,128)(2,1)S(1)}, u32[]{:S(2)}, u32[]{:S(2)}) async-start(bf16[8,64,512]{2,1,0:T(8,128)(2,1)} %convert_element_type.116), calls=%async_computation.1 | async-start | bytes 1048576 | tf_op jit(solution)/shard_map/all_to_all | solution.py:44
  80.2 21.4 %all-to-all-start.2 = ((bf16[8,64,512]{2,1,0:T(8,128)(2,1)}), bf16[8,64,512]{2,1,0:T(8,128)(2,1)S(1)}, u32[]{:S(2)}, u32[]{:S(2)}) async-start(bf16[8,64,512]{2,1,0:T(8,128)(2,1)} %broadcast_in_dim.48), calls=%async_computation.2 | async-start | bytes 1048576 | tf_op jit(solution)/shard_map/all_to_all | solution.py:32
  83.7 0.7 collective-permute-start
  101.7 13.6 %collective-permute-start.1 = (bf16[512,512]{1,0:T(8,128)(2,1)S(1)}, bf16[512,512]{1,0:T(8,128)(2,1)S(1)}, u32[]{:S(2)}, u32[]{:S(2)}) collective-permute-start(bf16[512,512]{1,0:T(8,128)(2,1)S(1)} %bitcast.45), channel_id=1, source_target_pairs={{0,1},{1,0},{2,3},{3,2},{4,5},{5,4},{6,7},{7,6},{8,9},{9,8},{10,11... | collective-permute-start | bytes 1572872 | tf_op jit(solution)/shard_map/ppermute | solution.py:60
  116.3 11.4 %all-to-all-start.3 = ((bf16[4,64,512]{2,1,0:T(8,128)(2,1)}), bf16[4,64,512]{2,1,0:T(8,128)(2,1)S(1)}, u32[]{:S(2)}, u32[]{:S(2)}) async-start(bf16[4,64,512]{2,1,0:T(8,128)(2,1)} %convert_element_type.127), calls=%async_computation.3 | async-start | bytes 524288 | tf_op jit(solution)/shard_map/all_to_all | solution.py:44
  146.5 2.2 %copy-start = (bf16[512,512]{1,0:T(8,128)(2,1)}, bf16[512,512]{1,0:T(8,128)(2,1)S(1)}, u32[]{:S(2)}) copy-start(bf16[512,512]{1,0:T(8,128)(2,1)S(1)} %all_gather.35) | copy-start | bytes 1572868
  148.7 25.8 %copy-start.1 = (f32[64,1536]{1,0:T(8,128)S(1)}, f32[64,1536]{1,0:T(8,128)}, u32[]{:S(2)}) copy-start(f32[64,1536]{1,0:T(8,128)} %param.1) | copy-start | bytes 1179652
  148.7 25.8 %all-to-all-start.4 = ((bf16[8,64,1536]{2,1,0:T(8,128)(2,1)}), bf16[8,64,1536]{2,1,0:T(8,128)(2,1)S(1)}, u32[]{:S(2)}, u32[]{:S(2)}) async-start(bf16[8,64,1536]{2,1,0:T(8,128)(2,1)} %bitcast.47), calls=%async_computation.4 | async-start | bytes 3145728 | tf_op jit(solution)/shard_map/all_to_all | solution.py:81

commit v9 on v8

--- a/solution.py
+++ b/solution.py
@@ -47,8 +47,8 @@
 
 def per_device(x_scaled):
     rows, cols = x_scaled.shape
-    xb = x_scaled.astype(jnp.bfloat16)
-    by_hi = spread(xb, "z").reshape(8 * rows, cols)
+    by_hi = spread(x_scaled.astype(jnp.bfloat16), "z").reshape(8 * rows, cols)
+    xb = lax.reduce_precision(x_scaled, exponent_bits=8, mantissa_bits=7).astype(jnp.bfloat16)
     pair = lax.all_gather(xb, "y_lo", axis=0)
     by_lo = [lax.all_gather(pair[y], "x", axis=0, tiled=True) for y in range(2)]
 
@@ -58,17 +58,17 @@
     rounded = gram.astype(jnp.bfloat16)
     right = spread(rounded, "z").reshape(8 * rows, 8 * rows)
     right_other = lax.ppermute(right, "core", [(0, 1), (1, 0)])
-    left = lax.all_gather(swap_x_y_hi(rounded), "y_lo", axis=0)
-    left = lax.all_gather(left, "x", axis=0).reshape(4, 2, rows, 8 * rows)
+    left = lax.all_gather(swap_x_y_hi(rounded), "x", axis=0)
+    left = lax.all_gather(left, "y_lo", axis=0)
     core = lax.axis_index("core")
-    own = jnp.where(core == 0, left[:, 0], left[:, 1]).reshape(4 * rows, 8 * rows)
-    other = jnp.where(core == 0, left[:, 1], left[:, 0]).reshape(4 * rows, 8 * rows)
+    own = jnp.where(core == 0, left[0], left[1]).reshape(4 * rows, 8 * rows)
+    other = jnp.where(core == 0, left[1], left[0]).reshape(4 * rows, 8 * rows)
     square = jnp.dot(own, right, preferred_element_type=jnp.float32) + jnp.dot(
         other, right_other, preferred_element_type=jnp.float32
     )
     square = sum_pieces(square.reshape(4, rows, 8 * rows), "y_hi")
 
-    at_home = lax.dynamic_slice(left, (lax.axis_index("y_hi"), core, 0, 0), (1, 1, rows, 8 * rows))[0, 0]
+    at_home = lax.dynamic_slice(left, (core, lax.axis_index("y_hi"), 0, 0), (1, 1, rows, 8 * rows))[0, 0]
     column = lax.broadcasted_iota(jnp.int32, at_home.shape, 1) - lax.axis_index("z") * rows
     on_diagonal = column == lax.broadcasted_iota(jnp.int32, at_home.shape, 0)
     diagonal = jnp.where(on_diagonal, at_home.astype(jnp.float32), 0.0).sum(1, keepdims=True)

time: 177 us -> 181 us (1.023)
  blocking collectives: 63.8 us -> 77.9 us
  waiting for transfers between devices: 66 us -> 53.1 us
  starting transfers between devices: 35.3 us -> 38.1 us
    all_gather x2, blocking collectives: 15.1 us -> 29.7 us  [the longest x1 21.1 us: per_device(): left = lax.all_gather(swap_x_y_hi(rounded), 'x', axis=0)]
    all_to_all x2, waiting for transfers between devices: 21.3 us -> 8.19 us  [spread(): lax.all_to_all(jnp.broadcast_to(block[None], (8,) + block.shape), axis, 0...]
    ppermute x1, starting transfers between devices: 2.36 us -> 5.43 us  [per_device(): right_other = lax.ppermute(right, 'core', [(0, 1), (1, 0)])]
  transfers between devices with their start and end apart: 7 -> 7, of which waited for: 5 -> 4; matrix products, arithmetic and copies ran while one was open for 0% -> 0% of each run, Pallas kernels for 0% -> 0%
where the time goes in v9:
time: 181 us
  blocking collectives  77.9 us (43%)
  waiting for transfers between devices  53.1 us (29%)
  starting transfers between devices  38.1 us (21%)
  matrix products  6.11 us (3%)
  other arithmetic  3.25 us (2%)
  local copies, waits for them, and re-layouts  2.16 us (1%)
    all_gather x2, blocking collectives, per_device(): by_lo = [lax.all_gather(pair[y], 'x', axis=0, tiled=True) for y in range(2)]  23.9 us
    all_to_all x2, waiting for transfers between devices, sum_pieces(): arrived = lax.all_to_all(pieces.astype(jnp.bfloat16), axis, 0, 0)  23.8 us
    all_gather x1, blocking collectives, per_device(): left = lax.all_gather(swap_x_y_hi(rounded), 'x', axis=0)  21.1 us
    all_to_all x1, waiting for transfers between devices, per_device(): arrived = lax.all_to_all(product.reshape(8, rows, cols), LO, 0, 0)  21 us
    all_gather x1, blocking collectives, per_device(): poly = lax.all_gather(poly, COL, axis=0, tiled=True)  18.2 us
    all_to_all x2, starting transfers between devices, spread(): lax.all_to_all(jnp.broadcast_to(block[None], (8,) + block.shape), axis, 0...  14.4 us
    all_to_all x2, starting transfers between devices, sum_pieces(): arrived = lax.all_to_all(pieces.astype(jnp.bfloat16), axis, 0, 0)  13.3 us
    all_gather x1, blocking collectives, per_device(): left = lax.all_gather(left, 'y_lo', axis=0)  8.6 us
  transfers between devices with their start and end apart: 7, of which 4 were waited for; matrix products, arithmetic and copies ran while one was open for 0% of the time, Pallas kernels for 0%

profile of v9, /device:TPU:1, one launch (start us, length us, event | category | flops | bytes accessed | tf_op | source)
XLA Modules:
  0.0 180.8 jit_solution(17049999690697523406)
XLA Ops:
  0.0 1.2 reduce-precision_convert_fusion
  1.2 1.3 broadcast_in_dim.45
  2.5 10.9 %all-to-all-start = ((bf16[8,64,1536]{2,1,0:T(8,128)(2,1)}), bf16[8,64,1536]{2,1,0:T(8,128)(2,1)S(1)}, u32[]{:S(2)}, u32[]{:S(2)}) async-start(bf16[8,64,1536]{2,1,0:T(8,128)(2,1)} %broadcast_in_dim.45), calls=%async_computation | async-start | bytes 3145728 | tf_op jit(solution)/shard_map/all_to_all | solution.py:32
  13.3 6.1 %all-gather = bf16[128,1536]{1,0:T(8,128)(2,1)S(1)} all-gather(bf16[64,1536]{1,0:T(8,128)(2,1)S(1)} %get-tuple-element.11), channel_id=2, replica_groups=mesh['y_lo'=2,'z'=8,'x'=4,'y_hi'=4,'core'=2] {'y_lo'}, dimensions={0}, use_global_device_ids=true | all-gather | bytes 589824 | tf_op jit(solution)/shard_map/all_gather | solution.py:52
  19.5 12.6 %all-gather.5 = bf16[256,1536]{1,0:T(8,128)(2,1)S(1)} all-gather(bf16[64,1536]{1,0:T(8,128)(2,1)S(1)} %get-tuple-element.9), channel_id=7, replica_groups=mesh['y_lo'=2,'z'=8,'x'=4,'y_hi'=4,'core'=2] {'x'}, dimensions={0}, use_global_device_ids=true | all-gather | bytes 983040 | tf_op jit(solution)/shard_map/all_gather | solution.py:53
  32.1 11.3 %all-gather.6 = bf16[256,1536]{1,0:T(8,128)(2,1)S(1)} all-gather(bf16[64,1536]{1,0:T(8,128)(2,1)S(1)} %get-tuple-element.10), channel_id=8, replica_groups=mesh['y_lo'=2,'z'=8,'x'=4,'y_hi'=4,'core'=2] {'x'}, dimensions={0}, use_global_device_ids=true | all-gather | bytes 983040 | tf_op jit(solution)/shard_map/all_gather | solution.py:53
  43.4 8.2 %all-to-all-done = bf16[8,64,1536]{2,1,0:T(8,128)(2,1)S(1)} async-done(((bf16[8,64,1536]{2,1,0:T(8,128)(2,1)}), bf16[8,64,1536]{2,1,0:T(8,128)(2,1)S(1)}, u32[]{:S(2)}, u32[]{:S(2)}) %all-to-all-start) | async-done | bytes 1572896 | tf_op jit(solution)/shard_map/all_to_all | solution.py:32
  51.6 0.6 fusion.10
  52.2 0.6 fusion.11
  52.8 0.1 maximum_multiply_fusion
  52.9 0.9 convert_element_type.120
  53.8 9.8 %all-to-all-start.1 = ((bf16[8,64,512]{2,1,0:T(8,128)(2,1)}), bf16[8,64,512]{2,1,0:T(8,128)(2,1)S(1)}, u32[]{:S(2)}, u32[]{:S(2)}) async-start(bf16[8,64,512]{2,1,0:T(8,128)(2,1)} %convert_element_type.120), calls=%async_computation.1 | async-start | bytes 1048576 | tf_op jit(solution)/shard_map/all_to_all | solution.py:44
  63.5 15.9 %all-to-all-done.1 = bf16[8,64,512]{2,1,0:T(8,128)(2,1)S(1)} async-done(((bf16[8,64,512]{2,1,0:T(8,128)(2,1)}), bf16[8,64,512]{2,1,0:T(8,128)(2,1)S(1)}, u32[]{:S(2)}, u32[]{:S(2)}) %all-to-all-start.1) | async-done | bytes 524320 | tf_op jit(solution)/shard_map/all_to_all | solution.py:44
  79.4 0.1 convert_bitcast_fusion
  79.5 0.8 broadcast_in_dim.48
  80.3 3.5 %all-to-all-start.2 = ((bf16[8,64,512]{2,1,0:T(8,128)(2,1)}), bf16[8,64,512]{2,1,0:T(8,128)(2,1)S(1)}, u32[]{:S(2)}, u32[]{:S(2)}) async-start(bf16[8,64,512]{2,1,0:T(8,128)(2,1)} %broadcast_in_dim.48), calls=%async_computation.2 | async-start | bytes 1048576 | tf_op jit(solution)/shard_map/all_to_all | solution.py:32
  83.9 0.7 collective-permute-start
  84.5 0.0 collective-permute-done
  84.6 21.1 %all-gather.3 = bf16[256,512]{1,0:T(8,128)(2,1)S(1)} all-gather(bf16[64,512]{1,0:T(8,128)(2,1)S(1)} %collective-permute-done), channel_id=5, replica_groups=mesh['y_lo'=2,'z'=8,'x'=4,'y_hi'=4,'core'=2] {'x'}, dimensions={0}, use_global_device_ids=true | all-gather | bytes 327680 | tf_op jit(solution)/shard_map/all_gather | solution.py:61
  105.6 0.0 all-to-all-done.2
  105.6 5.4 %collective-permute-start.1 = (bf16[512,512]{1,0:T(8,128)(2,1)S(1)}, bf16[512,512]{1,0:T(8,128)(2,1)S(1)}, u32[]{:S(2)}, u32[]{:S(2)}) collective-permute-start(bf16[512,512]{1,0:T(8,128)(2,1)S(1)} %bitcast.44), channel_id=1, source_target_pairs={{0,1},{1,0},{2,3},{3,2},{4,5},{5,4},{6,7},{7,6},{8,9},{9,8},{10,11... | collective-permute-start | bytes 1572872 | tf_op jit(solution)/shard_map/ppermute | solution.py:60
  111.1 8.6 %all-gather.4 = bf16[8,64,512]{2,1,0:T(8,128)(2,1)S(1)} all-gather(bf16[4,64,512]{2,1,0:T(8,128)(2,1)S(1)} %bitcast.47), channel_id=6, replica_groups=mesh['y_lo'=2,'z'=8,'x'=4,'y_hi'=4,'core'=2] {'y_lo'}, dimensions={0}, use_global_device_ids=true | all-gather | bytes 786432 | tf_op jit(solution)/shard_map/all_gather | solution.py:62
  119.7 0.3 fusion.12
  120.0 0.0 collective-permute-done.1
  120.0 0.3 convolution_add_fusion.1
  120.4 0.7 convert_element_type.131
  121.1 3.5 %all-to-all-start.3 = ((bf16[4,64,512]{2,1,0:T(8,128)(2,1)}), bf16[4,64,512]{2,1,0:T(8,128)(2,1)S(1)}, u32[]{:S(2)}, u32[]{:S(2)}) async-start(bf16[4,64,512]{2,1,0:T(8,128)(2,1)} %convert_element_type.131), calls=%async_computation.3 | async-start | bytes 524288 | tf_op jit(solution)/shard_map/all_to_all | solution.py:44
  124.6 0.1 fusion.6
  124.8 8.0 %all-to-all-done.3 = bf16[4,64,512]{2,1,0:T(8,128)(2,1)S(1)} async-done(((bf16[4,64,512]{2,1,0:T(8,128)(2,1)}), bf16[4,64,512]{2,1,0:T(8,128)(2,1)S(1)}, u32[]{:S(2)}, u32[]{:S(2)}) %all-to-all-start.3) | async-done | bytes 262176 | tf_op jit(solution)/shard_map/all_to_all | solution.py:44
  132.7 0.1 fusion.5
  132.8 18.2 %all_gather.35 = bf16[512,512]{1,0:T(8,128)(2,1)S(1)} all-gather(bf16[64,512]{1,0:T(8,128)(2,1)S(1)} %fusion.5), channel_id=1, replica_groups=mesh['y_lo'=2,'z'=8,'x'=4,'y_hi'=4,'core'=2] {'y_hi','core'}, dimensions={0}, use_global_device_ids=true | all-gather | bytes 589824 | tf_op jit(solution)/shard_map/all_gather | solution.py:78
  151.0 0.0 copy-start
  151.0 2.2 %convolution_convert_fusion = bf16[512,1536]{1,0:T(8,128)(2,1)} fusion(bf16[512,512]{1,0:T(8,128)(2,1)S(1)} %all_gather.35, bf16[512,1536]{1,0:T(8,128)(2,1)S(1)} %bitcast.37), kind=kOutput, calls=%fused_computation | convolution fusion | flops 806092800 | bytes 3670016 | tf_op jit(solution)/shard_map/dot_general | solution.py:80
  153.2 0.0 copy-done
  153.2 0.0 copy-start.1
  153.2 4.4 %all-to-all-start.4 = ((bf16[8,64,1536]{2,1,0:T(8,128)(2,1)}), bf16[8,64,1536]{2,1,0:T(8,128)(2,1)S(1)}, u32[]{:S(2)}, u32[]{:S(2)}) async-start(bf16[8,64,1536]{2,1,0:T(8,128)(2,1)} %bitcast.46), calls=%async_computation.4 | async-start | bytes 3145728 | tf_op jit(solution)/shard_map/all_to_all | solution.py:81
  157.6 21.0 %all-to-all-done.4 = bf16[8,64,1536]{2,1,0:T(8,128)(2,1)S(1)} async-done(((bf16[8,64,1536]{2,1,0:T(8,128)(2,1)}), bf16[8,64,1536]{2,1,0:T(8,128)(2,1)S(1)}, u32[]{:S(2)}, u32[]{:S(2)}) %all-to-all-start.4) | async-done | bytes 1572896 | tf_op jit(solution)/shard_map/all_to_all | solution.py:81
  178.6 0.0 copy-done.1
  178.6 2.2 %fusion = f32[64,1536]{1,0:T(8,128)} fusion(bf16[512,1536]{1,0:T(8,128)(2,1)S(1)} %bitcast.38, f32[64,1536]{1,0:T(8,128)S(1)} %copy-done.1, bf16[8,64,1536]{2,1,0:T(8,128)(2,1)S(1)} %all-to-all-done.4, pred[]{:T(512)S(6)} %eq.88, pred[]{:T(512)S(6)} %eq.87, pred[]{:T(512)S(6)} %eq.86, pred[]{:T(512)S(6)} %eq.85, pred[]{:T(512)S(6)} %eq.84, pred[]{:T(512)S(6)} %eq.83, ...), kind=kOutput, calls=%fused_computation.2 | convolution fusion | flops 103219200 | bytes 3997708 | tf_op jit(solution)/shard_map/dot_general | solution.py:83
  (5 shorter events, 0.1 us)
Async XLA Ops:
  2.5 49.1 %all-to-all-start = ((bf16[8,64,1536]{2,1,0:T(8,128)(2,1)}), bf16[8,64,1536]{2,1,0:T(8,128)(2,1)S(1)}, u32[]{:S(2)}, u32[]{:S(2)}) async-start(bf16[8,64,1536]{2,1,0:T(8,128)(2,1)} %broadcast_in_dim.45), calls=%async_computation | async-start | bytes 3145728 | tf_op jit(solution)/shard_map/all_to_all | solution.py:32
  53.8 25.6 %all-to-all-start.1 = ((bf16[8,64,512]{2,1,0:T(8,128)(2,1)}), bf16[8,64,512]{2,1,0:T(8,128)(2,1)S(1)}, u32[]{:S(2)}, u32[]{:S(2)}) async-start(bf16[8,64,512]{2,1,0:T(8,128)(2,1)} %convert_element_type.120), calls=%async_computation.1 | async-start | bytes 1048576 | tf_op jit(solution)/shard_map/all_to_all | solution.py:44
  80.3 25.3 %all-to-all-start.2 = ((bf16[8,64,512]{2,1,0:T(8,128)(2,1)}), bf16[8,64,512]{2,1,0:T(8,128)(2,1)S(1)}, u32[]{:S(2)}, u32[]{:S(2)}) async-start(bf16[8,64,512]{2,1,0:T(8,128)(2,1)} %broadcast_in_dim.48), calls=%async_computation.2 | async-start | bytes 1048576 | tf_op jit(solution)/shard_map/all_to_all | solution.py:32
  83.9 0.7 collective-permute-start
  105.6 14.4 %collective-permute-start.1 = (bf16[512,512]{1,0:T(8,128)(2,1)S(1)}, bf16[512,512]{1,0:T(8,128)(2,1)S(1)}, u32[]{:S(2)}, u32[]{:S(2)}) collective-permute-start(bf16[512,512]{1,0:T(8,128)(2,1)S(1)} %bitcast.44), channel_id=1, source_target_pairs={{0,1},{1,0},{2,3},{3,2},{4,5},{5,4},{6,7},{7,6},{8,9},{9,8},{10,11... | collective-permute-start | bytes 1572872 | tf_op jit(solution)/shard_map/ppermute | solution.py:60
  121.1 11.6 %all-to-all-start.3 = ((bf16[4,64,512]{2,1,0:T(8,128)(2,1)}), bf16[4,64,512]{2,1,0:T(8,128)(2,1)S(1)}, u32[]{:S(2)}, u32[]{:S(2)}) async-start(bf16[4,64,512]{2,1,0:T(8,128)(2,1)} %convert_element_type.131), calls=%async_computation.3 | async-start | bytes 524288 | tf_op jit(solution)/shard_map/all_to_all | solution.py:44
  151.0 2.2 %copy-start = (bf16[512,512]{1,0:T(8,128)(2,1)}, bf16[512,512]{1,0:T(8,128)(2,1)S(1)}, u32[]{:S(2)}) copy-start(bf16[512,512]{1,0:T(8,128)(2,1)S(1)} %all_gather.35) | copy-start | bytes 1572868
  153.2 25.4 %copy-start.1 = (f32[64,1536]{1,0:T(8,128)S(1)}, f32[64,1536]{1,0:T(8,128)}, u32[]{:S(2)}) copy-start(f32[64,1536]{1,0:T(8,128)} %param.1) | copy-start | bytes 1179652
  153.2 25.4 %all-to-all-start.4 = ((bf16[8,64,1536]{2,1,0:T(8,128)(2,1)}), bf16[8,64,1536]{2,1,0:T(8,128)(2,1)S(1)}, u32[]{:S(2)}, u32[]{:S(2)}) async-start(bf16[8,64,1536]{2,1,0:T(8,128)(2,1)} %bitcast.46), calls=%async_computation.4 | async-start | bytes 3145728 | tf_op jit(solution)/shard_map/all_to_all | solution.py:81

commit v10 on v8

--- a/solution.py
+++ b/solution.py
@@ -26,6 +26,19 @@
 def swap_x_y_hi(block):
     pairs = [((x * 4 + y) * 2 + k, (y * 4 + x) * 2 + k) for x in range(4) for y in range(4) for k in range(2)]
     return lax.ppermute(block, ("x", "y_hi", "core"), pairs)
+
+
+def swap_lo_col(block):
+    pairs = []
+    for y_lo in range(2):
+        for z in range(8):
+            for x in range(4):
+                for y_hi in range(4):
+                    for core in range(2):
+                        source = (((y_lo * 8 + z) * 4 + x) * 4 + y_hi) * 2 + core
+                        target = (((core * 8 + z) * 4 + y_hi) * 4 + x) * 2 + y_lo
+                        pairs.append((source, target))
+    return lax.ppermute(block, MESH, pairs)
 
 
 def spread(block, axis):
@@ -57,31 +70,26 @@
 
     rounded = gram.astype(jnp.bfloat16)
     right = spread(rounded, "z").reshape(8 * rows, 8 * rows)
-    right_other = lax.ppermute(right, "core", [(0, 1), (1, 0)])
-    left = lax.all_gather(swap_x_y_hi(rounded), "y_lo", axis=0)
-    left = lax.all_gather(left, "x", axis=0).reshape(4, 2, rows, 8 * rows)
-    core = lax.axis_index("core")
-    own = jnp.where(core == 0, left[:, 0], left[:, 1]).reshape(4 * rows, 8 * rows)
-    other = jnp.where(core == 0, left[:, 1], left[:, 0]).reshape(4 * rows, 8 * rows)
-    square = jnp.dot(own, right, preferred_element_type=jnp.float32) + jnp.dot(
-        other, right_other, preferred_element_type=jnp.float32
-    )
-    square = sum_pieces(square.reshape(4, rows, 8 * rows), "y_hi")
+    left = lax.all_gather(rounded, COL, axis=0, tiled=True)
+    by_hi_pair = lax.ppermute(by_hi, "y_lo", [(0, 1), (1, 0)])
+    gram = swap_lo_col(gram)
+    square = sum_pieces(dot_nt(left, right).reshape(8, rows, 8 * rows), LO)
 
-    at_home = lax.dynamic_slice(left, (lax.axis_index("y_hi"), core, 0, 0), (1, 1, rows, 8 * rows))[0, 0]
+    at_home = lax.dynamic_slice_in_dim(left, lax.axis_index(LO) * rows, rows)
     column = lax.broadcasted_iota(jnp.int32, at_home.shape, 1) - lax.axis_index("z") * rows
     on_diagonal = column == lax.broadcasted_iota(jnp.int32, at_home.shape, 0)
     diagonal = jnp.where(on_diagonal, at_home.astype(jnp.float32), 0.0).sum(1, keepdims=True)
     square = square + rest_of(gram) * (2.0 * diagonal)
 
-    poly = (coef_cubic * gram + coef_quintic * square).astype(jnp.bfloat16)
-    poly = lax.all_gather(poly, COL, axis=0, tiled=True)
-    me = lax.axis_index(LO)
-    product = jnp.dot(poly, by_hi, preferred_element_type=jnp.float32).astype(jnp.bfloat16)
-    arrived = lax.all_to_all(product.reshape(8, rows, cols), LO, 0, 0)
-    mine = lax.dynamic_slice_in_dim(poly, me * rows, rows)
-    own = jnp.dot(mine, by_hi, preferred_element_type=jnp.float32)
-    return coef_linear * x_scaled + own + sum_others(arrived, me)
+    poly = swap_x_y_hi((coef_cubic * gram + coef_quintic * square).astype(jnp.bfloat16))
+    poly = lax.all_gather(poly, COL, axis=0).reshape(4, 2, rows, 8 * rows)
+    y_lo = lax.axis_index("y_lo")
+    near = jnp.where(y_lo == 0, poly[:, 0], poly[:, 1]).reshape(4 * rows, 8 * rows)
+    far = jnp.where(y_lo == 0, poly[:, 1], poly[:, 0]).reshape(4 * rows, 8 * rows)
+    product = jnp.dot(near, by_hi, preferred_element_type=jnp.float32) + jnp.dot(
+        far, by_hi_pair, preferred_element_type=jnp.float32
+    )
+    return coef_linear * x_scaled + sum_pieces(product.reshape(4, rows, cols), "x")
 
 
 def solution(mesh):

time: 177 us -> 205 us (1.16)
  blocking collectives: 63.8 us -> 75.8 us
  waiting for transfers between devices: 66 us -> 76.9 us
  starting transfers between devices: 35.3 us -> 38.5 us
  other arithmetic: 3.12 us -> 5.26 us
    ppermute x1 -> x2, waiting for transfers between devices: 0.01 us -> 38.4 us  [the longest x1 38.4 us: swap_lo_col(): return lax.ppermute(block, MESH, pairs)]
    all_to_all x1 -> x0, waiting for transfers between devices: 21 us -> none  [per_device(): arrived = lax.all_to_all(product.reshape(8, rows, cols), LO, 0, 0)]
    all_gather x3 -> x2, blocking collectives: 33.7 us -> 45.8 us  [the longest x1 30.1 us: per_device(): poly = lax.all_gather(poly, COL, axis=0).reshape(4, 2, rows, 8 * rows)]
    all_to_all x2, waiting for transfers between devices: 21.3 us -> 10.4 us  [spread(): lax.all_to_all(jnp.broadcast_to(block[None], (8,) + block.shape), axis, 0...]
    all_to_all x1 -> x0, starting transfers between devices: 4.75 us -> none  [per_device(): arrived = lax.all_to_all(product.reshape(8, rows, cols), LO, 0, 0)]
    all_to_all x2 -> x3, waiting for transfers between devices: 23.7 us -> 28.1 us  [sum_pieces(): arrived = lax.all_to_all(pieces.astype(jnp.bfloat16), axis, 0, 0)]
    all_to_all x2 -> x3, starting transfers between devices: 13.2 us -> 17.3 us  [sum_pieces(): arrived = lax.all_to_all(pieces.astype(jnp.bfloat16), axis, 0, 0)]
    ppermute x1 -> x2, starting transfers between devices: 2.36 us -> 6.19 us  [the longest x1 3.36 us: per_device(): by_hi_pair = lax.ppermute(by_hi, 'y_lo', [(0, 1), (1, 0)])]
  transfers between devices with their start and end apart: 7 -> 8, of which waited for: 5 -> 5; matrix products, arithmetic and copies ran while one was open for 0% -> 1% of each run, Pallas kernels for 0% -> 0%
where the time goes in v10:
time: 205 us; the launch traced here: 204 us
  waiting for transfers between devices  76.9 us (38%)
  blocking collectives  75.8 us (37%)
  starting transfers between devices  38.5 us (19%)
  matrix products  5.35 us (3%)
  other arithmetic  5.26 us (3%)
  local copies, waits for them, and re-layouts  2.16 us (1%)
    ppermute x1, waiting for transfers between devices, swap_lo_col(): return lax.ppermute(block, MESH, pairs)  38.4 us
    all_gather x1, blocking collectives, per_device(): poly = lax.all_gather(poly, COL, axis=0).reshape(4, 2, rows, 8 * rows)  30.1 us
    all_to_all x3, waiting for transfers between devices, sum_pieces(): arrived = lax.all_to_all(pieces.astype(jnp.bfloat16), axis, 0, 0)  28.1 us
    all_gather x2, blocking collectives, per_device(): by_lo = [lax.all_gather(pair[y], 'x', axis=0, tiled=True) for y in range(2)]  23.9 us
    all_to_all x3, starting transfers between devices, sum_pieces(): arrived = lax.all_to_all(pieces.astype(jnp.bfloat16), axis, 0, 0)  17.3 us
    all_gather x1, blocking collectives, per_device(): left = lax.all_gather(rounded, COL, axis=0, tiled=True)  15.7 us
    all_to_all x2, starting transfers between devices, spread(): lax.all_to_all(jnp.broadcast_to(block[None], (8,) + block.shape), axis, 0...  14.4 us
    all_to_all x2, waiting for transfers between devices, spread(): lax.all_to_all(jnp.broadcast_to(block[None], (8,) + block.shape), axis, 0...  10.4 us
  transfers between devices with their start and end apart: 8, of which 5 were waited for; matrix products, arithmetic and copies ran while one was open for 1% of the time, Pallas kernels for 0%

profile of v10, /device:TPU:1, one launch (start us, length us, event | category | flops | bytes accessed | tf_op | source)
XLA Modules:
  0.0 204.2 jit_solution(12358634643803907072)
XLA Ops:
  0.0 1.0 convert_element_type.112
  1.0 1.3 broadcast_in_dim.45
  2.3 10.9 %all-to-all-start = ((bf16[8,64,1536]{2,1,0:T(8,128)(2,1)}), bf16[8,64,1536]{2,1,0:T(8,128)(2,1)S(1)}, u32[]{:S(2)}, u32[]{:S(2)}) async-start(bf16[8,64,1536]{2,1,0:T(8,128)(2,1)} %broadcast_in_dim.45), calls=%async_computation | async-start | bytes 3145728 | tf_op jit(solution)/shard_map/all_to_all | solution.py:45
  13.2 6.1 %all-gather = bf16[128,1536]{1,0:T(8,128)(2,1)S(1)} all-gather(bf16[64,1536]{1,0:T(8,128)(2,1)S(1)} %convert_element_type.112), channel_id=2, replica_groups=mesh['y_lo'=2,'z'=8,'x'=4,'y_hi'=4,'core'=2] {'y_lo'}, dimensions={0}, use_global_device_ids=true | all-gather | bytes 589824 | tf_op jit(solution)/shard_map/all_gather | solution.py:65
  19.3 12.6 %all-gather.4 = bf16[256,1536]{1,0:T(8,128)(2,1)S(1)} all-gather(bf16[64,1536]{1,0:T(8,128)(2,1)S(1)} %get-tuple-element.9), channel_id=6, replica_groups=mesh['y_lo'=2,'z'=8,'x'=4,'y_hi'=4,'core'=2] {'x'}, dimensions={0}, use_global_device_ids=true | all-gather | bytes 983040 | tf_op jit(solution)/shard_map/all_gather | solution.py:66
  32.0 11.3 %all-gather.5 = bf16[256,1536]{1,0:T(8,128)(2,1)S(1)} all-gather(bf16[64,1536]{1,0:T(8,128)(2,1)S(1)} %get-tuple-element.10), channel_id=7, replica_groups=mesh['y_lo'=2,'z'=8,'x'=4,'y_hi'=4,'core'=2] {'x'}, dimensions={0}, use_global_device_ids=true | all-gather | bytes 983040 | tf_op jit(solution)/shard_map/all_gather | solution.py:66
  43.3 8.2 %all-to-all-done = bf16[8,64,1536]{2,1,0:T(8,128)(2,1)S(1)} async-done(((bf16[8,64,1536]{2,1,0:T(8,128)(2,1)}), bf16[8,64,1536]{2,1,0:T(8,128)(2,1)S(1)}, u32[]{:S(2)}, u32[]{:S(2)}) %all-to-all-start) | async-done | bytes 1572896 | tf_op jit(solution)/shard_map/all_to_all | solution.py:45
  51.4 0.6 fusion.7
  52.0 0.6 fusion.8
  52.7 0.1 maximum_multiply_fusion
  52.8 0.9 convert_element_type.113
  53.6 9.8 %all-to-all-start.1 = ((bf16[8,64,512]{2,1,0:T(8,128)(2,1)}), bf16[8,64,512]{2,1,0:T(8,128)(2,1)S(1)}, u32[]{:S(2)}, u32[]{:S(2)}) async-start(bf16[8,64,512]{2,1,0:T(8,128)(2,1)} %convert_element_type.113), calls=%async_computation.1 | async-start | bytes 1048576 | tf_op jit(solution)/shard_map/all_to_all | solution.py:57
  63.4 15.9 %all-to-all-done.1 = bf16[8,64,512]{2,1,0:T(8,128)(2,1)S(1)} async-done(((bf16[8,64,512]{2,1,0:T(8,128)(2,1)}), bf16[8,64,512]{2,1,0:T(8,128)(2,1)S(1)}, u32[]{:S(2)}, u32[]{:S(2)}) %all-to-all-start.1) | async-done | bytes 524320 | tf_op jit(solution)/shard_map/all_to_all | solution.py:57
  79.3 0.1 convert_bitcast_fusion
  79.4 0.8 broadcast_in_dim.48
  80.2 3.5 %all-to-all-start.2 = ((bf16[8,64,512]{2,1,0:T(8,128)(2,1)}), bf16[8,64,512]{2,1,0:T(8,128)(2,1)S(1)}, u32[]{:S(2)}, u32[]{:S(2)}) async-start(bf16[8,64,512]{2,1,0:T(8,128)(2,1)} %broadcast_in_dim.48), calls=%async_computation.2 | async-start | bytes 1048576 | tf_op jit(solution)/shard_map/all_to_all | solution.py:45
  83.7 15.7 %all_gather.25 = bf16[512,512]{1,0:T(8,128)(2,1)S(1)} all-gather(bf16[64,512]{1,0:T(8,128)(2,1)S(1)} %bitcast_convert_fusion), channel_id=1, replica_groups=mesh['y_lo'=2,'z'=8,'x'=4,'y_hi'=4,'core'=2] {'y_hi','core'}, dimensions={0}, use_global_device_ids=true | all-gather | bytes 589824 | tf_op jit(solution)/shard_map/all_gather | solution.py:73
  99.4 2.3 %all-to-all-done.2 = bf16[8,64,512]{2,1,0:T(8,128)(2,1)S(1)} async-done(((bf16[8,64,512]{2,1,0:T(8,128)(2,1)}), bf16[8,64,512]{2,1,0:T(8,128)(2,1)S(1)}, u32[]{:S(2)}, u32[]{:S(2)}) %all-to-all-start.2) | async-done | bytes 524320 | tf_op jit(solution)/shard_map/all_to_all | solution.py:45
  101.7 1.6 fusion.6
  103.3 4.0 %all-to-all-start.3 = ((bf16[8,64,512]{2,1,0:T(8,128)(2,1)}), bf16[8,64,512]{2,1,0:T(8,128)(2,1)S(1)}, u32[]{:S(2)}, u32[]{:S(2)}) async-start(bf16[8,64,512]{2,1,0:T(8,128)(2,1)} %get-tuple-element.11), calls=%async_computation.3 | async-start | bytes 1048576 | tf_op jit(solution)/shard_map/all_to_all | solution.py:57
  107.3 3.4 %collective-permute-start.2 = (bf16[512,1536]{1,0:T(8,128)(2,1)S(1)}, bf16[512,1536]{1,0:T(8,128)(2,1)}, u32[]{:S(2)}, u32[]{:S(2)}) collective-permute-start(bf16[512,1536]{1,0:T(8,128)(2,1)S(1)} %bitcast.30), channel_id=1, source_target_pairs={{0,256},{256,0},{1,257},{257,1},{2,258},{258,2},{3,259},{259,3},{4... | collective-permute-start | bytes 4718600 | tf_op jit(solution)/shard_map/ppermute | solution.py:74
  110.7 2.8 %collective-permute-start = (f32[64,512]{1,0:T(8,128)S(1)}, f32[64,512]{1,0:T(8,128)S(1)}, u32[]{:S(2)}, u32[]{:S(2)}) collective-permute-start(f32[64,512]{1,0:T(8,128)S(1)} %bitcast.41), channel_id=1, source_target_pairs={{0,0},{1,256},{2,8},{3,264},{4,16},{5,272},{6,24},{7,280},{8,2},{9... | collective-permute-start | bytes 393224 | tf_op jit(solution)/shard_map/ppermute | solution.py:41
  113.5 0.1 select_reduce_fusion
  113.7 38.4 %collective-permute-done = f32[64,512]{1,0:T(8,128)S(1)} collective-permute-done((f32[64,512]{1,0:T(8,128)S(1)}, f32[64,512]{1,0:T(8,128)S(1)}, u32[]{:S(2)}, u32[]{:S(2)}) %collective-permute-start) | collective-permute-done | bytes 131104 | tf_op jit(solution)/shard_map/ppermute | solution.py:41
  152.0 0.0 all-to-all-done.3
  152.0 1.1 fusion.4
  153.1 0.7 collective-permute-start.1
  153.8 0.0 collective-permute-done.1
  153.8 30.1 %all-gather.3 = bf16[512,512]{1,0:T(8,128)(2,1)S(1)} all-gather(bf16[64,512]{1,0:T(8,128)(2,1)S(1)} %collective-permute-done.1), channel_id=5, replica_groups=mesh['y_lo'=2,'z'=8,'x'=4,'y_hi'=4,'core'=2] {'y_hi','core'}, dimensions={0}, use_global_device_ids=true | all-gather | bytes 589824 | tf_op jit(solution)/shard_map/all_gather | solution.py:85
  183.9 0.6 fusion.9
  184.5 0.0 collective-permute-done.2
  184.5 2.0 convolution_add_fusion
  186.5 0.0 copy-start
  186.5 1.0 convert_element_type.135
  187.5 3.5 %all-to-all-start.4 = ((bf16[4,64,1536]{2,1,0:T(8,128)(2,1)}), bf16[4,64,1536]{2,1,0:T(8,128)(2,1)S(1)}, u32[]{:S(2)}, u32[]{:S(2)}) async-start(bf16[4,64,1536]{2,1,0:T(8,128)(2,1)} %convert_element_type.135), calls=%async_computation.4 | async-start | bytes 1572864 | tf_op jit(solution)/shard_map/all_to_all | solution.py:57
  191.0 12.2 %all-to-all-done.4 = bf16[4,64,1536]{2,1,0:T(8,128)(2,1)S(1)} async-done(((bf16[4,64,1536]{2,1,0:T(8,128)(2,1)}), bf16[4,64,1536]{2,1,0:T(8,128)(2,1)S(1)}, u32[]{:S(2)}, u32[]{:S(2)}) %all-to-all-start.4) | async-done | bytes 786464 | tf_op jit(solution)/shard_map/all_to_all | solution.py:57
  203.3 0.0 copy-done
  203.3 0.9 bitcast_add_fusion
  (5 shorter events, 0.1 us)
Async XLA Ops:
  2.3 49.1 %all-to-all-start = ((bf16[8,64,1536]{2,1,0:T(8,128)(2,1)}), bf16[8,64,1536]{2,1,0:T(8,128)(2,1)S(1)}, u32[]{:S(2)}, u32[]{:S(2)}) async-start(bf16[8,64,1536]{2,1,0:T(8,128)(2,1)} %broadcast_in_dim.45), calls=%async_computation | async-start | bytes 3145728 | tf_op jit(solution)/shard_map/all_to_all | solution.py:45
  53.6 25.6 %all-to-all-start.1 = ((bf16[8,64,512]{2,1,0:T(8,128)(2,1)}), bf16[8,64,512]{2,1,0:T(8,128)(2,1)S(1)}, u32[]{:S(2)}, u32[]{:S(2)}) async-start(bf16[8,64,512]{2,1,0:T(8,128)(2,1)} %convert_element_type.113), calls=%async_computation.1 | async-start | bytes 1048576 | tf_op jit(solution)/shard_map/all_to_all | solution.py:57
  80.2 21.4 %all-to-all-start.2 = ((bf16[8,64,512]{2,1,0:T(8,128)(2,1)}), bf16[8,64,512]{2,1,0:T(8,128)(2,1)S(1)}, u32[]{:S(2)}, u32[]{:S(2)}) async-start(bf16[8,64,512]{2,1,0:T(8,128)(2,1)} %broadcast_in_dim.48), calls=%async_computation.2 | async-start | bytes 1048576 | tf_op jit(solution)/shard_map/all_to_all | solution.py:45
  103.3 48.8 %all-to-all-start.3 = ((bf16[8,64,512]{2,1,0:T(8,128)(2,1)}), bf16[8,64,512]{2,1,0:T(8,128)(2,1)S(1)}, u32[]{:S(2)}, u32[]{:S(2)}) async-start(bf16[8,64,512]{2,1,0:T(8,128)(2,1)} %get-tuple-element.11), calls=%async_computation.3 | async-start | bytes 1048576 | tf_op jit(solution)/shard_map/all_to_all | solution.py:57
  107.3 77.2 %collective-permute-start.2 = (bf16[512,1536]{1,0:T(8,128)(2,1)S(1)}, bf16[512,1536]{1,0:T(8,128)(2,1)}, u32[]{:S(2)}, u32[]{:S(2)}) collective-permute-start(bf16[512,1536]{1,0:T(8,128)(2,1)S(1)} %bitcast.30), channel_id=1, source_target_pairs={{0,256},{256,0},{1,257},{257,1},{2,258},{258,2},{3,259},{259,3},{4... | collective-permute-start | bytes 4718600 | tf_op jit(solution)/shard_map/ppermute | solution.py:74
  110.7 41.3 %collective-permute-start = (f32[64,512]{1,0:T(8,128)S(1)}, f32[64,512]{1,0:T(8,128)S(1)}, u32[]{:S(2)}, u32[]{:S(2)}) collective-permute-start(f32[64,512]{1,0:T(8,128)S(1)} %bitcast.41), channel_id=1, source_target_pairs={{0,0},{1,256},{2,8},{3,264},{4,16},{5,272},{6,24},{7,280},{8,2},{9... | collective-permute-start | bytes 393224 | tf_op jit(solution)/shard_map/ppermute | solution.py:41
  153.1 0.7 collective-permute-start.1
  186.5 16.7 %copy-start = (f32[64,1536]{1,0:T(8,128)S(1)}, f32[64,1536]{1,0:T(8,128)}, u32[]{:S(2)}) copy-start(f32[64,1536]{1,0:T(8,128)} %param.1) | copy-start | bytes 1179652
  187.5 15.7 %all-to-all-start.4 = ((bf16[4,64,1536]{2,1,0:T(8,128)(2,1)}), bf16[4,64,1536]{2,1,0:T(8,128)(2,1)S(1)}, u32[]{:S(2)}, u32[]{:S(2)}) async-start(bf16[4,64,1536]{2,1,0:T(8,128)(2,1)} %convert_element_type.135), calls=%async_computation.4 | async-start | bytes 1572864 | tf_op jit(solution)/shard_map/all_to_all | solution.py:57

commit v11 on v4

v11 whole, which is shorter than its diff:
```python
import jax
import jax.numpy as jnp
from jax import lax
from jax.sharding import Mesh, PartitionSpec as P

N = 12288

coef_linear = 3.4445
coef_cubic = -4.775
coef_quintic = 2.0315

LO = ("x", "y_lo")
COL = ("y_hi", "core")
ROW = ("y_lo", "z", "x")
MESH = ("y_lo", "z", "x", "y_hi", "core")


def dot_nt(a, b):
    return lax.dot_general(a, b, (((1,), (1,)), ((), ())), preferred_element_type=jnp.float32)


def rest_of(x):
    return x - lax.reduce_precision(x, exponent_bits=8, mantissa_bits=7)


def swap_lo_col(block):
    pairs = []
    for y_lo in range(2):
        for z in range(8):
            for x in range(4):
                for y_hi in range(4):
                    for core in range(2):
                        source = (((y_lo * 8 + z) * 4 + x) * 4 + y_hi) * 2 + core
                        target = (((core * 8 + z) * 4 + y_hi) * 4 + x) * 2 + y_lo
                        pairs.append((source, target))
    return lax.ppermute(block, MESH, pairs)


def spread(block, axis):
    return lax.all_to_all(jnp.broadcast_to(block[None], (8,) + block.shape), axis, 0, 0)


def sum_pieces(pieces, axis):
    me = lax.axis_index(axis)
    mine = jnp.arange(pieces.shape[0])[:, None, None] == me
    arrived = lax.all_to_all(jnp.where(mine, 0.0, pieces).astype(jnp.bfloat16), axis, 0, 0)
    own = lax.dynamic_index_in_dim(pieces, me, 0, keepdims=False)
    return own + arrived.astype(jnp.float32).sum(0)


def per_device(x_scaled):
    rows, cols = x_scaled.shape
    xb = x_scaled.astype(jnp.bfloat16)
    by_hi = spread(xb, "z").reshape(8 * rows, cols)
    pair = lax.all_gather(xb, "y_lo", axis=0)
    by_lo = jnp.concatenate([lax.all_gather(pair[y], "x", axis=0, tiled=True) for y in range(2)])

    tile = dot_nt(by_lo, by_hi) * (1.0 / N)
    gram = sum_pieces(tile.reshape(8, rows, 8 * rows), ("core", "y_hi"))

    rounded = gram.astype(jnp.bfloat16)
    left = lax.all_gather(rounded, COL, axis=0, tiled=True)
    right = spread(rounded, "z").reshape(8 * rows, 8 * rows)
    square = sum_pieces(dot_nt(left, right).reshape(8, rows, 8 * rows), LO)

    at_home = lax.dynamic_slice_in_dim(left, lax.axis_index(LO) * rows, rows)
    column = lax.broadcasted_iota(jnp.int32, at_home.shape, 1) - lax.axis_index("z") * rows
    on_diagonal = column == lax.broadcasted_iota(jnp.int32, at_home.shape, 0)
    diagonal = jnp.where(on_diagonal, at_home.astype(jnp.float32), 0.0).sum(1, keepdims=True)
    moved = swap_lo_col(jnp.concatenate([square, jnp.broadcast_to(diagonal, (rows, 128))], axis=1))
    square, diagonal = moved[:, : 8 * rows], moved[:, 8 * rows : 8 * rows + 1]

    square = square + rest_of(gram) * (2.0 * diagonal)
    poly = (coef_cubic * gram + coef_quintic * square).astype(jnp.bfloat16)
    poly = lax.all_gather(poly, COL, axis=0, tiled=True)
    product = jnp.dot(poly, by_hi, preferred_element_type=jnp.float32)
    return coef_linear * x_scaled + sum_pieces(product.reshape(8, rows, cols), LO)


def solution(mesh):
    fine = Mesh(mesh.devices.reshape(2, 8, 4, 4, 2), MESH)
    return jax.shard_map(
        per_device,
        mesh=fine,
        in_specs=(P(ROW, COL),),
        out_specs=P(ROW, COL),
        check_vma=False,
    )
```

time: 175 us -> 180 us (1.029)
  waiting for transfers between devices: 29.9 us -> 37.2 us
  blocking collectives: 98.4 us -> 95.2 us
  starting transfers between devices: 35 us -> 32.2 us
  other arithmetic: 4.26 us -> 6.45 us
    all_to_all x2, waiting for transfers between devices: 17.9 us -> 25.1 us  [sum_pieces(): lax.all_to_all(jnp.where(mine, 0.0, pieces).astype(jnp.bfloat16), axis, 0...]
    ppermute x2 -> x1, starting transfers between devices: 9.83 us -> 4.05 us  [swap_lo_col(): return lax.ppermute(block, MESH, pairs)]
    all_to_all x2, starting transfers between devices: 10.8 us -> 13.8 us  [sum_pieces(): lax.all_to_all(jnp.where(mine, 0.0, pieces).astype(jnp.bfloat16), axis, 0...]
    all_gather x1, blocking collectives: 18.4 us -> 15.7 us  [per_device(): left = lax.all_gather(rounded, COL, axis=0, tiled=True)]
    ppermute x2 -> x1, waiting for transfers between devices: 4.15 us -> 2.99 us  [swap_lo_col(): return lax.ppermute(block, MESH, pairs)]
    dot_general x3 -> x2, matrix products: 2.83 us -> 3.79 us  [dot_nt(): lax.dot_general(a, b, (((1,), (1,)), ((), ())), preferred_element_type=jn...]
  transfers between devices with their start and end apart: 6 -> 5, of which waited for: 5 -> 5; matrix products, arithmetic and copies ran while one was open for 0% -> 1% of each run, Pallas kernels for 0% -> 0%
where the time goes in v11:
time: 180 us; the launch traced here: 179 us
  blocking collectives  95.2 us (53%)
  waiting for transfers between devices  37.2 us (21%)
  starting transfers between devices  32.2 us (18%)
  other arithmetic  6.45 us (4%)
  matrix products  4.78 us (3%)
  local copies, waits for them, and re-layouts  3.03 us (2%)
    all_gather x1, blocking collectives, per_device(): poly = lax.all_gather(poly, COL, axis=0, tiled=True)  25.2 us
    all_to_all x2, waiting for transfers between devices, sum_pieces(): lax.all_to_all(jnp.where(mine, 0.0, pieces).astype(jnp.bfloat16), axis, 0...  25.1 us
    all_gather x2, blocking collectives, per_device(): lax.all_gather(pair[y], 'x', axis=0, tiled=True)  24.4 us
    all_to_all x1, blocking collectives, sum_pieces(): lax.all_to_all(jnp.where(mine, 0.0, pieces).astype(jnp.bfloat16), axis, 0...  23.9 us
    all_gather x1, blocking collectives, per_device(): left = lax.all_gather(rounded, COL, axis=0, tiled=True)  15.7 us
    all_to_all x2, starting transfers between devices, spread(): lax.all_to_all(jnp.broadcast_to(block[None], (8,) + block.shape), axis, 0...  14.4 us
    all_to_all x2, starting transfers between devices, sum_pieces(): lax.all_to_all(jnp.where(mine, 0.0, pieces).astype(jnp.bfloat16), axis, 0...  13.8 us
    all_to_all x2, waiting for transfers between devices, spread(): lax.all_to_all(jnp.broadcast_to(block[None], (8,) + block.shape), axis, 0...  9.1 us
  transfers between devices with their start and end apart: 5, of which 5 were waited for; matrix products, arithmetic and copies ran while one was open for 1% of the time, Pallas kernels for 0%

profile of v11, /device:TPU:1, one launch (start us, length us, event | category | flops | bytes accessed | tf_op | source)
XLA Modules:
  0.0 178.9 jit_solution(13624349797274019607)
XLA Ops:
  0.0 1.0 convert_element_type.33
  1.0 1.3 broadcast_in_dim.57
  2.3 10.9 %all-to-all-start = ((bf16[8,64,1536]{2,1,0:T(8,128)(2,1)}), bf16[8,64,1536]{2,1,0:T(8,128)(2,1)S(1)}, u32[]{:S(2)}, u32[]{:S(2)}) async-start(bf16[8,64,1536]{2,1,0:T(8,128)(2,1)} %broadcast_in_dim.57), calls=%async_computation | async-start | bytes 3145728 | tf_op jit(solution)/shard_map/all_to_all | solution.py:40
  13.2 6.1 %all-gather = bf16[128,1536]{1,0:T(8,128)(2,1)S(1)} all-gather(bf16[64,1536]{1,0:T(8,128)(2,1)S(1)} %convert_element_type.33), channel_id=2, replica_groups=mesh['y_lo'=2,'z'=8,'x'=4,'y_hi'=4,'core'=2] {'y_lo'}, dimensions={0}, use_global_device_ids=true | all-gather | bytes 589824 | tf_op jit(solution)/shard_map/all_gather | solution.py:55
  19.3 12.6 %all-gather.3 = bf16[256,1536]{1,0:T(8,128)(2,1)S(1)} all-gather(bf16[64,1536]{1,0:T(8,128)(2,1)S(1)} %get-tuple-element.5), channel_id=5, replica_groups=mesh['y_lo'=2,'z'=8,'x'=4,'y_hi'=4,'core'=2] {'x'}, dimensions={0}, use_global_device_ids=true | all-gather | bytes 983040 | tf_op jit(solution)/shard_map/all_gather | solution.py:56
  32.0 11.7 %all-gather.4 = bf16[256,1536]{1,0:T(8,128)(2,1)} all-gather(bf16[64,1536]{1,0:T(8,128)(2,1)S(1)} %get-tuple-element.6), channel_id=6, replica_groups=mesh['y_lo'=2,'z'=8,'x'=4,'y_hi'=4,'core'=2] {'x'}, dimensions={0}, use_global_device_ids=true | all-gather | bytes 983040 | tf_op jit(solution)/shard_map/all_gather | solution.py:56
  43.7 7.8 %all-to-all-done = bf16[8,64,1536]{2,1,0:T(8,128)(2,1)S(1)} async-done(((bf16[8,64,1536]{2,1,0:T(8,128)(2,1)}), bf16[8,64,1536]{2,1,0:T(8,128)(2,1)S(1)}, u32[]{:S(2)}, u32[]{:S(2)}) %all-to-all-start) | async-done | bytes 1572896 | tf_op jit(solution)/shard_map/all_to_all | solution.py:40
  51.4 2.1 %fusion.4 = f32[512,512]{1,0:T(8,128)S(1)} fusion(bf16[512,1536]{1,0:T(8,128)(2,1)S(1)} %bitcast.34, bf16[256,1536]{1,0:T(8,128)(2,1)} %all-gather.4, bf16[256,1536]{1,0:T(8,128)(2,1)S(1)} %all-gather.3), kind=kOutput, calls=%fused_computation.6 | convolution fusion | flops 808714240 | bytes 4194304 | tf_op jit(solution)/shard_map/dot_general | solution.py:19
  53.6 0.0 copy-start
  53.6 1.1 select_convert_fusion.2
  54.7 9.8 %all-to-all-start.1 = ((bf16[8,64,512]{2,1,0:T(8,128)(2,1)}), bf16[8,64,512]{2,1,0:T(8,128)(2,1)S(1)}, u32[]{:S(2)}, u32[]{:S(2)}) async-start(bf16[8,64,512]{2,1,0:T(8,128)(2,1)} %select_convert_fusion.2), calls=%async_computation.1 | async-start | bytes 1048576 | tf_op jit(solution)/shard_map/all_to_all | solution.py:46
  64.5 15.9 %all-to-all-done.1 = bf16[8,64,512]{2,1,0:T(8,128)(2,1)S(1)} async-done(((bf16[8,64,512]{2,1,0:T(8,128)(2,1)}), bf16[8,64,512]{2,1,0:T(8,128)(2,1)S(1)}, u32[]{:S(2)}, u32[]{:S(2)}) %all-to-all-start.1) | async-done | bytes 524320 | tf_op jit(solution)/shard_map/all_to_all | solution.py:46
  80.3 0.1 convert_reduce_fusion.2
  80.4 0.0 copy-done
  80.4 0.9 broadcast_in_dim.61
  81.3 3.5 %all-to-all-start.2 = ((bf16[8,64,512]{2,1,0:T(8,128)(2,1)}), bf16[8,64,512]{2,1,0:T(8,128)(2,1)S(1)}, u32[]{:S(2)}, u32[]{:S(2)}) async-start(bf16[8,64,512]{2,1,0:T(8,128)(2,1)} %broadcast_in_dim.61), calls=%async_computation.2 | async-start | bytes 1048576 | tf_op jit(solution)/shard_map/all_to_all | solution.py:40
  84.8 0.9 fusion.15
  85.8 15.7 %all_gather.22 = bf16[512,512]{1,0:T(8,128)(2,1)S(1)} all-gather(bf16[64,512]{1,0:T(8,128)(2,1)S(1)} %fusion.15), channel_id=1, replica_groups=mesh['y_lo'=2,'z'=8,'x'=4,'y_hi'=4,'core'=2] {'y_hi','core'}, dimensions={0}, use_global_device_ids=true | all-gather | bytes 589824 | tf_op jit(solution)/shard_map/all_gather | solution.py:62
  101.4 1.3 all-to-all-done.2
  102.7 1.7 select_convert_fusion.1
  104.4 4.0 %all-to-all-start.3 = ((bf16[8,64,512]{2,1,0:T(8,128)(2,1)}), bf16[8,64,512]{2,1,0:T(8,128)(2,1)S(1)}, u32[]{:S(2)}, u32[]{:S(2)}) async-start(bf16[8,64,512]{2,1,0:T(8,128)(2,1)} %get-tuple-element.7), calls=%async_computation.3 | async-start | bytes 1048576 | tf_op jit(solution)/shard_map/all_to_all | solution.py:46
  108.4 0.1 select_reduce_fusion
  108.5 9.2 %all-to-all-done.3 = bf16[8,64,512]{2,1,0:T(8,128)(2,1)S(1)} async-done(((bf16[8,64,512]{2,1,0:T(8,128)(2,1)}), bf16[8,64,512]{2,1,0:T(8,128)(2,1)S(1)}, u32[]{:S(2)}, u32[]{:S(2)}) %all-to-all-start.3) | async-done | bytes 524320 | tf_op jit(solution)/shard_map/all_to_all | solution.py:46
  117.8 0.1 convert_reduce_fusion.1
  117.8 0.9 bitcast_add_fusion.1
  118.8 0.1 broadcast_in_dim.64
  118.9 4.1 %collective-permute-start = (f32[64,640]{1,0:T(8,128)S(1)}, f32[64,640]{1,0:T(8,128)S(1)}, u32[]{:S(2)}, u32[]{:S(2)}) collective-permute-start(f32[64,640]{1,0:T(8,128)S(1)} %pad_maximum_fusion), channel_id=1, source_target_pairs={{0,0},{1,256},{2,8},{3,264},{4,16},{5,272},{6,24},{7,280},{8,2},{9... | collective-permute-start | bytes 491528 | tf_op jit(solution)/shard_map/ppermute | solution.py:36
  122.9 3.0 %collective-permute-done = f32[64,640]{1,0:T(8,128)S(1)} collective-permute-done((f32[64,640]{1,0:T(8,128)S(1)}, f32[64,640]{1,0:T(8,128)S(1)}, u32[]{:S(2)}, u32[]{:S(2)}) %collective-permute-start) | collective-permute-done | bytes 163872 | tf_op jit(solution)/shard_map/ppermute | solution.py:36
  125.9 0.1 fusion.16
  126.0 1.0 fusion.12
  127.0 25.2 %all_gather.23 = bf16[512,512]{1,0:T(8,128)(2,1)S(1)} all-gather(bf16[64,512]{1,0:T(8,128)(2,1)S(1)} %fusion.12), channel_id=1, replica_groups=mesh['y_lo'=2,'z'=8,'x'=4,'y_hi'=4,'core'=2] {'y_hi','core'}, dimensions={0}, use_global_device_ids=true | all-gather | bytes 589824 | tf_op jit(solution)/shard_map/all_gather | solution.py:75
  152.3 1.0 select_convert_fusion
  153.3 23.9 %all_to_all.25 = bf16[8,64,1536]{2,1,0:T(8,128)(2,1)S(1)} all-to-all(bf16[8,64,1536]{2,1,0:T(8,128)(2,1)S(1)} %get-tuple-element.9), channel_id=1, replica_groups=mesh['y_lo'=2,'z'=8,'x'=4,'y_hi'=4,'core'=2] {'x','y_lo'}, dimensions={0} | all-to-all | bytes 3145728 | tf_op jit(solution)/shard_map/all_to_all | solution.py:46
  177.1 0.0 copy-start.1
  177.1 0.2 convert_reduce_fusion
  177.3 0.8 copy-done.1
  178.1 0.8 fusion.7
  (6 shorter events, 0.1 us)
Async XLA Ops:
  2.3 49.1 %all-to-all-start = ((bf16[8,64,1536]{2,1,0:T(8,128)(2,1)}), bf16[8,64,1536]{2,1,0:T(8,128)(2,1)S(1)}, u32[]{:S(2)}, u32[]{:S(2)}) async-start(bf16[8,64,1536]{2,1,0:T(8,128)(2,1)} %broadcast_in_dim.57), calls=%async_computation | async-start | bytes 3145728 | tf_op jit(solution)/shard_map/all_to_all | solution.py:40
  53.6 26.8 %copy-start = (f32[512,512]{1,0:T(8,128)}, f32[512,512]{1,0:T(8,128)S(1)}, u32[]{:S(2)}) copy-start(f32[512,512]{1,0:T(8,128)S(1)} %fusion.4) | copy-start | bytes 3145732
  54.7 25.6 %all-to-all-start.1 = ((bf16[8,64,512]{2,1,0:T(8,128)(2,1)}), bf16[8,64,512]{2,1,0:T(8,128)(2,1)S(1)}, u32[]{:S(2)}, u32[]{:S(2)}) async-start(bf16[8,64,512]{2,1,0:T(8,128)(2,1)} %select_convert_fusion.2), calls=%async_computation.1 | async-start | bytes 1048576 | tf_op jit(solution)/shard_map/all_to_all | solution.py:46
  81.3 21.4 %all-to-all-start.2 = ((bf16[8,64,512]{2,1,0:T(8,128)(2,1)}), bf16[8,64,512]{2,1,0:T(8,128)(2,1)S(1)}, u32[]{:S(2)}, u32[]{:S(2)}) async-start(bf16[8,64,512]{2,1,0:T(8,128)(2,1)} %broadcast_in_dim.61), calls=%async_computation.2 | async-start | bytes 1048576 | tf_op jit(solution)/shard_map/all_to_all | solution.py:40
  104.4 13.4 %all-to-all-start.3 = ((bf16[8,64,512]{2,1,0:T(8,128)(2,1)}), bf16[8,64,512]{2,1,0:T(8,128)(2,1)S(1)}, u32[]{:S(2)}, u32[]{:S(2)}) async-start(bf16[8,64,512]{2,1,0:T(8,128)(2,1)} %get-tuple-element.7), calls=%async_computation.3 | async-start | bytes 1048576 | tf_op jit(solution)/shard_map/all_to_all | solution.py:46
  118.9 7.0 %collective-permute-start = (f32[64,640]{1,0:T(8,128)S(1)}, f32[64,640]{1,0:T(8,128)S(1)}, u32[]{:S(2)}, u32[]{:S(2)}) collective-permute-start(f32[64,640]{1,0:T(8,128)S(1)} %pad_maximum_fusion), channel_id=1, source_target_pairs={{0,0},{1,256},{2,8},{3,264},{4,16},{5,272},{6,24},{7,280},{8,2},{9... | collective-permute-start | bytes 491528 | tf_op jit(solution)/shard_map/ppermute | solution.py:36
  177.1 1.0 copy-start.1

commit v12 on v8

--- a/solution.py
+++ b/solution.py
@@ -32,17 +32,12 @@
     return lax.all_to_all(jnp.broadcast_to(block[None], (8,) + block.shape), axis, 0, 0)
 
 
-def sum_others(arrived, me):
-    total = 0.0
-    for i in range(arrived.shape[0]):
-        total = total + jnp.where(i == me, 0.0, arrived[i].astype(jnp.float32))
-    return total
-
-
 def sum_pieces(pieces, axis):
     me = lax.axis_index(axis)
-    arrived = lax.all_to_all(pieces.astype(jnp.bfloat16), axis, 0, 0)
-    return lax.dynamic_index_in_dim(pieces, me, 0, keepdims=False) + sum_others(arrived, me)
+    mine = jnp.arange(pieces.shape[0])[:, None, None] == me
+    arrived = lax.all_to_all(jnp.where(mine, 0.0, pieces).astype(jnp.bfloat16), axis, 0, 0)
+    own = lax.dynamic_index_in_dim(pieces, me, 0, keepdims=False)
+    return own + arrived.astype(jnp.float32).sum(0)
 
 
 def per_device(x_scaled):
@@ -76,12 +71,8 @@
 
     poly = (coef_cubic * gram + coef_quintic * square).astype(jnp.bfloat16)
     poly = lax.all_gather(poly, COL, axis=0, tiled=True)
-    me = lax.axis_index(LO)
-    product = jnp.dot(poly, by_hi, preferred_element_type=jnp.float32).astype(jnp.bfloat16)
-    arrived = lax.all_to_all(product.reshape(8, rows, cols), LO, 0, 0)
-    mine = lax.dynamic_slice_in_dim(poly, me * rows, rows)
-    own = jnp.dot(mine, by_hi, preferred_element_type=jnp.float32)
-    return coef_linear * x_scaled + own + sum_others(arrived, me)
+    product = jnp.dot(poly, by_hi, preferred_element_type=jnp.float32)
+    return coef_linear * x_scaled + sum_pieces(product.reshape(8, rows, cols), LO)
 
 
 def solution(mesh):

time: 177 us -> 178 us (level)
  other arithmetic: 3.12 us -> 6.19 us
    add x0 -> x1, other arithmetic: none -> 1.81 us  [per_device(): coef_linear * x_scaled + sum_pieces(product.reshape(8, rows, cols), LO)]
    dot_general x2 -> x1, matrix products: 4.33 us -> 3.12 us  [per_device(): product = jnp.dot(poly, by_hi, preferred_element_type=jnp.float32)]
  transfers between devices with their start and end apart: 7 -> 7, of which waited for: 5 -> 5; matrix products, arithmetic and copies ran while one was open for 0% -> 1% of each run, Pallas kernels for 0% -> 0%
where the time goes in v12:
time: 178 us
  waiting for transfers between devices  65.1 us (37%)
  blocking collectives  63.8 us (36%)
  starting transfers between devices  35.1 us (20%)
  other arithmetic  6.19 us (3%)
  matrix products  4.9 us (3%)
  local copies, waits for them, and re-layouts  2.27 us (1%)
    all_to_all x3, waiting for transfers between devices, sum_pieces(): lax.all_to_all(jnp.where(mine, 0.0, pieces).astype(jnp.bfloat16), axis, 0...  43.9 us
    all_gather x2, blocking collectives, per_device(): by_lo = [lax.all_gather(pair[y], 'x', axis=0, tiled=True) for y in range(2)]  23.9 us
    all_to_all x2, waiting for transfers between devices, spread(): lax.all_to_all(jnp.broadcast_to(block[None], (8,) + block.shape), axis, 0...  21.2 us
    all_gather x1, blocking collectives, per_device(): poly = lax.all_gather(poly, COL, axis=0, tiled=True)  18.7 us
    all_to_all x3, starting transfers between devices, sum_pieces(): lax.all_to_all(jnp.where(mine, 0.0, pieces).astype(jnp.bfloat16), axis, 0...  17.7 us
    all_to_all x2, starting transfers between devices, spread(): lax.all_to_all(jnp.broadcast_to(block[None], (8,) + block.shape), axis, 0...  14.4 us
    all_gather x1, blocking collectives, per_device(): left = lax.all_gather(left, 'x', axis=0).reshape(4, 2, rows, 8 * rows)  10.9 us
    all_gather x1, blocking collectives, per_device(): pair = lax.all_gather(xb, 'y_lo', axis=0)  6.12 us
  transfers between devices with their start and end apart: 7, of which 5 were waited for; matrix products, arithmetic and copies ran while one was open for 1% of the time, Pallas kernels for 0%

profile of v12, /device:TPU:1, one launch (start us, length us, event | category | flops | bytes accessed | tf_op | source)
XLA Modules:
  0.0 177.6 jit_solution(2883560966605245044)
XLA Ops:
  0.0 1.0 convert_element_type.36
  1.0 1.3 broadcast_in_dim.58
  2.3 10.9 %all-to-all-start = ((bf16[8,64,1536]{2,1,0:T(8,128)(2,1)}), bf16[8,64,1536]{2,1,0:T(8,128)(2,1)S(1)}, u32[]{:S(2)}, u32[]{:S(2)}) async-start(bf16[8,64,1536]{2,1,0:T(8,128)(2,1)} %broadcast_in_dim.58), calls=%async_computation | async-start | bytes 3145728 | tf_op jit(solution)/shard_map/all_to_all | solution.py:32
  13.2 6.1 %all-gather = bf16[128,1536]{1,0:T(8,128)(2,1)S(1)} all-gather(bf16[64,1536]{1,0:T(8,128)(2,1)S(1)} %convert_element_type.36), channel_id=2, replica_groups=mesh['y_lo'=2,'z'=8,'x'=4,'y_hi'=4,'core'=2] {'y_lo'}, dimensions={0}, use_global_device_ids=true | all-gather | bytes 589824 | tf_op jit(solution)/shard_map/all_gather | solution.py:47
  19.3 12.6 %all-gather.5 = bf16[256,1536]{1,0:T(8,128)(2,1)S(1)} all-gather(bf16[64,1536]{1,0:T(8,128)(2,1)S(1)} %get-tuple-element.7), channel_id=7, replica_groups=mesh['y_lo'=2,'z'=8,'x'=4,'y_hi'=4,'core'=2] {'x'}, dimensions={0}, use_global_device_ids=true | all-gather | bytes 983040 | tf_op jit(solution)/shard_map/all_gather | solution.py:48
  32.0 11.3 %all-gather.6 = bf16[256,1536]{1,0:T(8,128)(2,1)S(1)} all-gather(bf16[64,1536]{1,0:T(8,128)(2,1)S(1)} %get-tuple-element.8), channel_id=8, replica_groups=mesh['y_lo'=2,'z'=8,'x'=4,'y_hi'=4,'core'=2] {'x'}, dimensions={0}, use_global_device_ids=true | all-gather | bytes 983040 | tf_op jit(solution)/shard_map/all_gather | solution.py:48
  43.3 8.2 %all-to-all-done = bf16[8,64,1536]{2,1,0:T(8,128)(2,1)S(1)} async-done(((bf16[8,64,1536]{2,1,0:T(8,128)(2,1)}), bf16[8,64,1536]{2,1,0:T(8,128)(2,1)S(1)}, u32[]{:S(2)}, u32[]{:S(2)}) %all-to-all-start) | async-done | bytes 1572896 | tf_op jit(solution)/shard_map/all_to_all | solution.py:32
  51.4 0.6 fusion.12
  52.0 0.6 fusion.11
  52.6 0.1 maximum_multiply_fusion
  52.8 1.0 select_convert_fusion.1
  53.7 9.8 %all-to-all-start.1 = ((bf16[8,64,512]{2,1,0:T(8,128)(2,1)}), bf16[8,64,512]{2,1,0:T(8,128)(2,1)S(1)}, u32[]{:S(2)}, u32[]{:S(2)}) async-start(bf16[8,64,512]{2,1,0:T(8,128)(2,1)} %select_convert_fusion.1), calls=%async_computation.1 | async-start | bytes 1048576 | tf_op jit(solution)/shard_map/all_to_all | solution.py:38
  63.5 15.9 %all-to-all-done.1 = bf16[8,64,512]{2,1,0:T(8,128)(2,1)S(1)} async-done(((bf16[8,64,512]{2,1,0:T(8,128)(2,1)}), bf16[8,64,512]{2,1,0:T(8,128)(2,1)S(1)}, u32[]{:S(2)}, u32[]{:S(2)}) %all-to-all-start.1) | async-done | bytes 524320 | tf_op jit(solution)/shard_map/all_to_all | solution.py:38
  79.4 0.1 convert_reduce_fusion.1
  79.5 0.8 broadcast_in_dim.62
  80.3 3.5 %all-to-all-start.2 = ((bf16[8,64,512]{2,1,0:T(8,128)(2,1)}), bf16[8,64,512]{2,1,0:T(8,128)(2,1)S(1)}, u32[]{:S(2)}, u32[]{:S(2)}) async-start(bf16[8,64,512]{2,1,0:T(8,128)(2,1)} %broadcast_in_dim.62), calls=%async_computation.2 | async-start | bytes 1048576 | tf_op jit(solution)/shard_map/all_to_all | solution.py:32
  83.8 0.7 collective-permute-start
  84.5 0.0 collective-permute-done
  84.5 4.2 %all-gather.3 = bf16[128,512]{1,0:T(8,128)(2,1)S(1)} all-gather(bf16[64,512]{1,0:T(8,128)(2,1)S(1)} %collective-permute-done), channel_id=5, replica_groups=mesh['y_lo'=2,'z'=8,'x'=4,'y_hi'=4,'core'=2] {'y_lo'}, dimensions={0}, use_global_device_ids=true | all-gather | bytes 196608 | tf_op jit(solution)/shard_map/all_gather | solution.py:56
  88.7 13.0 %all-to-all-done.2 = bf16[8,64,512]{2,1,0:T(8,128)(2,1)S(1)} async-done(((bf16[8,64,512]{2,1,0:T(8,128)(2,1)}), bf16[8,64,512]{2,1,0:T(8,128)(2,1)S(1)}, u32[]{:S(2)}, u32[]{:S(2)}) %all-to-all-start.2) | async-done | bytes 524320 | tf_op jit(solution)/shard_map/all_to_all | solution.py:32
  101.7 2.4 %collective-permute-start.1 = (bf16[512,512]{1,0:T(8,128)(2,1)S(1)}, bf16[512,512]{1,0:T(8,128)(2,1)S(1)}, u32[]{:S(2)}, u32[]{:S(2)}) collective-permute-start(bf16[512,512]{1,0:T(8,128)(2,1)S(1)} %bitcast.57), channel_id=1, source_target_pairs={{0,1},{1,0},{2,3},{3,2},{4,5},{5,4},{6,7},{7,6},{8,9},{9,8},{10,11... | collective-permute-start | bytes 1572872 | tf_op jit(solution)/shard_map/ppermute | solution.py:55
  104.1 10.9 %all-gather.4 = bf16[8,64,512]{2,1,0:T(8,128)(2,1)S(1)} all-gather(bf16[2,64,512]{2,1,0:T(8,128)(2,1)S(1)} %bitcast.62), channel_id=6, replica_groups=mesh['y_lo'=2,'z'=8,'x'=4,'y_hi'=4,'core'=2] {'x'}, dimensions={0}, use_global_device_ids=true | all-gather | bytes 655360 | tf_op jit(solution)/shard_map/all_gather | solution.py:57
  115.0 0.0 copy-start
  115.0 0.3 fusion.13
  115.3 0.0 collective-permute-done.1
  115.4 0.3 convolution_add_fusion
  115.7 0.1 copy-done
  115.8 0.8 select_convert_fusion.2
  116.6 3.4 %all-to-all-start.3 = ((bf16[4,64,512]{2,1,0:T(8,128)(2,1)}), bf16[4,64,512]{2,1,0:T(8,128)(2,1)S(1)}, u32[]{:S(2)}, u32[]{:S(2)}) async-start(bf16[4,64,512]{2,1,0:T(8,128)(2,1)} %select_convert_fusion.2), calls=%async_computation.3 | async-start | bytes 524288 | tf_op jit(solution)/shard_map/all_to_all | solution.py:38
  120.0 1.0 fusion.6
  121.0 7.0 %all-to-all-done.3 = bf16[4,64,512]{2,1,0:T(8,128)(2,1)S(1)} async-done(((bf16[4,64,512]{2,1,0:T(8,128)(2,1)}), bf16[4,64,512]{2,1,0:T(8,128)(2,1)S(1)}, u32[]{:S(2)}, u32[]{:S(2)}) %all-to-all-start.3) | async-done | bytes 262176 | tf_op jit(solution)/shard_map/all_to_all | solution.py:38
  128.1 0.1 fusion.5
  128.2 18.7 %all_gather.35 = bf16[512,512]{1,0:T(8,128)(2,1)S(1)} all-gather(bf16[64,512]{1,0:T(8,128)(2,1)S(1)} %fusion.5), channel_id=1, replica_groups=mesh['y_lo'=2,'z'=8,'x'=4,'y_hi'=4,'core'=2] {'y_hi','core'}, dimensions={0}, use_global_device_ids=true | all-gather | bytes 589824 | tf_op jit(solution)/shard_map/all_gather | solution.py:73
  146.9 3.1 %select_convert_fusion = (bf16[8,64,1536]{2,1,0:T(8,128)(2,1)}, f32[8,64,1536]{2,1,0:T(8,128)}) fusion(pred[8]{0:T(512)(128)(4,1)S(1)} %iota_compare_fusion.1, bf16[8,64,512]{2,1,0:T(8,128)(2,1)S(1)} %bitcast.59, bf16[512,1536,1]{1,0,2:T(8,128)(2,1)S(1)} %bitcast.48), kind=kOutput, calls=%fused_computation.1 | convolution fusion | flops 806092800 | bytes 6815752 | tf_op jit(solution)/shard_map/dot_general | solution.py:74
  150.0 4.5 %all-to-all-start.4 = ((bf16[8,64,1536]{2,1,0:T(8,128)(2,1)}), bf16[8,64,1536]{2,1,0:T(8,128)(2,1)S(1)}, u32[]{:S(2)}, u32[]{:S(2)}) async-start(bf16[8,64,1536]{2,1,0:T(8,128)(2,1)} %get-tuple-element.9), calls=%async_computation.4 | async-start | bytes 3145728 | tf_op jit(solution)/shard_map/all_to_all | solution.py:38
  154.6 0.0 copy-start.1
  154.6 21.0 %all-to-all-done.4 = bf16[8,64,1536]{2,1,0:T(8,128)(2,1)S(1)} async-done(((bf16[8,64,1536]{2,1,0:T(8,128)(2,1)}), bf16[8,64,1536]{2,1,0:T(8,128)(2,1)S(1)}, u32[]{:S(2)}, u32[]{:S(2)}) %all-to-all-start.4) | async-done | bytes 1572896 | tf_op jit(solution)/shard_map/all_to_all | solution.py:38
  175.6 0.2 convert_reduce_fusion
  175.8 0.0 copy-done.1
  175.8 1.8 %fusion = f32[64,1536]{1,0:T(8,128)} fusion(f32[64,1536]{1,0:T(8,128)S(1)} %convert_reduce_fusion, f32[8,64,1536]{2,1,0:T(8,128)} %get-tuple-element.10, s32[]{:T(128)S(6)} %select_n.63, f32[64,1536]{1,0:T(8,128)S(1)} %copy-done.1), kind=kLoop, calls=%fused_computation.9 | loop fusion | flops 294912 | bytes 1572868 | tf_op jit(solution)/shard_map/add | solution.py:75
  (10 shorter events, 0.2 us)
Async XLA Ops:
  2.3 49.1 %all-to-all-start = ((bf16[8,64,1536]{2,1,0:T(8,128)(2,1)}), bf16[8,64,1536]{2,1,0:T(8,128)(2,1)S(1)}, u32[]{:S(2)}, u32[]{:S(2)}) async-start(bf16[8,64,1536]{2,1,0:T(8,128)(2,1)} %broadcast_in_dim.58), calls=%async_computation | async-start | bytes 3145728 | tf_op jit(solution)/shard_map/all_to_all | solution.py:32
  53.7 25.6 %all-to-all-start.1 = ((bf16[8,64,512]{2,1,0:T(8,128)(2,1)}), bf16[8,64,512]{2,1,0:T(8,128)(2,1)S(1)}, u32[]{:S(2)}, u32[]{:S(2)}) async-start(bf16[8,64,512]{2,1,0:T(8,128)(2,1)} %select_convert_fusion.1), calls=%async_computation.1 | async-start | bytes 1048576 | tf_op jit(solution)/shard_map/all_to_all | solution.py:38
  80.3 21.4 %all-to-all-start.2 = ((bf16[8,64,512]{2,1,0:T(8,128)(2,1)}), bf16[8,64,512]{2,1,0:T(8,128)(2,1)S(1)}, u32[]{:S(2)}, u32[]{:S(2)}) async-start(bf16[8,64,512]{2,1,0:T(8,128)(2,1)} %broadcast_in_dim.62), calls=%async_computation.2 | async-start | bytes 1048576 | tf_op jit(solution)/shard_map/all_to_all | solution.py:32
  83.8 0.7 collective-permute-start
  101.7 13.6 %collective-permute-start.1 = (bf16[512,512]{1,0:T(8,128)(2,1)S(1)}, bf16[512,512]{1,0:T(8,128)(2,1)S(1)}, u32[]{:S(2)}, u32[]{:S(2)}) collective-permute-start(bf16[512,512]{1,0:T(8,128)(2,1)S(1)} %bitcast.57), channel_id=1, source_target_pairs={{0,1},{1,0},{2,3},{3,2},{4,5},{5,4},{6,7},{7,6},{8,9},{9,8},{10,11... | collective-permute-start | bytes 1572872 | tf_op jit(solution)/shard_map/ppermute | solution.py:55
  115.0 0.8 copy-start
  116.6 11.4 %all-to-all-start.3 = ((bf16[4,64,512]{2,1,0:T(8,128)(2,1)}), bf16[4,64,512]{2,1,0:T(8,128)(2,1)S(1)}, u32[]{:S(2)}, u32[]{:S(2)}) async-start(bf16[4,64,512]{2,1,0:T(8,128)(2,1)} %select_convert_fusion.2), calls=%async_computation.3 | async-start | bytes 524288 | tf_op jit(solution)/shard_map/all_to_all | solution.py:38
  150.0 25.6 %all-to-all-start.4 = ((bf16[8,64,1536]{2,1,0:T(8,128)(2,1)}), bf16[8,64,1536]{2,1,0:T(8,128)(2,1)S(1)}, u32[]{:S(2)}, u32[]{:S(2)}) async-start(bf16[8,64,1536]{2,1,0:T(8,128)(2,1)} %get-tuple-element.9), calls=%async_computation.4 | async-start | bytes 3145728 | tf_op jit(solution)/shard_map/all_to_all | solution.py:38
  154.6 21.2 %copy-start.1 = (f32[64,1536]{1,0:T(8,128)S(1)}, f32[64,1536]{1,0:T(8,128)}, u32[]{:S(2)}) copy-start(f32[64,1536]{1,0:T(8,128)} %param.1) | copy-start | bytes 1179652

commit v13 on v12

--- a/solution.py
+++ b/solution.py
@@ -36,7 +36,7 @@
     me = lax.axis_index(axis)
     mine = jnp.arange(pieces.shape[0])[:, None, None] == me
     arrived = lax.all_to_all(jnp.where(mine, 0.0, pieces).astype(jnp.bfloat16), axis, 0, 0)
-    own = lax.dynamic_index_in_dim(pieces, me, 0, keepdims=False)
+    own = lax.dynamic_slice(pieces, (me, 0, 0), (1,) + pieces.shape[1:], allow_negative_indices=False)[0]
     return own + arrived.astype(jnp.float32).sum(0)
 
 
@@ -63,7 +63,8 @@
     )
     square = sum_pieces(square.reshape(4, rows, 8 * rows), "y_hi")
 
-    at_home = lax.dynamic_slice(left, (lax.axis_index("y_hi"), core, 0, 0), (1, 1, rows, 8 * rows))[0, 0]
+    place = (lax.axis_index("y_hi"), core, 0, 0)
+    at_home = lax.dynamic_slice(left, place, (1, 1, rows, 8 * rows), allow_negative_indices=False)[0, 0]
     column = lax.broadcasted_iota(jnp.int32, at_home.shape, 1) - lax.axis_index("z") * rows
     on_diagonal = column == lax.broadcasted_iota(jnp.int32, at_home.shape, 0)
     diagonal = jnp.where(on_diagonal, at_home.astype(jnp.float32), 0.0).sum(1, keepdims=True)

time: 178 us -> 174 us (0.978)
  blocking collectives: 63.8 us -> 115 us
  waiting for transfers between devices: 65.1 us -> 28.1 us
  starting transfers between devices: 35.1 us -> 20.8 us
  matrix products: 4.9 us -> 2.77 us
    all_to_all x0 -> x2, blocking collectives: none -> 49.7 us  [sum_pieces(): lax.all_to_all(jnp.where(mine, 0.0, pieces).astype(jnp.bfloat16), axis, 0...]
    all_to_all x3 -> x1, waiting for transfers between devices: 43.9 us -> 7.01 us  [sum_pieces(): lax.all_to_all(jnp.where(mine, 0.0, pieces).astype(jnp.bfloat16), axis, 0...]
    all_to_all x3 -> x1, starting transfers between devices: 17.7 us -> 3.41 us  [sum_pieces(): lax.all_to_all(jnp.where(mine, 0.0, pieces).astype(jnp.bfloat16), axis, 0...]
    dot_general x1, matrix products: 3.12 us -> 0.98 us  [per_device(): product = jnp.dot(poly, by_hi, preferred_element_type=jnp.float32)]
  transfers between devices with their start and end apart: 7 -> 5, of which waited for: 5 -> 3; matrix products, arithmetic and copies ran while one was open for 1% -> 1% of each run, Pallas kernels for 0% -> 0%
where the time goes in v13:
time: 174 us
  blocking collectives  115 us (66%)
  waiting for transfers between devices  28.1 us (16%)
  starting transfers between devices  20.8 us (12%)
  other arithmetic  4.42 us (3%)
  local copies, waits for them, and re-layouts  3.04 us (2%)
  matrix products  2.77 us (2%)
    all_to_all x2, blocking collectives, sum_pieces(): lax.all_to_all(jnp.where(mine, 0.0, pieces).astype(jnp.bfloat16), axis, 0...  49.7 us
    all_gather x2, blocking collectives, per_device(): by_lo = [lax.all_gather(pair[y], 'x', axis=0, tiled=True) for y in range(2)]  23.9 us
    all_to_all x2, waiting for transfers between devices, spread(): lax.all_to_all(jnp.broadcast_to(block[None], (8,) + block.shape), axis, 0...  21.1 us
    all_gather x1, blocking collectives, per_device(): poly = lax.all_gather(poly, COL, axis=0, tiled=True)  19.6 us
    all_to_all x2, starting transfers between devices, spread(): lax.all_to_all(jnp.broadcast_to(block[None], (8,) + block.shape), axis, 0...  14.4 us
    all_gather x1, blocking collectives, per_device(): left = lax.all_gather(left, 'x', axis=0).reshape(4, 2, rows, 8 * rows)  10.9 us
    all_to_all x1, waiting for transfers between devices, sum_pieces(): lax.all_to_all(jnp.where(mine, 0.0, pieces).astype(jnp.bfloat16), axis, 0...  7.01 us
    all_gather x1, blocking collectives, per_device(): pair = lax.all_gather(xb, 'y_lo', axis=0)  6.12 us
  transfers between devices with their start and end apart: 5, of which 3 were waited for; matrix products, arithmetic and copies ran while one was open for 1% of the time, Pallas kernels for 0%

profile of v13, /device:TPU:1, one launch (start us, length us, event | category | flops | bytes accessed | tf_op | source)
XLA Modules:
  0.0 173.9 jit_solution(5959108858830548969)
XLA Ops:
  0.0 1.0 convert_element_type.36
  1.0 1.3 broadcast_in_dim.58
  2.3 10.9 %all-to-all-start = ((bf16[8,64,1536]{2,1,0:T(8,128)(2,1)}), bf16[8,64,1536]{2,1,0:T(8,128)(2,1)S(1)}, u32[]{:S(2)}, u32[]{:S(2)}) async-start(bf16[8,64,1536]{2,1,0:T(8,128)(2,1)} %broadcast_in_dim.58), calls=%async_computation | async-start | bytes 3145728 | tf_op jit(solution)/shard_map/all_to_all | solution.py:32
  13.2 6.1 %all-gather = bf16[128,1536]{1,0:T(8,128)(2,1)S(1)} all-gather(bf16[64,1536]{1,0:T(8,128)(2,1)S(1)} %convert_element_type.36), channel_id=2, replica_groups=mesh['y_lo'=2,'z'=8,'x'=4,'y_hi'=4,'core'=2] {'y_lo'}, dimensions={0}, use_global_device_ids=true | all-gather | bytes 589824 | tf_op jit(solution)/shard_map/all_gather | solution.py:47
  19.3 12.6 %all-gather.5 = bf16[256,1536]{1,0:T(8,128)(2,1)S(1)} all-gather(bf16[64,1536]{1,0:T(8,128)(2,1)S(1)} %get-tuple-element.7), channel_id=7, replica_groups=mesh['y_lo'=2,'z'=8,'x'=4,'y_hi'=4,'core'=2] {'x'}, dimensions={0}, use_global_device_ids=true | all-gather | bytes 983040 | tf_op jit(solution)/shard_map/all_gather | solution.py:48
  32.0 11.3 %all-gather.6 = bf16[256,1536]{1,0:T(8,128)(2,1)S(1)} all-gather(bf16[64,1536]{1,0:T(8,128)(2,1)S(1)} %get-tuple-element.8), channel_id=8, replica_groups=mesh['y_lo'=2,'z'=8,'x'=4,'y_hi'=4,'core'=2] {'x'}, dimensions={0}, use_global_device_ids=true | all-gather | bytes 983040 | tf_op jit(solution)/shard_map/all_gather | solution.py:48
  43.3 8.2 %all-to-all-done = bf16[8,64,1536]{2,1,0:T(8,128)(2,1)S(1)} async-done(((bf16[8,64,1536]{2,1,0:T(8,128)(2,1)}), bf16[8,64,1536]{2,1,0:T(8,128)(2,1)S(1)}, u32[]{:S(2)}, u32[]{:S(2)}) %all-to-all-start) | async-done | bytes 1572896 | tf_op jit(solution)/shard_map/all_to_all | solution.py:32
  51.4 0.6 fusion.12
  52.0 0.6 fusion.11
  52.6 0.1 maximum_multiply_fusion
  52.8 0.2 select_convert_fusion.1
  52.9 25.4 %all_to_all.25 = bf16[8,64,512]{2,1,0:T(8,128)(2,1)S(1)} all-to-all(bf16[8,64,512]{2,1,0:T(8,128)(2,1)S(1)} %select_convert_fusion.1), channel_id=1, replica_groups=mesh['y_lo'=2,'z'=8,'x'=4,'y_hi'=4,'core'=2] {'core','y_hi'}, dimensions={0} | all-to-all | bytes 1048576 | tf_op jit(solution)/shard_map/all_to_all | solution.py:38
  78.4 0.1 convert_reduce_fusion.1
  78.5 0.8 broadcast_in_dim.62
  79.3 3.5 %all-to-all-start.2 = ((bf16[8,64,512]{2,1,0:T(8,128)(2,1)}), bf16[8,64,512]{2,1,0:T(8,128)(2,1)S(1)}, u32[]{:S(2)}, u32[]{:S(2)}) async-start(bf16[8,64,512]{2,1,0:T(8,128)(2,1)} %broadcast_in_dim.62), calls=%async_computation.2 | async-start | bytes 1048576 | tf_op jit(solution)/shard_map/all_to_all | solution.py:32
  82.8 0.7 collective-permute-start
  83.5 0.0 collective-permute-done
  83.5 4.3 %all-gather.3 = bf16[128,512]{1,0:T(8,128)(2,1)S(1)} all-gather(bf16[64,512]{1,0:T(8,128)(2,1)S(1)} %collective-permute-done), channel_id=5, replica_groups=mesh['y_lo'=2,'z'=8,'x'=4,'y_hi'=4,'core'=2] {'y_lo'}, dimensions={0}, use_global_device_ids=true | all-gather | bytes 196608 | tf_op jit(solution)/shard_map/all_gather | solution.py:56
  87.9 12.9 %all-to-all-done.2 = bf16[8,64,512]{2,1,0:T(8,128)(2,1)S(1)} async-done(((bf16[8,64,512]{2,1,0:T(8,128)(2,1)}), bf16[8,64,512]{2,1,0:T(8,128)(2,1)S(1)}, u32[]{:S(2)}, u32[]{:S(2)}) %all-to-all-start.2) | async-done | bytes 524320 | tf_op jit(solution)/shard_map/all_to_all | solution.py:32
  100.8 2.3 %collective-permute-start.1 = (bf16[512,512]{1,0:T(8,128)(2,1)S(1)}, bf16[512,512]{1,0:T(8,128)(2,1)S(1)}, u32[]{:S(2)}, u32[]{:S(2)}) collective-permute-start(bf16[512,512]{1,0:T(8,128)(2,1)S(1)} %bitcast.57), channel_id=1, source_target_pairs={{0,1},{1,0},{2,3},{3,2},{4,5},{5,4},{6,7},{7,6},{8,9},{9,8},{10,11... | collective-permute-start | bytes 1572872 | tf_op jit(solution)/shard_map/ppermute | solution.py:55
  103.1 10.9 %all-gather.4 = bf16[8,64,512]{2,1,0:T(8,128)(2,1)S(1)} all-gather(bf16[2,64,512]{2,1,0:T(8,128)(2,1)S(1)} %bitcast.62), channel_id=6, replica_groups=mesh['y_lo'=2,'z'=8,'x'=4,'y_hi'=4,'core'=2] {'x'}, dimensions={0}, use_global_device_ids=true | all-gather | bytes 655360 | tf_op jit(solution)/shard_map/all_gather | solution.py:57
  114.0 0.0 copy-start
  114.0 0.3 fusion.13
  114.4 0.0 collective-permute-done.1
  114.4 0.3 convolution_add_fusion
  114.7 0.1 copy-done
  114.8 0.8 select_convert_fusion.2
  115.6 3.4 %all-to-all-start.3 = ((bf16[4,64,512]{2,1,0:T(8,128)(2,1)}), bf16[4,64,512]{2,1,0:T(8,128)(2,1)S(1)}, u32[]{:S(2)}, u32[]{:S(2)}) async-start(bf16[4,64,512]{2,1,0:T(8,128)(2,1)} %select_convert_fusion.2), calls=%async_computation.3 | async-start | bytes 524288 | tf_op jit(solution)/shard_map/all_to_all | solution.py:38
  119.0 1.0 fusion.6
  120.0 7.0 %all-to-all-done.3 = bf16[4,64,512]{2,1,0:T(8,128)(2,1)S(1)} async-done(((bf16[4,64,512]{2,1,0:T(8,128)(2,1)}), bf16[4,64,512]{2,1,0:T(8,128)(2,1)S(1)}, u32[]{:S(2)}, u32[]{:S(2)}) %all-to-all-start.3) | async-done | bytes 262176 | tf_op jit(solution)/shard_map/all_to_all | solution.py:38
  127.0 0.1 fusion.5
  127.1 19.6 %all_gather.35 = bf16[512,512]{1,0:T(8,128)(2,1)S(1)} all-gather(bf16[64,512]{1,0:T(8,128)(2,1)S(1)} %fusion.5), channel_id=1, replica_groups=mesh['y_lo'=2,'z'=8,'x'=4,'y_hi'=4,'core'=2] {'y_hi','core'}, dimensions={0}, use_global_device_ids=true | all-gather | bytes 589824 | tf_op jit(solution)/shard_map/all_gather | solution.py:74
  146.8 1.0 select_convert_fusion
  147.7 24.3 %all_to_all.26 = bf16[8,64,1536]{2,1,0:T(8,128)(2,1)S(1)} all-to-all(bf16[8,64,1536]{2,1,0:T(8,128)(2,1)S(1)} %get-tuple-element.9), channel_id=1, replica_groups=mesh['y_lo'=2,'z'=8,'x'=4,'y_hi'=4,'core'=2] {'x','y_lo'}, dimensions={0} | all-to-all | bytes 3145728 | tf_op jit(solution)/shard_map/all_to_all | solution.py:38
  172.0 0.0 copy-start.1
  172.0 0.2 convert_reduce_fusion
  172.2 0.8 copy-done.1
  173.0 0.8 fusion
  (10 shorter events, 0.2 us)
Async XLA Ops:
  2.3 49.1 %all-to-all-start = ((bf16[8,64,1536]{2,1,0:T(8,128)(2,1)}), bf16[8,64,1536]{2,1,0:T(8,128)(2,1)S(1)}, u32[]{:S(2)}, u32[]{:S(2)}) async-start(bf16[8,64,1536]{2,1,0:T(8,128)(2,1)} %broadcast_in_dim.58), calls=%async_computation | async-start | bytes 3145728 | tf_op jit(solution)/shard_map/all_to_all | solution.py:32
  79.3 21.5 %all-to-all-start.2 = ((bf16[8,64,512]{2,1,0:T(8,128)(2,1)}), bf16[8,64,512]{2,1,0:T(8,128)(2,1)S(1)}, u32[]{:S(2)}, u32[]{:S(2)}) async-start(bf16[8,64,512]{2,1,0:T(8,128)(2,1)} %broadcast_in_dim.62), calls=%async_computation.2 | async-start | bytes 1048576 | tf_op jit(solution)/shard_map/all_to_all | solution.py:32
  82.8 0.7 collective-permute-start
  100.8 13.6 %collective-permute-start.1 = (bf16[512,512]{1,0:T(8,128)(2,1)S(1)}, bf16[512,512]{1,0:T(8,128)(2,1)S(1)}, u32[]{:S(2)}, u32[]{:S(2)}) collective-permute-start(bf16[512,512]{1,0:T(8,128)(2,1)S(1)} %bitcast.57), channel_id=1, source_target_pairs={{0,1},{1,0},{2,3},{3,2},{4,5},{5,4},{6,7},{7,6},{8,9},{9,8},{10,11... | collective-permute-start | bytes 1572872 | tf_op jit(solution)/shard_map/ppermute | solution.py:55
  114.0 0.8 copy-start
  115.6 11.4 %all-to-all-start.3 = ((bf16[4,64,512]{2,1,0:T(8,128)(2,1)}), bf16[4,64,512]{2,1,0:T(8,128)(2,1)S(1)}, u32[]{:S(2)}, u32[]{:S(2)}) async-start(bf16[4,64,512]{2,1,0:T(8,128)(2,1)} %select_convert_fusion.2), calls=%async_computation.3 | async-start | bytes 524288 | tf_op jit(solution)/shard_map/all_to_all | solution.py:38
  172.0 1.0 copy-start.1

commit v14 on v13

--- a/solution.py
+++ b/solution.py
@@ -51,10 +51,11 @@
     gram = sum_pieces(tile.reshape(8, rows, 8 * rows), ("core", "y_hi"))
 
     rounded = gram.astype(jnp.bfloat16)
-    right = spread(rounded, "z").reshape(8 * rows, 8 * rows)
+    moved = swap_x_y_hi(rounded)
+    left = lax.all_gather(moved, "y_lo", axis=0)
+    left = lax.all_gather(left, "x", axis=0).reshape(4, 2, rows, 8 * rows)
+    right = spread(rounded + 0 * moved[:1, :1], "z").reshape(8 * rows, 8 * rows)
     right_other = lax.ppermute(right, "core", [(0, 1), (1, 0)])
-    left = lax.all_gather(swap_x_y_hi(rounded), "y_lo", axis=0)
-    left = lax.all_gather(left, "x", axis=0).reshape(4, 2, rows, 8 * rows)
     core = lax.axis_index("core")
     own = jnp.where(core == 0, left[:, 0], left[:, 1]).reshape(4 * rows, 8 * rows)
     other = jnp.where(core == 0, left[:, 1], left[:, 0]).reshape(4 * rows, 8 * rows)

time: 174 us -> 187 us (1.075)
  blocking collectives: 115 us -> 126 us
    all_gather x1, blocking collectives: 10.9 us -> 22 us  [per_device(): left = lax.all_gather(left, 'x', axis=0).reshape(4, 2, rows, 8 * rows)]
where the time goes in v14:
time: 187 us
  blocking collectives  126 us (67%)
  waiting for transfers between devices  28.7 us (15%)
  starting transfers between devices  20.8 us (11%)
  other arithmetic  4.42 us (2%)
  local copies, waits for them, and re-layouts  3.55 us (2%)
  matrix products  2.77 us (1%)
    all_to_all x2, blocking collectives, sum_pieces(): lax.all_to_all(jnp.where(mine, 0.0, pieces).astype(jnp.bfloat16), axis, 0...  50.1 us
    all_gather x2, blocking collectives, per_device(): by_lo = [lax.all_gather(pair[y], 'x', axis=0, tiled=True) for y in range(2)]  23.9 us
    all_gather x1, blocking collectives, per_device(): left = lax.all_gather(left, 'x', axis=0).reshape(4, 2, rows, 8 * rows)  22 us
    all_to_all x2, waiting for transfers between devices, spread(): lax.all_to_all(jnp.broadcast_to(block[None], (8,) + block.shape), axis, 0...  21.8 us
    all_gather x1, blocking collectives, per_device(): poly = lax.all_gather(poly, COL, axis=0, tiled=True)  19.4 us
    all_to_all x2, starting transfers between devices, spread(): lax.all_to_all(jnp.broadcast_to(block[None], (8,) + block.shape), axis, 0...  14.4 us
    all_to_all x1, waiting for transfers between devices, sum_pieces(): lax.all_to_all(jnp.where(mine, 0.0, pieces).astype(jnp.bfloat16), axis, 0...  6.91 us
    all_gather x1, blocking collectives, per_device(): pair = lax.all_gather(xb, 'y_lo', axis=0)  6.12 us
  transfers between devices with their start and end apart: 5, of which 3 were waited for; matrix products, arithmetic and copies ran while one was open for 1% of the time, Pallas kernels for 0%

profile of v14, /device:TPU:1, one launch (start us, length us, event | category | flops | bytes accessed | tf_op | source)
XLA Modules:
  0.0 186.8 jit_solution(10758198611687944306)
XLA Ops:
  0.0 1.0 convert_element_type.36
  1.0 1.3 broadcast_in_dim.58
  2.3 10.9 %all-to-all-start = ((bf16[8,64,1536]{2,1,0:T(8,128)(2,1)}), bf16[8,64,1536]{2,1,0:T(8,128)(2,1)S(1)}, u32[]{:S(2)}, u32[]{:S(2)}) async-start(bf16[8,64,1536]{2,1,0:T(8,128)(2,1)} %broadcast_in_dim.58), calls=%async_computation | async-start | bytes 3145728 | tf_op jit(solution)/shard_map/all_to_all | solution.py:32
  13.2 6.1 %all-gather = bf16[128,1536]{1,0:T(8,128)(2,1)S(1)} all-gather(bf16[64,1536]{1,0:T(8,128)(2,1)S(1)} %convert_element_type.36), channel_id=2, replica_groups=mesh['y_lo'=2,'z'=8,'x'=4,'y_hi'=4,'core'=2] {'y_lo'}, dimensions={0}, use_global_device_ids=true | all-gather | bytes 589824 | tf_op jit(solution)/shard_map/all_gather | solution.py:47
  19.3 12.6 %all-gather.5 = bf16[256,1536]{1,0:T(8,128)(2,1)S(1)} all-gather(bf16[64,1536]{1,0:T(8,128)(2,1)S(1)} %get-tuple-element.7), channel_id=7, replica_groups=mesh['y_lo'=2,'z'=8,'x'=4,'y_hi'=4,'core'=2] {'x'}, dimensions={0}, use_global_device_ids=true | all-gather | bytes 983040 | tf_op jit(solution)/shard_map/all_gather | solution.py:48
  32.0 11.3 %all-gather.6 = bf16[256,1536]{1,0:T(8,128)(2,1)S(1)} all-gather(bf16[64,1536]{1,0:T(8,128)(2,1)S(1)} %get-tuple-element.8), channel_id=8, replica_groups=mesh['y_lo'=2,'z'=8,'x'=4,'y_hi'=4,'core'=2] {'x'}, dimensions={0}, use_global_device_ids=true | all-gather | bytes 983040 | tf_op jit(solution)/shard_map/all_gather | solution.py:48
  43.3 8.2 %all-to-all-done = bf16[8,64,1536]{2,1,0:T(8,128)(2,1)S(1)} async-done(((bf16[8,64,1536]{2,1,0:T(8,128)(2,1)}), bf16[8,64,1536]{2,1,0:T(8,128)(2,1)S(1)}, u32[]{:S(2)}, u32[]{:S(2)}) %all-to-all-start) | async-done | bytes 1572896 | tf_op jit(solution)/shard_map/all_to_all | solution.py:32
  51.4 0.6 fusion.13
  52.0 0.6 fusion.12
  52.6 0.1 maximum_multiply_fusion
  52.8 0.2 select_convert_fusion.1
  52.9 25.4 %all_to_all.25 = bf16[8,64,512]{2,1,0:T(8,128)(2,1)S(1)} all-to-all(bf16[8,64,512]{2,1,0:T(8,128)(2,1)S(1)} %select_convert_fusion.1), channel_id=1, replica_groups=mesh['y_lo'=2,'z'=8,'x'=4,'y_hi'=4,'core'=2] {'core','y_hi'}, dimensions={0} | all-to-all | bytes 1048576 | tf_op jit(solution)/shard_map/all_to_all | solution.py:38
  78.4 0.1 convert_reduce_fusion.1
  78.5 0.7 collective-permute-start
  79.1 0.0 collective-permute-done
  79.1 0.5 slice.28
  80.3 0.8 broadcast_in_dim.62
  81.2 3.5 %all-to-all-start.2 = ((bf16[8,64,512]{2,1,0:T(8,128)(2,1)}), bf16[8,64,512]{2,1,0:T(8,128)(2,1)S(1)}, u32[]{:S(2)}, u32[]{:S(2)}) async-start(bf16[8,64,512]{2,1,0:T(8,128)(2,1)} %broadcast_in_dim.62), calls=%async_computation.2 | async-start | bytes 1048576 | tf_op jit(solution)/shard_map/all_to_all | solution.py:32
  84.7 4.3 %all-gather.3 = bf16[128,512]{1,0:T(8,128)(2,1)S(1)} all-gather(bf16[64,512]{1,0:T(8,128)(2,1)S(1)} %collective-permute-done), channel_id=5, replica_groups=mesh['y_lo'=2,'z'=8,'x'=4,'y_hi'=4,'core'=2] {'y_lo'}, dimensions={0}, use_global_device_ids=true | all-gather | bytes 196608 | tf_op jit(solution)/shard_map/all_gather | solution.py:55
  89.0 13.6 %all-to-all-done.2 = bf16[8,64,512]{2,1,0:T(8,128)(2,1)S(1)} async-done(((bf16[8,64,512]{2,1,0:T(8,128)(2,1)}), bf16[8,64,512]{2,1,0:T(8,128)(2,1)S(1)}, u32[]{:S(2)}, u32[]{:S(2)}) %all-to-all-start.2) | async-done | bytes 524320 | tf_op jit(solution)/shard_map/all_to_all | solution.py:32
  102.6 2.3 %collective-permute-start.1 = (bf16[512,512]{1,0:T(8,128)(2,1)S(1)}, bf16[512,512]{1,0:T(8,128)(2,1)S(1)}, u32[]{:S(2)}, u32[]{:S(2)}) collective-permute-start(bf16[512,512]{1,0:T(8,128)(2,1)S(1)} %bitcast.60), channel_id=1, source_target_pairs={{0,1},{1,0},{2,3},{3,2},{4,5},{5,4},{6,7},{7,6},{8,9},{9,8},{10,11... | collective-permute-start | bytes 1572872 | tf_op jit(solution)/shard_map/ppermute | solution.py:58
  105.0 22.0 %all-gather.4 = bf16[8,64,512]{2,1,0:T(8,128)(2,1)S(1)} all-gather(bf16[2,64,512]{2,1,0:T(8,128)(2,1)S(1)} %bitcast.65), channel_id=6, replica_groups=mesh['y_lo'=2,'z'=8,'x'=4,'y_hi'=4,'core'=2] {'x'}, dimensions={0}, use_global_device_ids=true | all-gather | bytes 655360 | tf_op jit(solution)/shard_map/all_gather | solution.py:56
  127.0 0.0 copy-start
  127.0 0.3 fusion.14
  127.3 0.0 collective-permute-done.1
  127.3 0.3 convolution_add_fusion
  127.6 0.1 copy-done
  127.7 0.8 select_convert_fusion.2
  128.5 3.4 %all-to-all-start.3 = ((bf16[4,64,512]{2,1,0:T(8,128)(2,1)}), bf16[4,64,512]{2,1,0:T(8,128)(2,1)S(1)}, u32[]{:S(2)}, u32[]{:S(2)}) async-start(bf16[4,64,512]{2,1,0:T(8,128)(2,1)} %select_convert_fusion.2), calls=%async_computation.3 | async-start | bytes 524288 | tf_op jit(solution)/shard_map/all_to_all | solution.py:38
  132.0 1.0 fusion.6
  132.9 6.9 %all-to-all-done.3 = bf16[4,64,512]{2,1,0:T(8,128)(2,1)S(1)} async-done(((bf16[4,64,512]{2,1,0:T(8,128)(2,1)}), bf16[4,64,512]{2,1,0:T(8,128)(2,1)S(1)}, u32[]{:S(2)}, u32[]{:S(2)}) %all-to-all-start.3) | async-done | bytes 262176 | tf_op jit(solution)/shard_map/all_to_all | solution.py:38
  139.9 0.1 fusion.5
  140.0 19.4 %all_gather.35 = bf16[512,512]{1,0:T(8,128)(2,1)S(1)} all-gather(bf16[64,512]{1,0:T(8,128)(2,1)S(1)} %fusion.5), channel_id=1, replica_groups=mesh['y_lo'=2,'z'=8,'x'=4,'y_hi'=4,'core'=2] {'y_hi','core'}, dimensions={0}, use_global_device_ids=true | all-gather | bytes 589824 | tf_op jit(solution)/shard_map/all_gather | solution.py:75
  159.4 1.0 select_convert_fusion
  160.4 24.6 %all_to_all.26 = bf16[8,64,1536]{2,1,0:T(8,128)(2,1)S(1)} all-to-all(bf16[8,64,1536]{2,1,0:T(8,128)(2,1)S(1)} %get-tuple-element.9), channel_id=1, replica_groups=mesh['y_lo'=2,'z'=8,'x'=4,'y_hi'=4,'core'=2] {'x','y_lo'}, dimensions={0} | all-to-all | bytes 3145728 | tf_op jit(solution)/shard_map/all_to_all | solution.py:38
  185.0 0.0 copy-start.1
  185.0 0.2 convert_reduce_fusion
  185.2 0.8 copy-done.1
  186.0 0.8 fusion
  (10 shorter events, 0.2 us)
Async XLA Ops:
  2.3 49.1 %all-to-all-start = ((bf16[8,64,1536]{2,1,0:T(8,128)(2,1)}), bf16[8,64,1536]{2,1,0:T(8,128)(2,1)S(1)}, u32[]{:S(2)}, u32[]{:S(2)}) async-start(bf16[8,64,1536]{2,1,0:T(8,128)(2,1)} %broadcast_in_dim.58), calls=%async_computation | async-start | bytes 3145728 | tf_op jit(solution)/shard_map/all_to_all | solution.py:32
  78.5 0.7 collective-permute-start
  81.2 21.5 %all-to-all-start.2 = ((bf16[8,64,512]{2,1,0:T(8,128)(2,1)}), bf16[8,64,512]{2,1,0:T(8,128)(2,1)S(1)}, u32[]{:S(2)}, u32[]{:S(2)}) async-start(bf16[8,64,512]{2,1,0:T(8,128)(2,1)} %broadcast_in_dim.62), calls=%async_computation.2 | async-start | bytes 1048576 | tf_op jit(solution)/shard_map/all_to_all | solution.py:32
  102.6 24.7 %collective-permute-start.1 = (bf16[512,512]{1,0:T(8,128)(2,1)S(1)}, bf16[512,512]{1,0:T(8,128)(2,1)S(1)}, u32[]{:S(2)}, u32[]{:S(2)}) collective-permute-start(bf16[512,512]{1,0:T(8,128)(2,1)S(1)} %bitcast.60), channel_id=1, source_target_pairs={{0,1},{1,0},{2,3},{3,2},{4,5},{5,4},{6,7},{7,6},{8,9},{9,8},{10,11... | collective-permute-start | bytes 1572872 | tf_op jit(solution)/shard_map/ppermute | solution.py:58
  127.0 0.8 copy-start
  128.5 11.3 %all-to-all-start.3 = ((bf16[4,64,512]{2,1,0:T(8,128)(2,1)}), bf16[4,64,512]{2,1,0:T(8,128)(2,1)S(1)}, u32[]{:S(2)}, u32[]{:S(2)}) async-start(bf16[4,64,512]{2,1,0:T(8,128)(2,1)} %select_convert_fusion.2), calls=%async_computation.3 | async-start | bytes 524288 | tf_op jit(solution)/shard_map/all_to_all | solution.py:38
  185.0 1.0 copy-start.1

commit v15 on v11

--- a/solution.py
+++ b/solution.py
@@ -44,7 +44,7 @@
     me = lax.axis_index(axis)
     mine = jnp.arange(pieces.shape[0])[:, None, None] == me
     arrived = lax.all_to_all(jnp.where(mine, 0.0, pieces).astype(jnp.bfloat16), axis, 0, 0)
-    own = lax.dynamic_index_in_dim(pieces, me, 0, keepdims=False)
+    own = lax.dynamic_slice(pieces, (me, 0, 0), (1,) + pieces.shape[1:], allow_negative_indices=False)[0]
     return own + arrived.astype(jnp.float32).sum(0)
 
 
@@ -53,9 +53,9 @@
     xb = x_scaled.astype(jnp.bfloat16)
     by_hi = spread(xb, "z").reshape(8 * rows, cols)
     pair = lax.all_gather(xb, "y_lo", axis=0)
-    by_lo = jnp.concatenate([lax.all_gather(pair[y], "x", axis=0, tiled=True) for y in range(2)])
+    by_lo = [lax.all_gather(pair[y], "x", axis=0, tiled=True) for y in range(2)]
 
-    tile = dot_nt(by_lo, by_hi) * (1.0 / N)
+    tile = jnp.concatenate([dot_nt(part, by_hi) for part in by_lo]) * (1.0 / N)
     gram = sum_pieces(tile.reshape(8, rows, 8 * rows), ("core", "y_hi"))
 
     rounded = gram.astype(jnp.bfloat16)
@@ -63,12 +63,13 @@
     right = spread(rounded, "z").reshape(8 * rows, 8 * rows)
     square = sum_pieces(dot_nt(left, right).reshape(8, rows, 8 * rows), LO)
 
-    at_home = lax.dynamic_slice_in_dim(left, lax.axis_index(LO) * rows, rows)
+    place = (lax.axis_index(LO) * rows, 0)
+    at_home = lax.dynamic_slice(left, place, (rows, 8 * rows), allow_negative_indices=False)
     column = lax.broadcasted_iota(jnp.int32, at_home.shape, 1) - lax.axis_index("z") * rows
     on_diagonal = column == lax.broadcasted_iota(jnp.int32, at_home.shape, 0)
-    diagonal = jnp.where(on_diagonal, at_home.astype(jnp.float32), 0.0).sum(1, keepdims=True)
-    moved = swap_lo_col(jnp.concatenate([square, jnp.broadcast_to(diagonal, (rows, 128))], axis=1))
-    square, diagonal = moved[:, : 8 * rows], moved[:, 8 * rows : 8 * rows + 1]
+    diagonal = jnp.where(on_diagonal, at_home.astype(jnp.float32), 0.0).sum(0, keepdims=True)
+    moved = swap_lo_col(jnp.concatenate([square, jnp.broadcast_to(diagonal, (8, 8 * rows))]))
+    square, diagonal = moved[:rows], jnp.where(on_diagonal, moved[rows : rows + 1], 0.0).sum(1, keepdims=True)
 
     square = square + rest_of(gram) * (2.0 * diagonal)
     poly = (coef_cubic * gram + coef_quintic * square).astype(jnp.bfloat16)

time: 180 us -> 180 us (level)
  blocking collectives: 95.2 us -> 120 us
  waiting for transfers between devices: 37.2 us -> 23.3 us
  starting transfers between devices: 32.2 us -> 23.2 us
    all_to_all x1 -> x2, blocking collectives: 23.9 us -> 52 us  [sum_pieces(): lax.all_to_all(jnp.where(mine, 0.0, pieces).astype(jnp.bfloat16), axis, 0...]
    all_to_all x2 -> x1, waiting for transfers between devices: 25.1 us -> 9.25 us  [sum_pieces(): lax.all_to_all(jnp.where(mine, 0.0, pieces).astype(jnp.bfloat16), axis, 0...]
    all_to_all x2 -> x1, starting transfers between devices: 13.8 us -> 4.14 us  [sum_pieces(): lax.all_to_all(jnp.where(mine, 0.0, pieces).astype(jnp.bfloat16), axis, 0...]
    all_gather x1, blocking collectives: 25.2 us -> 22.9 us  [per_device(): poly = lax.all_gather(poly, COL, axis=0, tiled=True)]
    all_to_all x2, waiting for transfers between devices: 9.1 us -> 11.3 us  [spread(): lax.all_to_all(jnp.broadcast_to(block[None], (8,) + block.shape), axis, 0...]
    dot_general x2 -> x3, matrix products: 3.79 us -> 3.88 us  [dot_nt(): lax.dot_general(a, b, (((1,), (1,)), ((), ())), preferred_element_type=jn...]
  transfers between devices with their start and end apart: 5 -> 4, of which waited for: 5 -> 4; matrix products, arithmetic and copies ran while one was open for 1% -> 0% of each run, Pallas kernels for 0% -> 0%
where the time goes in v15:
time: 180 us; the launch traced here: 179 us
  blocking collectives  120 us (67%)
  waiting for transfers between devices  23.3 us (13%)
  starting transfers between devices  23.2 us (13%)
  matrix products  4.86 us (3%)
  other arithmetic  4.8 us (3%)
  local copies, waits for them, and re-layouts  2.93 us (2%)
    all_to_all x2, blocking collectives, sum_pieces(): lax.all_to_all(jnp.where(mine, 0.0, pieces).astype(jnp.bfloat16), axis, 0...  52 us
    all_gather x2, blocking collectives, per_device(): by_lo = [lax.all_gather(pair[y], 'x', axis=0, tiled=True) for y in range(2)]  23.9 us
    all_gather x1, blocking collectives, per_device(): poly = lax.all_gather(poly, COL, axis=0, tiled=True)  22.9 us
    all_to_all x2, starting transfers between devices, spread(): lax.all_to_all(jnp.broadcast_to(block[None], (8,) + block.shape), axis, 0...  15 us
    all_gather x1, blocking collectives, per_device(): left = lax.all_gather(rounded, COL, axis=0, tiled=True)  14.9 us
    all_to_all x2, waiting for transfers between devices, spread(): lax.all_to_all(jnp.broadcast_to(block[None], (8,) + block.shape), axis, 0...  11.3 us
    all_to_all x1, waiting for transfers between devices, sum_pieces(): lax.all_to_all(jnp.where(mine, 0.0, pieces).astype(jnp.bfloat16), axis, 0...  9.25 us
    all_gather x1, blocking collectives, per_device(): pair = lax.all_gather(xb, 'y_lo', axis=0)  6.12 us
  transfers between devices with their start and end apart: 4, of which 4 were waited for; matrix products, arithmetic and copies ran while one was open for 0% of the time, Pallas kernels for 0%

profile of v15, /device:TPU:1, one launch (start us, length us, event | category | flops | bytes accessed | tf_op | source)
XLA Modules:
  0.0 179.2 jit_solution(12325414516044049065)
XLA Ops:
  0.0 1.0 convert_element_type.33
  1.0 1.3 broadcast_in_dim.70
  2.3 10.9 %all-to-all-start = ((bf16[8,64,1536]{2,1,0:T(8,128)(2,1)}), bf16[8,64,1536]{2,1,0:T(8,128)(2,1)S(1)}, u32[]{:S(2)}, u32[]{:S(2)}) async-start(bf16[8,64,1536]{2,1,0:T(8,128)(2,1)} %broadcast_in_dim.70), calls=%async_computation | async-start | bytes 3145728 | tf_op jit(solution)/shard_map/all_to_all | solution.py:40
  13.2 6.1 %all-gather = bf16[128,1536]{1,0:T(8,128)(2,1)S(1)} all-gather(bf16[64,1536]{1,0:T(8,128)(2,1)S(1)} %convert_element_type.33), channel_id=2, replica_groups=mesh['y_lo'=2,'z'=8,'x'=4,'y_hi'=4,'core'=2] {'y_lo'}, dimensions={0}, use_global_device_ids=true | all-gather | bytes 589824 | tf_op jit(solution)/shard_map/all_gather | solution.py:55
  19.3 12.6 %all-gather.3 = bf16[256,1536]{1,0:T(8,128)(2,1)S(1)} all-gather(bf16[64,1536]{1,0:T(8,128)(2,1)S(1)} %get-tuple-element.5), channel_id=5, replica_groups=mesh['y_lo'=2,'z'=8,'x'=4,'y_hi'=4,'core'=2] {'x'}, dimensions={0}, use_global_device_ids=true | all-gather | bytes 983040 | tf_op jit(solution)/shard_map/all_gather | solution.py:56
  32.0 11.3 %all-gather.4 = bf16[256,1536]{1,0:T(8,128)(2,1)S(1)} all-gather(bf16[64,1536]{1,0:T(8,128)(2,1)S(1)} %get-tuple-element.6), channel_id=6, replica_groups=mesh['y_lo'=2,'z'=8,'x'=4,'y_hi'=4,'core'=2] {'x'}, dimensions={0}, use_global_device_ids=true | all-gather | bytes 983040 | tf_op jit(solution)/shard_map/all_gather | solution.py:56
  43.3 8.2 %all-to-all-done = bf16[8,64,1536]{2,1,0:T(8,128)(2,1)S(1)} async-done(((bf16[8,64,1536]{2,1,0:T(8,128)(2,1)}), bf16[8,64,1536]{2,1,0:T(8,128)(2,1)S(1)}, u32[]{:S(2)}, u32[]{:S(2)}) %all-to-all-start) | async-done | bytes 1572896 | tf_op jit(solution)/shard_map/all_to_all | solution.py:40
  51.4 0.6 fusion.11
  52.0 0.6 fusion.10
  52.6 0.1 maximum_multiply_fusion
  52.8 0.2 select_convert_fusion.2
  52.9 25.4 %all_to_all.25 = bf16[8,64,512]{2,1,0:T(8,128)(2,1)S(1)} all-to-all(bf16[8,64,512]{2,1,0:T(8,128)(2,1)S(1)} %select_convert_fusion.2), channel_id=1, replica_groups=mesh['y_lo'=2,'z'=8,'x'=4,'y_hi'=4,'core'=2] {'core','y_hi'}, dimensions={0} | all-to-all | bytes 1048576 | tf_op jit(solution)/shard_map/all_to_all | solution.py:46
  78.4 0.1 convert_reduce_fusion.2
  78.5 0.8 broadcast_in_dim.74
  79.3 4.1 %all-to-all-start.2 = ((bf16[8,64,512]{2,1,0:T(8,128)(2,1)}), bf16[8,64,512]{2,1,0:T(8,128)(2,1)}, u32[]{:S(2)}, u32[]{:S(2)}) async-start(bf16[8,64,512]{2,1,0:T(8,128)(2,1)} %broadcast_in_dim.74), calls=%async_computation.2 | async-start | bytes 1048576 | tf_op jit(solution)/shard_map/all_to_all | solution.py:40
  83.5 14.9 %all_gather.22 = bf16[512,512]{1,0:T(8,128)(2,1)S(1)} all-gather(bf16[64,512]{1,0:T(8,128)(2,1)S(1)} %fusion.8), channel_id=1, replica_groups=mesh['y_lo'=2,'z'=8,'x'=4,'y_hi'=4,'core'=2] {'y_hi','core'}, dimensions={0}, use_global_device_ids=true | all-gather | bytes 589824 | tf_op jit(solution)/shard_map/all_gather | solution.py:62
  98.4 3.1 %all-to-all-done.2 = bf16[8,64,512]{2,1,0:T(8,128)(2,1)} async-done(((bf16[8,64,512]{2,1,0:T(8,128)(2,1)}), bf16[8,64,512]{2,1,0:T(8,128)(2,1)}, u32[]{:S(2)}, u32[]{:S(2)}) %all-to-all-start.2) | async-done | bytes 524320 | tf_op jit(solution)/shard_map/all_to_all | solution.py:40
  101.5 2.7 %select_convert_fusion.1 = (bf16[8,64,512]{2,1,0:T(8,128)(2,1)}, f32[8,64,512]{2,1,0:T(8,128)}) fusion(pred[8]{0:T(512)(128)(4,1)S(1)} %iota_compare_fusion.1, bf16[8,64,512]{2,1,0:T(8,128)(2,1)S(1)} %bitcast.45, bf16[512,512,1]{1,0,2:T(8,128)(2,1)} %bitcast.7), kind=kOutput, calls=%fused_computation.4 | convolution fusion | flops 268697600 | bytes 2621448 | tf_op jit(solution)/shard_map/dot_general | solution.py:19
  104.2 4.1 %all-to-all-start.3 = ((bf16[8,64,512]{2,1,0:T(8,128)(2,1)}), bf16[8,64,512]{2,1,0:T(8,128)(2,1)}, u32[]{:S(2)}, u32[]{:S(2)}) async-start(bf16[8,64,512]{2,1,0:T(8,128)(2,1)} %get-tuple-element.7), calls=%async_computation.3 | async-start | bytes 1048576 | tf_op jit(solution)/shard_map/all_to_all | solution.py:46
  108.4 9.3 %all-to-all-done.3 = bf16[8,64,512]{2,1,0:T(8,128)(2,1)} async-done(((bf16[8,64,512]{2,1,0:T(8,128)(2,1)}), bf16[8,64,512]{2,1,0:T(8,128)(2,1)}, u32[]{:S(2)}, u32[]{:S(2)}) %all-to-all-start.3) | async-done | bytes 524320 | tf_op jit(solution)/shard_map/all_to_all | solution.py:46
  117.6 1.1 convert_reduce_fusion.1
  118.8 0.9 bitcast_add_fusion.1
  119.7 4.1 %collective-permute-start = (f32[72,512]{1,0:T(8,128)S(1)}, f32[72,512]{1,0:T(8,128)S(1)}, u32[]{:S(2)}, u32[]{:S(2)}) collective-permute-start(f32[72,512]{1,0:T(8,128)S(1)} %pad_maximum_fusion), channel_id=1, source_target_pairs={{0,0},{1,256},{2,8},{3,264},{4,16},{5,272},{6,24},{7,280},{8,2},{9... | collective-permute-start | bytes 442376 | tf_op jit(solution)/shard_map/ppermute | solution.py:36
  123.8 2.8 %collective-permute-done = f32[72,512]{1,0:T(8,128)S(1)} collective-permute-done((f32[72,512]{1,0:T(8,128)S(1)}, f32[72,512]{1,0:T(8,128)S(1)}, u32[]{:S(2)}, u32[]{:S(2)}) %collective-permute-start) | collective-permute-done | bytes 147488 | tf_op jit(solution)/shard_map/ppermute | solution.py:36
  126.6 0.1 select_reduce_fusion
  126.8 0.1 fusion.5
  126.9 22.9 %all_gather.23 = bf16[512,512]{1,0:T(8,128)(2,1)S(1)} all-gather(bf16[64,512]{1,0:T(8,128)(2,1)S(1)} %fusion.5), channel_id=1, replica_groups=mesh['y_lo'=2,'z'=8,'x'=4,'y_hi'=4,'core'=2] {'y_hi','core'}, dimensions={0}, use_global_device_ids=true | all-gather | bytes 589824 | tf_op jit(solution)/shard_map/all_gather | solution.py:76
  149.8 1.0 select_convert_fusion
  150.8 26.6 %all_to_all.26 = bf16[8,64,1536]{2,1,0:T(8,128)(2,1)S(1)} all-to-all(bf16[8,64,1536]{2,1,0:T(8,128)(2,1)S(1)} %get-tuple-element.9), channel_id=1, replica_groups=mesh['y_lo'=2,'z'=8,'x'=4,'y_hi'=4,'core'=2] {'x','y_lo'}, dimensions={0} | all-to-all | bytes 3145728 | tf_op jit(solution)/shard_map/all_to_all | solution.py:46
  177.4 0.0 copy-start
  177.4 0.2 convert_reduce_fusion
  177.6 0.8 copy-done
  178.4 0.8 fusion
  (11 shorter events, 0.2 us)
Async XLA Ops:
  2.3 49.1 %all-to-all-start = ((bf16[8,64,1536]{2,1,0:T(8,128)(2,1)}), bf16[8,64,1536]{2,1,0:T(8,128)(2,1)S(1)}, u32[]{:S(2)}, u32[]{:S(2)}) async-start(bf16[8,64,1536]{2,1,0:T(8,128)(2,1)} %broadcast_in_dim.70), calls=%async_computation | async-start | bytes 3145728 | tf_op jit(solution)/shard_map/all_to_all | solution.py:40
  79.3 22.2 %all-to-all-start.2 = ((bf16[8,64,512]{2,1,0:T(8,128)(2,1)}), bf16[8,64,512]{2,1,0:T(8,128)(2,1)}, u32[]{:S(2)}, u32[]{:S(2)}) async-start(bf16[8,64,512]{2,1,0:T(8,128)(2,1)} %broadcast_in_dim.74), calls=%async_computation.2 | async-start | bytes 1048576 | tf_op jit(solution)/shard_map/all_to_all | solution.py:40
  104.2 13.5 %all-to-all-start.3 = ((bf16[8,64,512]{2,1,0:T(8,128)(2,1)}), bf16[8,64,512]{2,1,0:T(8,128)(2,1)}, u32[]{:S(2)}, u32[]{:S(2)}) async-start(bf16[8,64,512]{2,1,0:T(8,128)(2,1)} %get-tuple-element.7), calls=%async_computation.3 | async-start | bytes 1048576 | tf_op jit(solution)/shard_map/all_to_all | solution.py:46
  119.7 6.9 %collective-permute-start = (f32[72,512]{1,0:T(8,128)S(1)}, f32[72,512]{1,0:T(8,128)S(1)}, u32[]{:S(2)}, u32[]{:S(2)}) collective-permute-start(f32[72,512]{1,0:T(8,128)S(1)} %pad_maximum_fusion), channel_id=1, source_target_pairs={{0,0},{1,256},{2,8},{3,264},{4,16},{5,272},{6,24},{7,280},{8,2},{9... | collective-permute-start | bytes 442376 | tf_op jit(solution)/shard_map/ppermute | solution.py:36
  177.4 1.0 copy-start

commit v16 on v13

--- a/solution.py
+++ b/solution.py
@@ -1,6 +1,7 @@
 import jax
 import jax.numpy as jnp
 from jax import lax
+from jax.experimental import pallas as pl
 from jax.sharding import Mesh, PartitionSpec as P
 
 N = 12288
@@ -28,6 +29,26 @@
     return lax.ppermute(block, ("x", "y_hi", "core"), pairs)
 
 
+def round_and_copy(x, count):
+    def body(x_ref, one_ref, copies_ref):
+        block = x_ref[...].astype(jnp.bfloat16)
+        one_ref[...] = block
+        copies_ref[0] = block
+
+    rows, cols = x.shape
+    whole = pl.BlockSpec((rows, cols), lambda i: (0, 0))
+    return pl.pallas_call(
+        body,
+        grid=(count,),
+        in_specs=[whole],
+        out_specs=[whole, pl.BlockSpec((1, rows, cols), lambda i: (i, 0, 0))],
+        out_shape=[
+            jax.ShapeDtypeStruct((rows, cols), jnp.bfloat16),
+            jax.ShapeDtypeStruct((count, rows, cols), jnp.bfloat16),
+        ],
+    )(x)
+
+
 def spread(block, axis):
     return lax.all_to_all(jnp.broadcast_to(block[None], (8,) + block.shape), axis, 0, 0)
 
@@ -42,8 +63,8 @@
 
 def per_device(x_scaled):
     rows, cols = x_scaled.shape
-    xb = x_scaled.astype(jnp.bfloat16)
-    by_hi = spread(xb, "z").reshape(8 * rows, cols)
+    xb, copies = round_and_copy(x_scaled, 8)
+    by_hi = lax.all_to_all(copies, "z", 0, 0).reshape(8 * rows, cols)
     pair = lax.all_gather(xb, "y_lo", axis=0)
     by_lo = [lax.all_gather(pair[y], "x", axis=0, tiled=True) for y in range(2)]
 

time: 174 us -> 176 us (1.011)
  Pallas kernels: 0 us -> 3.95 us
    all_to_all x0 -> x1, starting transfers between devices: none -> 11 us  [per_device(): by_hi = lax.all_to_all(copies, 'z', 0, 0).reshape(8 * rows, cols)]
    all_to_all x2 -> x1, starting transfers between devices: 14.4 us -> 3.49 us  [spread(): lax.all_to_all(jnp.broadcast_to(block[None], (8,) + block.shape), axis, 0...]
    all_to_all x2 -> x1, waiting for transfers between devices: 21.1 us -> 12.9 us  [spread(): lax.all_to_all(jnp.broadcast_to(block[None], (8,) + block.shape), axis, 0...]
    all_to_all x0 -> x1, waiting for transfers between devices: none -> 8.16 us  [per_device(): by_hi = lax.all_to_all(copies, 'z', 0, 0).reshape(8 * rows, cols)]
    pallas_call x0 -> x1, Pallas kernels: none -> 3.95 us  [round_and_copy(): pl.pallas_call(body, grid=(count,), in_specs=[whole], out_specs=[whole, p...]
where the time goes in v16:
time: 176 us
  blocking collectives  115 us (65%)
  waiting for transfers between devices  28.1 us (16%)
  starting transfers between devices  20.9 us (12%)
  Pallas kernels  3.95 us (2%)
  other arithmetic  3.4 us (2%)
  matrix products  2.77 us (2%)
  local copies, waits for them, and re-layouts  1.77 us (1%)
    all_to_all x2, blocking collectives, sum_pieces(): lax.all_to_all(jnp.where(mine, 0.0, pieces).astype(jnp.bfloat16), axis, 0...  49.8 us
    all_gather x2, blocking collectives, per_device(): by_lo = [lax.all_gather(pair[y], 'x', axis=0, tiled=True) for y in range(2)]  23.9 us
    all_gather x1, blocking collectives, per_device(): poly = lax.all_gather(poly, COL, axis=0, tiled=True)  19.5 us
    all_to_all x1, waiting for transfers between devices, spread(): lax.all_to_all(jnp.broadcast_to(block[None], (8,) + block.shape), axis, 0...  12.9 us
    all_to_all x1, starting transfers between devices, per_device(): by_hi = lax.all_to_all(copies, 'z', 0, 0).reshape(8 * rows, cols)  11 us
    all_gather x1, blocking collectives, per_device(): left = lax.all_gather(left, 'x', axis=0).reshape(4, 2, rows, 8 * rows)  10.9 us
    all_to_all x1, waiting for transfers between devices, per_device(): by_hi = lax.all_to_all(copies, 'z', 0, 0).reshape(8 * rows, cols)  8.16 us
    all_to_all x1, waiting for transfers between devices, sum_pieces(): lax.all_to_all(jnp.where(mine, 0.0, pieces).astype(jnp.bfloat16), axis, 0...  7.02 us
  transfers between devices with their start and end apart: 5, of which 3 were waited for; matrix products, arithmetic and copies ran while one was open for 1% of the time, Pallas kernels for 0%

profile of v16, /device:TPU:1, one launch (start us, length us, event | category | flops | bytes accessed | tf_op | source)
XLA Modules:
  0.0 175.7 jit_solution(3461562604622161796)
XLA Ops:
  0.0 4.0 %shard_map.17 = (bf16[64,1536]{1,0:T(8,128)(2,1)}, bf16[8,64,1536]{2,1,0:T(8,128)(2,1)}) custom-call(f32[64,1536]{1,0:T(8,128)} %x_ref.1), custom_call_target="tpu_custom_call" | custom-call | tf_op jit(solution)/shard_map/pallas_call | solution.py:40
  4.0 0.0 copy-start.2
  4.0 11.0 %all-to-all-start = ((bf16[8,64,1536]{2,1,0:T(8,128)(2,1)}), bf16[8,64,1536]{2,1,0:T(8,128)(2,1)S(1)}, u32[]{:S(2)}, u32[]{:S(2)}) async-start(bf16[8,64,1536]{2,1,0:T(8,128)(2,1)} %get-tuple-element.8), calls=%async_computation | async-start | bytes 3145728 | tf_op jit(solution)/shard_map/all_to_all | solution.py:67
  15.0 0.0 copy-done.2
  15.0 6.1 %all-gather = bf16[128,1536]{1,0:T(8,128)(2,1)S(1)} all-gather(bf16[64,1536]{1,0:T(8,128)(2,1)S(1)} %copy-done.2), channel_id=2, replica_groups=mesh['y_lo'=2,'z'=8,'x'=4,'y_hi'=4,'core'=2] {'y_lo'}, dimensions={0}, use_global_device_ids=true | all-gather | bytes 589824 | tf_op jit(solution)/shard_map/all_gather | solution.py:68
  21.1 12.6 %all-gather.5 = bf16[256,1536]{1,0:T(8,128)(2,1)S(1)} all-gather(bf16[64,1536]{1,0:T(8,128)(2,1)S(1)} %get-tuple-element.11), channel_id=7, replica_groups=mesh['y_lo'=2,'z'=8,'x'=4,'y_hi'=4,'core'=2] {'x'}, dimensions={0}, use_global_device_ids=true | all-gather | bytes 983040 | tf_op jit(solution)/shard_map/all_gather | solution.py:69
  33.8 11.3 %all-gather.6 = bf16[256,1536]{1,0:T(8,128)(2,1)S(1)} all-gather(bf16[64,1536]{1,0:T(8,128)(2,1)S(1)} %get-tuple-element.12), channel_id=8, replica_groups=mesh['y_lo'=2,'z'=8,'x'=4,'y_hi'=4,'core'=2] {'x'}, dimensions={0}, use_global_device_ids=true | all-gather | bytes 983040 | tf_op jit(solution)/shard_map/all_gather | solution.py:69
  45.1 8.2 %all-to-all-done = bf16[8,64,1536]{2,1,0:T(8,128)(2,1)S(1)} async-done(((bf16[8,64,1536]{2,1,0:T(8,128)(2,1)}), bf16[8,64,1536]{2,1,0:T(8,128)(2,1)S(1)}, u32[]{:S(2)}, u32[]{:S(2)}) %all-to-all-start) | async-done | bytes 1572896 | tf_op jit(solution)/shard_map/all_to_all | solution.py:67
  53.2 0.6 fusion.11
  53.8 0.6 fusion.12
  54.4 0.1 maximum_multiply_fusion
  54.6 0.2 select_convert_fusion.1
  54.7 25.4 %all_to_all.25 = bf16[8,64,512]{2,1,0:T(8,128)(2,1)S(1)} all-to-all(bf16[8,64,512]{2,1,0:T(8,128)(2,1)S(1)} %select_convert_fusion.1), channel_id=1, replica_groups=mesh['y_lo'=2,'z'=8,'x'=4,'y_hi'=4,'core'=2] {'core','y_hi'}, dimensions={0} | all-to-all | bytes 1048576 | tf_op jit(solution)/shard_map/all_to_all | solution.py:59
  80.1 0.1 convert_reduce_fusion.1
  80.2 0.8 broadcast_in_dim.55
  81.1 3.5 %all-to-all-start.2 = ((bf16[8,64,512]{2,1,0:T(8,128)(2,1)}), bf16[8,64,512]{2,1,0:T(8,128)(2,1)S(1)}, u32[]{:S(2)}, u32[]{:S(2)}) async-start(bf16[8,64,512]{2,1,0:T(8,128)(2,1)} %broadcast_in_dim.55), calls=%async_computation.2 | async-start | bytes 1048576 | tf_op jit(solution)/shard_map/all_to_all | solution.py:53
  84.6 0.7 collective-permute-start
  85.3 0.0 collective-permute-done
  85.3 4.3 %all-gather.3 = bf16[128,512]{1,0:T(8,128)(2,1)S(1)} all-gather(bf16[64,512]{1,0:T(8,128)(2,1)S(1)} %collective-permute-done), channel_id=5, replica_groups=mesh['y_lo'=2,'z'=8,'x'=4,'y_hi'=4,'core'=2] {'y_lo'}, dimensions={0}, use_global_device_ids=true | all-gather | bytes 196608 | tf_op jit(solution)/shard_map/all_gather | solution.py:77
  89.7 12.9 %all-to-all-done.2 = bf16[8,64,512]{2,1,0:T(8,128)(2,1)S(1)} async-done(((bf16[8,64,512]{2,1,0:T(8,128)(2,1)}), bf16[8,64,512]{2,1,0:T(8,128)(2,1)S(1)}, u32[]{:S(2)}, u32[]{:S(2)}) %all-to-all-start.2) | async-done | bytes 524320 | tf_op jit(solution)/shard_map/all_to_all | solution.py:53
  102.5 2.3 %collective-permute-start.1 = (bf16[512,512]{1,0:T(8,128)(2,1)S(1)}, bf16[512,512]{1,0:T(8,128)(2,1)S(1)}, u32[]{:S(2)}, u32[]{:S(2)}) collective-permute-start(bf16[512,512]{1,0:T(8,128)(2,1)S(1)} %bitcast.57), channel_id=1, source_target_pairs={{0,1},{1,0},{2,3},{3,2},{4,5},{5,4},{6,7},{7,6},{8,9},{9,8},{10,11... | collective-permute-start | bytes 1572872 | tf_op jit(solution)/shard_map/ppermute | solution.py:76
  104.9 10.9 %all-gather.4 = bf16[8,64,512]{2,1,0:T(8,128)(2,1)S(1)} all-gather(bf16[2,64,512]{2,1,0:T(8,128)(2,1)S(1)} %bitcast.62), channel_id=6, replica_groups=mesh['y_lo'=2,'z'=8,'x'=4,'y_hi'=4,'core'=2] {'x'}, dimensions={0}, use_global_device_ids=true | all-gather | bytes 655360 | tf_op jit(solution)/shard_map/all_gather | solution.py:78
  115.8 0.0 copy-start
  115.8 0.3 fusion.13
  116.1 0.0 collective-permute-done.1
  116.2 0.3 convolution_add_fusion
  116.5 0.1 copy-done
  116.6 0.8 select_convert_fusion.2
  117.4 3.4 %all-to-all-start.3 = ((bf16[4,64,512]{2,1,0:T(8,128)(2,1)}), bf16[4,64,512]{2,1,0:T(8,128)(2,1)S(1)}, u32[]{:S(2)}, u32[]{:S(2)}) async-start(bf16[4,64,512]{2,1,0:T(8,128)(2,1)} %select_convert_fusion.2), calls=%async_computation.3 | async-start | bytes 524288 | tf_op jit(solution)/shard_map/all_to_all | solution.py:59
  120.8 1.0 fusion.6
  121.8 7.0 %all-to-all-done.3 = bf16[4,64,512]{2,1,0:T(8,128)(2,1)S(1)} async-done(((bf16[4,64,512]{2,1,0:T(8,128)(2,1)}), bf16[4,64,512]{2,1,0:T(8,128)(2,1)S(1)}, u32[]{:S(2)}, u32[]{:S(2)}) %all-to-all-start.3) | async-done | bytes 262176 | tf_op jit(solution)/shard_map/all_to_all | solution.py:59
  128.9 0.1 fusion.5
  129.0 19.5 %all_gather.35 = bf16[512,512]{1,0:T(8,128)(2,1)S(1)} all-gather(bf16[64,512]{1,0:T(8,128)(2,1)S(1)} %fusion.5), channel_id=1, replica_groups=mesh['y_lo'=2,'z'=8,'x'=4,'y_hi'=4,'core'=2] {'y_hi','core'}, dimensions={0}, use_global_device_ids=true | all-gather | bytes 589824 | tf_op jit(solution)/shard_map/all_gather | solution.py:95
  148.5 1.0 select_convert_fusion
  149.5 24.4 %all_to_all.26 = bf16[8,64,1536]{2,1,0:T(8,128)(2,1)S(1)} all-to-all(bf16[8,64,1536]{2,1,0:T(8,128)(2,1)S(1)} %get-tuple-element.13), channel_id=1, replica_groups=mesh['y_lo'=2,'z'=8,'x'=4,'y_hi'=4,'core'=2] {'x','y_lo'}, dimensions={0} | all-to-all | bytes 3145728 | tf_op jit(solution)/shard_map/all_to_all | solution.py:59
  173.8 0.0 copy-start.1
  173.8 0.2 convert_reduce_fusion
  174.1 0.8 copy-done.1
  174.8 0.8 fusion
  (10 shorter events, 0.2 us)
Async XLA Ops:
  4.0 11.0 %copy-start.2 = (bf16[64,1536]{1,0:T(8,128)(2,1)S(1)}, bf16[64,1536]{1,0:T(8,128)(2,1)}, u32[]{:S(2)}) copy-start(bf16[64,1536]{1,0:T(8,128)(2,1)} %get-tuple-element.7) | copy-start | bytes 589828
  4.0 49.3 %all-to-all-start = ((bf16[8,64,1536]{2,1,0:T(8,128)(2,1)}), bf16[8,64,1536]{2,1,0:T(8,128)(2,1)S(1)}, u32[]{:S(2)}, u32[]{:S(2)}) async-start(bf16[8,64,1536]{2,1,0:T(8,128)(2,1)} %get-tuple-element.8), calls=%async_computation | async-start | bytes 3145728 | tf_op jit(solution)/shard_map/all_to_all | solution.py:67
  81.1 21.5 %all-to-all-start.2 = ((bf16[8,64,512]{2,1,0:T(8,128)(2,1)}), bf16[8,64,512]{2,1,0:T(8,128)(2,1)S(1)}, u32[]{:S(2)}, u32[]{:S(2)}) async-start(bf16[8,64,512]{2,1,0:T(8,128)(2,1)} %broadcast_in_dim.55), calls=%async_computation.2 | async-start | bytes 1048576 | tf_op jit(solution)/shard_map/all_to_all | solution.py:53
  84.6 0.7 collective-permute-start
  102.5 13.6 %collective-permute-start.1 = (bf16[512,512]{1,0:T(8,128)(2,1)S(1)}, bf16[512,512]{1,0:T(8,128)(2,1)S(1)}, u32[]{:S(2)}, u32[]{:S(2)}) collective-permute-start(bf16[512,512]{1,0:T(8,128)(2,1)S(1)} %bitcast.57), channel_id=1, source_target_pairs={{0,1},{1,0},{2,3},{3,2},{4,5},{5,4},{6,7},{7,6},{8,9},{9,8},{10,11... | collective-permute-start | bytes 1572872 | tf_op jit(solution)/shard_map/ppermute | solution.py:76
  115.8 0.8 copy-start
  117.4 11.4 %all-to-all-start.3 = ((bf16[4,64,512]{2,1,0:T(8,128)(2,1)}), bf16[4,64,512]{2,1,0:T(8,128)(2,1)S(1)}, u32[]{:S(2)}, u32[]{:S(2)}) async-start(bf16[4,64,512]{2,1,0:T(8,128)(2,1)} %select_convert_fusion.2), calls=%async_computation.3 | async-start | bytes 524288 | tf_op jit(solution)/shard_map/all_to_all | solution.py:59
  173.8 1.0 copy-start.1

commit v17 on v13

--- a/solution.py
+++ b/solution.py
@@ -43,6 +43,7 @@
 def per_device(x_scaled):
     rows, cols = x_scaled.shape
     xb = x_scaled.astype(jnp.bfloat16)
+    linear = lax.optimization_barrier(coef_linear * x_scaled)
     by_hi = spread(xb, "z").reshape(8 * rows, cols)
     pair = lax.all_gather(xb, "y_lo", axis=0)
     by_lo = [lax.all_gather(pair[y], "x", axis=0, tiled=True) for y in range(2)]
@@ -73,7 +74,7 @@
     poly = (coef_cubic * gram + coef_quintic * square).astype(jnp.bfloat16)
     poly = lax.all_gather(poly, COL, axis=0, tiled=True)
     product = jnp.dot(poly, by_hi, preferred_element_type=jnp.float32)
-    return coef_linear * x_scaled + sum_pieces(product.reshape(8, rows, cols), LO)
+    return linear + sum_pieces(product.reshape(8, rows, cols), LO)
 
 
 def solution(mesh):

time: 174 us -> 178 us (1.023)
  blocking collectives: 115 us -> 90.2 us
  waiting for transfers between devices: 28.1 us -> 49.1 us
  starting transfers between devices: 20.8 us -> 24.4 us
  matrix products: 2.77 us -> 4.89 us
  other arithmetic: 4.42 us -> 6.37 us
    all_to_all x2 -> x1, blocking collectives: 49.7 us -> 25.4 us  [sum_pieces(): lax.all_to_all(jnp.where(mine, 0.0, pieces).astype(jnp.bfloat16), axis, 0...]
    all_to_all x1 -> x2, waiting for transfers between devices: 7.01 us -> 28 us  [sum_pieces(): lax.all_to_all(jnp.where(mine, 0.0, pieces).astype(jnp.bfloat16), axis, 0...]
    all_to_all x1 -> x2, starting transfers between devices: 3.41 us -> 7.02 us  [sum_pieces(): lax.all_to_all(jnp.where(mine, 0.0, pieces).astype(jnp.bfloat16), axis, 0...]
    dot_general x1, matrix products: 0.98 us -> 3.1 us  [per_device(): product = jnp.dot(poly, by_hi, preferred_element_type=jnp.float32)]
  transfers between devices with their start and end apart: 5 -> 6, of which waited for: 3 -> 4; matrix products, arithmetic and copies ran while one was open for 1% -> 1% of each run, Pallas kernels for 0% -> 0%
where the time goes in v17:
time: 178 us; the launch traced here: 177 us
  blocking collectives  90.2 us (51%)
  waiting for transfers between devices  49.1 us (28%)
  starting transfers between devices  24.4 us (14%)
  other arithmetic  6.37 us (4%)
  matrix products  4.89 us (3%)
  local copies, waits for them, and re-layouts  2.3 us (1%)
    all_to_all x2, waiting for transfers between devices, sum_pieces(): lax.all_to_all(jnp.where(mine, 0.0, pieces).astype(jnp.bfloat16), axis, 0...  28 us
    all_to_all x1, blocking collectives, sum_pieces(): lax.all_to_all(jnp.where(mine, 0.0, pieces).astype(jnp.bfloat16), axis, 0...  25.4 us
    all_gather x2, blocking collectives, per_device(): by_lo = [lax.all_gather(pair[y], 'x', axis=0, tiled=True) for y in range(2)]  23.9 us
    all_to_all x2, waiting for transfers between devices, spread(): lax.all_to_all(jnp.broadcast_to(block[None], (8,) + block.shape), axis, 0...  21.1 us
    all_gather x1, blocking collectives, per_device(): poly = lax.all_gather(poly, COL, axis=0, tiled=True)  19.5 us
    all_to_all x2, starting transfers between devices, spread(): lax.all_to_all(jnp.broadcast_to(block[None], (8,) + block.shape), axis, 0...  14.4 us
    all_gather x1, blocking collectives, per_device(): left = lax.all_gather(left, 'x', axis=0).reshape(4, 2, rows, 8 * rows)  10.9 us
    all_to_all x2, starting transfers between devices, sum_pieces(): lax.all_to_all(jnp.where(mine, 0.0, pieces).astype(jnp.bfloat16), axis, 0...  7.02 us
  transfers between devices with their start and end apart: 6, of which 4 were waited for; matrix products, arithmetic and copies ran while one was open for 1% of the time, Pallas kernels for 0%

profile of v17, /device:TPU:1, one launch (start us, length us, event | category | flops | bytes accessed | tf_op | source)
XLA Modules:
  0.0 177.4 jit_solution(10814328634938556736)
XLA Ops:
  0.0 2.0 %fusion.11 = (bf16[64,1536]{1,0:T(8,128)(2,1)S(1)}, f32[64,1536]{1,0:T(8,128)}) fusion(f32[64,1536]{1,0:T(8,128)} %param.1), kind=kLoop, calls=%fused_computation.34 | loop fusion | flops 196608 | bytes 983040 | tf_op jit(solution)/shard_map/convert_element_type | solution.py:45
  2.0 1.3 broadcast_in_dim.58
  3.3 10.9 %all-to-all-start = ((bf16[8,64,1536]{2,1,0:T(8,128)(2,1)}), bf16[8,64,1536]{2,1,0:T(8,128)(2,1)S(1)}, u32[]{:S(2)}, u32[]{:S(2)}) async-start(bf16[8,64,1536]{2,1,0:T(8,128)(2,1)} %broadcast_in_dim.58), calls=%async_computation | async-start | bytes 3145728 | tf_op jit(solution)/shard_map/all_to_all | solution.py:32
  14.2 6.1 %all-gather = bf16[128,1536]{1,0:T(8,128)(2,1)S(1)} all-gather(bf16[64,1536]{1,0:T(8,128)(2,1)S(1)} %get-tuple-element.9), channel_id=2, replica_groups=mesh['y_lo'=2,'z'=8,'x'=4,'y_hi'=4,'core'=2] {'y_lo'}, dimensions={0}, use_global_device_ids=true | all-gather | bytes 589824 | tf_op jit(solution)/shard_map/all_gather | solution.py:48
  20.3 12.6 %all-gather.5 = bf16[256,1536]{1,0:T(8,128)(2,1)S(1)} all-gather(bf16[64,1536]{1,0:T(8,128)(2,1)S(1)} %get-tuple-element.7), channel_id=7, replica_groups=mesh['y_lo'=2,'z'=8,'x'=4,'y_hi'=4,'core'=2] {'x'}, dimensions={0}, use_global_device_ids=true | all-gather | bytes 983040 | tf_op jit(solution)/shard_map/all_gather | solution.py:49
  32.9 11.3 %all-gather.6 = bf16[256,1536]{1,0:T(8,128)(2,1)S(1)} all-gather(bf16[64,1536]{1,0:T(8,128)(2,1)S(1)} %get-tuple-element.8), channel_id=8, replica_groups=mesh['y_lo'=2,'z'=8,'x'=4,'y_hi'=4,'core'=2] {'x'}, dimensions={0}, use_global_device_ids=true | all-gather | bytes 983040 | tf_op jit(solution)/shard_map/all_gather | solution.py:49
  44.2 8.2 %all-to-all-done = bf16[8,64,1536]{2,1,0:T(8,128)(2,1)S(1)} async-done(((bf16[8,64,1536]{2,1,0:T(8,128)(2,1)}), bf16[8,64,1536]{2,1,0:T(8,128)(2,1)S(1)}, u32[]{:S(2)}, u32[]{:S(2)}) %all-to-all-start) | async-done | bytes 1572896 | tf_op jit(solution)/shard_map/all_to_all | solution.py:32
  52.4 0.6 fusion.13
  53.0 0.6 fusion.12
  53.6 0.1 maximum_multiply_fusion
  53.8 0.2 select_convert_fusion.1
  53.9 25.4 %all_to_all.25 = bf16[8,64,512]{2,1,0:T(8,128)(2,1)S(1)} all-to-all(bf16[8,64,512]{2,1,0:T(8,128)(2,1)S(1)} %select_convert_fusion.1), channel_id=1, replica_groups=mesh['y_lo'=2,'z'=8,'x'=4,'y_hi'=4,'core'=2] {'core','y_hi'}, dimensions={0} | all-to-all | bytes 1048576 | tf_op jit(solution)/shard_map/all_to_all | solution.py:38
  79.3 0.1 convert_reduce_fusion.1
  79.4 0.8 broadcast_in_dim.62
  80.3 3.5 %all-to-all-start.2 = ((bf16[8,64,512]{2,1,0:T(8,128)(2,1)}), bf16[8,64,512]{2,1,0:T(8,128)(2,1)S(1)}, u32[]{:S(2)}, u32[]{:S(2)}) async-start(bf16[8,64,512]{2,1,0:T(8,128)(2,1)} %broadcast_in_dim.62), calls=%async_computation.2 | async-start | bytes 1048576 | tf_op jit(solution)/shard_map/all_to_all | solution.py:32
  83.8 0.7 collective-permute-start
  84.5 0.0 collective-permute-done
  84.5 4.3 %all-gather.3 = bf16[128,512]{1,0:T(8,128)(2,1)S(1)} all-gather(bf16[64,512]{1,0:T(8,128)(2,1)S(1)} %collective-permute-done), channel_id=5, replica_groups=mesh['y_lo'=2,'z'=8,'x'=4,'y_hi'=4,'core'=2] {'y_lo'}, dimensions={0}, use_global_device_ids=true | all-gather | bytes 196608 | tf_op jit(solution)/shard_map/all_gather | solution.py:57
  88.9 12.9 %all-to-all-done.2 = bf16[8,64,512]{2,1,0:T(8,128)(2,1)S(1)} async-done(((bf16[8,64,512]{2,1,0:T(8,128)(2,1)}), bf16[8,64,512]{2,1,0:T(8,128)(2,1)S(1)}, u32[]{:S(2)}, u32[]{:S(2)}) %all-to-all-start.2) | async-done | bytes 524320 | tf_op jit(solution)/shard_map/all_to_all | solution.py:32
  101.8 2.3 %collective-permute-start.1 = (bf16[512,512]{1,0:T(8,128)(2,1)S(1)}, bf16[512,512]{1,0:T(8,128)(2,1)S(1)}, u32[]{:S(2)}, u32[]{:S(2)}) collective-permute-start(bf16[512,512]{1,0:T(8,128)(2,1)S(1)} %bitcast.57), channel_id=1, source_target_pairs={{0,1},{1,0},{2,3},{3,2},{4,5},{5,4},{6,7},{7,6},{8,9},{9,8},{10,11... | collective-permute-start | bytes 1572872 | tf_op jit(solution)/shard_map/ppermute | solution.py:56
  104.1 10.9 %all-gather.4 = bf16[8,64,512]{2,1,0:T(8,128)(2,1)S(1)} all-gather(bf16[2,64,512]{2,1,0:T(8,128)(2,1)S(1)} %bitcast.62), channel_id=6, replica_groups=mesh['y_lo'=2,'z'=8,'x'=4,'y_hi'=4,'core'=2] {'x'}, dimensions={0}, use_global_device_ids=true | all-gather | bytes 655360 | tf_op jit(solution)/shard_map/all_gather | solution.py:58
  115.0 0.0 copy-start
  115.0 0.3 fusion.14
  115.4 0.0 collective-permute-done.1
  115.4 0.3 convolution_add_fusion
  115.7 0.1 copy-done
  115.8 0.8 select_convert_fusion.2
  116.6 3.4 %all-to-all-start.3 = ((bf16[4,64,512]{2,1,0:T(8,128)(2,1)}), bf16[4,64,512]{2,1,0:T(8,128)(2,1)S(1)}, u32[]{:S(2)}, u32[]{:S(2)}) async-start(bf16[4,64,512]{2,1,0:T(8,128)(2,1)} %select_convert_fusion.2), calls=%async_computation.3 | async-start | bytes 524288 | tf_op jit(solution)/shard_map/all_to_all | solution.py:38
  120.0 1.0 fusion.6
  121.0 7.0 %all-to-all-done.3 = bf16[4,64,512]{2,1,0:T(8,128)(2,1)S(1)} async-done(((bf16[4,64,512]{2,1,0:T(8,128)(2,1)}), bf16[4,64,512]{2,1,0:T(8,128)(2,1)S(1)}, u32[]{:S(2)}, u32[]{:S(2)}) %all-to-all-start.3) | async-done | bytes 262176 | tf_op jit(solution)/shard_map/all_to_all | solution.py:38
  128.1 0.1 fusion.5
  128.2 19.5 %all_gather.35 = bf16[512,512]{1,0:T(8,128)(2,1)S(1)} all-gather(bf16[64,512]{1,0:T(8,128)(2,1)S(1)} %fusion.5), channel_id=1, replica_groups=mesh['y_lo'=2,'z'=8,'x'=4,'y_hi'=4,'core'=2] {'y_hi','core'}, dimensions={0}, use_global_device_ids=true | all-gather | bytes 589824 | tf_op jit(solution)/shard_map/all_gather | solution.py:75
  147.7 3.1 %select_convert_fusion = (bf16[8,64,1536]{2,1,0:T(8,128)(2,1)}, f32[8,64,1536]{2,1,0:T(8,128)}) fusion(pred[8]{0:T(512)(128)(4,1)S(1)} %iota_compare_fusion.1, bf16[8,64,512]{2,1,0:T(8,128)(2,1)S(1)} %bitcast.59, bf16[512,1536,1]{1,0,2:T(8,128)(2,1)S(1)} %bitcast.48), kind=kOutput, calls=%fused_computation.1 | convolution fusion | flops 806092800 | bytes 6815752 | tf_op jit(solution)/shard_map/dot_general | solution.py:76
  150.8 3.6 %all-to-all-start.4 = ((bf16[8,64,1536]{2,1,0:T(8,128)(2,1)}), bf16[8,64,1536]{2,1,0:T(8,128)(2,1)S(1)}, u32[]{:S(2)}, u32[]{:S(2)}) async-start(bf16[8,64,1536]{2,1,0:T(8,128)(2,1)} %get-tuple-element.11), calls=%async_computation.4 | async-start | bytes 3145728 | tf_op jit(solution)/shard_map/all_to_all | solution.py:38
  154.4 0.0 copy-start.1
  154.4 21.0 %all-to-all-done.4 = bf16[8,64,1536]{2,1,0:T(8,128)(2,1)S(1)} async-done(((bf16[8,64,1536]{2,1,0:T(8,128)(2,1)}), bf16[8,64,1536]{2,1,0:T(8,128)(2,1)S(1)}, u32[]{:S(2)}, u32[]{:S(2)}) %all-to-all-start.4) | async-done | bytes 1572896 | tf_op jit(solution)/shard_map/all_to_all | solution.py:38
  175.4 0.2 convert_reduce_fusion
  175.6 0.0 copy-done.1
  175.6 1.8 %fusion = f32[64,1536]{1,0:T(8,128)} fusion(f32[64,1536]{1,0:T(8,128)S(1)} %copy-done.1, f32[64,1536]{1,0:T(8,128)S(1)} %convert_reduce_fusion, f32[8,64,1536]{2,1,0:T(8,128)} %get-tuple-element.12, s32[]{:T(128)S(6)} %add.37), kind=kLoop, calls=%fused_computation.9 | loop fusion | flops 196608 | bytes 1572868 | tf_op jit(solution)/shard_map/add | solution.py:77
  (10 shorter events, 0.2 us)
Async XLA Ops:
  3.3 49.1 %all-to-all-start = ((bf16[8,64,1536]{2,1,0:T(8,128)(2,1)}), bf16[8,64,1536]{2,1,0:T(8,128)(2,1)S(1)}, u32[]{:S(2)}, u32[]{:S(2)}) async-start(bf16[8,64,1536]{2,1,0:T(8,128)(2,1)} %broadcast_in_dim.58), calls=%async_computation | async-start | bytes 3145728 | tf_op jit(solution)/shard_map/all_to_all | solution.py:32
  80.3 21.5 %all-to-all-start.2 = ((bf16[8,64,512]{2,1,0:T(8,128)(2,1)}), bf16[8,64,512]{2,1,0:T(8,128)(2,1)S(1)}, u32[]{:S(2)}, u32[]{:S(2)}) async-start(bf16[8,64,512]{2,1,0:T(8,128)(2,1)} %broadcast_in_dim.62), calls=%async_computation.2 | async-start | bytes 1048576 | tf_op jit(solution)/shard_map/all_to_all | solution.py:32
  83.8 0.7 collective-permute-start
  101.8 13.6 %collective-permute-start.1 = (bf16[512,512]{1,0:T(8,128)(2,1)S(1)}, bf16[512,512]{1,0:T(8,128)(2,1)S(1)}, u32[]{:S(2)}, u32[]{:S(2)}) collective-permute-start(bf16[512,512]{1,0:T(8,128)(2,1)S(1)} %bitcast.57), channel_id=1, source_target_pairs={{0,1},{1,0},{2,3},{3,2},{4,5},{5,4},{6,7},{7,6},{8,9},{9,8},{10,11... | collective-permute-start | bytes 1572872 | tf_op jit(solution)/shard_map/ppermute | solution.py:56
  115.0 0.8 copy-start
  116.6 11.4 %all-to-all-start.3 = ((bf16[4,64,512]{2,1,0:T(8,128)(2,1)}), bf16[4,64,512]{2,1,0:T(8,128)(2,1)S(1)}, u32[]{:S(2)}, u32[]{:S(2)}) async-start(bf16[4,64,512]{2,1,0:T(8,128)(2,1)} %select_convert_fusion.2), calls=%async_computation.3 | async-start | bytes 524288 | tf_op jit(solution)/shard_map/all_to_all | solution.py:38
  150.8 24.6 %all-to-all-start.4 = ((bf16[8,64,1536]{2,1,0:T(8,128)(2,1)}), bf16[8,64,1536]{2,1,0:T(8,128)(2,1)S(1)}, u32[]{:S(2)}, u32[]{:S(2)}) async-start(bf16[8,64,1536]{2,1,0:T(8,128)(2,1)} %get-tuple-element.11), calls=%async_computation.4 | async-start | bytes 3145728 | tf_op jit(solution)/shard_map/all_to_all | solution.py:38
  154.4 21.2 %copy-start.1 = (f32[64,1536]{1,0:T(8,128)S(1)}, f32[64,1536]{1,0:T(8,128)}, u32[]{:S(2)}) copy-start(f32[64,1536]{1,0:T(8,128)} %get-tuple-element.10) | copy-start | bytes 1179652

commit v18 on v13

--- a/solution.py
+++ b/solution.py
@@ -29,7 +29,8 @@
 
 
 def spread(block, axis):
-    return lax.all_to_all(jnp.broadcast_to(block[None], (8,) + block.shape), axis, 0, 0)
+    count = lax.axis_size(axis)
+    return lax.all_to_all(jnp.broadcast_to(block[None], (count,) + block.shape), axis, 0, 0)
 
 
 def sum_pieces(pieces, axis):
@@ -54,7 +55,7 @@
     right = spread(rounded, "z").reshape(8 * rows, 8 * rows)
     right_other = lax.ppermute(right, "core", [(0, 1), (1, 0)])
     left = lax.all_gather(swap_x_y_hi(rounded), "y_lo", axis=0)
-    left = lax.all_gather(left, "x", axis=0).reshape(4, 2, rows, 8 * rows)
+    left = spread(left, "x")
     core = lax.axis_index("core")
     own = jnp.where(core == 0, left[:, 0], left[:, 1]).reshape(4 * rows, 8 * rows)
     other = jnp.where(core == 0, left[:, 1], left[:, 0]).reshape(4 * rows, 8 * rows)

time: 174 us -> 176 us (1.011)
  blocking collectives: 115 us -> 102 us
  waiting for transfers between devices: 28.1 us -> 34.7 us
  starting transfers between devices: 20.8 us -> 25.1 us
  matrix products: 2.77 us -> 5.01 us
    all_gather x1 -> x0, blocking collectives: 10.9 us -> none  [per_device(): left = lax.all_gather(left, 'x', axis=0).reshape(4, 2, rows, 8 * rows)]
    all_to_all x2 -> x3, waiting for transfers between devices: 21.1 us -> 27.3 us  [spread(): lax.all_to_all(jnp.broadcast_to(block[None], (count,) + block.shape), axi...]
    all_to_all x2 -> x3, starting transfers between devices: 14.4 us -> 18.4 us  [spread(): lax.all_to_all(jnp.broadcast_to(block[None], (count,) + block.shape), axi...]
  transfers between devices with their start and end apart: 5 -> 6, of which waited for: 3 -> 4; matrix products, arithmetic and copies ran while one was open for 1% -> 1% of each run, Pallas kernels for 0% -> 0%
where the time goes in v18:
time: 176 us; the launch traced here: 175 us
  blocking collectives  102 us (58%)
  waiting for transfers between devices  34.7 us (20%)
  starting transfers between devices  25.1 us (14%)
  matrix products  5.01 us (3%)
  other arithmetic  4.42 us (3%)
  local copies, waits for them, and re-layouts  3.94 us (2%)
    all_to_all x2, blocking collectives, sum_pieces(): lax.all_to_all(jnp.where(mine, 0.0, pieces).astype(jnp.bfloat16), axis, 0...  49.1 us
    all_to_all x3, waiting for transfers between devices, spread(): lax.all_to_all(jnp.broadcast_to(block[None], (count,) + block.shape), axi...  27.3 us
    all_gather x2, blocking collectives, per_device(): by_lo = [lax.all_gather(pair[y], 'x', axis=0, tiled=True) for y in range(2)]  23.9 us
    all_to_all x3, starting transfers between devices, spread(): lax.all_to_all(jnp.broadcast_to(block[None], (count,) + block.shape), axi...  18.4 us
    all_gather x1, blocking collectives, per_device(): poly = lax.all_gather(poly, COL, axis=0, tiled=True)  18.2 us
    all_to_all x1, waiting for transfers between devices, sum_pieces(): lax.all_to_all(jnp.where(mine, 0.0, pieces).astype(jnp.bfloat16), axis, 0...  7.45 us
    all_gather x1, blocking collectives, per_device(): pair = lax.all_gather(xb, 'y_lo', axis=0)  6.12 us
    all_gather x1, blocking collectives, per_device(): left = lax.all_gather(swap_x_y_hi(rounded), 'y_lo', axis=0)  4.34 us
  transfers between devices with their start and end apart: 6, of which 4 were waited for; matrix products, arithmetic and copies ran while one was open for 1% of the time, Pallas kernels for 0%

profile of v18, /device:TPU:1, one launch (start us, length us, event | category | flops | bytes accessed | tf_op | source)
XLA Modules:
  0.0 175.1 jit_solution(12256214811024685749)
XLA Ops:
  0.0 1.0 convert_element_type.36
  1.0 1.3 broadcast_in_dim.64
  2.3 10.9 %all-to-all-start = ((bf16[8,64,1536]{2,1,0:T(8,128)(2,1)}), bf16[8,64,1536]{2,1,0:T(8,128)(2,1)S(1)}, u32[]{:S(2)}, u32[]{:S(2)}) async-start(bf16[8,64,1536]{2,1,0:T(8,128)(2,1)} %broadcast_in_dim.64), calls=%async_computation | async-start | bytes 3145728 | tf_op jit(solution)/shard_map/all_to_all | solution.py:33
  13.2 6.1 %all-gather = bf16[128,1536]{1,0:T(8,128)(2,1)S(1)} all-gather(bf16[64,1536]{1,0:T(8,128)(2,1)S(1)} %convert_element_type.36), channel_id=2, replica_groups=mesh['y_lo'=2,'z'=8,'x'=4,'y_hi'=4,'core'=2] {'y_lo'}, dimensions={0}, use_global_device_ids=true | all-gather | bytes 589824 | tf_op jit(solution)/shard_map/all_gather | solution.py:48
  19.3 12.6 %all-gather.4 = bf16[256,1536]{1,0:T(8,128)(2,1)S(1)} all-gather(bf16[64,1536]{1,0:T(8,128)(2,1)S(1)} %get-tuple-element.7), channel_id=6, replica_groups=mesh['y_lo'=2,'z'=8,'x'=4,'y_hi'=4,'core'=2] {'x'}, dimensions={0}, use_global_device_ids=true | all-gather | bytes 983040 | tf_op jit(solution)/shard_map/all_gather | solution.py:49
  32.0 11.3 %all-gather.5 = bf16[256,1536]{1,0:T(8,128)(2,1)S(1)} all-gather(bf16[64,1536]{1,0:T(8,128)(2,1)S(1)} %get-tuple-element.8), channel_id=7, replica_groups=mesh['y_lo'=2,'z'=8,'x'=4,'y_hi'=4,'core'=2] {'x'}, dimensions={0}, use_global_device_ids=true | all-gather | bytes 983040 | tf_op jit(solution)/shard_map/all_gather | solution.py:49
  43.3 8.2 %all-to-all-done = bf16[8,64,1536]{2,1,0:T(8,128)(2,1)S(1)} async-done(((bf16[8,64,1536]{2,1,0:T(8,128)(2,1)}), bf16[8,64,1536]{2,1,0:T(8,128)(2,1)S(1)}, u32[]{:S(2)}, u32[]{:S(2)}) %all-to-all-start) | async-done | bytes 1572896 | tf_op jit(solution)/shard_map/all_to_all | solution.py:33
  51.4 0.6 fusion.12
  52.1 0.6 fusion.11
  52.7 0.1 maximum_multiply_fusion
  52.8 0.2 select_convert_fusion.1
  53.0 25.4 %all_to_all.30 = bf16[8,64,512]{2,1,0:T(8,128)(2,1)S(1)} all-to-all(bf16[8,64,512]{2,1,0:T(8,128)(2,1)S(1)} %select_convert_fusion.1), channel_id=1, replica_groups=mesh['y_lo'=2,'z'=8,'x'=4,'y_hi'=4,'core'=2] {'core','y_hi'}, dimensions={0} | all-to-all | bytes 1048576 | tf_op jit(solution)/shard_map/all_to_all | solution.py:39
  78.4 0.1 convert_reduce_fusion.1
  78.5 0.8 broadcast_in_dim.69
  79.3 3.5 %all-to-all-start.3 = ((bf16[8,64,512]{2,1,0:T(8,128)(2,1)}), bf16[8,64,512]{2,1,0:T(8,128)(2,1)S(1)}, u32[]{:S(2)}, u32[]{:S(2)}) async-start(bf16[8,64,512]{2,1,0:T(8,128)(2,1)} %broadcast_in_dim.69), calls=%async_computation.3 | async-start | bytes 1048576 | tf_op jit(solution)/shard_map/all_to_all | solution.py:33
  82.8 0.7 collective-permute-start
  83.5 0.0 collective-permute-done
  83.5 4.3 %all-gather.3 = bf16[128,512]{1,0:T(8,128)(2,1)S(1)} all-gather(bf16[64,512]{1,0:T(8,128)(2,1)S(1)} %collective-permute-done), channel_id=5, replica_groups=mesh['y_lo'=2,'z'=8,'x'=4,'y_hi'=4,'core'=2] {'y_lo'}, dimensions={0}, use_global_device_ids=true | all-gather | bytes 196608 | tf_op jit(solution)/shard_map/all_gather | solution.py:57
  87.9 12.9 %all-to-all-done.3 = bf16[8,64,512]{2,1,0:T(8,128)(2,1)S(1)} async-done(((bf16[8,64,512]{2,1,0:T(8,128)(2,1)}), bf16[8,64,512]{2,1,0:T(8,128)(2,1)S(1)}, u32[]{:S(2)}, u32[]{:S(2)}) %all-to-all-start.3) | async-done | bytes 524320 | tf_op jit(solution)/shard_map/all_to_all | solution.py:33
  100.8 0.0 copy-start.1
  100.8 0.9 broadcast_in_dim.67
  101.7 0.1 copy-done.1
  101.8 4.0 %all-to-all-start.2 = ((bf16[4,2,64,512]{3,2,1,0:T(8,128)(2,1)}), bf16[4,2,64,512]{3,2,1,0:T(8,128)(2,1)S(1)}, u32[]{:S(2)}, u32[]{:S(2)}) async-start(bf16[4,2,64,512]{3,2,1,0:T(8,128)(2,1)} %broadcast_in_dim.67), calls=%async_computation.2 | async-start | bytes 1048576 | tf_op jit(solution)/shard_map/all_to_all | solution.py:33
  105.8 2.6 %collective-permute-start.1 = (bf16[512,512]{1,0:T(8,128)(2,1)}, bf16[512,512]{1,0:T(8,128)(2,1)}, u32[]{:S(2)}, u32[]{:S(2)}) collective-permute-start(bf16[512,512]{1,0:T(8,128)(2,1)} %bitcast.54), channel_id=1, source_target_pairs={{0,1},{1,0},{2,3},{3,2},{4,5},{5,4},{6,7},{7,6},{8,9},{9,8},{10,11... | collective-permute-start | bytes 1572872 | tf_op jit(solution)/shard_map/ppermute | solution.py:56
  108.4 6.2 %all-to-all-done.2 = bf16[4,2,64,512]{3,2,1,0:T(8,128)(2,1)S(1)} async-done(((bf16[4,2,64,512]{3,2,1,0:T(8,128)(2,1)}), bf16[4,2,64,512]{3,2,1,0:T(8,128)(2,1)S(1)}, u32[]{:S(2)}, u32[]{:S(2)}) %all-to-all-start.2) | async-done | bytes 524320 | tf_op jit(solution)/shard_map/all_to_all | solution.py:33
  114.6 0.0 copy-start
  114.7 1.5 fusion.13
  116.2 0.0 collective-permute-done.1
  116.2 0.0 copy-done
  116.2 1.3 convolution_add_fusion
  117.5 0.8 select_convert_fusion.2
  118.3 3.4 %all-to-all-start.4 = ((bf16[4,64,512]{2,1,0:T(8,128)(2,1)}), bf16[4,64,512]{2,1,0:T(8,128)(2,1)S(1)}, u32[]{:S(2)}, u32[]{:S(2)}) async-start(bf16[4,64,512]{2,1,0:T(8,128)(2,1)} %select_convert_fusion.2), calls=%async_computation.4 | async-start | bytes 524288 | tf_op jit(solution)/shard_map/all_to_all | solution.py:39
  121.8 1.0 fusion.6
  122.7 7.4 %all-to-all-done.4 = bf16[4,64,512]{2,1,0:T(8,128)(2,1)S(1)} async-done(((bf16[4,64,512]{2,1,0:T(8,128)(2,1)}), bf16[4,64,512]{2,1,0:T(8,128)(2,1)S(1)}, u32[]{:S(2)}, u32[]{:S(2)}) %all-to-all-start.4) | async-done | bytes 262176 | tf_op jit(solution)/shard_map/all_to_all | solution.py:39
  130.2 0.1 fusion.5
  130.3 18.2 %all_gather.27 = bf16[512,512]{1,0:T(8,128)(2,1)S(1)} all-gather(bf16[64,512]{1,0:T(8,128)(2,1)S(1)} %fusion.5), channel_id=1, replica_groups=mesh['y_lo'=2,'z'=8,'x'=4,'y_hi'=4,'core'=2] {'y_hi','core'}, dimensions={0}, use_global_device_ids=true | all-gather | bytes 589824 | tf_op jit(solution)/shard_map/all_gather | solution.py:75
  148.6 1.0 select_convert_fusion
  149.6 23.7 %all_to_all.31 = bf16[8,64,1536]{2,1,0:T(8,128)(2,1)S(1)} all-to-all(bf16[8,64,1536]{2,1,0:T(8,128)(2,1)S(1)} %get-tuple-element.9), channel_id=1, replica_groups=mesh['y_lo'=2,'z'=8,'x'=4,'y_hi'=4,'core'=2] {'x','y_lo'}, dimensions={0} | all-to-all | bytes 3145728 | tf_op jit(solution)/shard_map/all_to_all | solution.py:39
  173.3 0.0 copy-start.2
  173.3 0.2 convert_reduce_fusion
  173.5 0.8 copy-done.2
  174.3 0.8 fusion
  (10 shorter events, 0.2 us)
Async XLA Ops:
  2.3 49.1 %all-to-all-start = ((bf16[8,64,1536]{2,1,0:T(8,128)(2,1)}), bf16[8,64,1536]{2,1,0:T(8,128)(2,1)S(1)}, u32[]{:S(2)}, u32[]{:S(2)}) async-start(bf16[8,64,1536]{2,1,0:T(8,128)(2,1)} %broadcast_in_dim.64), calls=%async_computation | async-start | bytes 3145728 | tf_op jit(solution)/shard_map/all_to_all | solution.py:33
  79.3 21.5 %all-to-all-start.3 = ((bf16[8,64,512]{2,1,0:T(8,128)(2,1)}), bf16[8,64,512]{2,1,0:T(8,128)(2,1)S(1)}, u32[]{:S(2)}, u32[]{:S(2)}) async-start(bf16[8,64,512]{2,1,0:T(8,128)(2,1)} %broadcast_in_dim.69), calls=%async_computation.3 | async-start | bytes 1048576 | tf_op jit(solution)/shard_map/all_to_all | solution.py:33
  82.8 0.7 collective-permute-start
  100.8 1.0 copy-start.1
  101.8 12.8 %all-to-all-start.2 = ((bf16[4,2,64,512]{3,2,1,0:T(8,128)(2,1)}), bf16[4,2,64,512]{3,2,1,0:T(8,128)(2,1)S(1)}, u32[]{:S(2)}, u32[]{:S(2)}) async-start(bf16[4,2,64,512]{3,2,1,0:T(8,128)(2,1)} %broadcast_in_dim.67), calls=%async_computation.2 | async-start | bytes 1048576 | tf_op jit(solution)/shard_map/all_to_all | solution.py:33
  105.8 10.4 %collective-permute-start.1 = (bf16[512,512]{1,0:T(8,128)(2,1)}, bf16[512,512]{1,0:T(8,128)(2,1)}, u32[]{:S(2)}, u32[]{:S(2)}) collective-permute-start(bf16[512,512]{1,0:T(8,128)(2,1)} %bitcast.54), channel_id=1, source_target_pairs={{0,1},{1,0},{2,3},{3,2},{4,5},{5,4},{6,7},{7,6},{8,9},{9,8},{10,11... | collective-permute-start | bytes 1572872 | tf_op jit(solution)/shard_map/ppermute | solution.py:56
  114.6 1.6 copy-start
  118.3 11.9 %all-to-all-start.4 = ((bf16[4,64,512]{2,1,0:T(8,128)(2,1)}), bf16[4,64,512]{2,1,0:T(8,128)(2,1)S(1)}, u32[]{:S(2)}, u32[]{:S(2)}) async-start(bf16[4,64,512]{2,1,0:T(8,128)(2,1)} %select_convert_fusion.2), calls=%async_computation.4 | async-start | bytes 524288 | tf_op jit(solution)/shard_map/all_to_all | solution.py:39
  173.3 1.0 copy-start.2

commit v19 on v18

--- a/solution.py
+++ b/solution.py
@@ -55,17 +55,19 @@
     right = spread(rounded, "z").reshape(8 * rows, 8 * rows)
     right_other = lax.ppermute(right, "core", [(0, 1), (1, 0)])
     left = lax.all_gather(swap_x_y_hi(rounded), "y_lo", axis=0)
-    left = spread(left, "x")
     core = lax.axis_index("core")
-    own = jnp.where(core == 0, left[:, 0], left[:, 1]).reshape(4 * rows, 8 * rows)
-    other = jnp.where(core == 0, left[:, 1], left[:, 0]).reshape(4 * rows, 8 * rows)
+    left = jnp.concatenate(
+        [jnp.where(core == 0, left[0], left[1]), jnp.where(core == 0, left[1], left[0])], axis=1
+    )
+    left = spread(left, "x").reshape(4 * rows, 16 * rows)
+    own, other = left[:, : 8 * rows], left[:, 8 * rows :]
     square = jnp.dot(own, right, preferred_element_type=jnp.float32) + jnp.dot(
         other, right_other, preferred_element_type=jnp.float32
     )
     square = sum_pieces(square.reshape(4, rows, 8 * rows), "y_hi")
 
-    place = (lax.axis_index("y_hi"), core, 0, 0)
-    at_home = lax.dynamic_slice(left, place, (1, 1, rows, 8 * rows), allow_negative_indices=False)[0, 0]
+    place = (lax.axis_index("y_hi") * rows, 0)
+    at_home = lax.dynamic_slice(own, place, (rows, 8 * rows), allow_negative_indices=False)
     column = lax.broadcasted_iota(jnp.int32, at_home.shape, 1) - lax.axis_index("z") * rows
     on_diagonal = column == lax.broadcasted_iota(jnp.int32, at_home.shape, 0)
     diagonal = jnp.where(on_diagonal, at_home.astype(jnp.float32), 0.0).sum(1, keepdims=True)

time: 176 us -> 177 us (level)
  no operation moved by 1% of the time
where the time goes in v19:
time: 177 us
  blocking collectives  102 us (58%)
  waiting for transfers between devices  35.5 us (20%)
  starting transfers between devices  25.1 us (14%)
  matrix products  4.87 us (3%)
  local copies, waits for them, and re-layouts  4.74 us (3%)
  other arithmetic  4.46 us (3%)
    all_to_all x2, blocking collectives, sum_pieces(): lax.all_to_all(jnp.where(mine, 0.0, pieces).astype(jnp.bfloat16), axis, 0...  49.2 us
    all_to_all x3, waiting for transfers between devices, spread(): lax.all_to_all(jnp.broadcast_to(block[None], (count,) + block.shape), axi...  27.2 us
    all_gather x2, blocking collectives, per_device(): by_lo = [lax.all_gather(pair[y], 'x', axis=0, tiled=True) for y in range(2)]  23.9 us
    all_to_all x3, starting transfers between devices, spread(): lax.all_to_all(jnp.broadcast_to(block[None], (count,) + block.shape), axi...  18.4 us
    all_gather x1, blocking collectives, per_device(): poly = lax.all_gather(poly, COL, axis=0, tiled=True)  18.2 us
    all_to_all x1, waiting for transfers between devices, sum_pieces(): lax.all_to_all(jnp.where(mine, 0.0, pieces).astype(jnp.bfloat16), axis, 0...  8.28 us
    all_gather x1, blocking collectives, per_device(): pair = lax.all_gather(xb, 'y_lo', axis=0)  6.12 us
    all_gather x1, blocking collectives, per_device(): left = lax.all_gather(swap_x_y_hi(rounded), 'y_lo', axis=0)  4.34 us
  transfers between devices with their start and end apart: 6, of which 4 were waited for; matrix products, arithmetic and copies ran while one was open for 1% of the time, Pallas kernels for 0%

profile of v19, /device:TPU:1, one launch (start us, length us, event | category | flops | bytes accessed | tf_op | source)
XLA Modules:
  0.0 176.6 jit_solution(12610194321075343513)
XLA Ops:
  0.0 1.0 convert_element_type.33
  1.0 1.3 broadcast_in_dim.64
  2.3 10.9 %all-to-all-start = ((bf16[8,64,1536]{2,1,0:T(8,128)(2,1)}), bf16[8,64,1536]{2,1,0:T(8,128)(2,1)S(1)}, u32[]{:S(2)}, u32[]{:S(2)}) async-start(bf16[8,64,1536]{2,1,0:T(8,128)(2,1)} %broadcast_in_dim.64), calls=%async_computation | async-start | bytes 3145728 | tf_op jit(solution)/shard_map/all_to_all | solution.py:33
  13.2 6.1 %all-gather = bf16[128,1536]{1,0:T(8,128)(2,1)S(1)} all-gather(bf16[64,1536]{1,0:T(8,128)(2,1)S(1)} %convert_element_type.33), channel_id=2, replica_groups=mesh['y_lo'=2,'z'=8,'x'=4,'y_hi'=4,'core'=2] {'y_lo'}, dimensions={0}, use_global_device_ids=true | all-gather | bytes 589824 | tf_op jit(solution)/shard_map/all_gather | solution.py:48
  19.3 12.6 %all-gather.4 = bf16[256,1536]{1,0:T(8,128)(2,1)S(1)} all-gather(bf16[64,1536]{1,0:T(8,128)(2,1)S(1)} %get-tuple-element.5), channel_id=6, replica_groups=mesh['y_lo'=2,'z'=8,'x'=4,'y_hi'=4,'core'=2] {'x'}, dimensions={0}, use_global_device_ids=true | all-gather | bytes 983040 | tf_op jit(solution)/shard_map/all_gather | solution.py:49
  32.0 11.3 %all-gather.5 = bf16[256,1536]{1,0:T(8,128)(2,1)S(1)} all-gather(bf16[64,1536]{1,0:T(8,128)(2,1)S(1)} %get-tuple-element.6), channel_id=7, replica_groups=mesh['y_lo'=2,'z'=8,'x'=4,'y_hi'=4,'core'=2] {'x'}, dimensions={0}, use_global_device_ids=true | all-gather | bytes 983040 | tf_op jit(solution)/shard_map/all_gather | solution.py:49
  43.3 8.2 %all-to-all-done = bf16[8,64,1536]{2,1,0:T(8,128)(2,1)S(1)} async-done(((bf16[8,64,1536]{2,1,0:T(8,128)(2,1)}), bf16[8,64,1536]{2,1,0:T(8,128)(2,1)S(1)}, u32[]{:S(2)}, u32[]{:S(2)}) %all-to-all-start) | async-done | bytes 1572896 | tf_op jit(solution)/shard_map/all_to_all | solution.py:33
  51.4 0.6 fusion.14
  52.1 0.6 fusion.13
  52.7 0.1 maximum_multiply_fusion
  52.8 0.2 select_convert_fusion.1
  53.0 25.4 %all_to_all.30 = bf16[8,64,512]{2,1,0:T(8,128)(2,1)S(1)} all-to-all(bf16[8,64,512]{2,1,0:T(8,128)(2,1)S(1)} %select_convert_fusion.1), channel_id=1, replica_groups=mesh['y_lo'=2,'z'=8,'x'=4,'y_hi'=4,'core'=2] {'core','y_hi'}, dimensions={0} | all-to-all | bytes 1048576 | tf_op jit(solution)/shard_map/all_to_all | solution.py:39
  78.4 0.1 convert_reduce_fusion.1
  78.5 0.8 broadcast_in_dim.69
  79.3 3.5 %all-to-all-start.3 = ((bf16[8,64,512]{2,1,0:T(8,128)(2,1)}), bf16[8,64,512]{2,1,0:T(8,128)(2,1)S(1)}, u32[]{:S(2)}, u32[]{:S(2)}) async-start(bf16[8,64,512]{2,1,0:T(8,128)(2,1)} %broadcast_in_dim.69), calls=%async_computation.3 | async-start | bytes 1048576 | tf_op jit(solution)/shard_map/all_to_all | solution.py:33
  82.8 0.7 collective-permute-start
  83.5 0.0 collective-permute-done
  83.5 4.3 %all-gather.3 = bf16[128,512]{1,0:T(8,128)(2,1)S(1)} all-gather(bf16[64,512]{1,0:T(8,128)(2,1)S(1)} %collective-permute-done), channel_id=5, replica_groups=mesh['y_lo'=2,'z'=8,'x'=4,'y_hi'=4,'core'=2] {'y_lo'}, dimensions={0}, use_global_device_ids=true | all-gather | bytes 196608 | tf_op jit(solution)/shard_map/all_gather | solution.py:57
  87.9 12.9 %all-to-all-done.3 = bf16[8,64,512]{2,1,0:T(8,128)(2,1)S(1)} async-done(((bf16[8,64,512]{2,1,0:T(8,128)(2,1)}), bf16[8,64,512]{2,1,0:T(8,128)(2,1)S(1)}, u32[]{:S(2)}, u32[]{:S(2)}) %all-to-all-start.3) | async-done | bytes 524320 | tf_op jit(solution)/shard_map/all_to_all | solution.py:33
  100.8 0.0 copy-start.1
  100.8 0.9 broadcast_in_dim.67
  101.7 0.1 copy-done.1
  101.8 4.0 %all-to-all-start.2 = ((bf16[4,64,1024]{2,1,0:T(8,128)(2,1)}), bf16[4,64,1024]{2,1,0:T(8,128)(2,1)S(1)}, u32[]{:S(2)}, u32[]{:S(2)}) async-start(bf16[4,64,1024]{2,1,0:T(8,128)(2,1)} %broadcast_in_dim.67), calls=%async_computation.2 | async-start | bytes 1048576 | tf_op jit(solution)/shard_map/all_to_all | solution.py:33
  105.8 2.6 %collective-permute-start.1 = (bf16[512,512]{1,0:T(8,128)(2,1)}, bf16[512,512]{1,0:T(8,128)(2,1)}, u32[]{:S(2)}, u32[]{:S(2)}) collective-permute-start(bf16[512,512]{1,0:T(8,128)(2,1)} %bitcast.50), channel_id=1, source_target_pairs={{0,1},{1,0},{2,3},{3,2},{4,5},{5,4},{6,7},{7,6},{8,9},{9,8},{10,11... | collective-permute-start | bytes 1572872 | tf_op jit(solution)/shard_map/ppermute | solution.py:56
  108.5 6.2 %all-to-all-done.2 = bf16[4,64,1024]{2,1,0:T(8,128)(2,1)S(1)} async-done(((bf16[4,64,1024]{2,1,0:T(8,128)(2,1)}), bf16[4,64,1024]{2,1,0:T(8,128)(2,1)S(1)}, u32[]{:S(2)}, u32[]{:S(2)}) %all-to-all-start.2) | async-done | bytes 524320 | tf_op jit(solution)/shard_map/all_to_all | solution.py:33
  114.6 1.3 fusion.10
  116.0 0.0 collective-permute-done.1
  116.0 1.3 convolution_add_fusion
  117.3 0.0 copy-start
  117.3 0.8 copy-done
  118.1 0.8 select_convert_fusion.2
  118.9 3.4 %all-to-all-start.4 = ((bf16[4,64,512]{2,1,0:T(8,128)(2,1)}), bf16[4,64,512]{2,1,0:T(8,128)(2,1)S(1)}, u32[]{:S(2)}, u32[]{:S(2)}) async-start(bf16[4,64,512]{2,1,0:T(8,128)(2,1)} %select_convert_fusion.2), calls=%async_computation.4 | async-start | bytes 524288 | tf_op jit(solution)/shard_map/all_to_all | solution.py:39
  122.4 0.1 select_reduce_fusion
  122.5 8.3 %all-to-all-done.4 = bf16[4,64,512]{2,1,0:T(8,128)(2,1)S(1)} async-done(((bf16[4,64,512]{2,1,0:T(8,128)(2,1)}), bf16[4,64,512]{2,1,0:T(8,128)(2,1)S(1)}, u32[]{:S(2)}, u32[]{:S(2)}) %all-to-all-start.4) | async-done | bytes 262176 | tf_op jit(solution)/shard_map/all_to_all | solution.py:39
  130.8 1.0 fusion.6
  131.8 18.2 %all_gather.27 = bf16[512,512]{1,0:T(8,128)(2,1)S(1)} all-gather(bf16[64,512]{1,0:T(8,128)(2,1)S(1)} %fusion.6), channel_id=1, replica_groups=mesh['y_lo'=2,'z'=8,'x'=4,'y_hi'=4,'core'=2] {'y_hi','core'}, dimensions={0}, use_global_device_ids=true | all-gather | bytes 589824 | tf_op jit(solution)/shard_map/all_gather | solution.py:77
  150.1 1.0 select_convert_fusion
  151.1 23.7 %all_to_all.31 = bf16[8,64,1536]{2,1,0:T(8,128)(2,1)S(1)} all-to-all(bf16[8,64,1536]{2,1,0:T(8,128)(2,1)S(1)} %get-tuple-element.9), channel_id=1, replica_groups=mesh['y_lo'=2,'z'=8,'x'=4,'y_hi'=4,'core'=2] {'x','y_lo'}, dimensions={0} | all-to-all | bytes 3145728 | tf_op jit(solution)/shard_map/all_to_all | solution.py:39
  174.8 0.0 copy-start.2
  174.8 0.2 convert_reduce_fusion
  175.0 0.8 copy-done.2
  175.8 0.8 fusion
  (12 shorter events, 0.2 us)
Async XLA Ops:
  2.3 49.1 %all-to-all-start = ((bf16[8,64,1536]{2,1,0:T(8,128)(2,1)}), bf16[8,64,1536]{2,1,0:T(8,128)(2,1)S(1)}, u32[]{:S(2)}, u32[]{:S(2)}) async-start(bf16[8,64,1536]{2,1,0:T(8,128)(2,1)} %broadcast_in_dim.64), calls=%async_computation | async-start | bytes 3145728 | tf_op jit(solution)/shard_map/all_to_all | solution.py:33
  79.3 21.5 %all-to-all-start.3 = ((bf16[8,64,512]{2,1,0:T(8,128)(2,1)}), bf16[8,64,512]{2,1,0:T(8,128)(2,1)S(1)}, u32[]{:S(2)}, u32[]{:S(2)}) async-start(bf16[8,64,512]{2,1,0:T(8,128)(2,1)} %broadcast_in_dim.69), calls=%async_computation.3 | async-start | bytes 1048576 | tf_op jit(solution)/shard_map/all_to_all | solution.py:33
  82.8 0.7 collective-permute-start
  100.8 1.0 copy-start.1
  101.8 12.8 %all-to-all-start.2 = ((bf16[4,64,1024]{2,1,0:T(8,128)(2,1)}), bf16[4,64,1024]{2,1,0:T(8,128)(2,1)S(1)}, u32[]{:S(2)}, u32[]{:S(2)}) async-start(bf16[4,64,1024]{2,1,0:T(8,128)(2,1)} %broadcast_in_dim.67), calls=%async_computation.2 | async-start | bytes 1048576 | tf_op jit(solution)/shard_map/all_to_all | solution.py:33
  105.8 10.2 %collective-permute-start.1 = (bf16[512,512]{1,0:T(8,128)(2,1)}, bf16[512,512]{1,0:T(8,128)(2,1)}, u32[]{:S(2)}, u32[]{:S(2)}) collective-permute-start(bf16[512,512]{1,0:T(8,128)(2,1)} %bitcast.50), channel_id=1, source_target_pairs={{0,1},{1,0},{2,3},{3,2},{4,5},{5,4},{6,7},{7,6},{8,9},{9,8},{10,11... | collective-permute-start | bytes 1572872 | tf_op jit(solution)/shard_map/ppermute | solution.py:56
  117.3 0.8 copy-start
  118.9 11.9 %all-to-all-start.4 = ((bf16[4,64,512]{2,1,0:T(8,128)(2,1)}), bf16[4,64,512]{2,1,0:T(8,128)(2,1)S(1)}, u32[]{:S(2)}, u32[]{:S(2)}) async-start(bf16[4,64,512]{2,1,0:T(8,128)(2,1)} %select_convert_fusion.2), calls=%async_computation.4 | async-start | bytes 524288 | tf_op jit(solution)/shard_map/all_to_all | solution.py:39
  174.8 1.0 copy-start.2

commit v20 on v18

--- a/solution.py
+++ b/solution.py
@@ -55,7 +55,7 @@
     right = spread(rounded, "z").reshape(8 * rows, 8 * rows)
     right_other = lax.ppermute(right, "core", [(0, 1), (1, 0)])
     left = lax.all_gather(swap_x_y_hi(rounded), "y_lo", axis=0)
-    left = spread(left, "x")
+    left = lax.all_gather(left, "x", axis=0).reshape(4, 2, rows, 8 * rows)
     core = lax.axis_index("core")
     own = jnp.where(core == 0, left[:, 0], left[:, 1]).reshape(4 * rows, 8 * rows)
     other = jnp.where(core == 0, left[:, 1], left[:, 0]).reshape(4 * rows, 8 * rows)
@@ -72,9 +72,9 @@
     square = square + rest_of(gram) * (2.0 * diagonal)
 
     poly = (coef_cubic * gram + coef_quintic * square).astype(jnp.bfloat16)
-    poly = lax.all_gather(poly, COL, axis=0, tiled=True)
+    poly = lax.all_gather(spread(poly, "y_hi"), "core", axis=0).reshape(8 * rows, 8 * rows)
     product = jnp.dot(poly, by_hi, preferred_element_type=jnp.float32)
-    return coef_linear * x_scaled + sum_pieces(product.reshape(8, rows, cols), LO)
+    return coef_linear * x_scaled + sum_pieces(product.reshape(8, rows, cols), ("y_lo", "x"))
 
 
 def solution(mesh):

time: 176 us -> 174 us (0.989)
  matrix products: 5.01 us -> 2.78 us
    all_gather x1 -> x2, blocking collectives: 18.2 us -> 17.9 us  [the longest x1 10.9 us: per_device(): left = lax.all_gather(left, 'x', axis=0).reshape(4, 2, rows, 8 * rows)]
where the time goes in v20:
time: 174 us
  blocking collectives  102 us (59%)
  waiting for transfers between devices  36 us (21%)
  starting transfers between devices  24.2 us (14%)
  other arithmetic  4.43 us (3%)
  local copies, waits for them, and re-layouts  3.79 us (2%)
  matrix products  2.78 us (2%)
    all_to_all x2, blocking collectives, sum_pieces(): lax.all_to_all(jnp.where(mine, 0.0, pieces).astype(jnp.bfloat16), axis, 0...  49.8 us
    all_to_all x3, waiting for transfers between devices, spread(): lax.all_to_all(jnp.broadcast_to(block[None], (count,) + block.shape), axi...  29 us
    all_gather x2, blocking collectives, per_device(): by_lo = [lax.all_gather(pair[y], 'x', axis=0, tiled=True) for y in range(2)]  23.9 us
    all_to_all x3, starting transfers between devices, spread(): lax.all_to_all(jnp.broadcast_to(block[None], (count,) + block.shape), axi...  17.8 us
    all_gather x1, blocking collectives, per_device(): left = lax.all_gather(left, 'x', axis=0).reshape(4, 2, rows, 8 * rows)  10.9 us
    all_gather x1, blocking collectives, per_device(): lax.all_gather(spread(poly, 'y_hi'), 'core', axis=0)  7.06 us
    all_to_all x1, waiting for transfers between devices, sum_pieces(): lax.all_to_all(jnp.where(mine, 0.0, pieces).astype(jnp.bfloat16), axis, 0...  7.01 us
    all_gather x1, blocking collectives, per_device(): pair = lax.all_gather(xb, 'y_lo', axis=0)  6.12 us
  transfers between devices with their start and end apart: 6, of which 4 were waited for; matrix products, arithmetic and copies ran while one was open for 1% of the time, Pallas kernels for 0%

profile of v20, /device:TPU:1, one launch (start us, length us, event | category | flops | bytes accessed | tf_op | source)
XLA Modules:
  0.0 173.5 jit_solution(6282648597124990048)
XLA Ops:
  0.0 1.0 convert_element_type.37
  1.0 1.3 broadcast_in_dim.66
  2.3 10.9 %all-to-all-start = ((bf16[8,64,1536]{2,1,0:T(8,128)(2,1)}), bf16[8,64,1536]{2,1,0:T(8,128)(2,1)S(1)}, u32[]{:S(2)}, u32[]{:S(2)}) async-start(bf16[8,64,1536]{2,1,0:T(8,128)(2,1)} %broadcast_in_dim.66), calls=%async_computation | async-start | bytes 3145728 | tf_op jit(solution)/shard_map/all_to_all | solution.py:33
  13.2 6.1 %all-gather = bf16[128,1536]{1,0:T(8,128)(2,1)S(1)} all-gather(bf16[64,1536]{1,0:T(8,128)(2,1)S(1)} %convert_element_type.37), channel_id=2, replica_groups=mesh['y_lo'=2,'z'=8,'x'=4,'y_hi'=4,'core'=2] {'y_lo'}, dimensions={0}, use_global_device_ids=true | all-gather | bytes 589824 | tf_op jit(solution)/shard_map/all_gather | solution.py:48
  19.3 12.6 %all-gather.6 = bf16[256,1536]{1,0:T(8,128)(2,1)S(1)} all-gather(bf16[64,1536]{1,0:T(8,128)(2,1)S(1)} %get-tuple-element.7), channel_id=8, replica_groups=mesh['y_lo'=2,'z'=8,'x'=4,'y_hi'=4,'core'=2] {'x'}, dimensions={0}, use_global_device_ids=true | all-gather | bytes 983040 | tf_op jit(solution)/shard_map/all_gather | solution.py:49
  32.0 11.3 %all-gather.7 = bf16[256,1536]{1,0:T(8,128)(2,1)S(1)} all-gather(bf16[64,1536]{1,0:T(8,128)(2,1)S(1)} %get-tuple-element.8), channel_id=9, replica_groups=mesh['y_lo'=2,'z'=8,'x'=4,'y_hi'=4,'core'=2] {'x'}, dimensions={0}, use_global_device_ids=true | all-gather | bytes 983040 | tf_op jit(solution)/shard_map/all_gather | solution.py:49
  43.3 8.2 %all-to-all-done = bf16[8,64,1536]{2,1,0:T(8,128)(2,1)S(1)} async-done(((bf16[8,64,1536]{2,1,0:T(8,128)(2,1)}), bf16[8,64,1536]{2,1,0:T(8,128)(2,1)S(1)}, u32[]{:S(2)}, u32[]{:S(2)}) %all-to-all-start) | async-done | bytes 1572896 | tf_op jit(solution)/shard_map/all_to_all | solution.py:33
  51.4 0.6 fusion.11
  52.1 0.6 fusion.10
  52.7 0.1 maximum_multiply_fusion
  52.8 0.2 select_convert_fusion.1
  53.0 25.4 %all_to_all.30 = bf16[8,64,512]{2,1,0:T(8,128)(2,1)S(1)} all-to-all(bf16[8,64,512]{2,1,0:T(8,128)(2,1)S(1)} %select_convert_fusion.1), channel_id=1, replica_groups=mesh['y_lo'=2,'z'=8,'x'=4,'y_hi'=4,'core'=2] {'core','y_hi'}, dimensions={0} | all-to-all | bytes 1048576 | tf_op jit(solution)/shard_map/all_to_all | solution.py:39
  78.4 0.1 convert_reduce_fusion.1
  78.5 0.8 broadcast_in_dim.70
  79.3 3.5 %all-to-all-start.2 = ((bf16[8,64,512]{2,1,0:T(8,128)(2,1)}), bf16[8,64,512]{2,1,0:T(8,128)(2,1)S(1)}, u32[]{:S(2)}, u32[]{:S(2)}) async-start(bf16[8,64,512]{2,1,0:T(8,128)(2,1)} %broadcast_in_dim.70), calls=%async_computation.2 | async-start | bytes 1048576 | tf_op jit(solution)/shard_map/all_to_all | solution.py:33
  82.8 0.7 collective-permute-start
  83.5 0.0 collective-permute-done
  83.5 4.3 %all-gather.3 = bf16[128,512]{1,0:T(8,128)(2,1)S(1)} all-gather(bf16[64,512]{1,0:T(8,128)(2,1)S(1)} %collective-permute-done), channel_id=5, replica_groups=mesh['y_lo'=2,'z'=8,'x'=4,'y_hi'=4,'core'=2] {'y_lo'}, dimensions={0}, use_global_device_ids=true | all-gather | bytes 196608 | tf_op jit(solution)/shard_map/all_gather | solution.py:57
  87.9 12.9 %all-to-all-done.2 = bf16[8,64,512]{2,1,0:T(8,128)(2,1)S(1)} async-done(((bf16[8,64,512]{2,1,0:T(8,128)(2,1)}), bf16[8,64,512]{2,1,0:T(8,128)(2,1)S(1)}, u32[]{:S(2)}, u32[]{:S(2)}) %all-to-all-start.2) | async-done | bytes 524320 | tf_op jit(solution)/shard_map/all_to_all | solution.py:33
  100.8 2.3 %collective-permute-start.1 = (bf16[512,512]{1,0:T(8,128)(2,1)S(1)}, bf16[512,512]{1,0:T(8,128)(2,1)S(1)}, u32[]{:S(2)}, u32[]{:S(2)}) collective-permute-start(bf16[512,512]{1,0:T(8,128)(2,1)S(1)} %bitcast.58), channel_id=1, source_target_pairs={{0,1},{1,0},{2,3},{3,2},{4,5},{5,4},{6,7},{7,6},{8,9},{9,8},{10,11... | collective-permute-start | bytes 1572872 | tf_op jit(solution)/shard_map/ppermute | solution.py:56
  103.1 10.9 %all-gather.4 = bf16[8,64,512]{2,1,0:T(8,128)(2,1)S(1)} all-gather(bf16[2,64,512]{2,1,0:T(8,128)(2,1)S(1)} %bitcast.62), channel_id=6, replica_groups=mesh['y_lo'=2,'z'=8,'x'=4,'y_hi'=4,'core'=2] {'x'}, dimensions={0}, use_global_device_ids=true | all-gather | bytes 655360 | tf_op jit(solution)/shard_map/all_gather | solution.py:58
  114.0 0.0 copy-start
  114.1 0.3 fusion.12
  114.4 0.0 collective-permute-done.1
  114.4 0.3 convolution_add_fusion
  114.7 0.1 copy-done
  114.8 0.8 select_convert_fusion.2
  115.6 3.4 %all-to-all-start.3 = ((bf16[4,64,512]{2,1,0:T(8,128)(2,1)}), bf16[4,64,512]{2,1,0:T(8,128)(2,1)S(1)}, u32[]{:S(2)}, u32[]{:S(2)}) async-start(bf16[4,64,512]{2,1,0:T(8,128)(2,1)} %select_convert_fusion.2), calls=%async_computation.3 | async-start | bytes 524288 | tf_op jit(solution)/shard_map/all_to_all | solution.py:39
  119.0 1.0 fusion.6
  120.0 7.0 %all-to-all-done.3 = bf16[4,64,512]{2,1,0:T(8,128)(2,1)S(1)} async-done(((bf16[4,64,512]{2,1,0:T(8,128)(2,1)}), bf16[4,64,512]{2,1,0:T(8,128)(2,1)S(1)}, u32[]{:S(2)}, u32[]{:S(2)}) %all-to-all-start.3) | async-done | bytes 262176 | tf_op jit(solution)/shard_map/all_to_all | solution.py:39
  127.1 0.1 fusion.8
  127.2 0.7 broadcast_in_dim.75
  127.9 3.4 %all-to-all-start.4 = ((bf16[4,64,512]{2,1,0:T(8,128)(2,1)}), bf16[4,64,512]{2,1,0:T(8,128)(2,1)S(1)}, u32[]{:S(2)}, u32[]{:S(2)}) async-start(bf16[4,64,512]{2,1,0:T(8,128)(2,1)} %broadcast_in_dim.75), calls=%async_computation.4 | async-start | bytes 524288 | tf_op jit(solution)/shard_map/all_to_all | solution.py:33
  131.3 7.9 %all-to-all-done.4 = bf16[4,64,512]{2,1,0:T(8,128)(2,1)S(1)} async-done(((bf16[4,64,512]{2,1,0:T(8,128)(2,1)}), bf16[4,64,512]{2,1,0:T(8,128)(2,1)S(1)}, u32[]{:S(2)}, u32[]{:S(2)}) %all-to-all-start.4) | async-done | bytes 262176 | tf_op jit(solution)/shard_map/all_to_all | solution.py:33
  139.2 7.1 %all-gather.5 = bf16[8,64,512]{2,1,0:T(8,128)(2,1)S(1)} all-gather(bf16[4,64,512]{2,1,0:T(8,128)(2,1)S(1)} %all-to-all-done.4), channel_id=7, replica_groups=mesh['y_lo'=2,'z'=8,'x'=4,'y_hi'=4,'core'=2] {'core'}, dimensions={0}, use_global_device_ids=true | all-gather | bytes 786432 | tf_op jit(solution)/shard_map/all_gather | solution.py:75
  146.3 1.0 select_convert_fusion
  147.3 24.4 %all_to_all.31 = bf16[8,64,1536]{2,1,0:T(8,128)(2,1)S(1)} all-to-all(bf16[8,64,1536]{2,1,0:T(8,128)(2,1)S(1)} %get-tuple-element.9), channel_id=1, replica_groups=mesh['y_lo'=2,'z'=8,'x'=4,'y_hi'=4,'core'=2] {'y_lo','x'}, dimensions={0} | all-to-all | bytes 3145728 | tf_op jit(solution)/shard_map/all_to_all | solution.py:39
  171.7 0.0 copy-start.1
  171.7 0.2 convert_reduce_fusion
  171.9 0.8 copy-done.1
  172.7 0.8 fusion
  (10 shorter events, 0.2 us)
Async XLA Ops:
  2.3 49.1 %all-to-all-start = ((bf16[8,64,1536]{2,1,0:T(8,128)(2,1)}), bf16[8,64,1536]{2,1,0:T(8,128)(2,1)S(1)}, u32[]{:S(2)}, u32[]{:S(2)}) async-start(bf16[8,64,1536]{2,1,0:T(8,128)(2,1)} %broadcast_in_dim.66), calls=%async_computation | async-start | bytes 3145728 | tf_op jit(solution)/shard_map/all_to_all | solution.py:33
  79.3 21.5 %all-to-all-start.2 = ((bf16[8,64,512]{2,1,0:T(8,128)(2,1)}), bf16[8,64,512]{2,1,0:T(8,128)(2,1)S(1)}, u32[]{:S(2)}, u32[]{:S(2)}) async-start(bf16[8,64,512]{2,1,0:T(8,128)(2,1)} %broadcast_in_dim.70), calls=%async_computation.2 | async-start | bytes 1048576 | tf_op jit(solution)/shard_map/all_to_all | solution.py:33
  82.8 0.7 collective-permute-start
  100.8 13.6 %collective-permute-start.1 = (bf16[512,512]{1,0:T(8,128)(2,1)S(1)}, bf16[512,512]{1,0:T(8,128)(2,1)S(1)}, u32[]{:S(2)}, u32[]{:S(2)}) collective-permute-start(bf16[512,512]{1,0:T(8,128)(2,1)S(1)} %bitcast.58), channel_id=1, source_target_pairs={{0,1},{1,0},{2,3},{3,2},{4,5},{5,4},{6,7},{7,6},{8,9},{9,8},{10,11... | collective-permute-start | bytes 1572872 | tf_op jit(solution)/shard_map/ppermute | solution.py:56
  114.0 0.8 copy-start
  115.6 11.4 %all-to-all-start.3 = ((bf16[4,64,512]{2,1,0:T(8,128)(2,1)}), bf16[4,64,512]{2,1,0:T(8,128)(2,1)S(1)}, u32[]{:S(2)}, u32[]{:S(2)}) async-start(bf16[4,64,512]{2,1,0:T(8,128)(2,1)} %select_convert_fusion.2), calls=%async_computation.3 | async-start | bytes 524288 | tf_op jit(solution)/shard_map/all_to_all | solution.py:39
  127.9 11.3 %all-to-all-start.4 = ((bf16[4,64,512]{2,1,0:T(8,128)(2,1)}), bf16[4,64,512]{2,1,0:T(8,128)(2,1)S(1)}, u32[]{:S(2)}, u32[]{:S(2)}) async-start(bf16[4,64,512]{2,1,0:T(8,128)(2,1)} %broadcast_in_dim.75), calls=%async_computation.4 | async-start | bytes 524288 | tf_op jit(solution)/shard_map/all_to_all | solution.py:33
  171.7 1.0 copy-start.1

commit v21 on v13

--- a/solution.py
+++ b/solution.py
@@ -42,8 +42,10 @@
 
 def per_device(x_scaled):
     rows, cols = x_scaled.shape
-    xb = x_scaled.astype(jnp.bfloat16)
-    by_hi = spread(xb, "z").reshape(8 * rows, cols)
+    mine = jnp.arange(8)[:, None, None] == lax.axis_index("z")
+    copies = jnp.where(mine, x_scaled, lax.reduce_precision(x_scaled, 8, 7)).astype(jnp.bfloat16)
+    xb = copies[0]
+    by_hi = lax.all_to_all(copies, "z", 0, 0).reshape(8 * rows, cols)
     pair = lax.all_gather(xb, "y_lo", axis=0)
     by_lo = [lax.all_gather(pair[y], "x", axis=0, tiled=True) for y in range(2)]
 

time: 174 us -> 176 us (1.011)
  other arithmetic: 4.42 us -> 6.77 us
    all_to_all x0 -> x1, starting transfers between devices: none -> 10.9 us  [per_device(): by_hi = lax.all_to_all(copies, 'z', 0, 0).reshape(8 * rows, cols)]
    all_to_all x2 -> x1, starting transfers between devices: 14.4 us -> 3.49 us  [spread(): lax.all_to_all(jnp.broadcast_to(block[None], (8,) + block.shape), axis, 0...]
    all_to_all x2 -> x1, waiting for transfers between devices: 21.1 us -> 12.9 us  [spread(): lax.all_to_all(jnp.broadcast_to(block[None], (8,) + block.shape), axis, 0...]
    all_to_all x0 -> x1, waiting for transfers between devices: none -> 7.38 us  [per_device(): by_hi = lax.all_to_all(copies, 'z', 0, 0).reshape(8 * rows, cols)]
where the time goes in v21:
time: 176 us; the launch traced here: 175 us
  blocking collectives  114 us (65%)
  waiting for transfers between devices  27.3 us (16%)
  starting transfers between devices  20.8 us (12%)
  other arithmetic  6.77 us (4%)
  matrix products  2.77 us (2%)
  local copies, waits for them, and re-layouts  2.69 us (2%)
    all_to_all x2, blocking collectives, sum_pieces(): lax.all_to_all(jnp.where(mine, 0.0, pieces).astype(jnp.bfloat16), axis, 0...  49.7 us
    all_gather x2, blocking collectives, per_device(): by_lo = [lax.all_gather(pair[y], 'x', axis=0, tiled=True) for y in range(2)]  23.8 us
    all_gather x1, blocking collectives, per_device(): poly = lax.all_gather(poly, COL, axis=0, tiled=True)  19.6 us
    all_to_all x1, waiting for transfers between devices, spread(): lax.all_to_all(jnp.broadcast_to(block[None], (8,) + block.shape), axis, 0...  12.9 us
    all_gather x1, blocking collectives, per_device(): left = lax.all_gather(left, 'x', axis=0).reshape(4, 2, rows, 8 * rows)  10.9 us
    all_to_all x1, starting transfers between devices, per_device(): by_hi = lax.all_to_all(copies, 'z', 0, 0).reshape(8 * rows, cols)  10.9 us
    all_to_all x1, waiting for transfers between devices, per_device(): by_hi = lax.all_to_all(copies, 'z', 0, 0).reshape(8 * rows, cols)  7.38 us
    all_to_all x1, waiting for transfers between devices, sum_pieces(): lax.all_to_all(jnp.where(mine, 0.0, pieces).astype(jnp.bfloat16), axis, 0...  7.02 us
  transfers between devices with their start and end apart: 5, of which 3 were waited for; matrix products, arithmetic and copies ran while one was open for 1% of the time, Pallas kernels for 0%

profile of v21, /device:TPU:1, one launch (start us, length us, event | category | flops | bytes accessed | tf_op | source)
XLA Modules:
  0.0 174.9 jit_solution(14025589945404731095)
XLA Ops:
  0.0 1.0 reduce_precision.6
  1.0 2.4 %select_convert_fusion.1 = bf16[8,64,1536]{2,1,0:T(8,128)(2,1)} fusion(bf16[64,1536]{1,0:T(8,128)(2,1)S(1)} %reduce_precision.6, f32[64,1536]{1,0:T(8,128)} %param.1, pred[8]{0:T(512)(128)(4,1)S(1)} %iota_compare_fusion.4), kind=kLoop, calls=%fused_computation.2 | loop fusion | flops 786432 | bytes 2162696 | tf_op jit(solution)/shard_map/convert_element_type | solution.py:46
  3.4 10.9 %all-to-all-start = ((bf16[8,64,1536]{2,1,0:T(8,128)(2,1)}), bf16[8,64,1536]{2,1,0:T(8,128)(2,1)S(1)}, u32[]{:S(2)}, u32[]{:S(2)}) async-start(bf16[8,64,1536]{2,1,0:T(8,128)(2,1)} %select_convert_fusion.1), calls=%async_computation | async-start | bytes 3145728 | tf_op jit(solution)/shard_map/all_to_all | solution.py:48
  14.2 0.9 slice.22
  15.2 6.1 %all_gather.24 = bf16[2,64,1536]{2,1,0:T(8,128)(2,1)S(1)} all-gather(bf16[1,64,1536]{2,1,0:T(8,128)(2,1)S(1)} %slice.22), channel_id=1, replica_groups=mesh['y_lo'=2,'z'=8,'x'=4,'y_hi'=4,'core'=2] {'y_lo'}, dimensions={0}, use_global_device_ids=true | all-gather | bytes 589824 | tf_op jit(solution)/shard_map/all_gather | solution.py:49
  21.4 12.6 %all-gather = bf16[1,256,1536]{2,1,0:T(8,128)(2,1)S(1)} all-gather(bf16[1,64,1536]{2,1,0:T(8,128)(2,1)S(1)} %get-tuple-element.7), channel_id=2, replica_groups=mesh['y_lo'=2,'z'=8,'x'=4,'y_hi'=4,'core'=2] {'x'}, dimensions={1}, use_global_device_ids=true | all-gather | bytes 983040 | tf_op jit(solution)/shard_map/all_gather | solution.py:50
  34.0 11.1 %all-gather.1 = bf16[1,256,1536]{2,1,0:T(8,128)(2,1)S(1)} all-gather(bf16[1,64,1536]{2,1,0:T(8,128)(2,1)S(1)} %get-tuple-element.8), channel_id=3, replica_groups=mesh['y_lo'=2,'z'=8,'x'=4,'y_hi'=4,'core'=2] {'x'}, dimensions={1}, use_global_device_ids=true | all-gather | bytes 983040 | tf_op jit(solution)/shard_map/all_gather | solution.py:50
  45.1 7.4 %all-to-all-done = bf16[8,64,1536]{2,1,0:T(8,128)(2,1)S(1)} async-done(((bf16[8,64,1536]{2,1,0:T(8,128)(2,1)}), bf16[8,64,1536]{2,1,0:T(8,128)(2,1)S(1)}, u32[]{:S(2)}, u32[]{:S(2)}) %all-to-all-start) | async-done | bytes 1572896 | tf_op jit(solution)/shard_map/all_to_all | solution.py:48
  52.5 0.6 fusion.2
  53.1 0.6 fusion
  53.7 0.1 maximum_multiply_fusion
  53.8 0.2 select_convert_fusion.2
  54.0 25.4 %all_to_all.25 = bf16[8,64,512]{2,1,0:T(8,128)(2,1)S(1)} all-to-all(bf16[8,64,512]{2,1,0:T(8,128)(2,1)S(1)} %select_convert_fusion.2), channel_id=1, replica_groups=mesh['y_lo'=2,'z'=8,'x'=4,'y_hi'=4,'core'=2] {'core','y_hi'}, dimensions={0} | all-to-all | bytes 1048576 | tf_op jit(solution)/shard_map/all_to_all | solution.py:38
  79.4 0.1 convert_reduce_fusion.1
  79.5 0.8 broadcast_in_dim.75
  80.4 3.5 %all-to-all-start.2 = ((bf16[8,64,512]{2,1,0:T(8,128)(2,1)}), bf16[8,64,512]{2,1,0:T(8,128)(2,1)S(1)}, u32[]{:S(2)}, u32[]{:S(2)}) async-start(bf16[8,64,512]{2,1,0:T(8,128)(2,1)} %broadcast_in_dim.75), calls=%async_computation.2 | async-start | bytes 1048576 | tf_op jit(solution)/shard_map/all_to_all | solution.py:32
  83.9 0.7 collective-permute-start
  84.6 0.0 collective-permute-done
  84.6 4.3 %all-gather.2 = bf16[128,512]{1,0:T(8,128)(2,1)S(1)} all-gather(bf16[64,512]{1,0:T(8,128)(2,1)S(1)} %collective-permute-done), channel_id=4, replica_groups=mesh['y_lo'=2,'z'=8,'x'=4,'y_hi'=4,'core'=2] {'y_lo'}, dimensions={0}, use_global_device_ids=true | all-gather | bytes 196608 | tf_op jit(solution)/shard_map/all_gather | solution.py:58
  88.9 12.9 %all-to-all-done.2 = bf16[8,64,512]{2,1,0:T(8,128)(2,1)S(1)} async-done(((bf16[8,64,512]{2,1,0:T(8,128)(2,1)}), bf16[8,64,512]{2,1,0:T(8,128)(2,1)S(1)}, u32[]{:S(2)}, u32[]{:S(2)}) %all-to-all-start.2) | async-done | bytes 524320 | tf_op jit(solution)/shard_map/all_to_all | solution.py:32
  101.8 2.3 %collective-permute-start.1 = (bf16[512,512]{1,0:T(8,128)(2,1)S(1)}, bf16[512,512]{1,0:T(8,128)(2,1)S(1)}, u32[]{:S(2)}, u32[]{:S(2)}) collective-permute-start(bf16[512,512]{1,0:T(8,128)(2,1)S(1)} %bitcast.61), channel_id=1, source_target_pairs={{0,1},{1,0},{2,3},{3,2},{4,5},{5,4},{6,7},{7,6},{8,9},{9,8},{10,11... | collective-permute-start | bytes 1572872 | tf_op jit(solution)/shard_map/ppermute | solution.py:57
  104.2 10.9 %all-gather.3 = bf16[8,64,512]{2,1,0:T(8,128)(2,1)S(1)} all-gather(bf16[2,64,512]{2,1,0:T(8,128)(2,1)S(1)} %bitcast.66), channel_id=5, replica_groups=mesh['y_lo'=2,'z'=8,'x'=4,'y_hi'=4,'core'=2] {'x'}, dimensions={0}, use_global_device_ids=true | all-gather | bytes 655360 | tf_op jit(solution)/shard_map/all_gather | solution.py:59
  115.1 0.0 copy-start.1
  115.1 0.3 fusion.15
  115.4 0.0 collective-permute-done.1
  115.4 0.3 convolution_add_fusion
  115.7 0.1 copy-done.1
  115.9 0.8 select_convert_fusion.3
  116.7 3.4 %all-to-all-start.3 = ((bf16[4,64,512]{2,1,0:T(8,128)(2,1)}), bf16[4,64,512]{2,1,0:T(8,128)(2,1)S(1)}, u32[]{:S(2)}, u32[]{:S(2)}) async-start(bf16[4,64,512]{2,1,0:T(8,128)(2,1)} %select_convert_fusion.3), calls=%async_computation.3 | async-start | bytes 524288 | tf_op jit(solution)/shard_map/all_to_all | solution.py:38
  120.1 1.0 fusion.10
  121.1 7.0 %all-to-all-done.3 = bf16[4,64,512]{2,1,0:T(8,128)(2,1)S(1)} async-done(((bf16[4,64,512]{2,1,0:T(8,128)(2,1)}), bf16[4,64,512]{2,1,0:T(8,128)(2,1)S(1)}, u32[]{:S(2)}, u32[]{:S(2)}) %all-to-all-start.3) | async-done | bytes 262176 | tf_op jit(solution)/shard_map/all_to_all | solution.py:38
  128.1 0.1 fusion.9
  128.2 19.6 %all_gather.31 = bf16[512,512]{1,0:T(8,128)(2,1)S(1)} all-gather(bf16[64,512]{1,0:T(8,128)(2,1)S(1)} %fusion.9), channel_id=1, replica_groups=mesh['y_lo'=2,'z'=8,'x'=4,'y_hi'=4,'core'=2] {'y_hi','core'}, dimensions={0}, use_global_device_ids=true | all-gather | bytes 589824 | tf_op jit(solution)/shard_map/all_gather | solution.py:76
  147.8 1.0 select_convert_fusion
  148.8 24.3 %all_to_all.26 = bf16[8,64,1536]{2,1,0:T(8,128)(2,1)S(1)} all-to-all(bf16[8,64,1536]{2,1,0:T(8,128)(2,1)S(1)} %get-tuple-element.9), channel_id=1, replica_groups=mesh['y_lo'=2,'z'=8,'x'=4,'y_hi'=4,'core'=2] {'x','y_lo'}, dimensions={0} | all-to-all | bytes 3145728 | tf_op jit(solution)/shard_map/all_to_all | solution.py:38
  173.1 0.0 copy-start
  173.1 0.2 convert_reduce_fusion
  173.3 0.8 copy-done
  174.1 0.8 fusion.4
  (11 shorter events, 0.2 us)
Async XLA Ops:
  3.4 49.1 %all-to-all-start = ((bf16[8,64,1536]{2,1,0:T(8,128)(2,1)}), bf16[8,64,1536]{2,1,0:T(8,128)(2,1)S(1)}, u32[]{:S(2)}, u32[]{:S(2)}) async-start(bf16[8,64,1536]{2,1,0:T(8,128)(2,1)} %select_convert_fusion.1), calls=%async_computation | async-start | bytes 3145728 | tf_op jit(solution)/shard_map/all_to_all | solution.py:48
  80.4 21.5 %all-to-all-start.2 = ((bf16[8,64,512]{2,1,0:T(8,128)(2,1)}), bf16[8,64,512]{2,1,0:T(8,128)(2,1)S(1)}, u32[]{:S(2)}, u32[]{:S(2)}) async-start(bf16[8,64,512]{2,1,0:T(8,128)(2,1)} %broadcast_in_dim.75), calls=%async_computation.2 | async-start | bytes 1048576 | tf_op jit(solution)/shard_map/all_to_all | solution.py:32
  83.9 0.7 collective-permute-start
  101.8 13.6 %collective-permute-start.1 = (bf16[512,512]{1,0:T(8,128)(2,1)S(1)}, bf16[512,512]{1,0:T(8,128)(2,1)S(1)}, u32[]{:S(2)}, u32[]{:S(2)}) collective-permute-start(bf16[512,512]{1,0:T(8,128)(2,1)S(1)} %bitcast.61), channel_id=1, source_target_pairs={{0,1},{1,0},{2,3},{3,2},{4,5},{5,4},{6,7},{7,6},{8,9},{9,8},{10,11... | collective-permute-start | bytes 1572872 | tf_op jit(solution)/shard_map/ppermute | solution.py:57
  115.1 0.8 copy-start.1
  116.7 11.4 %all-to-all-start.3 = ((bf16[4,64,512]{2,1,0:T(8,128)(2,1)}), bf16[4,64,512]{2,1,0:T(8,128)(2,1)S(1)}, u32[]{:S(2)}, u32[]{:S(2)}) async-start(bf16[4,64,512]{2,1,0:T(8,128)(2,1)} %select_convert_fusion.3), calls=%async_computation.3 | async-start | bytes 524288 | tf_op jit(solution)/shard_map/all_to_all | solution.py:38
  173.1 1.0 copy-start

commit v22 on v13

--- a/solution.py
+++ b/solution.py
@@ -73,7 +73,9 @@
     poly = (coef_cubic * gram + coef_quintic * square).astype(jnp.bfloat16)
     poly = lax.all_gather(poly, COL, axis=0, tiled=True)
     product = jnp.dot(poly, by_hi, preferred_element_type=jnp.float32)
-    return coef_linear * x_scaled + sum_pieces(product.reshape(8, rows, cols), LO)
+    mine = jnp.arange(8)[:, None, None] == lax.axis_index(LO)
+    linear = jnp.where(mine, coef_linear * x_scaled, 0.0)
+    return sum_pieces(product.reshape(8, rows, cols) + linear, LO)
 
 
 def solution(mesh):

time: 174 us -> 175 us (level)
    mul x0 -> x1, other arithmetic: none -> 1.92 us  [per_device(): linear = jnp.where(mine, coef_linear * x_scaled, 0.0)]
where the time goes in v22:
time: 175 us; the launch traced here: 174 us
  blocking collectives  115 us (66%)
  waiting for transfers between devices  28.1 us (16%)
  starting transfers between devices  20.8 us (12%)
  other arithmetic  5.29 us (3%)
  matrix products  2.78 us (2%)
  local copies, waits for them, and re-layouts  2.3 us (1%)
    all_to_all x2, blocking collectives, sum_pieces(): lax.all_to_all(jnp.where(mine, 0.0, pieces).astype(jnp.bfloat16), axis, 0...  49.7 us
    all_gather x2, blocking collectives, per_device(): by_lo = [lax.all_gather(pair[y], 'x', axis=0, tiled=True) for y in range(2)]  23.9 us
    all_to_all x2, waiting for transfers between devices, spread(): lax.all_to_all(jnp.broadcast_to(block[None], (8,) + block.shape), axis, 0...  21.1 us
    all_gather x1, blocking collectives, per_device(): poly = lax.all_gather(poly, COL, axis=0, tiled=True)  19.6 us
    all_to_all x2, starting transfers between devices, spread(): lax.all_to_all(jnp.broadcast_to(block[None], (8,) + block.shape), axis, 0...  14.4 us
    all_gather x1, blocking collectives, per_device(): left = lax.all_gather(left, 'x', axis=0).reshape(4, 2, rows, 8 * rows)  10.9 us
    all_to_all x1, waiting for transfers between devices, sum_pieces(): lax.all_to_all(jnp.where(mine, 0.0, pieces).astype(jnp.bfloat16), axis, 0...  7.02 us
    all_gather x1, blocking collectives, per_device(): pair = lax.all_gather(xb, 'y_lo', axis=0)  6.12 us
  transfers between devices with their start and end apart: 5, of which 3 were waited for; matrix products, arithmetic and copies ran while one was open for 1% of the time, Pallas kernels for 0%

profile of v22, /device:TPU:1, one launch (start us, length us, event | category | flops | bytes accessed | tf_op | source)
XLA Modules:
  0.0 174.0 jit_solution(14705464674799853657)
XLA Ops:
  0.0 1.9 %broadcast_multiply_fusion = (f32[64,1536]{1,0:T(8,128)}, bf16[64,1536]{1,0:T(8,128)(2,1)S(1)}) fusion(f32[64,1536]{1,0:T(8,128)} %param.1), kind=kLoop, calls=%fused_computation.12 | loop fusion | flops 196608 | bytes 983040 | tf_op jit(solution)/shard_map/mul | solution.py:77
  1.9 1.3 broadcast_in_dim.71
  3.2 10.9 %all-to-all-start = ((bf16[8,64,1536]{2,1,0:T(8,128)(2,1)}), bf16[8,64,1536]{2,1,0:T(8,128)(2,1)S(1)}, u32[]{:S(2)}, u32[]{:S(2)}) async-start(bf16[8,64,1536]{2,1,0:T(8,128)(2,1)} %broadcast_in_dim.71), calls=%async_computation | async-start | bytes 3145728 | tf_op jit(solution)/shard_map/all_to_all | solution.py:32
  14.1 6.1 %all-gather = bf16[128,1536]{1,0:T(8,128)(2,1)S(1)} all-gather(bf16[64,1536]{1,0:T(8,128)(2,1)S(1)} %get-tuple-element.8), channel_id=2, replica_groups=mesh['y_lo'=2,'z'=8,'x'=4,'y_hi'=4,'core'=2] {'y_lo'}, dimensions={0}, use_global_device_ids=true | all-gather | bytes 589824 | tf_op jit(solution)/shard_map/all_gather | solution.py:47
  20.2 12.6 %all-gather.5 = bf16[256,1536]{1,0:T(8,128)(2,1)S(1)} all-gather(bf16[64,1536]{1,0:T(8,128)(2,1)S(1)} %get-tuple-element.9), channel_id=7, replica_groups=mesh['y_lo'=2,'z'=8,'x'=4,'y_hi'=4,'core'=2] {'x'}, dimensions={0}, use_global_device_ids=true | all-gather | bytes 983040 | tf_op jit(solution)/shard_map/all_gather | solution.py:48
  32.9 11.3 %all-gather.6 = bf16[256,1536]{1,0:T(8,128)(2,1)S(1)} all-gather(bf16[64,1536]{1,0:T(8,128)(2,1)S(1)} %get-tuple-element.10), channel_id=8, replica_groups=mesh['y_lo'=2,'z'=8,'x'=4,'y_hi'=4,'core'=2] {'x'}, dimensions={0}, use_global_device_ids=true | all-gather | bytes 983040 | tf_op jit(solution)/shard_map/all_gather | solution.py:48
  44.2 8.2 %all-to-all-done = bf16[8,64,1536]{2,1,0:T(8,128)(2,1)S(1)} async-done(((bf16[8,64,1536]{2,1,0:T(8,128)(2,1)}), bf16[8,64,1536]{2,1,0:T(8,128)(2,1)S(1)}, u32[]{:S(2)}, u32[]{:S(2)}) %all-to-all-start) | async-done | bytes 1572896 | tf_op jit(solution)/shard_map/all_to_all | solution.py:32
  52.4 0.6 fusion.11
  53.0 0.6 fusion.10
  53.6 0.1 maximum_multiply_fusion
  53.7 0.2 select_convert_fusion.1
  53.9 25.4 %all_to_all.25 = bf16[8,64,512]{2,1,0:T(8,128)(2,1)S(1)} all-to-all(bf16[8,64,512]{2,1,0:T(8,128)(2,1)S(1)} %select_convert_fusion.1), channel_id=1, replica_groups=mesh['y_lo'=2,'z'=8,'x'=4,'y_hi'=4,'core'=2] {'core','y_hi'}, dimensions={0} | all-to-all | bytes 1048576 | tf_op jit(solution)/shard_map/all_to_all | solution.py:38
  79.3 0.1 convert_reduce_fusion.1
  79.4 0.8 broadcast_in_dim.75
  80.2 3.5 %all-to-all-start.2 = ((bf16[8,64,512]{2,1,0:T(8,128)(2,1)}), bf16[8,64,512]{2,1,0:T(8,128)(2,1)S(1)}, u32[]{:S(2)}, u32[]{:S(2)}) async-start(bf16[8,64,512]{2,1,0:T(8,128)(2,1)} %broadcast_in_dim.75), calls=%async_computation.2 | async-start | bytes 1048576 | tf_op jit(solution)/shard_map/all_to_all | solution.py:32
  83.8 0.7 collective-permute-start
  84.4 0.0 collective-permute-done
  84.5 4.3 %all-gather.3 = bf16[128,512]{1,0:T(8,128)(2,1)S(1)} all-gather(bf16[64,512]{1,0:T(8,128)(2,1)S(1)} %collective-permute-done), channel_id=5, replica_groups=mesh['y_lo'=2,'z'=8,'x'=4,'y_hi'=4,'core'=2] {'y_lo'}, dimensions={0}, use_global_device_ids=true | all-gather | bytes 196608 | tf_op jit(solution)/shard_map/all_gather | solution.py:56
  88.8 12.9 %all-to-all-done.2 = bf16[8,64,512]{2,1,0:T(8,128)(2,1)S(1)} async-done(((bf16[8,64,512]{2,1,0:T(8,128)(2,1)}), bf16[8,64,512]{2,1,0:T(8,128)(2,1)S(1)}, u32[]{:S(2)}, u32[]{:S(2)}) %all-to-all-start.2) | async-done | bytes 524320 | tf_op jit(solution)/shard_map/all_to_all | solution.py:32
  101.7 2.3 %collective-permute-start.1 = (bf16[512,512]{1,0:T(8,128)(2,1)S(1)}, bf16[512,512]{1,0:T(8,128)(2,1)S(1)}, u32[]{:S(2)}, u32[]{:S(2)}) collective-permute-start(bf16[512,512]{1,0:T(8,128)(2,1)S(1)} %bitcast.55), channel_id=1, source_target_pairs={{0,1},{1,0},{2,3},{3,2},{4,5},{5,4},{6,7},{7,6},{8,9},{9,8},{10,11... | collective-permute-start | bytes 1572872 | tf_op jit(solution)/shard_map/ppermute | solution.py:55
  104.0 10.9 %all-gather.4 = bf16[8,64,512]{2,1,0:T(8,128)(2,1)S(1)} all-gather(bf16[2,64,512]{2,1,0:T(8,128)(2,1)S(1)} %bitcast.59), channel_id=6, replica_groups=mesh['y_lo'=2,'z'=8,'x'=4,'y_hi'=4,'core'=2] {'x'}, dimensions={0}, use_global_device_ids=true | all-gather | bytes 655360 | tf_op jit(solution)/shard_map/all_gather | solution.py:57
  114.9 0.0 copy-start
  115.0 0.3 fusion.12
  115.3 0.0 collective-permute-done.1
  115.3 0.3 convolution_add_fusion.1
  115.6 0.1 copy-done
  115.7 0.8 select_convert_fusion.2
  116.5 3.4 %all-to-all-start.3 = ((bf16[4,64,512]{2,1,0:T(8,128)(2,1)}), bf16[4,64,512]{2,1,0:T(8,128)(2,1)S(1)}, u32[]{:S(2)}, u32[]{:S(2)}) async-start(bf16[4,64,512]{2,1,0:T(8,128)(2,1)} %select_convert_fusion.2), calls=%async_computation.3 | async-start | bytes 524288 | tf_op jit(solution)/shard_map/all_to_all | solution.py:38
  119.9 1.0 fusion.5
  120.9 7.0 %all-to-all-done.3 = bf16[4,64,512]{2,1,0:T(8,128)(2,1)S(1)} async-done(((bf16[4,64,512]{2,1,0:T(8,128)(2,1)}), bf16[4,64,512]{2,1,0:T(8,128)(2,1)S(1)}, u32[]{:S(2)}, u32[]{:S(2)}) %all-to-all-start.3) | async-done | bytes 262176 | tf_op jit(solution)/shard_map/all_to_all | solution.py:38
  127.9 0.0 copy-start.1
  128.0 0.1 fusion.4
  128.1 19.6 %all_gather.35 = bf16[512,512]{1,0:T(8,128)(2,1)S(1)} all-gather(bf16[64,512]{1,0:T(8,128)(2,1)S(1)} %fusion.4), channel_id=1, replica_groups=mesh['y_lo'=2,'z'=8,'x'=4,'y_hi'=4,'core'=2] {'y_hi','core'}, dimensions={0}, use_global_device_ids=true | all-gather | bytes 589824 | tf_op jit(solution)/shard_map/all_gather | solution.py:74
  147.7 0.0 copy-done.1
  147.7 1.0 select_convert_fusion
  148.7 24.3 %all_to_all.26 = bf16[8,64,1536]{2,1,0:T(8,128)(2,1)S(1)} all-to-all(bf16[8,64,1536]{2,1,0:T(8,128)(2,1)S(1)} %get-tuple-element.11), channel_id=1, replica_groups=mesh['y_lo'=2,'z'=8,'x'=4,'y_hi'=4,'core'=2] {'x','y_lo'}, dimensions={0} | all-to-all | bytes 3145728 | tf_op jit(solution)/shard_map/all_to_all | solution.py:38
  173.0 0.2 convert_reduce_fusion
  173.2 0.8 bitcast_add_fusion
  (10 shorter events, 0.2 us)
Async XLA Ops:
  3.2 49.1 %all-to-all-start = ((bf16[8,64,1536]{2,1,0:T(8,128)(2,1)}), bf16[8,64,1536]{2,1,0:T(8,128)(2,1)S(1)}, u32[]{:S(2)}, u32[]{:S(2)}) async-start(bf16[8,64,1536]{2,1,0:T(8,128)(2,1)} %broadcast_in_dim.71), calls=%async_computation | async-start | bytes 3145728 | tf_op jit(solution)/shard_map/all_to_all | solution.py:32
  80.2 21.5 %all-to-all-start.2 = ((bf16[8,64,512]{2,1,0:T(8,128)(2,1)}), bf16[8,64,512]{2,1,0:T(8,128)(2,1)S(1)}, u32[]{:S(2)}, u32[]{:S(2)}) async-start(bf16[8,64,512]{2,1,0:T(8,128)(2,1)} %broadcast_in_dim.75), calls=%async_computation.2 | async-start | bytes 1048576 | tf_op jit(solution)/shard_map/all_to_all | solution.py:32
  83.8 0.7 collective-permute-start
  101.7 13.6 %collective-permute-start.1 = (bf16[512,512]{1,0:T(8,128)(2,1)S(1)}, bf16[512,512]{1,0:T(8,128)(2,1)S(1)}, u32[]{:S(2)}, u32[]{:S(2)}) collective-permute-start(bf16[512,512]{1,0:T(8,128)(2,1)S(1)} %bitcast.55), channel_id=1, source_target_pairs={{0,1},{1,0},{2,3},{3,2},{4,5},{5,4},{6,7},{7,6},{8,9},{9,8},{10,11... | collective-permute-start | bytes 1572872 | tf_op jit(solution)/shard_map/ppermute | solution.py:55
  114.9 0.8 copy-start
  116.5 11.4 %all-to-all-start.3 = ((bf16[4,64,512]{2,1,0:T(8,128)(2,1)}), bf16[4,64,512]{2,1,0:T(8,128)(2,1)S(1)}, u32[]{:S(2)}, u32[]{:S(2)}) async-start(bf16[4,64,512]{2,1,0:T(8,128)(2,1)} %select_convert_fusion.2), calls=%async_computation.3 | async-start | bytes 524288 | tf_op jit(solution)/shard_map/all_to_all | solution.py:38
  127.9 19.7 %copy-start.1 = (f32[64,1536]{1,0:T(8,128)S(1)}, f32[64,1536]{1,0:T(8,128)}, u32[]{:S(2)}) copy-start(f32[64,1536]{1,0:T(8,128)} %get-tuple-element.7) | copy-start | bytes 1179652

commit v23 on v22

--- a/solution.py
+++ b/solution.py
@@ -74,7 +74,7 @@
     poly = lax.all_gather(poly, COL, axis=0, tiled=True)
     product = jnp.dot(poly, by_hi, preferred_element_type=jnp.float32)
     mine = jnp.arange(8)[:, None, None] == lax.axis_index(LO)
-    linear = jnp.where(mine, coef_linear * x_scaled, 0.0)
+    linear = coef_linear * jnp.where(mine, x_scaled, 0.0)
     return sum_pieces(product.reshape(8, rows, cols) + linear, LO)
 
 

time: 175 us -> 174 us (level)
    mul x1 -> x0, other arithmetic: 1.92 us -> none  [per_device(): linear = jnp.where(mine, coef_linear * x_scaled, 0.0)]
where the time goes in v23:
time: 174 us; the launch traced here: 173 us
  blocking collectives  115 us (66%)
  waiting for transfers between devices  28.1 us (16%)
  starting transfers between devices  20.8 us (12%)
  other arithmetic  4.4 us (3%)
  matrix products  2.95 us (2%)
  local copies, waits for them, and re-layouts  2.25 us (1%)
    all_to_all x2, blocking collectives, sum_pieces(): lax.all_to_all(jnp.where(mine, 0.0, pieces).astype(jnp.bfloat16), axis, 0...  49.7 us
    all_gather x2, blocking collectives, per_device(): by_lo = [lax.all_gather(pair[y], 'x', axis=0, tiled=True) for y in range(2)]  23.9 us
    all_to_all x2, waiting for transfers between devices, spread(): lax.all_to_all(jnp.broadcast_to(block[None], (8,) + block.shape), axis, 0...  21.1 us
    all_gather x1, blocking collectives, per_device(): poly = lax.all_gather(poly, COL, axis=0, tiled=True)  19.6 us
    all_to_all x2, starting transfers between devices, spread(): lax.all_to_all(jnp.broadcast_to(block[None], (8,) + block.shape), axis, 0...  14.4 us
    all_gather x1, blocking collectives, per_device(): left = lax.all_gather(left, 'x', axis=0).reshape(4, 2, rows, 8 * rows)  10.9 us
    all_to_all x1, waiting for transfers between devices, sum_pieces(): lax.all_to_all(jnp.where(mine, 0.0, pieces).astype(jnp.bfloat16), axis, 0...  7.01 us
    all_gather x1, blocking collectives, per_device(): pair = lax.all_gather(xb, 'y_lo', axis=0)  6.12 us
  transfers between devices with their start and end apart: 5, of which 3 were waited for; matrix products, arithmetic and copies ran while one was open for 1% of the time, Pallas kernels for 0%

profile of v23, /device:TPU:1, one launch (start us, length us, event | category | flops | bytes accessed | tf_op | source)
XLA Modules:
  0.0 173.3 jit_solution(1108818715039043714)
XLA Ops:
  0.0 1.0 convert_element_type.36
  1.0 1.3 broadcast_in_dim.71
  2.3 10.9 %all-to-all-start = ((bf16[8,64,1536]{2,1,0:T(8,128)(2,1)}), bf16[8,64,1536]{2,1,0:T(8,128)(2,1)S(1)}, u32[]{:S(2)}, u32[]{:S(2)}) async-start(bf16[8,64,1536]{2,1,0:T(8,128)(2,1)} %broadcast_in_dim.71), calls=%async_computation | async-start | bytes 3145728 | tf_op jit(solution)/shard_map/all_to_all | solution.py:32
  13.2 6.1 %all-gather = bf16[128,1536]{1,0:T(8,128)(2,1)S(1)} all-gather(bf16[64,1536]{1,0:T(8,128)(2,1)S(1)} %convert_element_type.36), channel_id=2, replica_groups=mesh['y_lo'=2,'z'=8,'x'=4,'y_hi'=4,'core'=2] {'y_lo'}, dimensions={0}, use_global_device_ids=true | all-gather | bytes 589824 | tf_op jit(solution)/shard_map/all_gather | solution.py:47
  19.3 12.6 %all-gather.5 = bf16[256,1536]{1,0:T(8,128)(2,1)S(1)} all-gather(bf16[64,1536]{1,0:T(8,128)(2,1)S(1)} %get-tuple-element.7), channel_id=7, replica_groups=mesh['y_lo'=2,'z'=8,'x'=4,'y_hi'=4,'core'=2] {'x'}, dimensions={0}, use_global_device_ids=true | all-gather | bytes 983040 | tf_op jit(solution)/shard_map/all_gather | solution.py:48
  32.0 11.3 %all-gather.6 = bf16[256,1536]{1,0:T(8,128)(2,1)S(1)} all-gather(bf16[64,1536]{1,0:T(8,128)(2,1)S(1)} %get-tuple-element.8), channel_id=8, replica_groups=mesh['y_lo'=2,'z'=8,'x'=4,'y_hi'=4,'core'=2] {'x'}, dimensions={0}, use_global_device_ids=true | all-gather | bytes 983040 | tf_op jit(solution)/shard_map/all_gather | solution.py:48
  43.3 8.2 %all-to-all-done = bf16[8,64,1536]{2,1,0:T(8,128)(2,1)S(1)} async-done(((bf16[8,64,1536]{2,1,0:T(8,128)(2,1)}), bf16[8,64,1536]{2,1,0:T(8,128)(2,1)S(1)}, u32[]{:S(2)}, u32[]{:S(2)}) %all-to-all-start) | async-done | bytes 1572896 | tf_op jit(solution)/shard_map/all_to_all | solution.py:32
  51.4 0.6 fusion.11
  52.0 0.6 fusion.10
  52.6 0.1 maximum_multiply_fusion
  52.8 0.2 select_convert_fusion.1
  52.9 25.4 %all_to_all.25 = bf16[8,64,512]{2,1,0:T(8,128)(2,1)S(1)} all-to-all(bf16[8,64,512]{2,1,0:T(8,128)(2,1)S(1)} %select_convert_fusion.1), channel_id=1, replica_groups=mesh['y_lo'=2,'z'=8,'x'=4,'y_hi'=4,'core'=2] {'core','y_hi'}, dimensions={0} | all-to-all | bytes 1048576 | tf_op jit(solution)/shard_map/all_to_all | solution.py:38
  78.4 0.1 convert_reduce_fusion.1
  78.5 0.8 broadcast_in_dim.75
  79.3 3.5 %all-to-all-start.2 = ((bf16[8,64,512]{2,1,0:T(8,128)(2,1)}), bf16[8,64,512]{2,1,0:T(8,128)(2,1)S(1)}, u32[]{:S(2)}, u32[]{:S(2)}) async-start(bf16[8,64,512]{2,1,0:T(8,128)(2,1)} %broadcast_in_dim.75), calls=%async_computation.2 | async-start | bytes 1048576 | tf_op jit(solution)/shard_map/all_to_all | solution.py:32
  82.8 0.7 collective-permute-start
  83.5 0.0 collective-permute-done
  83.5 4.3 %all-gather.3 = bf16[128,512]{1,0:T(8,128)(2,1)S(1)} all-gather(bf16[64,512]{1,0:T(8,128)(2,1)S(1)} %collective-permute-done), channel_id=5, replica_groups=mesh['y_lo'=2,'z'=8,'x'=4,'y_hi'=4,'core'=2] {'y_lo'}, dimensions={0}, use_global_device_ids=true | all-gather | bytes 196608 | tf_op jit(solution)/shard_map/all_gather | solution.py:56
  87.9 12.9 %all-to-all-done.2 = bf16[8,64,512]{2,1,0:T(8,128)(2,1)S(1)} async-done(((bf16[8,64,512]{2,1,0:T(8,128)(2,1)}), bf16[8,64,512]{2,1,0:T(8,128)(2,1)S(1)}, u32[]{:S(2)}, u32[]{:S(2)}) %all-to-all-start.2) | async-done | bytes 524320 | tf_op jit(solution)/shard_map/all_to_all | solution.py:32
  100.8 2.3 %collective-permute-start.1 = (bf16[512,512]{1,0:T(8,128)(2,1)S(1)}, bf16[512,512]{1,0:T(8,128)(2,1)S(1)}, u32[]{:S(2)}, u32[]{:S(2)}) collective-permute-start(bf16[512,512]{1,0:T(8,128)(2,1)S(1)} %bitcast.55), channel_id=1, source_target_pairs={{0,1},{1,0},{2,3},{3,2},{4,5},{5,4},{6,7},{7,6},{8,9},{9,8},{10,11... | collective-permute-start | bytes 1572872 | tf_op jit(solution)/shard_map/ppermute | solution.py:55
  103.1 10.9 %all-gather.4 = bf16[8,64,512]{2,1,0:T(8,128)(2,1)S(1)} all-gather(bf16[2,64,512]{2,1,0:T(8,128)(2,1)S(1)} %bitcast.59), channel_id=6, replica_groups=mesh['y_lo'=2,'z'=8,'x'=4,'y_hi'=4,'core'=2] {'x'}, dimensions={0}, use_global_device_ids=true | all-gather | bytes 655360 | tf_op jit(solution)/shard_map/all_gather | solution.py:57
  114.0 0.0 copy-start
  114.0 0.3 fusion.12
  114.4 0.0 collective-permute-done.1
  114.4 0.3 convolution_add_fusion.1
  114.7 0.1 copy-done
  114.8 0.8 select_convert_fusion.2
  115.6 3.4 %all-to-all-start.3 = ((bf16[4,64,512]{2,1,0:T(8,128)(2,1)}), bf16[4,64,512]{2,1,0:T(8,128)(2,1)S(1)}, u32[]{:S(2)}, u32[]{:S(2)}) async-start(bf16[4,64,512]{2,1,0:T(8,128)(2,1)} %select_convert_fusion.2), calls=%async_computation.3 | async-start | bytes 524288 | tf_op jit(solution)/shard_map/all_to_all | solution.py:38
  119.0 1.0 fusion.5
  120.0 7.0 %all-to-all-done.3 = bf16[4,64,512]{2,1,0:T(8,128)(2,1)S(1)} async-done(((bf16[4,64,512]{2,1,0:T(8,128)(2,1)}), bf16[4,64,512]{2,1,0:T(8,128)(2,1)S(1)}, u32[]{:S(2)}, u32[]{:S(2)}) %all-to-all-start.3) | async-done | bytes 262176 | tf_op jit(solution)/shard_map/all_to_all | solution.py:38
  127.0 0.0 copy-start.1
  127.0 0.1 fusion.4
  127.1 19.6 %all_gather.35 = bf16[512,512]{1,0:T(8,128)(2,1)S(1)} all-gather(bf16[64,512]{1,0:T(8,128)(2,1)S(1)} %fusion.4), channel_id=1, replica_groups=mesh['y_lo'=2,'z'=8,'x'=4,'y_hi'=4,'core'=2] {'y_hi','core'}, dimensions={0}, use_global_device_ids=true | all-gather | bytes 589824 | tf_op jit(solution)/shard_map/all_gather | solution.py:74
  146.8 0.0 copy-done.1
  146.8 1.2 select_convert_fusion
  147.9 24.3 %all_to_all.26 = bf16[8,64,1536]{2,1,0:T(8,128)(2,1)S(1)} all-to-all(bf16[8,64,1536]{2,1,0:T(8,128)(2,1)S(1)} %get-tuple-element.9), channel_id=1, replica_groups=mesh['y_lo'=2,'z'=8,'x'=4,'y_hi'=4,'core'=2] {'x','y_lo'}, dimensions={0} | all-to-all | bytes 3145728 | tf_op jit(solution)/shard_map/all_to_all | solution.py:38
  172.2 0.2 convert_reduce_fusion
  172.4 0.8 bitcast_add_fusion
  (10 shorter events, 0.2 us)
Async XLA Ops:
  2.3 49.1 %all-to-all-start = ((bf16[8,64,1536]{2,1,0:T(8,128)(2,1)}), bf16[8,64,1536]{2,1,0:T(8,128)(2,1)S(1)}, u32[]{:S(2)}, u32[]{:S(2)}) async-start(bf16[8,64,1536]{2,1,0:T(8,128)(2,1)} %broadcast_in_dim.71), calls=%async_computation | async-start | bytes 3145728 | tf_op jit(solution)/shard_map/all_to_all | solution.py:32
  79.3 21.5 %all-to-all-start.2 = ((bf16[8,64,512]{2,1,0:T(8,128)(2,1)}), bf16[8,64,512]{2,1,0:T(8,128)(2,1)S(1)}, u32[]{:S(2)}, u32[]{:S(2)}) async-start(bf16[8,64,512]{2,1,0:T(8,128)(2,1)} %broadcast_in_dim.75), calls=%async_computation.2 | async-start | bytes 1048576 | tf_op jit(solution)/shard_map/all_to_all | solution.py:32
  82.8 0.7 collective-permute-start
  100.8 13.6 %collective-permute-start.1 = (bf16[512,512]{1,0:T(8,128)(2,1)S(1)}, bf16[512,512]{1,0:T(8,128)(2,1)S(1)}, u32[]{:S(2)}, u32[]{:S(2)}) collective-permute-start(bf16[512,512]{1,0:T(8,128)(2,1)S(1)} %bitcast.55), channel_id=1, source_target_pairs={{0,1},{1,0},{2,3},{3,2},{4,5},{5,4},{6,7},{7,6},{8,9},{9,8},{10,11... | collective-permute-start | bytes 1572872 | tf_op jit(solution)/shard_map/ppermute | solution.py:55
  114.0 0.8 copy-start
  115.6 11.4 %all-to-all-start.3 = ((bf16[4,64,512]{2,1,0:T(8,128)(2,1)}), bf16[4,64,512]{2,1,0:T(8,128)(2,1)S(1)}, u32[]{:S(2)}, u32[]{:S(2)}) async-start(bf16[4,64,512]{2,1,0:T(8,128)(2,1)} %select_convert_fusion.2), calls=%async_computation.3 | async-start | bytes 524288 | tf_op jit(solution)/shard_map/all_to_all | solution.py:38
  127.0 19.7 %copy-start.1 = (f32[64,1536]{1,0:T(8,128)S(1)}, f32[64,1536]{1,0:T(8,128)}, u32[]{:S(2)}) copy-start(f32[64,1536]{1,0:T(8,128)} %param.1) | copy-start | bytes 1179652

commit v24 on v23

--- a/solution.py
+++ b/solution.py
@@ -42,8 +42,9 @@
 
 def per_device(x_scaled):
     rows, cols = x_scaled.shape
-    xb = x_scaled.astype(jnp.bfloat16)
-    by_hi = spread(xb, "z").reshape(8 * rows, cols)
+    copies = lax.optimization_barrier(jnp.broadcast_to(x_scaled.astype(jnp.bfloat16)[None], (8, rows, cols)))
+    xb = copies[0]
+    by_hi = lax.all_to_all(copies, "z", 0, 0).reshape(8 * rows, cols)
     pair = lax.all_gather(xb, "y_lo", axis=0)
     by_lo = [lax.all_gather(pair[y], "x", axis=0, tiled=True) for y in range(2)]
 

time: 174 us -> 174 us (level)
    all_to_all x0 -> x1, starting transfers between devices: none -> 10.9 us  [per_device(): by_hi = lax.all_to_all(copies, 'z', 0, 0).reshape(8 * rows, cols)]
    all_to_all x2 -> x1, starting transfers between devices: 14.4 us -> 3.49 us  [spread(): lax.all_to_all(jnp.broadcast_to(block[None], (8,) + block.shape), axis, 0...]
    all_to_all x2 -> x1, waiting for transfers between devices: 21.1 us -> 12.9 us  [spread(): lax.all_to_all(jnp.broadcast_to(block[None], (8,) + block.shape), axis, 0...]
    all_to_all x0 -> x1, waiting for transfers between devices: none -> 7.38 us  [per_device(): by_hi = lax.all_to_all(copies, 'z', 0, 0).reshape(8 * rows, cols)]
where the time goes in v24:
time: 174 us; the launch traced here: 173 us
  blocking collectives  114 us (66%)
  waiting for transfers between devices  27.3 us (16%)
  starting transfers between devices  20.8 us (12%)
  other arithmetic  4.4 us (3%)
  local copies, waits for them, and re-layouts  3.19 us (2%)
  matrix products  2.95 us (2%)
    all_to_all x2, blocking collectives, sum_pieces(): lax.all_to_all(jnp.where(mine, 0.0, pieces).astype(jnp.bfloat16), axis, 0...  49.7 us
    all_gather x2, blocking collectives, per_device(): by_lo = [lax.all_gather(pair[y], 'x', axis=0, tiled=True) for y in range(2)]  23.8 us
    all_gather x1, blocking collectives, per_device(): poly = lax.all_gather(poly, COL, axis=0, tiled=True)  19.6 us
    all_to_all x1, waiting for transfers between devices, spread(): lax.all_to_all(jnp.broadcast_to(block[None], (8,) + block.shape), axis, 0...  12.9 us
    all_gather x1, blocking collectives, per_device(): left = lax.all_gather(left, 'x', axis=0).reshape(4, 2, rows, 8 * rows)  10.9 us
    all_to_all x1, starting transfers between devices, per_device(): by_hi = lax.all_to_all(copies, 'z', 0, 0).reshape(8 * rows, cols)  10.9 us
    all_to_all x1, waiting for transfers between devices, per_device(): by_hi = lax.all_to_all(copies, 'z', 0, 0).reshape(8 * rows, cols)  7.38 us
    all_to_all x1, waiting for transfers between devices, sum_pieces(): lax.all_to_all(jnp.where(mine, 0.0, pieces).astype(jnp.bfloat16), axis, 0...  7.01 us
  transfers between devices with their start and end apart: 5, of which 3 were waited for; matrix products, arithmetic and copies ran while one was open for 1% of the time, Pallas kernels for 0%

profile of v24, /device:TPU:1, one launch (start us, length us, event | category | flops | bytes accessed | tf_op | source)
XLA Modules:
  0.0 173.3 jit_solution(13771269366781320248)
XLA Ops:
  0.0 1.0 convert_element_type.36
  1.0 1.3 broadcast_in_dim.71
  2.3 10.9 %all-to-all-start = ((bf16[8,64,1536]{2,1,0:T(8,128)(2,1)}), bf16[8,64,1536]{2,1,0:T(8,128)(2,1)S(1)}, u32[]{:S(2)}, u32[]{:S(2)}) async-start(bf16[8,64,1536]{2,1,0:T(8,128)(2,1)} %broadcast_in_dim.71), calls=%async_computation | async-start | bytes 3145728 | tf_op jit(solution)/shard_map/all_to_all | solution.py:47
  13.2 0.9 slice.22
  14.1 6.1 %all_gather.24 = bf16[2,64,1536]{2,1,0:T(8,128)(2,1)S(1)} all-gather(bf16[1,64,1536]{2,1,0:T(8,128)(2,1)S(1)} %slice.22), channel_id=1, replica_groups=mesh['y_lo'=2,'z'=8,'x'=4,'y_hi'=4,'core'=2] {'y_lo'}, dimensions={0}, use_global_device_ids=true | all-gather | bytes 589824 | tf_op jit(solution)/shard_map/all_gather | solution.py:48
  20.3 12.6 %all-gather = bf16[1,256,1536]{2,1,0:T(8,128)(2,1)S(1)} all-gather(bf16[1,64,1536]{2,1,0:T(8,128)(2,1)S(1)} %get-tuple-element.7), channel_id=2, replica_groups=mesh['y_lo'=2,'z'=8,'x'=4,'y_hi'=4,'core'=2] {'x'}, dimensions={1}, use_global_device_ids=true | all-gather | bytes 983040 | tf_op jit(solution)/shard_map/all_gather | solution.py:49
  32.9 11.1 %all-gather.1 = bf16[1,256,1536]{2,1,0:T(8,128)(2,1)S(1)} all-gather(bf16[1,64,1536]{2,1,0:T(8,128)(2,1)S(1)} %get-tuple-element.8), channel_id=3, replica_groups=mesh['y_lo'=2,'z'=8,'x'=4,'y_hi'=4,'core'=2] {'x'}, dimensions={1}, use_global_device_ids=true | all-gather | bytes 983040 | tf_op jit(solution)/shard_map/all_gather | solution.py:49
  44.1 7.4 %all-to-all-done = bf16[8,64,1536]{2,1,0:T(8,128)(2,1)S(1)} async-done(((bf16[8,64,1536]{2,1,0:T(8,128)(2,1)}), bf16[8,64,1536]{2,1,0:T(8,128)(2,1)S(1)}, u32[]{:S(2)}, u32[]{:S(2)}) %all-to-all-start) | async-done | bytes 1572896 | tf_op jit(solution)/shard_map/all_to_all | solution.py:47
  51.4 0.6 fusion.2
  52.0 0.6 fusion
  52.6 0.1 maximum_multiply_fusion
  52.8 0.2 select_convert_fusion.1
  52.9 25.4 %all_to_all.25 = bf16[8,64,512]{2,1,0:T(8,128)(2,1)S(1)} all-to-all(bf16[8,64,512]{2,1,0:T(8,128)(2,1)S(1)} %select_convert_fusion.1), channel_id=1, replica_groups=mesh['y_lo'=2,'z'=8,'x'=4,'y_hi'=4,'core'=2] {'core','y_hi'}, dimensions={0} | all-to-all | bytes 1048576 | tf_op jit(solution)/shard_map/all_to_all | solution.py:38
  78.4 0.1 convert_reduce_fusion.1
  78.5 0.8 broadcast_in_dim.75
  79.3 3.5 %all-to-all-start.2 = ((bf16[8,64,512]{2,1,0:T(8,128)(2,1)}), bf16[8,64,512]{2,1,0:T(8,128)(2,1)S(1)}, u32[]{:S(2)}, u32[]{:S(2)}) async-start(bf16[8,64,512]{2,1,0:T(8,128)(2,1)} %broadcast_in_dim.75), calls=%async_computation.2 | async-start | bytes 1048576 | tf_op jit(solution)/shard_map/all_to_all | solution.py:32
  82.8 0.7 collective-permute-start
  83.5 0.0 collective-permute-done
  83.5 4.3 %all-gather.2 = bf16[128,512]{1,0:T(8,128)(2,1)S(1)} all-gather(bf16[64,512]{1,0:T(8,128)(2,1)S(1)} %collective-permute-done), channel_id=4, replica_groups=mesh['y_lo'=2,'z'=8,'x'=4,'y_hi'=4,'core'=2] {'y_lo'}, dimensions={0}, use_global_device_ids=true | all-gather | bytes 196608 | tf_op jit(solution)/shard_map/all_gather | solution.py:57
  87.9 12.9 %all-to-all-done.2 = bf16[8,64,512]{2,1,0:T(8,128)(2,1)S(1)} async-done(((bf16[8,64,512]{2,1,0:T(8,128)(2,1)}), bf16[8,64,512]{2,1,0:T(8,128)(2,1)S(1)}, u32[]{:S(2)}, u32[]{:S(2)}) %all-to-all-start.2) | async-done | bytes 524320 | tf_op jit(solution)/shard_map/all_to_all | solution.py:32
  100.8 2.3 %collective-permute-start.1 = (bf16[512,512]{1,0:T(8,128)(2,1)S(1)}, bf16[512,512]{1,0:T(8,128)(2,1)S(1)}, u32[]{:S(2)}, u32[]{:S(2)}) collective-permute-start(bf16[512,512]{1,0:T(8,128)(2,1)S(1)} %bitcast.59), channel_id=1, source_target_pairs={{0,1},{1,0},{2,3},{3,2},{4,5},{5,4},{6,7},{7,6},{8,9},{9,8},{10,11... | collective-permute-start | bytes 1572872 | tf_op jit(solution)/shard_map/ppermute | solution.py:56
  103.1 10.9 %all-gather.3 = bf16[8,64,512]{2,1,0:T(8,128)(2,1)S(1)} all-gather(bf16[2,64,512]{2,1,0:T(8,128)(2,1)S(1)} %bitcast.63), channel_id=5, replica_groups=mesh['y_lo'=2,'z'=8,'x'=4,'y_hi'=4,'core'=2] {'x'}, dimensions={0}, use_global_device_ids=true | all-gather | bytes 655360 | tf_op jit(solution)/shard_map/all_gather | solution.py:58
  114.0 0.0 copy-start
  114.0 0.3 fusion.14
  114.4 0.0 collective-permute-done.1
  114.4 0.3 convolution_add_fusion.1
  114.7 0.1 copy-done
  114.8 0.8 select_convert_fusion.2
  115.6 3.4 %all-to-all-start.3 = ((bf16[4,64,512]{2,1,0:T(8,128)(2,1)}), bf16[4,64,512]{2,1,0:T(8,128)(2,1)S(1)}, u32[]{:S(2)}, u32[]{:S(2)}) async-start(bf16[4,64,512]{2,1,0:T(8,128)(2,1)} %select_convert_fusion.2), calls=%async_computation.3 | async-start | bytes 524288 | tf_op jit(solution)/shard_map/all_to_all | solution.py:38
  119.0 1.0 fusion.9
  120.0 7.0 %all-to-all-done.3 = bf16[4,64,512]{2,1,0:T(8,128)(2,1)S(1)} async-done(((bf16[4,64,512]{2,1,0:T(8,128)(2,1)}), bf16[4,64,512]{2,1,0:T(8,128)(2,1)S(1)}, u32[]{:S(2)}, u32[]{:S(2)}) %all-to-all-start.3) | async-done | bytes 262176 | tf_op jit(solution)/shard_map/all_to_all | solution.py:38
  127.0 0.0 copy-start.1
  127.0 0.1 fusion.8
  127.1 19.6 %all_gather.31 = bf16[512,512]{1,0:T(8,128)(2,1)S(1)} all-gather(bf16[64,512]{1,0:T(8,128)(2,1)S(1)} %fusion.8), channel_id=1, replica_groups=mesh['y_lo'=2,'z'=8,'x'=4,'y_hi'=4,'core'=2] {'y_hi','core'}, dimensions={0}, use_global_device_ids=true | all-gather | bytes 589824 | tf_op jit(solution)/shard_map/all_gather | solution.py:75
  146.8 0.0 copy-done.1
  146.8 1.2 select_convert_fusion
  147.9 24.3 %all_to_all.26 = bf16[8,64,1536]{2,1,0:T(8,128)(2,1)S(1)} all-to-all(bf16[8,64,1536]{2,1,0:T(8,128)(2,1)S(1)} %get-tuple-element.9), channel_id=1, replica_groups=mesh['y_lo'=2,'z'=8,'x'=4,'y_hi'=4,'core'=2] {'x','y_lo'}, dimensions={0} | all-to-all | bytes 3145728 | tf_op jit(solution)/shard_map/all_to_all | solution.py:38
  172.2 0.2 convert_reduce_fusion
  172.4 0.8 bitcast_add_fusion
  (10 shorter events, 0.2 us)
Async XLA Ops:
  2.3 49.1 %all-to-all-start = ((bf16[8,64,1536]{2,1,0:T(8,128)(2,1)}), bf16[8,64,1536]{2,1,0:T(8,128)(2,1)S(1)}, u32[]{:S(2)}, u32[]{:S(2)}) async-start(bf16[8,64,1536]{2,1,0:T(8,128)(2,1)} %broadcast_in_dim.71), calls=%async_computation | async-start | bytes 3145728 | tf_op jit(solution)/shard_map/all_to_all | solution.py:47
  79.3 21.5 %all-to-all-start.2 = ((bf16[8,64,512]{2,1,0:T(8,128)(2,1)}), bf16[8,64,512]{2,1,0:T(8,128)(2,1)S(1)}, u32[]{:S(2)}, u32[]{:S(2)}) async-start(bf16[8,64,512]{2,1,0:T(8,128)(2,1)} %broadcast_in_dim.75), calls=%async_computation.2 | async-start | bytes 1048576 | tf_op jit(solution)/shard_map/all_to_all | solution.py:32
  82.8 0.7 collective-permute-start
  100.8 13.6 %collective-permute-start.1 = (bf16[512,512]{1,0:T(8,128)(2,1)S(1)}, bf16[512,512]{1,0:T(8,128)(2,1)S(1)}, u32[]{:S(2)}, u32[]{:S(2)}) collective-permute-start(bf16[512,512]{1,0:T(8,128)(2,1)S(1)} %bitcast.59), channel_id=1, source_target_pairs={{0,1},{1,0},{2,3},{3,2},{4,5},{5,4},{6,7},{7,6},{8,9},{9,8},{10,11... | collective-permute-start | bytes 1572872 | tf_op jit(solution)/shard_map/ppermute | solution.py:56
  114.0 0.8 copy-start
  115.6 11.4 %all-to-all-start.3 = ((bf16[4,64,512]{2,1,0:T(8,128)(2,1)}), bf16[4,64,512]{2,1,0:T(8,128)(2,1)S(1)}, u32[]{:S(2)}, u32[]{:S(2)}) async-start(bf16[4,64,512]{2,1,0:T(8,128)(2,1)} %select_convert_fusion.2), calls=%async_computation.3 | async-start | bytes 524288 | tf_op jit(solution)/shard_map/all_to_all | solution.py:38
  127.0 19.7 %copy-start.1 = (f32[64,1536]{1,0:T(8,128)S(1)}, f32[64,1536]{1,0:T(8,128)}, u32[]{:S(2)}) copy-start(f32[64,1536]{1,0:T(8,128)} %param.1) | copy-start | bytes 1179652

commit v25 on v23

--- a/solution.py
+++ b/solution.py
@@ -32,10 +32,10 @@
     return lax.all_to_all(jnp.broadcast_to(block[None], (8,) + block.shape), axis, 0, 0)
 
 
-def sum_pieces(pieces, axis):
+def sum_pieces(pieces, axis, zero=0.0):
     me = lax.axis_index(axis)
     mine = jnp.arange(pieces.shape[0])[:, None, None] == me
-    arrived = lax.all_to_all(jnp.where(mine, 0.0, pieces).astype(jnp.bfloat16), axis, 0, 0)
+    arrived = lax.all_to_all(jnp.where(mine, zero, pieces).astype(jnp.bfloat16), axis, 0, 0)
     own = lax.dynamic_slice(pieces, (me, 0, 0), (1,) + pieces.shape[1:], allow_negative_indices=False)[0]
     return own + arrived.astype(jnp.float32).sum(0)
 
@@ -61,13 +61,12 @@
     square = jnp.dot(own, right, preferred_element_type=jnp.float32) + jnp.dot(
         other, right_other, preferred_element_type=jnp.float32
     )
-    square = sum_pieces(square.reshape(4, rows, 8 * rows), "y_hi")
-
-    place = (lax.axis_index("y_hi"), core, 0, 0)
-    at_home = lax.dynamic_slice(left, place, (1, 1, rows, 8 * rows), allow_negative_indices=False)[0, 0]
+    place = (lax.axis_index("y_hi") * rows, 0)
+    at_home = lax.dynamic_slice(own, place, (rows, 8 * rows), allow_negative_indices=False)
     column = lax.broadcasted_iota(jnp.int32, at_home.shape, 1) - lax.axis_index("z") * rows
     on_diagonal = column == lax.broadcasted_iota(jnp.int32, at_home.shape, 0)
     diagonal = jnp.where(on_diagonal, at_home.astype(jnp.float32), 0.0).sum(1, keepdims=True)
+    square = sum_pieces(square.reshape(4, rows, 8 * rows), "y_hi", 0.0 * diagonal[0, 0])
     square = square + rest_of(gram) * (2.0 * diagonal)
 
     poly = (coef_cubic * gram + coef_quintic * square).astype(jnp.bfloat16)

time: 174 us -> 176 us (1.011)
  waiting for transfers between devices: 28.1 us -> 17 us
  blocking collectives: 115 us -> 124 us
  starting transfers between devices: 20.8 us -> 25 us
    all_to_all x2, waiting for transfers between devices: 21.1 us -> 8.19 us  [spread(): lax.all_to_all(jnp.broadcast_to(block[None], (8,) + block.shape), axis, 0...]
    all_gather x1, blocking collectives: 10.9 us -> 21.9 us  [per_device(): left = lax.all_gather(left, 'x', axis=0).reshape(4, 2, rows, 8 * rows)]
    ppermute x1, starting transfers between devices: 2.35 us -> 6.55 us  [per_device(): right_other = lax.ppermute(right, 'core', [(0, 1), (1, 0)])]
    all_to_all x1, waiting for transfers between devices: 7.01 us -> 8.8 us  [sum_pieces(): lax.all_to_all(jnp.where(mine, zero, pieces).astype(jnp.bfloat16), axis,...]
  transfers between devices with their start and end apart: 5 -> 5, of which waited for: 3 -> 2; matrix products, arithmetic and copies ran while one was open for 1% -> 1% of each run, Pallas kernels for 0% -> 0%
where the time goes in v25:
time: 176 us
  blocking collectives  124 us (70%)
  starting transfers between devices  25 us (14%)
  waiting for transfers between devices  17 us (10%)
  other arithmetic  4.61 us (3%)
  matrix products  2.96 us (2%)
  local copies, waits for them, and re-layouts  2.17 us (1%)
    all_to_all x2, blocking collectives, sum_pieces(): lax.all_to_all(jnp.where(mine, zero, pieces).astype(jnp.bfloat16), axis,...  49.3 us
    all_gather x2, blocking collectives, per_device(): by_lo = [lax.all_gather(pair[y], 'x', axis=0, tiled=True) for y in range(2)]  23.9 us
    all_gather x1, blocking collectives, per_device(): left = lax.all_gather(left, 'x', axis=0).reshape(4, 2, rows, 8 * rows)  21.9 us
    all_gather x1, blocking collectives, per_device(): poly = lax.all_gather(poly, COL, axis=0, tiled=True)  18.2 us
    all_to_all x2, starting transfers between devices, spread(): lax.all_to_all(jnp.broadcast_to(block[None], (8,) + block.shape), axis, 0...  14.4 us
    all_to_all x1, waiting for transfers between devices, sum_pieces(): lax.all_to_all(jnp.where(mine, zero, pieces).astype(jnp.bfloat16), axis,...  8.8 us
    all_to_all x2, waiting for transfers between devices, spread(): lax.all_to_all(jnp.broadcast_to(block[None], (8,) + block.shape), axis, 0...  8.19 us
    ppermute x1, starting transfers between devices, per_device(): right_other = lax.ppermute(right, 'core', [(0, 1), (1, 0)])  6.55 us
  transfers between devices with their start and end apart: 5, of which 2 were waited for; matrix products, arithmetic and copies ran while one was open for 1% of the time, Pallas kernels for 0%

profile of v25, /device:TPU:1, one launch (start us, length us, event | category | flops | bytes accessed | tf_op | source)
XLA Modules:
  0.0 175.7 jit_solution(18165617220734564761)
XLA Ops:
  0.0 1.0 convert_element_type.33
  1.0 1.3 broadcast_in_dim.71
  2.3 10.9 %all-to-all-start = ((bf16[8,64,1536]{2,1,0:T(8,128)(2,1)}), bf16[8,64,1536]{2,1,0:T(8,128)(2,1)S(1)}, u32[]{:S(2)}, u32[]{:S(2)}) async-start(bf16[8,64,1536]{2,1,0:T(8,128)(2,1)} %broadcast_in_dim.71), calls=%async_computation | async-start | bytes 3145728 | tf_op jit(solution)/shard_map/all_to_all | solution.py:32
  13.2 6.1 %all-gather = bf16[128,1536]{1,0:T(8,128)(2,1)S(1)} all-gather(bf16[64,1536]{1,0:T(8,128)(2,1)S(1)} %convert_element_type.33), channel_id=2, replica_groups=mesh['y_lo'=2,'z'=8,'x'=4,'y_hi'=4,'core'=2] {'y_lo'}, dimensions={0}, use_global_device_ids=true | all-gather | bytes 589824 | tf_op jit(solution)/shard_map/all_gather | solution.py:47
  19.3 12.6 %all-gather.5 = bf16[256,1536]{1,0:T(8,128)(2,1)S(1)} all-gather(bf16[64,1536]{1,0:T(8,128)(2,1)S(1)} %get-tuple-element.7), channel_id=7, replica_groups=mesh['y_lo'=2,'z'=8,'x'=4,'y_hi'=4,'core'=2] {'x'}, dimensions={0}, use_global_device_ids=true | all-gather | bytes 983040 | tf_op jit(solution)/shard_map/all_gather | solution.py:48
  32.0 11.3 %all-gather.6 = bf16[256,1536]{1,0:T(8,128)(2,1)S(1)} all-gather(bf16[64,1536]{1,0:T(8,128)(2,1)S(1)} %get-tuple-element.8), channel_id=8, replica_groups=mesh['y_lo'=2,'z'=8,'x'=4,'y_hi'=4,'core'=2] {'x'}, dimensions={0}, use_global_device_ids=true | all-gather | bytes 983040 | tf_op jit(solution)/shard_map/all_gather | solution.py:48
  43.3 8.2 %all-to-all-done = bf16[8,64,1536]{2,1,0:T(8,128)(2,1)S(1)} async-done(((bf16[8,64,1536]{2,1,0:T(8,128)(2,1)}), bf16[8,64,1536]{2,1,0:T(8,128)(2,1)S(1)}, u32[]{:S(2)}, u32[]{:S(2)}) %all-to-all-start) | async-done | bytes 1572896 | tf_op jit(solution)/shard_map/all_to_all | solution.py:32
  51.4 0.6 fusion.10
  52.0 0.6 fusion.9
  52.6 0.1 maximum_multiply_fusion
  52.8 0.2 select_convert_fusion.1
  52.9 25.4 %all_to_all.25 = bf16[8,64,512]{2,1,0:T(8,128)(2,1)S(1)} all-to-all(bf16[8,64,512]{2,1,0:T(8,128)(2,1)S(1)} %select_convert_fusion.1), channel_id=1, replica_groups=mesh['y_lo'=2,'z'=8,'x'=4,'y_hi'=4,'core'=2] {'core','y_hi'}, dimensions={0} | all-to-all | bytes 1048576 | tf_op jit(solution)/shard_map/all_to_all | solution.py:38
  78.4 0.1 convert_reduce_fusion.1
  78.5 0.9 broadcast_in_dim.75
  79.3 3.5 %all-to-all-start.2 = ((bf16[8,64,512]{2,1,0:T(8,128)(2,1)}), bf16[8,64,512]{2,1,0:T(8,128)(2,1)S(1)}, u32[]{:S(2)}, u32[]{:S(2)}) async-start(bf16[8,64,512]{2,1,0:T(8,128)(2,1)} %broadcast_in_dim.75), calls=%async_computation.2 | async-start | bytes 1048576 | tf_op jit(solution)/shard_map/all_to_all | solution.py:32
  82.9 0.7 collective-permute-start
  83.5 0.0 collective-permute-done
  83.6 4.3 %all-gather.3 = bf16[128,512]{1,0:T(8,128)(2,1)S(1)} all-gather(bf16[64,512]{1,0:T(8,128)(2,1)S(1)} %collective-permute-done), channel_id=5, replica_groups=mesh['y_lo'=2,'z'=8,'x'=4,'y_hi'=4,'core'=2] {'y_lo'}, dimensions={0}, use_global_device_ids=true | all-gather | bytes 196608 | tf_op jit(solution)/shard_map/all_gather | solution.py:56
  87.9 21.9 %all-gather.4 = bf16[8,64,512]{2,1,0:T(8,128)(2,1)} all-gather(bf16[2,64,512]{2,1,0:T(8,128)(2,1)S(1)} %bitcast.58), channel_id=6, replica_groups=mesh['y_lo'=2,'z'=8,'x'=4,'y_hi'=4,'core'=2] {'x'}, dimensions={0}, use_global_device_ids=true | all-gather | bytes 655360 | tf_op jit(solution)/shard_map/all_gather | solution.py:57
  109.8 0.0 all-to-all-done.2
  109.8 6.5 %collective-permute-start.1 = (bf16[512,512]{1,0:T(8,128)(2,1)S(1)}, bf16[512,512]{1,0:T(8,128)(2,1)S(1)}, u32[]{:S(2)}, u32[]{:S(2)}) collective-permute-start(bf16[512,512]{1,0:T(8,128)(2,1)S(1)} %bitcast.52), channel_id=1, source_target_pairs={{0,1},{1,0},{2,3},{3,2},{4,5},{5,4},{6,7},{7,6},{8,9},{9,8},{10,11... | collective-permute-start | bytes 1572872 | tf_op jit(solution)/shard_map/ppermute | solution.py:55
  116.3 1.1 broadcast_select_fusion
  117.4 0.1 select_reduce_fusion
  117.6 0.3 fusion.11
  117.9 0.0 collective-permute-done.1
  117.9 0.3 convolution_add_fusion.1
  118.2 0.8 select_convert_fusion.2
  119.0 3.4 %all-to-all-start.3 = ((bf16[4,64,512]{2,1,0:T(8,128)(2,1)}), bf16[4,64,512]{2,1,0:T(8,128)(2,1)S(1)}, u32[]{:S(2)}, u32[]{:S(2)}) async-start(bf16[4,64,512]{2,1,0:T(8,128)(2,1)} %select_convert_fusion.2), calls=%async_computation.3 | async-start | bytes 524288 | tf_op jit(solution)/shard_map/all_to_all | solution.py:38
  122.5 8.8 %all-to-all-done.3 = bf16[4,64,512]{2,1,0:T(8,128)(2,1)S(1)} async-done(((bf16[4,64,512]{2,1,0:T(8,128)(2,1)}), bf16[4,64,512]{2,1,0:T(8,128)(2,1)S(1)}, u32[]{:S(2)}, u32[]{:S(2)}) %all-to-all-start.3) | async-done | bytes 262176 | tf_op jit(solution)/shard_map/all_to_all | solution.py:38
  131.3 0.0 copy-start
  131.3 0.1 fusion.4
  131.4 18.2 %all_gather.35 = bf16[512,512]{1,0:T(8,128)(2,1)S(1)} all-gather(bf16[64,512]{1,0:T(8,128)(2,1)S(1)} %fusion.4), channel_id=1, replica_groups=mesh['y_lo'=2,'z'=8,'x'=4,'y_hi'=4,'core'=2] {'y_hi','core'}, dimensions={0}, use_global_device_ids=true | all-gather | bytes 589824 | tf_op jit(solution)/shard_map/all_gather | solution.py:73
  149.6 0.0 copy-done
  149.6 1.2 select_convert_fusion
  150.8 23.9 %all_to_all.26 = bf16[8,64,1536]{2,1,0:T(8,128)(2,1)S(1)} all-to-all(bf16[8,64,1536]{2,1,0:T(8,128)(2,1)S(1)} %get-tuple-element.9), channel_id=1, replica_groups=mesh['y_lo'=2,'z'=8,'x'=4,'y_hi'=4,'core'=2] {'x','y_lo'}, dimensions={0} | all-to-all | bytes 3145728 | tf_op jit(solution)/shard_map/all_to_all | solution.py:38
  174.7 0.2 convert_reduce_fusion
  174.9 0.8 bitcast_add_fusion
  (9 shorter events, 0.1 us)
Async XLA Ops:
  2.3 49.1 %all-to-all-start = ((bf16[8,64,1536]{2,1,0:T(8,128)(2,1)}), bf16[8,64,1536]{2,1,0:T(8,128)(2,1)S(1)}, u32[]{:S(2)}, u32[]{:S(2)}) async-start(bf16[8,64,1536]{2,1,0:T(8,128)(2,1)} %broadcast_in_dim.71), calls=%async_computation | async-start | bytes 3145728 | tf_op jit(solution)/shard_map/all_to_all | solution.py:32
  79.3 30.4 %all-to-all-start.2 = ((bf16[8,64,512]{2,1,0:T(8,128)(2,1)}), bf16[8,64,512]{2,1,0:T(8,128)(2,1)S(1)}, u32[]{:S(2)}, u32[]{:S(2)}) async-start(bf16[8,64,512]{2,1,0:T(8,128)(2,1)} %broadcast_in_dim.75), calls=%async_computation.2 | async-start | bytes 1048576 | tf_op jit(solution)/shard_map/all_to_all | solution.py:32
  82.9 0.7 collective-permute-start
  109.8 8.1 %collective-permute-start.1 = (bf16[512,512]{1,0:T(8,128)(2,1)S(1)}, bf16[512,512]{1,0:T(8,128)(2,1)S(1)}, u32[]{:S(2)}, u32[]{:S(2)}) collective-permute-start(bf16[512,512]{1,0:T(8,128)(2,1)S(1)} %bitcast.52), channel_id=1, source_target_pairs={{0,1},{1,0},{2,3},{3,2},{4,5},{5,4},{6,7},{7,6},{8,9},{9,8},{10,11... | collective-permute-start | bytes 1572872 | tf_op jit(solution)/shard_map/ppermute | solution.py:55
  119.0 12.2 %all-to-all-start.3 = ((bf16[4,64,512]{2,1,0:T(8,128)(2,1)}), bf16[4,64,512]{2,1,0:T(8,128)(2,1)S(1)}, u32[]{:S(2)}, u32[]{:S(2)}) async-start(bf16[4,64,512]{2,1,0:T(8,128)(2,1)} %select_convert_fusion.2), calls=%async_computation.3 | async-start | bytes 524288 | tf_op jit(solution)/shard_map/all_to_all | solution.py:38
  131.3 18.4 %copy-start = (f32[64,1536]{1,0:T(8,128)S(1)}, f32[64,1536]{1,0:T(8,128)}, u32[]{:S(2)}) copy-start(f32[64,1536]{1,0:T(8,128)} %param.1) | copy-start | bytes 1179652

commit v26 on v23

--- a/solution.py
+++ b/solution.py
@@ -11,8 +11,9 @@
 
 LO = ("x", "y_lo")
 COL = ("y_hi", "core")
-ROW = ("y_lo", "z", "x")
-MESH = ("y_lo", "z", "x", "y_hi", "core")
+HI = ("z_hi", "z_lo")
+ROW = ("y_lo",) + HI + ("x",)
+MESH = ("y_lo", "z_hi", "z_lo", "x", "y_hi", "core")
 
 
 def rest_of(x):
@@ -43,7 +44,7 @@
 def per_device(x_scaled):
     rows, cols = x_scaled.shape
     xb = x_scaled.astype(jnp.bfloat16)
-    by_hi = spread(xb, "z").reshape(8 * rows, cols)
+    by_hi = spread(xb, HI).reshape(8 * rows, cols)
     pair = lax.all_gather(xb, "y_lo", axis=0)
     by_lo = [lax.all_gather(pair[y], "x", axis=0, tiled=True) for y in range(2)]
 
@@ -51,10 +52,10 @@
     gram = sum_pieces(tile.reshape(8, rows, 8 * rows), ("core", "y_hi"))
 
     rounded = gram.astype(jnp.bfloat16)
-    right = spread(rounded, "z").reshape(8 * rows, 8 * rows)
+    left = spread(swap_x_y_hi(rounded), LO).reshape(4, 2, rows, 8 * rows)
+    right = lax.all_gather(rounded, "z_lo", axis=0, tiled=True)
+    right = lax.all_gather(right, "z_hi", axis=0, tiled=True)
     right_other = lax.ppermute(right, "core", [(0, 1), (1, 0)])
-    left = lax.all_gather(swap_x_y_hi(rounded), "y_lo", axis=0)
-    left = lax.all_gather(left, "x", axis=0).reshape(4, 2, rows, 8 * rows)
     core = lax.axis_index("core")
     own = jnp.where(core == 0, left[:, 0], left[:, 1]).reshape(4 * rows, 8 * rows)
     other = jnp.where(core == 0, left[:, 1], left[:, 0]).reshape(4 * rows, 8 * rows)
@@ -65,7 +66,7 @@
 
     place = (lax.axis_index("y_hi"), core, 0, 0)
     at_home = lax.dynamic_slice(left, place, (1, 1, rows, 8 * rows), allow_negative_indices=False)[0, 0]
-    column = lax.broadcasted_iota(jnp.int32, at_home.shape, 1) - lax.axis_index("z") * rows
+    column = lax.broadcasted_iota(jnp.int32, at_home.shape, 1) - lax.axis_index(HI) * rows
     on_diagonal = column == lax.broadcasted_iota(jnp.int32, at_home.shape, 0)
     diagonal = jnp.where(on_diagonal, at_home.astype(jnp.float32), 0.0).sum(1, keepdims=True)
     square = square + rest_of(gram) * (2.0 * diagonal)
@@ -79,7 +80,7 @@
 
 
 def solution(mesh):
-    fine = Mesh(mesh.devices.reshape(2, 8, 4, 4, 2), MESH)
+    fine = Mesh(mesh.devices.reshape(2, 4, 2, 4, 4, 2), MESH)
     return jax.shard_map(
         per_device,
         mesh=fine,

time: 174 us -> 184 us (1.057)
  starting transfers between devices: 20.8 us -> 36.8 us
  waiting for transfers between devices: 28.1 us -> 16.3 us
  blocking collectives: 115 us -> 118 us
  matrix products: 2.95 us -> 5.18 us
    all_to_all x2, waiting for transfers between devices: 21.1 us -> 8.19 us  [spread(): lax.all_to_all(jnp.broadcast_to(block[None], (8,) + block.shape), axis, 0...]
    all_to_all x2, starting transfers between devices: 14.4 us -> 26.1 us  [spread(): lax.all_to_all(jnp.broadcast_to(block[None], (8,) + block.shape), axis, 0...]
    ppermute x1, starting transfers between devices: 2.35 us -> 6.7 us  [per_device(): right_other = lax.ppermute(right, 'core', [(0, 1), (1, 0)])]
    all_gather x2, blocking collectives: 15.2 us -> 18 us  [the longest x1 14.2 us: per_device(): right = lax.all_gather(right, 'z_hi', axis=0, tiled=True)]
    all_to_all x2, blocking collectives: 49.7 us -> 52 us  [sum_pieces(): lax.all_to_all(jnp.where(mine, 0.0, pieces).astype(jnp.bfloat16), axis, 0...]
where the time goes in v26:
time: 184 us; the launch traced here: 183 us
  blocking collectives  118 us (64%)
  starting transfers between devices  36.8 us (20%)
  waiting for transfers between devices  16.3 us (9%)
  matrix products  5.18 us (3%)
  other arithmetic  4.39 us (2%)
  local copies, waits for them, and re-layouts  2.17 us (1%)
    all_to_all x2, blocking collectives, sum_pieces(): lax.all_to_all(jnp.where(mine, 0.0, pieces).astype(jnp.bfloat16), axis, 0...  52 us
    all_to_all x2, starting transfers between devices, spread(): lax.all_to_all(jnp.broadcast_to(block[None], (8,) + block.shape), axis, 0...  26.1 us
    all_gather x2, blocking collectives, per_device(): by_lo = [lax.all_gather(pair[y], 'x', axis=0, tiled=True) for y in range(2)]  23.9 us
    all_gather x1, blocking collectives, per_device(): poly = lax.all_gather(poly, COL, axis=0, tiled=True)  18.2 us
    all_gather x1, blocking collectives, per_device(): right = lax.all_gather(right, 'z_hi', axis=0, tiled=True)  14.2 us
    all_to_all x2, waiting for transfers between devices, spread(): lax.all_to_all(jnp.broadcast_to(block[None], (8,) + block.shape), axis, 0...  8.19 us
    all_to_all x1, waiting for transfers between devices, sum_pieces(): lax.all_to_all(jnp.where(mine, 0.0, pieces).astype(jnp.bfloat16), axis, 0...  7.88 us
    ppermute x1, starting transfers between devices, per_device(): right_other = lax.ppermute(right, 'core', [(0, 1), (1, 0)])  6.7 us
  transfers between devices with their start and end apart: 5, of which 3 were waited for; matrix products, arithmetic and copies ran while one was open for 1% of the time, Pallas kernels for 0%

profile of v26, /device:TPU:1, one launch (start us, length us, event | category | flops | bytes accessed | tf_op | source)
XLA Modules:
  0.0 183.3 jit_solution(8369848738854772327)
XLA Ops:
  0.0 1.0 convert_element_type.33
  1.0 1.3 broadcast_in_dim.69
  2.3 10.9 %all-to-all-start = ((bf16[8,64,1536]{2,1,0:T(8,128)(2,1)}), bf16[8,64,1536]{2,1,0:T(8,128)(2,1)S(1)}, u32[]{:S(2)}, u32[]{:S(2)}) async-start(bf16[8,64,1536]{2,1,0:T(8,128)(2,1)} %broadcast_in_dim.69), calls=%async_computation | async-start | bytes 3145728 | tf_op jit(solution)/shard_map/all_to_all | solution.py:33
  13.2 6.1 %all-gather = bf16[128,1536]{1,0:T(8,128)(2,1)S(1)} all-gather(bf16[64,1536]{1,0:T(8,128)(2,1)S(1)} %convert_element_type.33), channel_id=2, replica_groups=mesh['y_lo'=2,'z_hi'=4,'z_lo'=2,'x'=4,'y_hi'=4,'core'=2] {'y_lo'}, dimensions={0}, use_global_device_ids=true | all-gather | bytes 589824 | tf_op jit(solution)/shard_map/all_gather | solution.py:48
  19.3 12.6 %all-gather.3 = bf16[256,1536]{1,0:T(8,128)(2,1)S(1)} all-gather(bf16[64,1536]{1,0:T(8,128)(2,1)S(1)} %get-tuple-element.7), channel_id=5, replica_groups=mesh['y_lo'=2,'z_hi'=4,'z_lo'=2,'x'=4,'y_hi'=4,'core'=2] {'x'}, dimensions={0}, use_global_device_ids=true | all-gather | bytes 983040 | tf_op jit(solution)/shard_map/all_gather | solution.py:49
  32.0 11.3 %all-gather.4 = bf16[256,1536]{1,0:T(8,128)(2,1)S(1)} all-gather(bf16[64,1536]{1,0:T(8,128)(2,1)S(1)} %get-tuple-element.8), channel_id=6, replica_groups=mesh['y_lo'=2,'z_hi'=4,'z_lo'=2,'x'=4,'y_hi'=4,'core'=2] {'x'}, dimensions={0}, use_global_device_ids=true | all-gather | bytes 983040 | tf_op jit(solution)/shard_map/all_gather | solution.py:49
  43.3 8.2 %all-to-all-done = bf16[8,64,1536]{2,1,0:T(8,128)(2,1)S(1)} async-done(((bf16[8,64,1536]{2,1,0:T(8,128)(2,1)}), bf16[8,64,1536]{2,1,0:T(8,128)(2,1)S(1)}, u32[]{:S(2)}, u32[]{:S(2)}) %all-to-all-start) | async-done | bytes 1572896 | tf_op jit(solution)/shard_map/all_to_all | solution.py:33
  51.4 0.6 fusion.9
  52.0 0.6 fusion.8
  52.6 0.1 maximum_multiply_fusion
  52.8 0.2 select_convert_fusion.1
  52.9 25.4 %all_to_all.25 = bf16[8,64,512]{2,1,0:T(8,128)(2,1)S(1)} all-to-all(bf16[8,64,512]{2,1,0:T(8,128)(2,1)S(1)} %select_convert_fusion.1), channel_id=1, replica_groups=mesh['y_lo'=2,'z_hi'=4,'z_lo'=2,'x'=4,'y_hi'=4,'core'=2] {'core','y_hi'}, dimensions={0} | all-to-all | bytes 1048576 | tf_op jit(solution)/shard_map/all_to_all | solution.py:39
  78.4 0.1 convert_reduce_fusion.1
  78.5 0.7 collective-permute-start
  79.1 0.0 collective-permute-done
  79.1 0.9 broadcast_in_dim.72
  80.0 15.2 %all-to-all-start.2 = ((bf16[8,64,512]{2,1,0:T(8,128)(2,1)}), bf16[8,64,512]{2,1,0:T(8,128)(2,1)S(1)}, u32[]{:S(2)}, u32[]{:S(2)}) async-start(bf16[8,64,512]{2,1,0:T(8,128)(2,1)} %broadcast_in_dim.72), calls=%async_computation.2 | async-start | bytes 1048576 | tf_op jit(solution)/shard_map/all_to_all | solution.py:33
  95.2 3.8 %all_gather.25 = bf16[128,512]{1,0:T(8,128)(2,1)S(1)} all-gather(bf16[64,512]{1,0:T(8,128)(2,1)S(1)} %fusion.6), channel_id=1, replica_groups=mesh['y_lo'=2,'z_hi'=4,'z_lo'=2,'x'=4,'y_hi'=4,'core'=2] {'z_lo'}, dimensions={0}, use_global_device_ids=true | all-gather | bytes 196608 | tf_op jit(solution)/shard_map/all_gather | solution.py:56
  99.0 14.2 %all_gather.26 = bf16[512,512]{1,0:T(8,128)(2,1)} all-gather(bf16[128,512]{1,0:T(8,128)(2,1)S(1)} %all_gather.25), channel_id=1, replica_groups=mesh['y_lo'=2,'z_hi'=4,'z_lo'=2,'x'=4,'y_hi'=4,'core'=2] {'z_hi'}, dimensions={0}, use_global_device_ids=true | all-gather | bytes 655360 | tf_op jit(solution)/shard_map/all_gather | solution.py:57
  113.2 6.7 %collective-permute-start.1 = (bf16[512,512]{1,0:T(8,128)(2,1)}, bf16[512,512]{1,0:T(8,128)(2,1)}, u32[]{:S(2)}, u32[]{:S(2)}) collective-permute-start(bf16[512,512]{1,0:T(8,128)(2,1)} %all_gather.26), channel_id=1, source_target_pairs={{0,1},{1,0},{2,3},{3,2},{4,5},{5,4},{6,7},{7,6},{8,9},{9,8},{10,11... | collective-permute-start | bytes 1572872 | tf_op jit(solution)/shard_map/ppermute | solution.py:58
  119.9 0.0 all-to-all-done.2
  119.9 0.0 copy-start
  120.0 1.5 fusion.10
  121.5 0.3 collective-permute-done.1
  121.7 0.0 copy-done
  121.7 1.3 convolution_add_fusion.1
  123.1 0.8 select_convert_fusion.2
  123.9 3.4 %all-to-all-start.3 = ((bf16[4,64,512]{2,1,0:T(8,128)(2,1)}), bf16[4,64,512]{2,1,0:T(8,128)(2,1)S(1)}, u32[]{:S(2)}, u32[]{:S(2)}) async-start(bf16[4,64,512]{2,1,0:T(8,128)(2,1)} %select_convert_fusion.2), calls=%async_computation.3 | async-start | bytes 524288 | tf_op jit(solution)/shard_map/all_to_all | solution.py:39
  127.3 1.0 fusion.5
  128.3 7.9 %all-to-all-done.3 = bf16[4,64,512]{2,1,0:T(8,128)(2,1)S(1)} async-done(((bf16[4,64,512]{2,1,0:T(8,128)(2,1)}), bf16[4,64,512]{2,1,0:T(8,128)(2,1)S(1)}, u32[]{:S(2)}, u32[]{:S(2)}) %all-to-all-start.3) | async-done | bytes 262176 | tf_op jit(solution)/shard_map/all_to_all | solution.py:39
  136.2 0.0 copy-start.1
  136.2 0.1 fusion.4
  136.3 18.2 %all_gather.27 = bf16[512,512]{1,0:T(8,128)(2,1)S(1)} all-gather(bf16[64,512]{1,0:T(8,128)(2,1)S(1)} %fusion.4), channel_id=1, replica_groups=mesh['y_lo'=2,'z_hi'=4,'z_lo'=2,'x'=4,'y_hi'=4,'core'=2] {'y_hi','core'}, dimensions={0}, use_global_device_ids=true | all-gather | bytes 589824 | tf_op jit(solution)/shard_map/all_gather | solution.py:75
  154.5 0.0 copy-done.1
  154.5 1.2 select_convert_fusion
  155.7 26.6 %all_to_all.26 = bf16[8,64,1536]{2,1,0:T(8,128)(2,1)S(1)} all-to-all(bf16[8,64,1536]{2,1,0:T(8,128)(2,1)S(1)} %get-tuple-element.9), channel_id=1, replica_groups=mesh['y_lo'=2,'z_hi'=4,'z_lo'=2,'x'=4,'y_hi'=4,'core'=2] {'x','y_lo'}, dimensions={0} | all-to-all | bytes 3145728 | tf_op jit(solution)/shard_map/all_to_all | solution.py:39
  182.3 0.2 convert_reduce_fusion
  182.5 0.8 bitcast_add_fusion
  (9 shorter events, 0.1 us)
Async XLA Ops:
  2.3 49.1 %all-to-all-start = ((bf16[8,64,1536]{2,1,0:T(8,128)(2,1)}), bf16[8,64,1536]{2,1,0:T(8,128)(2,1)S(1)}, u32[]{:S(2)}, u32[]{:S(2)}) async-start(bf16[8,64,1536]{2,1,0:T(8,128)(2,1)} %broadcast_in_dim.69), calls=%async_computation | async-start | bytes 3145728 | tf_op jit(solution)/shard_map/all_to_all | solution.py:33
  78.5 0.7 collective-permute-start
  80.0 39.9 %all-to-all-start.2 = ((bf16[8,64,512]{2,1,0:T(8,128)(2,1)}), bf16[8,64,512]{2,1,0:T(8,128)(2,1)S(1)}, u32[]{:S(2)}, u32[]{:S(2)}) async-start(bf16[8,64,512]{2,1,0:T(8,128)(2,1)} %broadcast_in_dim.72), calls=%async_computation.2 | async-start | bytes 1048576 | tf_op jit(solution)/shard_map/all_to_all | solution.py:33
  113.2 8.6 %collective-permute-start.1 = (bf16[512,512]{1,0:T(8,128)(2,1)}, bf16[512,512]{1,0:T(8,128)(2,1)}, u32[]{:S(2)}, u32[]{:S(2)}) collective-permute-start(bf16[512,512]{1,0:T(8,128)(2,1)} %all_gather.26), channel_id=1, source_target_pairs={{0,1},{1,0},{2,3},{3,2},{4,5},{5,4},{6,7},{7,6},{8,9},{9,8},{10,11... | collective-permute-start | bytes 1572872 | tf_op jit(solution)/shard_map/ppermute | solution.py:58
  119.9 1.8 copy-start
  123.9 12.3 %all-to-all-start.3 = ((bf16[4,64,512]{2,1,0:T(8,128)(2,1)}), bf16[4,64,512]{2,1,0:T(8,128)(2,1)S(1)}, u32[]{:S(2)}, u32[]{:S(2)}) async-start(bf16[4,64,512]{2,1,0:T(8,128)(2,1)} %select_convert_fusion.2), calls=%async_computation.3 | async-start | bytes 524288 | tf_op jit(solution)/shard_map/all_to_all | solution.py:39
  136.2 18.3 %copy-start.1 = (f32[64,1536]{1,0:T(8,128)S(1)}, f32[64,1536]{1,0:T(8,128)}, u32[]{:S(2)}) copy-start(f32[64,1536]{1,0:T(8,128)} %param.1) | copy-start | bytes 1179652

commit v27 on v23

--- a/solution.py
+++ b/solution.py
@@ -29,7 +29,8 @@
 
 
 def spread(block, axis):
-    return lax.all_to_all(jnp.broadcast_to(block[None], (8,) + block.shape), axis, 0, 0)
+    count = lax.axis_size(axis)
+    return lax.all_to_all(jnp.broadcast_to(block[None], (count,) + block.shape), axis, 0, 0)
 
 
 def sum_pieces(pieces, axis):
@@ -54,7 +55,7 @@
     right = spread(rounded, "z").reshape(8 * rows, 8 * rows)
     right_other = lax.ppermute(right, "core", [(0, 1), (1, 0)])
     left = lax.all_gather(swap_x_y_hi(rounded), "y_lo", axis=0)
-    left = lax.all_gather(left, "x", axis=0).reshape(4, 2, rows, 8 * rows)
+    left = spread(left + 0 * right_other[:1, :1], "x")
     core = lax.axis_index("core")
     own = jnp.where(core == 0, left[:, 0], left[:, 1]).reshape(4 * rows, 8 * rows)
     other = jnp.where(core == 0, left[:, 1], left[:, 0]).reshape(4 * rows, 8 * rows)

time: 174 us -> 193 us (1.11)
  starting transfers between devices: 20.8 us -> 31.9 us
  blocking collectives: 115 us -> 124 us
  waiting for transfers between devices: 28.1 us -> 22.1 us
  local copies, waits for them, and re-layouts: 2.25 us -> 4.33 us
    all_to_all x0 -> x1, blocking collectives: none -> 20.4 us  [spread(): lax.all_to_all(jnp.broadcast_to(block[None], (count,) + block.shape), axi...]
    all_to_all x2, starting transfers between devices: 14.4 us -> 25.5 us  [spread(): lax.all_to_all(jnp.broadcast_to(block[None], (count,) + block.shape), axi...]
    all_gather x1 -> x0, blocking collectives: 10.9 us -> none  [per_device(): left = lax.all_gather(left, 'x', axis=0).reshape(4, 2, rows, 8 * rows)]
    all_to_all x2, waiting for transfers between devices: 21.1 us -> 15.1 us  [spread(): lax.all_to_all(jnp.broadcast_to(block[None], (count,) + block.shape), axi...]
where the time goes in v27:
time: 193 us; the launch traced here: 192 us
  blocking collectives  124 us (64%)
  starting transfers between devices  31.9 us (17%)
  waiting for transfers between devices  22.1 us (11%)
  other arithmetic  4.42 us (2%)
  local copies, waits for them, and re-layouts  4.33 us (2%)
  matrix products  4.21 us (2%)
    all_to_all x2, blocking collectives, sum_pieces(): lax.all_to_all(jnp.where(mine, 0.0, pieces).astype(jnp.bfloat16), axis, 0...  49.2 us
    all_to_all x2, starting transfers between devices, spread(): lax.all_to_all(jnp.broadcast_to(block[None], (count,) + block.shape), axi...  25.5 us
    all_gather x2, blocking collectives, per_device(): by_lo = [lax.all_gather(pair[y], 'x', axis=0, tiled=True) for y in range(2)]  23.9 us
    all_to_all x1, blocking collectives, spread(): lax.all_to_all(jnp.broadcast_to(block[None], (count,) + block.shape), axi...  20.4 us
    all_gather x1, blocking collectives, per_device(): poly = lax.all_gather(poly, COL, axis=0, tiled=True)  20.3 us
    all_to_all x2, waiting for transfers between devices, spread(): lax.all_to_all(jnp.broadcast_to(block[None], (count,) + block.shape), axi...  15.1 us
    all_to_all x1, waiting for transfers between devices, sum_pieces(): lax.all_to_all(jnp.where(mine, 0.0, pieces).astype(jnp.bfloat16), axis, 0...  6.94 us
    all_gather x1, blocking collectives, per_device(): pair = lax.all_gather(xb, 'y_lo', axis=0)  6.12 us
  transfers between devices with their start and end apart: 5, of which 3 were waited for; matrix products, arithmetic and copies ran while one was open for 1% of the time, Pallas kernels for 0%

profile of v27, /device:TPU:1, one launch (start us, length us, event | category | flops | bytes accessed | tf_op | source)
XLA Modules:
  0.0 192.1 jit_solution(7868126467978992982)
XLA Ops:
  0.0 1.0 convert_element_type.36
  1.0 1.3 broadcast_in_dim.78
  2.3 10.9 %all-to-all-start = ((bf16[8,64,1536]{2,1,0:T(8,128)(2,1)}), bf16[8,64,1536]{2,1,0:T(8,128)(2,1)S(1)}, u32[]{:S(2)}, u32[]{:S(2)}) async-start(bf16[8,64,1536]{2,1,0:T(8,128)(2,1)} %broadcast_in_dim.78), calls=%async_computation | async-start | bytes 3145728 | tf_op jit(solution)/shard_map/all_to_all | solution.py:33
  13.2 6.1 %all-gather = bf16[128,1536]{1,0:T(8,128)(2,1)S(1)} all-gather(bf16[64,1536]{1,0:T(8,128)(2,1)S(1)} %convert_element_type.36), channel_id=2, replica_groups=mesh['y_lo'=2,'z'=8,'x'=4,'y_hi'=4,'core'=2] {'y_lo'}, dimensions={0}, use_global_device_ids=true | all-gather | bytes 589824 | tf_op jit(solution)/shard_map/all_gather | solution.py:48
  19.3 12.6 %all-gather.4 = bf16[256,1536]{1,0:T(8,128)(2,1)S(1)} all-gather(bf16[64,1536]{1,0:T(8,128)(2,1)S(1)} %get-tuple-element.7), channel_id=6, replica_groups=mesh['y_lo'=2,'z'=8,'x'=4,'y_hi'=4,'core'=2] {'x'}, dimensions={0}, use_global_device_ids=true | all-gather | bytes 983040 | tf_op jit(solution)/shard_map/all_gather | solution.py:49
  32.0 11.3 %all-gather.5 = bf16[256,1536]{1,0:T(8,128)(2,1)S(1)} all-gather(bf16[64,1536]{1,0:T(8,128)(2,1)S(1)} %get-tuple-element.8), channel_id=7, replica_groups=mesh['y_lo'=2,'z'=8,'x'=4,'y_hi'=4,'core'=2] {'x'}, dimensions={0}, use_global_device_ids=true | all-gather | bytes 983040 | tf_op jit(solution)/shard_map/all_gather | solution.py:49
  43.3 8.2 %all-to-all-done = bf16[8,64,1536]{2,1,0:T(8,128)(2,1)S(1)} async-done(((bf16[8,64,1536]{2,1,0:T(8,128)(2,1)}), bf16[8,64,1536]{2,1,0:T(8,128)(2,1)S(1)}, u32[]{:S(2)}, u32[]{:S(2)}) %all-to-all-start) | async-done | bytes 1572896 | tf_op jit(solution)/shard_map/all_to_all | solution.py:33
  51.4 0.6 fusion.11
  52.1 0.6 fusion.10
  52.7 0.1 maximum_multiply_fusion
  52.8 0.2 select_convert_fusion.1
  53.0 25.4 %all_to_all.30 = bf16[8,64,512]{2,1,0:T(8,128)(2,1)S(1)} all-to-all(bf16[8,64,512]{2,1,0:T(8,128)(2,1)S(1)} %select_convert_fusion.1), channel_id=1, replica_groups=mesh['y_lo'=2,'z'=8,'x'=4,'y_hi'=4,'core'=2] {'core','y_hi'}, dimensions={0} | all-to-all | bytes 1048576 | tf_op jit(solution)/shard_map/all_to_all | solution.py:39
  78.4 0.1 convert_reduce_fusion.1
  78.5 20.4 %all_to_all.31 = bf16[8,64,512]{2,1,0:T(8,128)(2,1)S(1)} all-to-all(bf16[8,64,512]{2,1,0:T(8,128)(2,1)S(1)} %broadcast_in_dim.82), channel_id=1, replica_groups=mesh['y_lo'=2,'z'=8,'x'=4,'y_hi'=4,'core'=2] {'z'}, dimensions={0} | all-to-all | bytes 1048576 | tf_op jit(solution)/shard_map/all_to_all | solution.py:33
  98.9 0.0 copy-start.1
  98.9 0.8 copy-done.1
  99.7 2.3 %collective-permute-start.1 = (bf16[512,512]{1,0:T(8,128)(2,1)S(1)}, bf16[512,512]{1,0:T(8,128)(2,1)S(1)}, u32[]{:S(2)}, u32[]{:S(2)}) collective-permute-start(bf16[512,512]{1,0:T(8,128)(2,1)S(1)} %bitcast.53), channel_id=1, source_target_pairs={{0,1},{1,0},{2,3},{3,2},{4,5},{5,4},{6,7},{7,6},{8,9},{9,8},{10,11... | collective-permute-start | bytes 1572872 | tf_op jit(solution)/shard_map/ppermute | solution.py:56
  102.1 0.7 collective-permute-start
  102.8 0.0 collective-permute-done
  102.8 4.3 %all-gather.3 = bf16[128,512]{1,0:T(8,128)(2,1)S(1)} all-gather(bf16[64,512]{1,0:T(8,128)(2,1)S(1)} %collective-permute-done), channel_id=5, replica_groups=mesh['y_lo'=2,'z'=8,'x'=4,'y_hi'=4,'core'=2] {'y_lo'}, dimensions={0}, use_global_device_ids=true | all-gather | bytes 196608 | tf_op jit(solution)/shard_map/all_gather | solution.py:57
  107.1 0.0 collective-permute-done.1
  107.1 0.0 copy-start.2
  107.1 0.8 copy-done.2
  107.9 0.5 slice.26
  109.1 0.9 broadcast_in_dim.83
  110.0 14.6 %all-to-all-start.3 = ((bf16[4,2,64,512]{3,2,1,0:T(8,128)(2,1)}), bf16[4,2,64,512]{3,2,1,0:T(8,128)(2,1)S(1)}, u32[]{:S(2)}, u32[]{:S(2)}) async-start(bf16[4,2,64,512]{3,2,1,0:T(8,128)(2,1)} %broadcast_in_dim.83), calls=%async_computation.3 | async-start | bytes 1048576 | tf_op jit(solution)/shard_map/all_to_all | solution.py:33
  124.6 7.0 %all-to-all-done.3 = bf16[4,2,64,512]{3,2,1,0:T(8,128)(2,1)S(1)} async-done(((bf16[4,2,64,512]{3,2,1,0:T(8,128)(2,1)}), bf16[4,2,64,512]{3,2,1,0:T(8,128)(2,1)S(1)}, u32[]{:S(2)}, u32[]{:S(2)}) %all-to-all-start.3) | async-done | bytes 524320 | tf_op jit(solution)/shard_map/all_to_all | solution.py:33
  131.6 0.0 copy-start
  131.6 0.0 copy-start.3
  131.6 1.6 fusion.12
  133.2 0.0 copy-done
  133.2 0.0 copy-done.3
  133.2 0.3 convolution_add_fusion.1
  133.5 0.8 select_convert_fusion.2
  134.3 3.4 %all-to-all-start.4 = ((bf16[4,64,512]{2,1,0:T(8,128)(2,1)}), bf16[4,64,512]{2,1,0:T(8,128)(2,1)S(1)}, u32[]{:S(2)}, u32[]{:S(2)}) async-start(bf16[4,64,512]{2,1,0:T(8,128)(2,1)} %select_convert_fusion.2), calls=%async_computation.4 | async-start | bytes 524288 | tf_op jit(solution)/shard_map/all_to_all | solution.py:39
  137.8 1.0 fusion.5
  138.7 6.9 %all-to-all-done.4 = bf16[4,64,512]{2,1,0:T(8,128)(2,1)S(1)} async-done(((bf16[4,64,512]{2,1,0:T(8,128)(2,1)}), bf16[4,64,512]{2,1,0:T(8,128)(2,1)S(1)}, u32[]{:S(2)}, u32[]{:S(2)}) %all-to-all-start.4) | async-done | bytes 262176 | tf_op jit(solution)/shard_map/all_to_all | solution.py:39
  145.7 0.0 copy-start.4
  145.7 0.1 fusion.4
  145.8 20.3 %all_gather.27 = bf16[512,512]{1,0:T(8,128)(2,1)S(1)} all-gather(bf16[64,512]{1,0:T(8,128)(2,1)S(1)} %fusion.4), channel_id=1, replica_groups=mesh['y_lo'=2,'z'=8,'x'=4,'y_hi'=4,'core'=2] {'y_hi','core'}, dimensions={0}, use_global_device_ids=true | all-gather | bytes 589824 | tf_op jit(solution)/shard_map/all_gather | solution.py:75
  166.1 0.0 copy-done.4
  166.1 1.2 select_convert_fusion
  167.3 23.7 %all_to_all.32 = bf16[8,64,1536]{2,1,0:T(8,128)(2,1)S(1)} all-to-all(bf16[8,64,1536]{2,1,0:T(8,128)(2,1)S(1)} %get-tuple-element.9), channel_id=1, replica_groups=mesh['y_lo'=2,'z'=8,'x'=4,'y_hi'=4,'core'=2] {'x','y_lo'}, dimensions={0} | all-to-all | bytes 3145728 | tf_op jit(solution)/shard_map/all_to_all | solution.py:39
  191.0 0.2 convert_reduce_fusion
  191.3 0.8 bitcast_add_fusion
  (12 shorter events, 0.2 us)
Async XLA Ops:
  2.3 49.1 %all-to-all-start = ((bf16[8,64,1536]{2,1,0:T(8,128)(2,1)}), bf16[8,64,1536]{2,1,0:T(8,128)(2,1)S(1)}, u32[]{:S(2)}, u32[]{:S(2)}) async-start(bf16[8,64,1536]{2,1,0:T(8,128)(2,1)} %broadcast_in_dim.78), calls=%async_computation | async-start | bytes 3145728 | tf_op jit(solution)/shard_map/all_to_all | solution.py:33
  98.9 0.8 copy-start.1
  99.7 7.4 %collective-permute-start.1 = (bf16[512,512]{1,0:T(8,128)(2,1)S(1)}, bf16[512,512]{1,0:T(8,128)(2,1)S(1)}, u32[]{:S(2)}, u32[]{:S(2)}) collective-permute-start(bf16[512,512]{1,0:T(8,128)(2,1)S(1)} %bitcast.53), channel_id=1, source_target_pairs={{0,1},{1,0},{2,3},{3,2},{4,5},{5,4},{6,7},{7,6},{8,9},{9,8},{10,11... | collective-permute-start | bytes 1572872 | tf_op jit(solution)/shard_map/ppermute | solution.py:56
  102.1 0.7 collective-permute-start
  107.1 0.8 copy-start.2
  110.0 21.6 %all-to-all-start.3 = ((bf16[4,2,64,512]{3,2,1,0:T(8,128)(2,1)}), bf16[4,2,64,512]{3,2,1,0:T(8,128)(2,1)S(1)}, u32[]{:S(2)}, u32[]{:S(2)}) async-start(bf16[4,2,64,512]{3,2,1,0:T(8,128)(2,1)} %broadcast_in_dim.83), calls=%async_computation.3 | async-start | bytes 1048576 | tf_op jit(solution)/shard_map/all_to_all | solution.py:33
  131.6 1.6 copy-start
  131.6 1.6 copy-start.3
  134.3 11.3 %all-to-all-start.4 = ((bf16[4,64,512]{2,1,0:T(8,128)(2,1)}), bf16[4,64,512]{2,1,0:T(8,128)(2,1)S(1)}, u32[]{:S(2)}, u32[]{:S(2)}) async-start(bf16[4,64,512]{2,1,0:T(8,128)(2,1)} %select_convert_fusion.2), calls=%async_computation.4 | async-start | bytes 524288 | tf_op jit(solution)/shard_map/all_to_all | solution.py:39
  145.7 20.4 %copy-start.4 = (f32[64,1536]{1,0:T(8,128)S(1)}, f32[64,1536]{1,0:T(8,128)}, u32[]{:S(2)}) copy-start(f32[64,1536]{1,0:T(8,128)} %param.1) | copy-start | bytes 1179652

commit v28 on v23

--- a/solution.py
+++ b/solution.py
@@ -47,15 +47,17 @@
     pair = lax.all_gather(xb, "y_lo", axis=0)
     by_lo = [lax.all_gather(pair[y], "x", axis=0, tiled=True) for y in range(2)]
 
-    tile = jnp.concatenate([dot_nt(part, by_hi) for part in by_lo]) * (1.0 / N)
-    gram = sum_pieces(tile.reshape(8, rows, 8 * rows), ("core", "y_hi"))
+    core = lax.axis_index("core")
+    tiles = [dot_nt(part, by_hi) * (1.0 / N) for part in by_lo]
+    away = lax.ppermute(jnp.where(core == 0, tiles[1], tiles[0]), "core", [(0, 1), (1, 0)])
+    home = jnp.where(core == 0, tiles[0], tiles[1]) + away
+    gram = sum_pieces(home.reshape(4, rows, 8 * rows), "y_hi")
 
     rounded = gram.astype(jnp.bfloat16)
     right = spread(rounded, "z").reshape(8 * rows, 8 * rows)
     right_other = lax.ppermute(right, "core", [(0, 1), (1, 0)])
     left = lax.all_gather(swap_x_y_hi(rounded), "y_lo", axis=0)
     left = lax.all_gather(left, "x", axis=0).reshape(4, 2, rows, 8 * rows)
-    core = lax.axis_index("core")
     own = jnp.where(core == 0, left[:, 0], left[:, 1]).reshape(4 * rows, 8 * rows)
     other = jnp.where(core == 0, left[:, 1], left[:, 0]).reshape(4 * rows, 8 * rows)
     square = jnp.dot(own, right, preferred_element_type=jnp.float32) + jnp.dot(

time: 174 us -> 176 us (1.011)
  blocking collectives: 115 us -> 108 us
  starting transfers between devices: 20.8 us -> 25.4 us
  matrix products: 2.95 us -> 4.88 us
  waiting for transfers between devices: 28.1 us -> 29.9 us
    all_to_all x2, blocking collectives: 49.7 us -> 43 us  [sum_pieces(): lax.all_to_all(jnp.where(mine, 0.0, pieces).astype(jnp.bfloat16), axis, 0...]
    ppermute x0 -> x1, starting transfers between devices: none -> 4.55 us  [per_device(): lax.ppermute(jnp.where(core == 0, tiles[1], tiles[0]), 'core', [(0, 1), (...]
    dot_general x2, matrix products: 1.19 us -> 3.13 us  [dot_nt(): lax.dot_general(a, b, (((1,), (1,)), ((), ())), preferred_element_type=jn...]
  transfers between devices with their start and end apart: 5 -> 6, of which waited for: 3 -> 4; matrix products, arithmetic and copies ran while one was open for 1% -> 0% of each run, Pallas kernels for 0% -> 0%
where the time goes in v28:
time: 176 us; the launch traced here: 175 us
  blocking collectives  108 us (61%)
  waiting for transfers between devices  29.9 us (17%)
  starting transfers between devices  25.4 us (14%)
  matrix products  4.88 us (3%)
  other arithmetic  4.54 us (3%)
  local copies, waits for them, and re-layouts  2.17 us (1%)
    all_to_all x2, blocking collectives, sum_pieces(): lax.all_to_all(jnp.where(mine, 0.0, pieces).astype(jnp.bfloat16), axis, 0...  43 us
    all_gather x2, blocking collectives, per_device(): by_lo = [lax.all_gather(pair[y], 'x', axis=0, tiled=True) for y in range(2)]  24.7 us
    all_to_all x2, waiting for transfers between devices, spread(): lax.all_to_all(jnp.broadcast_to(block[None], (8,) + block.shape), axis, 0...  20.5 us
    all_gather x1, blocking collectives, per_device(): poly = lax.all_gather(poly, COL, axis=0, tiled=True)  19.2 us
    all_to_all x2, starting transfers between devices, spread(): lax.all_to_all(jnp.broadcast_to(block[None], (8,) + block.shape), axis, 0...  14.4 us
    all_gather x1, blocking collectives, per_device(): left = lax.all_gather(left, 'x', axis=0).reshape(4, 2, rows, 8 * rows)  10.9 us
    all_to_all x1, waiting for transfers between devices, sum_pieces(): lax.all_to_all(jnp.where(mine, 0.0, pieces).astype(jnp.bfloat16), axis, 0...  7.94 us
    all_gather x1, blocking collectives, per_device(): pair = lax.all_gather(xb, 'y_lo', axis=0)  6.12 us
  transfers between devices with their start and end apart: 6, of which 4 were waited for; matrix products, arithmetic and copies ran while one was open for 0% of the time, Pallas kernels for 0%

profile of v28, /device:TPU:1, one launch (start us, length us, event | category | flops | bytes accessed | tf_op | source)
XLA Modules:
  0.0 175.0 jit_solution(7922965894245235938)
XLA Ops:
  0.0 1.0 convert_element_type.36
  1.0 1.3 broadcast_in_dim.63
  2.3 10.9 %all-to-all-start = ((bf16[8,64,1536]{2,1,0:T(8,128)(2,1)}), bf16[8,64,1536]{2,1,0:T(8,128)(2,1)S(1)}, u32[]{:S(2)}, u32[]{:S(2)}) async-start(bf16[8,64,1536]{2,1,0:T(8,128)(2,1)} %broadcast_in_dim.63), calls=%async_computation | async-start | bytes 3145728 | tf_op jit(solution)/shard_map/all_to_all | solution.py:32
  13.2 6.1 %all-gather = bf16[128,1536]{1,0:T(8,128)(2,1)S(1)} all-gather(bf16[64,1536]{1,0:T(8,128)(2,1)S(1)} %convert_element_type.36), channel_id=2, replica_groups=mesh['y_lo'=2,'z'=8,'x'=4,'y_hi'=4,'core'=2] {'y_lo'}, dimensions={0}, use_global_device_ids=true | all-gather | bytes 589824 | tf_op jit(solution)/shard_map/all_gather | solution.py:47
  19.3 13.4 %all-gather.5 = bf16[256,1536]{1,0:T(8,128)(2,1)} all-gather(bf16[64,1536]{1,0:T(8,128)(2,1)S(1)} %get-tuple-element.7), channel_id=7, replica_groups=mesh['y_lo'=2,'z'=8,'x'=4,'y_hi'=4,'core'=2] {'x'}, dimensions={0}, use_global_device_ids=true | all-gather | bytes 983040 | tf_op jit(solution)/shard_map/all_gather | solution.py:48
  32.7 11.3 %all-gather.6 = bf16[256,1536]{1,0:T(8,128)(2,1)S(1)} all-gather(bf16[64,1536]{1,0:T(8,128)(2,1)S(1)} %get-tuple-element.8), channel_id=8, replica_groups=mesh['y_lo'=2,'z'=8,'x'=4,'y_hi'=4,'core'=2] {'x'}, dimensions={0}, use_global_device_ids=true | all-gather | bytes 983040 | tf_op jit(solution)/shard_map/all_gather | solution.py:48
  44.0 7.4 %all-to-all-done = bf16[8,64,1536]{2,1,0:T(8,128)(2,1)S(1)} async-done(((bf16[8,64,1536]{2,1,0:T(8,128)(2,1)}), bf16[8,64,1536]{2,1,0:T(8,128)(2,1)S(1)}, u32[]{:S(2)}, u32[]{:S(2)}) %all-to-all-start) | async-done | bytes 1572896 | tf_op jit(solution)/shard_map/all_to_all | solution.py:32
  51.5 1.7 convolution_multiply_fusion.1
  53.2 1.4 broadcast_select_fusion.2
  54.6 4.5 %collective-permute-start = (f32[256,512]{1,0:T(8,128)S(1)}, f32[256,512]{1,0:T(8,128)S(1)}, u32[]{:S(2)}, u32[]{:S(2)}) collective-permute-start(f32[256,512]{1,0:T(8,128)S(1)} %get-tuple-element.9), channel_id=1, source_target_pairs={{0,1},{1,0},{2,3},{3,2},{4,5},{5,4},{6,7},{7,6},{8,9},{9,8},{10,11... | collective-permute-start | bytes 1572872 | tf_op jit(solution)/shard_map/ppermute | solution.py:52
  59.2 1.5 collective-permute-done
  60.7 1.2 select_add_fusion
  61.9 0.1 select_convert_fusion.2
  62.0 17.5 %all_to_all.25 = bf16[4,64,512]{2,1,0:T(8,128)(2,1)S(1)} all-to-all(bf16[4,64,512]{2,1,0:T(8,128)(2,1)S(1)} %select_convert_fusion.2), channel_id=1, replica_groups=mesh['y_lo'=2,'z'=8,'x'=4,'y_hi'=4,'core'=2] {'y_hi'}, dimensions={0} | all-to-all | bytes 524288 | tf_op jit(solution)/shard_map/all_to_all | solution.py:38
  79.5 0.8 broadcast_in_dim.67
  80.3 3.5 %all-to-all-start.2 = ((bf16[8,64,512]{2,1,0:T(8,128)(2,1)}), bf16[8,64,512]{2,1,0:T(8,128)(2,1)S(1)}, u32[]{:S(2)}, u32[]{:S(2)}) async-start(bf16[8,64,512]{2,1,0:T(8,128)(2,1)} %broadcast_in_dim.67), calls=%async_computation.2 | async-start | bytes 1048576 | tf_op jit(solution)/shard_map/all_to_all | solution.py:32
  83.9 0.7 collective-permute-start.1
  84.5 0.0 collective-permute-done.1
  84.6 4.1 %all-gather.3 = bf16[128,512]{1,0:T(8,128)(2,1)S(1)} all-gather(bf16[64,512]{1,0:T(8,128)(2,1)S(1)} %collective-permute-done.1), channel_id=5, replica_groups=mesh['y_lo'=2,'z'=8,'x'=4,'y_hi'=4,'core'=2] {'y_lo'}, dimensions={0}, use_global_device_ids=true | all-gather | bytes 196608 | tf_op jit(solution)/shard_map/all_gather | solution.py:59
  88.6 13.0 %all-to-all-done.2 = bf16[8,64,512]{2,1,0:T(8,128)(2,1)S(1)} async-done(((bf16[8,64,512]{2,1,0:T(8,128)(2,1)}), bf16[8,64,512]{2,1,0:T(8,128)(2,1)S(1)}, u32[]{:S(2)}, u32[]{:S(2)}) %all-to-all-start.2) | async-done | bytes 524320 | tf_op jit(solution)/shard_map/all_to_all | solution.py:32
  101.7 2.4 %collective-permute-start.2 = (bf16[512,512]{1,0:T(8,128)(2,1)S(1)}, bf16[512,512]{1,0:T(8,128)(2,1)S(1)}, u32[]{:S(2)}, u32[]{:S(2)}) collective-permute-start(bf16[512,512]{1,0:T(8,128)(2,1)S(1)} %bitcast.55), channel_id=1, source_target_pairs={{0,1},{1,0},{2,3},{3,2},{4,5},{5,4},{6,7},{7,6},{8,9},{9,8},{10,11... | collective-permute-start | bytes 1572872 | tf_op jit(solution)/shard_map/ppermute | solution.py:58
  104.1 10.9 %all-gather.4 = bf16[8,64,512]{2,1,0:T(8,128)(2,1)S(1)} all-gather(bf16[2,64,512]{2,1,0:T(8,128)(2,1)S(1)} %bitcast.59), channel_id=6, replica_groups=mesh['y_lo'=2,'z'=8,'x'=4,'y_hi'=4,'core'=2] {'x'}, dimensions={0}, use_global_device_ids=true | all-gather | bytes 655360 | tf_op jit(solution)/shard_map/all_gather | solution.py:60
  115.0 0.3 fusion.10
  115.3 0.0 collective-permute-done.2
  115.3 0.3 convolution_add_fusion.1
  115.6 0.8 select_convert_fusion.1
  116.4 3.4 %all-to-all-start.3 = ((bf16[4,64,512]{2,1,0:T(8,128)(2,1)}), bf16[4,64,512]{2,1,0:T(8,128)(2,1)S(1)}, u32[]{:S(2)}, u32[]{:S(2)}) async-start(bf16[4,64,512]{2,1,0:T(8,128)(2,1)} %select_convert_fusion.1), calls=%async_computation.3 | async-start | bytes 524288 | tf_op jit(solution)/shard_map/all_to_all | solution.py:38
  119.9 0.1 fusion.5
  120.0 0.0 copy-start
  120.0 7.9 %all-to-all-done.3 = bf16[4,64,512]{2,1,0:T(8,128)(2,1)S(1)} async-done(((bf16[4,64,512]{2,1,0:T(8,128)(2,1)}), bf16[4,64,512]{2,1,0:T(8,128)(2,1)S(1)}, u32[]{:S(2)}, u32[]{:S(2)}) %all-to-all-start.3) | async-done | bytes 262176 | tf_op jit(solution)/shard_map/all_to_all | solution.py:38
  128.0 0.1 fusion.4
  128.1 19.2 %all_gather.35 = bf16[512,512]{1,0:T(8,128)(2,1)S(1)} all-gather(bf16[64,512]{1,0:T(8,128)(2,1)S(1)} %fusion.4), channel_id=1, replica_groups=mesh['y_lo'=2,'z'=8,'x'=4,'y_hi'=4,'core'=2] {'y_hi','core'}, dimensions={0}, use_global_device_ids=true | all-gather | bytes 589824 | tf_op jit(solution)/shard_map/all_gather | solution.py:76
  147.3 0.0 copy-done
  147.3 1.1 select_convert_fusion
  148.5 25.5 %all_to_all.26 = bf16[8,64,1536]{2,1,0:T(8,128)(2,1)S(1)} all-to-all(bf16[8,64,1536]{2,1,0:T(8,128)(2,1)S(1)} %get-tuple-element.11), channel_id=1, replica_groups=mesh['y_lo'=2,'z'=8,'x'=4,'y_hi'=4,'core'=2] {'x','y_lo'}, dimensions={0} | all-to-all | bytes 3145728 | tf_op jit(solution)/shard_map/all_to_all | solution.py:38
  174.0 0.2 convert_reduce_fusion
  174.2 0.8 bitcast_add_fusion
  (10 shorter events, 0.2 us)
Async XLA Ops:
  2.3 49.1 %all-to-all-start = ((bf16[8,64,1536]{2,1,0:T(8,128)(2,1)}), bf16[8,64,1536]{2,1,0:T(8,128)(2,1)S(1)}, u32[]{:S(2)}, u32[]{:S(2)}) async-start(bf16[8,64,1536]{2,1,0:T(8,128)(2,1)} %broadcast_in_dim.63), calls=%async_computation | async-start | bytes 3145728 | tf_op jit(solution)/shard_map/all_to_all | solution.py:32
  54.6 6.1 %collective-permute-start = (f32[256,512]{1,0:T(8,128)S(1)}, f32[256,512]{1,0:T(8,128)S(1)}, u32[]{:S(2)}, u32[]{:S(2)}) collective-permute-start(f32[256,512]{1,0:T(8,128)S(1)} %get-tuple-element.9), channel_id=1, source_target_pairs={{0,1},{1,0},{2,3},{3,2},{4,5},{5,4},{6,7},{7,6},{8,9},{9,8},{10,11... | collective-permute-start | bytes 1572872 | tf_op jit(solution)/shard_map/ppermute | solution.py:52
  80.3 21.4 %all-to-all-start.2 = ((bf16[8,64,512]{2,1,0:T(8,128)(2,1)}), bf16[8,64,512]{2,1,0:T(8,128)(2,1)S(1)}, u32[]{:S(2)}, u32[]{:S(2)}) async-start(bf16[8,64,512]{2,1,0:T(8,128)(2,1)} %broadcast_in_dim.67), calls=%async_computation.2 | async-start | bytes 1048576 | tf_op jit(solution)/shard_map/all_to_all | solution.py:32
  83.9 0.7 collective-permute-start.1
  101.7 13.6 %collective-permute-start.2 = (bf16[512,512]{1,0:T(8,128)(2,1)S(1)}, bf16[512,512]{1,0:T(8,128)(2,1)S(1)}, u32[]{:S(2)}, u32[]{:S(2)}) collective-permute-start(bf16[512,512]{1,0:T(8,128)(2,1)S(1)} %bitcast.55), channel_id=1, source_target_pairs={{0,1},{1,0},{2,3},{3,2},{4,5},{5,4},{6,7},{7,6},{8,9},{9,8},{10,11... | collective-permute-start | bytes 1572872 | tf_op jit(solution)/shard_map/ppermute | solution.py:58
  116.4 11.5 %all-to-all-start.3 = ((bf16[4,64,512]{2,1,0:T(8,128)(2,1)}), bf16[4,64,512]{2,1,0:T(8,128)(2,1)S(1)}, u32[]{:S(2)}, u32[]{:S(2)}) async-start(bf16[4,64,512]{2,1,0:T(8,128)(2,1)} %select_convert_fusion.1), calls=%async_computation.3 | async-start | bytes 524288 | tf_op jit(solution)/shard_map/all_to_all | solution.py:38
  120.0 27.4 %copy-start = (f32[64,1536]{1,0:T(8,128)S(1)}, f32[64,1536]{1,0:T(8,128)}, u32[]{:S(2)}) copy-start(f32[64,1536]{1,0:T(8,128)} %param.1) | copy-start | bytes 1179652

commit v29 on v23

--- a/solution.py
+++ b/solution.py
@@ -10,9 +10,10 @@
 coef_quintic = 2.0315
 
 LO = ("x", "y_lo")
-COL = ("y_hi", "core")
+Y_HI = ("y_hh", "y_hl")
+COL = Y_HI + ("core",)
 ROW = ("y_lo", "z", "x")
-MESH = ("y_lo", "z", "x", "y_hi", "core")
+MESH = ("y_lo", "z", "x") + COL
 
 
 def rest_of(x):
@@ -25,7 +26,7 @@
 
 def swap_x_y_hi(block):
     pairs = [((x * 4 + y) * 2 + k, (y * 4 + x) * 2 + k) for x in range(4) for y in range(4) for k in range(2)]
-    return lax.ppermute(block, ("x", "y_hi", "core"), pairs)
+    return lax.ppermute(block, ("x",) + COL, pairs)
 
 
 def spread(block, axis):
@@ -44,11 +45,11 @@
     rows, cols = x_scaled.shape
     xb = x_scaled.astype(jnp.bfloat16)
     by_hi = spread(xb, "z").reshape(8 * rows, cols)
-    pair = lax.all_gather(xb, "y_lo", axis=0)
-    by_lo = [lax.all_gather(pair[y], "x", axis=0, tiled=True) for y in range(2)]
+    four = lax.all_gather(xb, "x", axis=0, tiled=True)
+    by_lo = [lax.all_gather(half, "y_lo", axis=0, tiled=True) for half in (four[: 2 * rows], four[2 * rows :])]
 
     tile = jnp.concatenate([dot_nt(part, by_hi) for part in by_lo]) * (1.0 / N)
-    gram = sum_pieces(tile.reshape(8, rows, 8 * rows), ("core", "y_hi"))
+    gram = sum_pieces(tile.reshape(8, rows, 8 * rows), ("y_hh", "core", "y_hl"))
 
     rounded = gram.astype(jnp.bfloat16)
     right = spread(rounded, "z").reshape(8 * rows, 8 * rows)
@@ -61,9 +62,9 @@
     square = jnp.dot(own, right, preferred_element_type=jnp.float32) + jnp.dot(
         other, right_other, preferred_element_type=jnp.float32
     )
-    square = sum_pieces(square.reshape(4, rows, 8 * rows), "y_hi")
+    square = sum_pieces(square.reshape(4, rows, 8 * rows), Y_HI)
 
-    place = (lax.axis_index("y_hi"), core, 0, 0)
+    place = (lax.axis_index(Y_HI), core, 0, 0)
     at_home = lax.dynamic_slice(left, place, (1, 1, rows, 8 * rows), allow_negative_indices=False)[0, 0]
     column = lax.broadcasted_iota(jnp.int32, at_home.shape, 1) - lax.axis_index("z") * rows
     on_diagonal = column == lax.broadcasted_iota(jnp.int32, at_home.shape, 0)
@@ -79,7 +80,7 @@
 
 
 def solution(mesh):
-    fine = Mesh(mesh.devices.reshape(2, 8, 4, 4, 2), MESH)
+    fine = Mesh(mesh.devices.reshape(2, 8, 4, 2, 2, 2), MESH)
     return jax.shard_map(
         per_device,
         mesh=fine,

time: 174 us -> 174 us (level)
  no operation moved by 1% of the time
where the time goes in v29:
time: 174 us
  blocking collectives  115 us (66%)
  waiting for transfers between devices  27.8 us (16%)
  starting transfers between devices  20.8 us (12%)
  other arithmetic  4.4 us (3%)
  matrix products  2.95 us (2%)
  local copies, waits for them, and re-layouts  2.28 us (1%)
    all_to_all x2, blocking collectives, sum_pieces(): lax.all_to_all(jnp.where(mine, 0.0, pieces).astype(jnp.bfloat16), axis, 0...  50.2 us
    all_to_all x2, waiting for transfers between devices, spread(): lax.all_to_all(jnp.broadcast_to(block[None], (8,) + block.shape), axis, 0...  20.9 us
    all_gather x1, blocking collectives, per_device(): poly = lax.all_gather(poly, COL, axis=0, tiled=True)  19.6 us
    all_gather x2, blocking collectives, per_device(): lax.all_gather(half, 'y_lo', axis=0, tiled=True)  17.7 us
    all_to_all x2, starting transfers between devices, spread(): lax.all_to_all(jnp.broadcast_to(block[None], (8,) + block.shape), axis, 0...  14.4 us
    all_gather x1, blocking collectives, per_device(): four = lax.all_gather(xb, 'x', axis=0, tiled=True)  12.6 us
    all_gather x1, blocking collectives, per_device(): left = lax.all_gather(left, 'x', axis=0).reshape(4, 2, rows, 8 * rows)  10.9 us
    all_to_all x1, waiting for transfers between devices, sum_pieces(): lax.all_to_all(jnp.where(mine, 0.0, pieces).astype(jnp.bfloat16), axis, 0...  6.93 us
  transfers between devices with their start and end apart: 5, of which 3 were waited for; matrix products, arithmetic and copies ran while one was open for 1% of the time, Pallas kernels for 0%

profile of v29, /device:TPU:1, one launch (start us, length us, event | category | flops | bytes accessed | tf_op | source)
XLA Modules:
  0.0 173.6 jit_solution(5427084548119837194)
XLA Ops:
  0.0 1.0 convert_element_type.36
  1.0 1.3 broadcast_in_dim.71
  2.3 10.9 %all-to-all-start = ((bf16[8,64,1536]{2,1,0:T(8,128)(2,1)}), bf16[8,64,1536]{2,1,0:T(8,128)(2,1)S(1)}, u32[]{:S(2)}, u32[]{:S(2)}) async-start(bf16[8,64,1536]{2,1,0:T(8,128)(2,1)} %broadcast_in_dim.71), calls=%async_computation | async-start | bytes 3145728 | tf_op jit(solution)/shard_map/all_to_all | solution.py:33
  13.2 12.6 %all_gather.24 = bf16[256,1536]{1,0:T(8,128)(2,1)S(1)} all-gather(bf16[64,1536]{1,0:T(8,128)(2,1)S(1)} %convert_element_type.36), channel_id=1, replica_groups=mesh['y_lo'=2,'z'=8,'x'=4,'y_hh'=2,'y_hl'=2,'core'=2] {'x'}, dimensions={0}, use_global_device_ids=true | all-gather | bytes 983040 | tf_op jit(solution)/shard_map/all_gather | solution.py:48
  25.8 0.1 fusion.9
  25.9 9.3 %all_gather.25 = bf16[256,1536]{1,0:T(8,128)(2,1)S(1)} all-gather(bf16[128,1536]{1,0:T(8,128)(2,1)S(1)} %get-tuple-element.5), channel_id=1, replica_groups=mesh['y_lo'=2,'z'=8,'x'=4,'y_hh'=2,'y_hl'=2,'core'=2] {'y_lo'}, dimensions={0}, use_global_device_ids=true | all-gather | bytes 1179648 | tf_op jit(solution)/shard_map/all_gather | solution.py:49
  35.2 8.4 %all_gather.26 = bf16[256,1536]{1,0:T(8,128)(2,1)S(1)} all-gather(bf16[128,1536]{1,0:T(8,128)(2,1)S(1)} %get-tuple-element.6), channel_id=1, replica_groups=mesh['y_lo'=2,'z'=8,'x'=4,'y_hh'=2,'y_hl'=2,'core'=2] {'y_lo'}, dimensions={0}, use_global_device_ids=true | all-gather | bytes 1179648 | tf_op jit(solution)/shard_map/all_gather | solution.py:49
  43.6 7.9 %all-to-all-done = bf16[8,64,1536]{2,1,0:T(8,128)(2,1)S(1)} async-done(((bf16[8,64,1536]{2,1,0:T(8,128)(2,1)}), bf16[8,64,1536]{2,1,0:T(8,128)(2,1)S(1)}, u32[]{:S(2)}, u32[]{:S(2)}) %all-to-all-start) | async-done | bytes 1572896 | tf_op jit(solution)/shard_map/all_to_all | solution.py:33
  51.4 0.6 fusion.11
  52.0 0.6 fusion.10
  52.6 0.1 maximum_multiply_fusion
  52.8 0.2 select_convert_fusion.1
  52.9 26.0 %all_to_all.25 = bf16[8,64,512]{2,1,0:T(8,128)(2,1)S(1)} all-to-all(bf16[8,64,512]{2,1,0:T(8,128)(2,1)S(1)} %select_convert_fusion.1), channel_id=1, replica_groups=mesh['y_lo'=2,'z'=8,'x'=4,'y_hh'=2,'y_hl'=2,'core'=2] {'y_hh','core','y_..., dimensions={0} | all-to-all | bytes 1048576 | tf_op jit(solution)/shard_map/all_to_all | solution.py:39
  78.9 0.1 convert_reduce_fusion.1
  79.0 0.8 broadcast_in_dim.75
  79.8 3.5 %all-to-all-start.2 = ((bf16[8,64,512]{2,1,0:T(8,128)(2,1)}), bf16[8,64,512]{2,1,0:T(8,128)(2,1)S(1)}, u32[]{:S(2)}, u32[]{:S(2)}) async-start(bf16[8,64,512]{2,1,0:T(8,128)(2,1)} %broadcast_in_dim.75), calls=%async_computation.2 | async-start | bytes 1048576 | tf_op jit(solution)/shard_map/all_to_all | solution.py:33
  83.4 0.7 collective-permute-start
  84.1 0.0 collective-permute-done
  84.1 4.1 %all-gather = bf16[128,512]{1,0:T(8,128)(2,1)S(1)} all-gather(bf16[64,512]{1,0:T(8,128)(2,1)S(1)} %collective-permute-done), channel_id=2, replica_groups=mesh['y_lo'=2,'z'=8,'x'=4,'y_hh'=2,'y_hl'=2,'core'=2] {'y_lo'}, dimensions={0}, use_global_device_ids=true | all-gather | bytes 196608 | tf_op jit(solution)/shard_map/all_gather | solution.py:57
  88.2 13.0 %all-to-all-done.2 = bf16[8,64,512]{2,1,0:T(8,128)(2,1)S(1)} async-done(((bf16[8,64,512]{2,1,0:T(8,128)(2,1)}), bf16[8,64,512]{2,1,0:T(8,128)(2,1)S(1)}, u32[]{:S(2)}, u32[]{:S(2)}) %all-to-all-start.2) | async-done | bytes 524320 | tf_op jit(solution)/shard_map/all_to_all | solution.py:33
  101.2 2.4 %collective-permute-start.1 = (bf16[512,512]{1,0:T(8,128)(2,1)S(1)}, bf16[512,512]{1,0:T(8,128)(2,1)S(1)}, u32[]{:S(2)}, u32[]{:S(2)}) collective-permute-start(bf16[512,512]{1,0:T(8,128)(2,1)S(1)} %bitcast.55), channel_id=1, source_target_pairs={{0,1},{1,0},{2,3},{3,2},{4,5},{5,4},{6,7},{7,6},{8,9},{9,8},{10,11... | collective-permute-start | bytes 1572872 | tf_op jit(solution)/shard_map/ppermute | solution.py:56
  103.6 10.9 %all-gather.1 = bf16[8,64,512]{2,1,0:T(8,128)(2,1)S(1)} all-gather(bf16[2,64,512]{2,1,0:T(8,128)(2,1)S(1)} %bitcast.59), channel_id=3, replica_groups=mesh['y_lo'=2,'z'=8,'x'=4,'y_hh'=2,'y_hl'=2,'core'=2] {'x'}, dimensions={0}, use_global_device_ids=true | all-gather | bytes 655360 | tf_op jit(solution)/shard_map/all_gather | solution.py:58
  114.5 0.0 copy-start
  114.5 0.3 fusion.12
  114.8 0.0 collective-permute-done.1
  114.8 0.3 convolution_add_fusion.1
  115.1 0.1 copy-done
  115.3 0.8 select_convert_fusion.2
  116.1 3.4 %all-to-all-start.3 = ((bf16[4,64,512]{2,1,0:T(8,128)(2,1)}), bf16[4,64,512]{2,1,0:T(8,128)(2,1)S(1)}, u32[]{:S(2)}, u32[]{:S(2)}) async-start(bf16[4,64,512]{2,1,0:T(8,128)(2,1)} %select_convert_fusion.2), calls=%async_computation.3 | async-start | bytes 524288 | tf_op jit(solution)/shard_map/all_to_all | solution.py:39
  119.5 1.0 fusion.5
  120.5 6.9 %all-to-all-done.3 = bf16[4,64,512]{2,1,0:T(8,128)(2,1)S(1)} async-done(((bf16[4,64,512]{2,1,0:T(8,128)(2,1)}), bf16[4,64,512]{2,1,0:T(8,128)(2,1)S(1)}, u32[]{:S(2)}, u32[]{:S(2)}) %all-to-all-start.3) | async-done | bytes 262176 | tf_op jit(solution)/shard_map/all_to_all | solution.py:39
  127.4 0.0 copy-start.1
  127.4 0.1 fusion.4
  127.5 19.6 %all_gather.31 = bf16[512,512]{1,0:T(8,128)(2,1)S(1)} all-gather(bf16[64,512]{1,0:T(8,128)(2,1)S(1)} %fusion.4), channel_id=1, replica_groups=mesh['y_lo'=2,'z'=8,'x'=4,'y_hh'=2,'y_hl'=2,'core'=2] {'y_hh','y_hl','co..., dimensions={0}, use_global_device_ids=true | all-gather | bytes 589824 | tf_op jit(solution)/shard_map/all_gather | solution.py:75
  147.1 0.0 copy-done.1
  147.1 1.2 select_convert_fusion
  148.3 24.2 %all_to_all.26 = bf16[8,64,1536]{2,1,0:T(8,128)(2,1)S(1)} all-to-all(bf16[8,64,1536]{2,1,0:T(8,128)(2,1)S(1)} %get-tuple-element.9), channel_id=1, replica_groups=mesh['y_lo'=2,'z'=8,'x'=4,'y_hh'=2,'y_hl'=2,'core'=2] {'x','y_lo'}, dimensions={0} | all-to-all | bytes 3145728 | tf_op jit(solution)/shard_map/all_to_all | solution.py:39
  172.5 0.2 convert_reduce_fusion
  172.7 0.8 bitcast_add_fusion
  (9 shorter events, 0.1 us)
Async XLA Ops:
  2.3 49.1 %all-to-all-start = ((bf16[8,64,1536]{2,1,0:T(8,128)(2,1)}), bf16[8,64,1536]{2,1,0:T(8,128)(2,1)S(1)}, u32[]{:S(2)}, u32[]{:S(2)}) async-start(bf16[8,64,1536]{2,1,0:T(8,128)(2,1)} %broadcast_in_dim.71), calls=%async_computation | async-start | bytes 3145728 | tf_op jit(solution)/shard_map/all_to_all | solution.py:33
  79.8 21.4 %all-to-all-start.2 = ((bf16[8,64,512]{2,1,0:T(8,128)(2,1)}), bf16[8,64,512]{2,1,0:T(8,128)(2,1)S(1)}, u32[]{:S(2)}, u32[]{:S(2)}) async-start(bf16[8,64,512]{2,1,0:T(8,128)(2,1)} %broadcast_in_dim.75), calls=%async_computation.2 | async-start | bytes 1048576 | tf_op jit(solution)/shard_map/all_to_all | solution.py:33
  83.4 0.7 collective-permute-start
  101.2 13.6 %collective-permute-start.1 = (bf16[512,512]{1,0:T(8,128)(2,1)S(1)}, bf16[512,512]{1,0:T(8,128)(2,1)S(1)}, u32[]{:S(2)}, u32[]{:S(2)}) collective-permute-start(bf16[512,512]{1,0:T(8,128)(2,1)S(1)} %bitcast.55), channel_id=1, source_target_pairs={{0,1},{1,0},{2,3},{3,2},{4,5},{5,4},{6,7},{7,6},{8,9},{9,8},{10,11... | collective-permute-start | bytes 1572872 | tf_op jit(solution)/shard_map/ppermute | solution.py:56
  114.5 0.8 copy-start
  116.1 11.3 %all-to-all-start.3 = ((bf16[4,64,512]{2,1,0:T(8,128)(2,1)}), bf16[4,64,512]{2,1,0:T(8,128)(2,1)S(1)}, u32[]{:S(2)}, u32[]{:S(2)}) async-start(bf16[4,64,512]{2,1,0:T(8,128)(2,1)} %select_convert_fusion.2), calls=%async_computation.3 | async-start | bytes 524288 | tf_op jit(solution)/shard_map/all_to_all | solution.py:39
  127.4 19.7 %copy-start.1 = (f32[64,1536]{1,0:T(8,128)S(1)}, f32[64,1536]{1,0:T(8,128)}, u32[]{:S(2)}) copy-start(f32[64,1536]{1,0:T(8,128)} %param.1) | copy-start | bytes 1179652

commit v30 on v29

--- a/solution.py
+++ b/solution.py
@@ -43,13 +43,15 @@
 
 def per_device(x_scaled):
     rows, cols = x_scaled.shape
-    xb = x_scaled.astype(jnp.bfloat16)
-    by_hi = spread(xb, "z").reshape(8 * rows, cols)
+    ones = 1.0 + 0.0 * (jnp.arange(8) * lax.axis_index("z")).astype(jnp.float32)
+    copies = lax.optimization_barrier((x_scaled * ones[:, None, None]).astype(jnp.bfloat16))
+    xb = copies[0]
+    by_hi = lax.all_to_all(copies, "z", 0, 0).reshape(8 * rows, cols)
     four = lax.all_gather(xb, "x", axis=0, tiled=True)
     by_lo = [lax.all_gather(half, "y_lo", axis=0, tiled=True) for half in (four[: 2 * rows], four[2 * rows :])]
 
-    tile = jnp.concatenate([dot_nt(part, by_hi) for part in by_lo]) * (1.0 / N)
-    gram = sum_pieces(tile.reshape(8, rows, 8 * rows), ("y_hh", "core", "y_hl"))
+    tile = jnp.concatenate([dot_nt(part, by_hi).reshape(2, 2 * rows, 8 * rows) for part in by_lo], axis=1) * (1.0 / N)
+    gram = sum_pieces(tile.reshape(8, rows, 8 * rows), ("core",) + Y_HI)
 
     rounded = gram.astype(jnp.bfloat16)
     right = spread(rounded, "z").reshape(8 * rows, 8 * rows)

time: 174 us -> 174 us (level)
    all_to_all x0 -> x1, starting transfers between devices: none -> 10.9 us  [per_device(): by_hi = lax.all_to_all(copies, 'z', 0, 0).reshape(8 * rows, cols)]
    all_to_all x2 -> x1, starting transfers between devices: 14.4 us -> 3.49 us  [spread(): lax.all_to_all(jnp.broadcast_to(block[None], (8,) + block.shape), axis, 0...]
    all_to_all x2 -> x1, waiting for transfers between devices: 20.9 us -> 12.9 us  [spread(): lax.all_to_all(jnp.broadcast_to(block[None], (8,) + block.shape), axis, 0...]
    all_to_all x0 -> x1, waiting for transfers between devices: none -> 6.91 us  [per_device(): by_hi = lax.all_to_all(copies, 'z', 0, 0).reshape(8 * rows, cols)]
where the time goes in v30:
time: 174 us; the launch traced here: 173 us
  blocking collectives  115 us (66%)
  waiting for transfers between devices  26.8 us (15%)
  starting transfers between devices  20.8 us (12%)
  other arithmetic  5.84 us (3%)
  matrix products  2.97 us (2%)
  local copies, waits for them, and re-layouts  1.93 us (1%)
    all_to_all x2, blocking collectives, sum_pieces(): lax.all_to_all(jnp.where(mine, 0.0, pieces).astype(jnp.bfloat16), axis, 0...  49.7 us
    all_gather x1, blocking collectives, per_device(): poly = lax.all_gather(poly, COL, axis=0, tiled=True)  19.6 us
    all_gather x2, blocking collectives, per_device(): lax.all_gather(half, 'y_lo', axis=0, tiled=True)  17.7 us
    all_to_all x1, waiting for transfers between devices, spread(): lax.all_to_all(jnp.broadcast_to(block[None], (8,) + block.shape), axis, 0...  12.9 us
    all_gather x1, blocking collectives, per_device(): four = lax.all_gather(xb, 'x', axis=0, tiled=True)  12.6 us
    all_gather x1, blocking collectives, per_device(): left = lax.all_gather(left, 'x', axis=0).reshape(4, 2, rows, 8 * rows)  10.9 us
    all_to_all x1, starting transfers between devices, per_device(): by_hi = lax.all_to_all(copies, 'z', 0, 0).reshape(8 * rows, cols)  10.9 us
    all_to_all x1, waiting for transfers between devices, sum_pieces(): lax.all_to_all(jnp.where(mine, 0.0, pieces).astype(jnp.bfloat16), axis, 0...  7.02 us
  transfers between devices with their start and end apart: 5, of which 3 were waited for; matrix products, arithmetic and copies ran while one was open for 1% of the time, Pallas kernels for 0%

profile of v30, /device:TPU:1, one launch (start us, length us, event | category | flops | bytes accessed | tf_op | source)
XLA Modules:
  0.0 173.4 jit_solution(15438416756026406293)
XLA Ops:
  0.0 2.4 %multiply_convert_fusion = bf16[8,64,1536]{2,1,0:T(8,128)(2,1)} fusion(f32[8]{0:T(128)S(1)} %multiply_add_fusion, f32[64,1536]{1,0:T(8,128)} %param.1), kind=kLoop, calls=%fused_computation.3 | loop fusion | flops 1572864 | bytes 1966112 | tf_op jit(solution)/shard_map/convert_element_type | solution.py:47
  2.5 10.9 %all-to-all-start = ((bf16[8,64,1536]{2,1,0:T(8,128)(2,1)}), bf16[8,64,1536]{2,1,0:T(8,128)(2,1)S(1)}, u32[]{:S(2)}, u32[]{:S(2)}) async-start(bf16[8,64,1536]{2,1,0:T(8,128)(2,1)} %multiply_convert_fusion), calls=%async_computation | async-start | bytes 3145728 | tf_op jit(solution)/shard_map/all_to_all | solution.py:49
  13.3 0.9 slice.24
  14.3 12.6 %all-gather = bf16[1,256,1536]{2,1,0:T(8,128)(2,1)S(1)} all-gather(bf16[1,64,1536]{2,1,0:T(8,128)(2,1)S(1)} %slice.24), channel_id=2, replica_groups=mesh['y_lo'=2,'z'=8,'x'=4,'y_hh'=2,'y_hl'=2,'core'=2] {'x'}, dimensions={1}, use_global_device_ids=true | all-gather | bytes 983040 | tf_op jit(solution)/shard_map/all_gather | solution.py:50
  26.9 0.1 fusion.9
  27.0 9.3 %all-gather.3 = bf16[1,256,1536]{2,1,0:T(8,128)(2,1)S(1)} all-gather(bf16[1,128,1536]{2,1,0:T(8,128)(2,1)S(1)} %get-tuple-element.5), channel_id=5, replica_groups=mesh['y_lo'=2,'z'=8,'x'=4,'y_hh'=2,'y_hl'=2,'core'=2] {'y_lo'}, dimensions={1}, use_global_device_ids=true | all-gather | bytes 1179648 | tf_op jit(solution)/shard_map/all_gather | solution.py:51
  36.3 8.4 %all-gather.4 = bf16[1,256,1536]{2,1,0:T(8,128)(2,1)S(1)} all-gather(bf16[1,128,1536]{2,1,0:T(8,128)(2,1)S(1)} %get-tuple-element.6), channel_id=6, replica_groups=mesh['y_lo'=2,'z'=8,'x'=4,'y_hh'=2,'y_hl'=2,'core'=2] {'y_lo'}, dimensions={1}, use_global_device_ids=true | all-gather | bytes 1179648 | tf_op jit(solution)/shard_map/all_gather | solution.py:51
  44.7 6.9 %all-to-all-done = bf16[8,64,1536]{2,1,0:T(8,128)(2,1)S(1)} async-done(((bf16[8,64,1536]{2,1,0:T(8,128)(2,1)}), bf16[8,64,1536]{2,1,0:T(8,128)(2,1)S(1)}, u32[]{:S(2)}, u32[]{:S(2)}) %all-to-all-start) | async-done | bytes 1572896 | tf_op jit(solution)/shard_map/all_to_all | solution.py:49
  51.6 0.6 fusion.10
  52.2 0.6 fusion.11
  52.8 0.1 maximum_multiply_fusion
  52.9 0.2 select_convert_fusion.1
  53.1 25.4 %all_to_all.25 = bf16[8,64,512]{2,1,0:T(8,128)(2,1)S(1)} all-to-all(bf16[8,64,512]{2,1,0:T(8,128)(2,1)S(1)} %select_convert_fusion.1), channel_id=1, replica_groups=mesh['y_lo'=2,'z'=8,'x'=4,'y_hh'=2,'y_hl'=2,'core'=2] {'core','y_hh','y_..., dimensions={0} | all-to-all | bytes 1048576 | tf_op jit(solution)/shard_map/all_to_all | solution.py:39
  78.5 0.1 convert_reduce_fusion.1
  78.6 0.8 broadcast_in_dim.68
  79.4 3.5 %all-to-all-start.2 = ((bf16[8,64,512]{2,1,0:T(8,128)(2,1)}), bf16[8,64,512]{2,1,0:T(8,128)(2,1)S(1)}, u32[]{:S(2)}, u32[]{:S(2)}) async-start(bf16[8,64,512]{2,1,0:T(8,128)(2,1)} %broadcast_in_dim.68), calls=%async_computation.2 | async-start | bytes 1048576 | tf_op jit(solution)/shard_map/all_to_all | solution.py:33
  83.0 0.7 collective-permute-start
  83.7 0.0 collective-permute-done
  83.7 4.3 %all-gather.1 = bf16[128,512]{1,0:T(8,128)(2,1)S(1)} all-gather(bf16[64,512]{1,0:T(8,128)(2,1)S(1)} %collective-permute-done), channel_id=3, replica_groups=mesh['y_lo'=2,'z'=8,'x'=4,'y_hh'=2,'y_hl'=2,'core'=2] {'y_lo'}, dimensions={0}, use_global_device_ids=true | all-gather | bytes 196608 | tf_op jit(solution)/shard_map/all_gather | solution.py:59
  88.0 12.9 %all-to-all-done.2 = bf16[8,64,512]{2,1,0:T(8,128)(2,1)S(1)} async-done(((bf16[8,64,512]{2,1,0:T(8,128)(2,1)}), bf16[8,64,512]{2,1,0:T(8,128)(2,1)S(1)}, u32[]{:S(2)}, u32[]{:S(2)}) %all-to-all-start.2) | async-done | bytes 524320 | tf_op jit(solution)/shard_map/all_to_all | solution.py:33
  100.9 2.3 %collective-permute-start.1 = (bf16[512,512]{1,0:T(8,128)(2,1)S(1)}, bf16[512,512]{1,0:T(8,128)(2,1)S(1)}, u32[]{:S(2)}, u32[]{:S(2)}) collective-permute-start(bf16[512,512]{1,0:T(8,128)(2,1)S(1)} %bitcast.59), channel_id=1, source_target_pairs={{0,1},{1,0},{2,3},{3,2},{4,5},{5,4},{6,7},{7,6},{8,9},{9,8},{10,11... | collective-permute-start | bytes 1572872 | tf_op jit(solution)/shard_map/ppermute | solution.py:58
  103.3 10.9 %all-gather.2 = bf16[8,64,512]{2,1,0:T(8,128)(2,1)S(1)} all-gather(bf16[2,64,512]{2,1,0:T(8,128)(2,1)S(1)} %bitcast.63), channel_id=4, replica_groups=mesh['y_lo'=2,'z'=8,'x'=4,'y_hh'=2,'y_hl'=2,'core'=2] {'x'}, dimensions={0}, use_global_device_ids=true | all-gather | bytes 655360 | tf_op jit(solution)/shard_map/all_gather | solution.py:60
  114.1 0.0 copy-start
  114.2 0.3 fusion.12
  114.5 0.0 collective-permute-done.1
  114.5 0.3 convolution_add_fusion.1
  114.8 0.1 copy-done
  114.9 0.8 select_convert_fusion.2
  115.7 3.4 %all-to-all-start.3 = ((bf16[4,64,512]{2,1,0:T(8,128)(2,1)}), bf16[4,64,512]{2,1,0:T(8,128)(2,1)S(1)}, u32[]{:S(2)}, u32[]{:S(2)}) async-start(bf16[4,64,512]{2,1,0:T(8,128)(2,1)} %select_convert_fusion.2), calls=%async_computation.3 | async-start | bytes 524288 | tf_op jit(solution)/shard_map/all_to_all | solution.py:39
  119.2 1.0 fusion.5
  120.1 7.0 %all-to-all-done.3 = bf16[4,64,512]{2,1,0:T(8,128)(2,1)S(1)} async-done(((bf16[4,64,512]{2,1,0:T(8,128)(2,1)}), bf16[4,64,512]{2,1,0:T(8,128)(2,1)S(1)}, u32[]{:S(2)}, u32[]{:S(2)}) %all-to-all-start.3) | async-done | bytes 262176 | tf_op jit(solution)/shard_map/all_to_all | solution.py:39
  127.2 0.0 copy-start.1
  127.2 0.1 fusion.4
  127.3 19.6 %all_gather.31 = bf16[512,512]{1,0:T(8,128)(2,1)S(1)} all-gather(bf16[64,512]{1,0:T(8,128)(2,1)S(1)} %fusion.4), channel_id=1, replica_groups=mesh['y_lo'=2,'z'=8,'x'=4,'y_hh'=2,'y_hl'=2,'core'=2] {'y_hh','y_hl','co..., dimensions={0}, use_global_device_ids=true | all-gather | bytes 589824 | tf_op jit(solution)/shard_map/all_gather | solution.py:77
  146.9 0.0 copy-done.1
  146.9 1.2 select_convert_fusion
  148.1 24.3 %all_to_all.26 = bf16[8,64,1536]{2,1,0:T(8,128)(2,1)S(1)} all-to-all(bf16[8,64,1536]{2,1,0:T(8,128)(2,1)S(1)} %get-tuple-element.9), channel_id=1, replica_groups=mesh['y_lo'=2,'z'=8,'x'=4,'y_hh'=2,'y_hl'=2,'core'=2] {'x','y_lo'}, dimensions={0} | all-to-all | bytes 3145728 | tf_op jit(solution)/shard_map/all_to_all | solution.py:39
  172.4 0.2 convert_reduce_fusion
  172.6 0.8 bitcast_add_fusion
  (10 shorter events, 0.1 us)
Async XLA Ops:
  2.5 49.1 %all-to-all-start = ((bf16[8,64,1536]{2,1,0:T(8,128)(2,1)}), bf16[8,64,1536]{2,1,0:T(8,128)(2,1)S(1)}, u32[]{:S(2)}, u32[]{:S(2)}) async-start(bf16[8,64,1536]{2,1,0:T(8,128)(2,1)} %multiply_convert_fusion), calls=%async_computation | async-start | bytes 3145728 | tf_op jit(solution)/shard_map/all_to_all | solution.py:49
  79.4 21.5 %all-to-all-start.2 = ((bf16[8,64,512]{2,1,0:T(8,128)(2,1)}), bf16[8,64,512]{2,1,0:T(8,128)(2,1)S(1)}, u32[]{:S(2)}, u32[]{:S(2)}) async-start(bf16[8,64,512]{2,1,0:T(8,128)(2,1)} %broadcast_in_dim.68), calls=%async_computation.2 | async-start | bytes 1048576 | tf_op jit(solution)/shard_map/all_to_all | solution.py:33
  83.0 0.7 collective-permute-start
  100.9 13.6 %collective-permute-start.1 = (bf16[512,512]{1,0:T(8,128)(2,1)S(1)}, bf16[512,512]{1,0:T(8,128)(2,1)S(1)}, u32[]{:S(2)}, u32[]{:S(2)}) collective-permute-start(bf16[512,512]{1,0:T(8,128)(2,1)S(1)} %bitcast.59), channel_id=1, source_target_pairs={{0,1},{1,0},{2,3},{3,2},{4,5},{5,4},{6,7},{7,6},{8,9},{9,8},{10,11... | collective-permute-start | bytes 1572872 | tf_op jit(solution)/shard_map/ppermute | solution.py:58
  114.1 0.8 copy-start
  115.7 11.4 %all-to-all-start.3 = ((bf16[4,64,512]{2,1,0:T(8,128)(2,1)}), bf16[4,64,512]{2,1,0:T(8,128)(2,1)S(1)}, u32[]{:S(2)}, u32[]{:S(2)}) async-start(bf16[4,64,512]{2,1,0:T(8,128)(2,1)} %select_convert_fusion.2), calls=%async_computation.3 | async-start | bytes 524288 | tf_op jit(solution)/shard_map/all_to_all | solution.py:39
  127.2 19.7 %copy-start.1 = (f32[64,1536]{1,0:T(8,128)S(1)}, f32[64,1536]{1,0:T(8,128)}, u32[]{:S(2)}) copy-start(f32[64,1536]{1,0:T(8,128)} %param.1) | copy-start | bytes 1179652

commit v31 on v29

--- a/solution.py
+++ b/solution.py
@@ -48,8 +48,8 @@
     four = lax.all_gather(xb, "x", axis=0, tiled=True)
     by_lo = [lax.all_gather(half, "y_lo", axis=0, tiled=True) for half in (four[: 2 * rows], four[2 * rows :])]
 
-    tile = jnp.concatenate([dot_nt(part, by_hi) for part in by_lo]) * (1.0 / N)
-    gram = sum_pieces(tile.reshape(8, rows, 8 * rows), ("y_hh", "core", "y_hl"))
+    tile = jnp.concatenate([dot_nt(part, by_hi).reshape(2, 2 * rows, 8 * rows) for part in by_lo], axis=1) * (1.0 / N)
+    gram = sum_pieces(tile.reshape(8, rows, 8 * rows), ("core",) + Y_HI)
 
     rounded = gram.astype(jnp.bfloat16)
     right = spread(rounded, "z").reshape(8 * rows, 8 * rows)

time: 174 us -> 174 us (level)
  no operation moved by 1% of the time
where the time goes in v31:
time: 174 us; the launch traced here: 173 us
  blocking collectives  115 us (66%)
  waiting for transfers between devices  27.8 us (16%)
  starting transfers between devices  20.8 us (12%)
  other arithmetic  4.4 us (3%)
  matrix products  2.95 us (2%)
  local copies, waits for them, and re-layouts  2.28 us (1%)
    all_to_all x2, blocking collectives, sum_pieces(): lax.all_to_all(jnp.where(mine, 0.0, pieces).astype(jnp.bfloat16), axis, 0...  49.7 us
    all_to_all x2, waiting for transfers between devices, spread(): lax.all_to_all(jnp.broadcast_to(block[None], (8,) + block.shape), axis, 0...  20.8 us
    all_gather x1, blocking collectives, per_device(): poly = lax.all_gather(poly, COL, axis=0, tiled=True)  19.6 us
    all_gather x2, blocking collectives, per_device(): lax.all_gather(half, 'y_lo', axis=0, tiled=True)  17.7 us
    all_to_all x2, starting transfers between devices, spread(): lax.all_to_all(jnp.broadcast_to(block[None], (8,) + block.shape), axis, 0...  14.4 us
    all_gather x1, blocking collectives, per_device(): four = lax.all_gather(xb, 'x', axis=0, tiled=True)  12.6 us
    all_gather x1, blocking collectives, per_device(): left = lax.all_gather(left, 'x', axis=0).reshape(4, 2, rows, 8 * rows)  10.9 us
    all_to_all x1, waiting for transfers between devices, sum_pieces(): lax.all_to_all(jnp.where(mine, 0.0, pieces).astype(jnp.bfloat16), axis, 0...  7.01 us
  transfers between devices with their start and end apart: 5, of which 3 were waited for; matrix products, arithmetic and copies ran while one was open for 1% of the time, Pallas kernels for 0%

profile of v31, /device:TPU:1, one launch (start us, length us, event | category | flops | bytes accessed | tf_op | source)
XLA Modules:
  0.0 173.3 jit_solution(11917254252651719064)
XLA Ops:
  0.0 1.0 convert_element_type.36
  1.0 1.3 broadcast_in_dim.71
  2.3 10.9 %all-to-all-start = ((bf16[8,64,1536]{2,1,0:T(8,128)(2,1)}), bf16[8,64,1536]{2,1,0:T(8,128)(2,1)S(1)}, u32[]{:S(2)}, u32[]{:S(2)}) async-start(bf16[8,64,1536]{2,1,0:T(8,128)(2,1)} %broadcast_in_dim.71), calls=%async_computation | async-start | bytes 3145728 | tf_op jit(solution)/shard_map/all_to_all | solution.py:33
  13.2 12.6 %all_gather.24 = bf16[256,1536]{1,0:T(8,128)(2,1)S(1)} all-gather(bf16[64,1536]{1,0:T(8,128)(2,1)S(1)} %convert_element_type.36), channel_id=1, replica_groups=mesh['y_lo'=2,'z'=8,'x'=4,'y_hh'=2,'y_hl'=2,'core'=2] {'x'}, dimensions={0}, use_global_device_ids=true | all-gather | bytes 983040 | tf_op jit(solution)/shard_map/all_gather | solution.py:48
  25.8 0.1 fusion.9
  25.9 9.3 %all_gather.25 = bf16[256,1536]{1,0:T(8,128)(2,1)S(1)} all-gather(bf16[128,1536]{1,0:T(8,128)(2,1)S(1)} %get-tuple-element.5), channel_id=1, replica_groups=mesh['y_lo'=2,'z'=8,'x'=4,'y_hh'=2,'y_hl'=2,'core'=2] {'y_lo'}, dimensions={0}, use_global_device_ids=true | all-gather | bytes 1179648 | tf_op jit(solution)/shard_map/all_gather | solution.py:49
  35.2 8.4 %all_gather.26 = bf16[256,1536]{1,0:T(8,128)(2,1)S(1)} all-gather(bf16[128,1536]{1,0:T(8,128)(2,1)S(1)} %get-tuple-element.6), channel_id=1, replica_groups=mesh['y_lo'=2,'z'=8,'x'=4,'y_hh'=2,'y_hl'=2,'core'=2] {'y_lo'}, dimensions={0}, use_global_device_ids=true | all-gather | bytes 1179648 | tf_op jit(solution)/shard_map/all_gather | solution.py:49
  43.6 7.9 %all-to-all-done = bf16[8,64,1536]{2,1,0:T(8,128)(2,1)S(1)} async-done(((bf16[8,64,1536]{2,1,0:T(8,128)(2,1)}), bf16[8,64,1536]{2,1,0:T(8,128)(2,1)S(1)}, u32[]{:S(2)}, u32[]{:S(2)}) %all-to-all-start) | async-done | bytes 1572896 | tf_op jit(solution)/shard_map/all_to_all | solution.py:33
  51.4 0.6 fusion.11
  52.0 0.6 fusion.10
  52.6 0.1 maximum_multiply_fusion
  52.8 0.2 select_convert_fusion.1
  52.9 25.4 %all_to_all.25 = bf16[8,64,512]{2,1,0:T(8,128)(2,1)S(1)} all-to-all(bf16[8,64,512]{2,1,0:T(8,128)(2,1)S(1)} %select_convert_fusion.1), channel_id=1, replica_groups=mesh['y_lo'=2,'z'=8,'x'=4,'y_hh'=2,'y_hl'=2,'core'=2] {'core','y_hh','y_..., dimensions={0} | all-to-all | bytes 1048576 | tf_op jit(solution)/shard_map/all_to_all | solution.py:39
  78.4 0.1 convert_reduce_fusion.1
  78.5 0.8 broadcast_in_dim.75
  79.3 3.5 %all-to-all-start.2 = ((bf16[8,64,512]{2,1,0:T(8,128)(2,1)}), bf16[8,64,512]{2,1,0:T(8,128)(2,1)S(1)}, u32[]{:S(2)}, u32[]{:S(2)}) async-start(bf16[8,64,512]{2,1,0:T(8,128)(2,1)} %broadcast_in_dim.75), calls=%async_computation.2 | async-start | bytes 1048576 | tf_op jit(solution)/shard_map/all_to_all | solution.py:33
  82.8 0.7 collective-permute-start
  83.5 0.0 collective-permute-done
  83.5 4.3 %all-gather = bf16[128,512]{1,0:T(8,128)(2,1)S(1)} all-gather(bf16[64,512]{1,0:T(8,128)(2,1)S(1)} %collective-permute-done), channel_id=2, replica_groups=mesh['y_lo'=2,'z'=8,'x'=4,'y_hh'=2,'y_hl'=2,'core'=2] {'y_lo'}, dimensions={0}, use_global_device_ids=true | all-gather | bytes 196608 | tf_op jit(solution)/shard_map/all_gather | solution.py:57
  87.9 12.9 %all-to-all-done.2 = bf16[8,64,512]{2,1,0:T(8,128)(2,1)S(1)} async-done(((bf16[8,64,512]{2,1,0:T(8,128)(2,1)}), bf16[8,64,512]{2,1,0:T(8,128)(2,1)S(1)}, u32[]{:S(2)}, u32[]{:S(2)}) %all-to-all-start.2) | async-done | bytes 524320 | tf_op jit(solution)/shard_map/all_to_all | solution.py:33
  100.8 2.3 %collective-permute-start.1 = (bf16[512,512]{1,0:T(8,128)(2,1)S(1)}, bf16[512,512]{1,0:T(8,128)(2,1)S(1)}, u32[]{:S(2)}, u32[]{:S(2)}) collective-permute-start(bf16[512,512]{1,0:T(8,128)(2,1)S(1)} %bitcast.59), channel_id=1, source_target_pairs={{0,1},{1,0},{2,3},{3,2},{4,5},{5,4},{6,7},{7,6},{8,9},{9,8},{10,11... | collective-permute-start | bytes 1572872 | tf_op jit(solution)/shard_map/ppermute | solution.py:56
  103.1 10.9 %all-gather.1 = bf16[8,64,512]{2,1,0:T(8,128)(2,1)S(1)} all-gather(bf16[2,64,512]{2,1,0:T(8,128)(2,1)S(1)} %bitcast.63), channel_id=3, replica_groups=mesh['y_lo'=2,'z'=8,'x'=4,'y_hh'=2,'y_hl'=2,'core'=2] {'x'}, dimensions={0}, use_global_device_ids=true | all-gather | bytes 655360 | tf_op jit(solution)/shard_map/all_gather | solution.py:58
  114.0 0.0 copy-start
  114.0 0.3 fusion.12
  114.4 0.0 collective-permute-done.1
  114.4 0.3 convolution_add_fusion.1
  114.7 0.1 copy-done
  114.8 0.8 select_convert_fusion.2
  115.6 3.4 %all-to-all-start.3 = ((bf16[4,64,512]{2,1,0:T(8,128)(2,1)}), bf16[4,64,512]{2,1,0:T(8,128)(2,1)S(1)}, u32[]{:S(2)}, u32[]{:S(2)}) async-start(bf16[4,64,512]{2,1,0:T(8,128)(2,1)} %select_convert_fusion.2), calls=%async_computation.3 | async-start | bytes 524288 | tf_op jit(solution)/shard_map/all_to_all | solution.py:39
  119.0 1.0 fusion.5
  120.0 7.0 %all-to-all-done.3 = bf16[4,64,512]{2,1,0:T(8,128)(2,1)S(1)} async-done(((bf16[4,64,512]{2,1,0:T(8,128)(2,1)}), bf16[4,64,512]{2,1,0:T(8,128)(2,1)S(1)}, u32[]{:S(2)}, u32[]{:S(2)}) %all-to-all-start.3) | async-done | bytes 262176 | tf_op jit(solution)/shard_map/all_to_all | solution.py:39
  127.0 0.0 copy-start.1
  127.0 0.1 fusion.4
  127.1 19.6 %all_gather.31 = bf16[512,512]{1,0:T(8,128)(2,1)S(1)} all-gather(bf16[64,512]{1,0:T(8,128)(2,1)S(1)} %fusion.4), channel_id=1, replica_groups=mesh['y_lo'=2,'z'=8,'x'=4,'y_hh'=2,'y_hl'=2,'core'=2] {'y_hh','y_hl','co..., dimensions={0}, use_global_device_ids=true | all-gather | bytes 589824 | tf_op jit(solution)/shard_map/all_gather | solution.py:75
  146.8 0.0 copy-done.1
  146.8 1.2 select_convert_fusion
  147.9 24.3 %all_to_all.26 = bf16[8,64,1536]{2,1,0:T(8,128)(2,1)S(1)} all-to-all(bf16[8,64,1536]{2,1,0:T(8,128)(2,1)S(1)} %get-tuple-element.9), channel_id=1, replica_groups=mesh['y_lo'=2,'z'=8,'x'=4,'y_hh'=2,'y_hl'=2,'core'=2] {'x','y_lo'}, dimensions={0} | all-to-all | bytes 3145728 | tf_op jit(solution)/shard_map/all_to_all | solution.py:39
  172.2 0.2 convert_reduce_fusion
  172.4 0.8 bitcast_add_fusion
  (9 shorter events, 0.1 us)
Async XLA Ops:
  2.3 49.1 %all-to-all-start = ((bf16[8,64,1536]{2,1,0:T(8,128)(2,1)}), bf16[8,64,1536]{2,1,0:T(8,128)(2,1)S(1)}, u32[]{:S(2)}, u32[]{:S(2)}) async-start(bf16[8,64,1536]{2,1,0:T(8,128)(2,1)} %broadcast_in_dim.71), calls=%async_computation | async-start | bytes 3145728 | tf_op jit(solution)/shard_map/all_to_all | solution.py:33
  79.3 21.5 %all-to-all-start.2 = ((bf16[8,64,512]{2,1,0:T(8,128)(2,1)}), bf16[8,64,512]{2,1,0:T(8,128)(2,1)S(1)}, u32[]{:S(2)}, u32[]{:S(2)}) async-start(bf16[8,64,512]{2,1,0:T(8,128)(2,1)} %broadcast_in_dim.75), calls=%async_computation.2 | async-start | bytes 1048576 | tf_op jit(solution)/shard_map/all_to_all | solution.py:33
  82.8 0.7 collective-permute-start
  100.8 13.6 %collective-permute-start.1 = (bf16[512,512]{1,0:T(8,128)(2,1)S(1)}, bf16[512,512]{1,0:T(8,128)(2,1)S(1)}, u32[]{:S(2)}, u32[]{:S(2)}) collective-permute-start(bf16[512,512]{1,0:T(8,128)(2,1)S(1)} %bitcast.59), channel_id=1, source_target_pairs={{0,1},{1,0},{2,3},{3,2},{4,5},{5,4},{6,7},{7,6},{8,9},{9,8},{10,11... | collective-permute-start | bytes 1572872 | tf_op jit(solution)/shard_map/ppermute | solution.py:56
  114.0 0.8 copy-start
  115.6 11.4 %all-to-all-start.3 = ((bf16[4,64,512]{2,1,0:T(8,128)(2,1)}), bf16[4,64,512]{2,1,0:T(8,128)(2,1)S(1)}, u32[]{:S(2)}, u32[]{:S(2)}) async-start(bf16[4,64,512]{2,1,0:T(8,128)(2,1)} %select_convert_fusion.2), calls=%async_computation.3 | async-start | bytes 524288 | tf_op jit(solution)/shard_map/all_to_all | solution.py:39
  127.0 19.7 %copy-start.1 = (f32[64,1536]{1,0:T(8,128)S(1)}, f32[64,1536]{1,0:T(8,128)}, u32[]{:S(2)}) copy-start(f32[64,1536]{1,0:T(8,128)} %param.1) | copy-start | bytes 1179652

commit v32 on v25

--- a/solution.py
+++ b/solution.py
@@ -61,13 +61,14 @@
     square = jnp.dot(own, right, preferred_element_type=jnp.float32) + jnp.dot(
         other, right_other, preferred_element_type=jnp.float32
     )
-    place = (lax.axis_index("y_hi") * rows, 0)
-    at_home = lax.dynamic_slice(own, place, (rows, 8 * rows), allow_negative_indices=False)
+    place = (lax.axis_index("y_hi"), core, 0, 0)
+    at_home = lax.dynamic_slice(left, place, (1, 1, rows, 8 * rows), allow_negative_indices=False)[0, 0]
     column = lax.broadcasted_iota(jnp.int32, at_home.shape, 1) - lax.axis_index("z") * rows
     on_diagonal = column == lax.broadcasted_iota(jnp.int32, at_home.shape, 0)
     diagonal = jnp.where(on_diagonal, at_home.astype(jnp.float32), 0.0).sum(1, keepdims=True)
-    square = sum_pieces(square.reshape(4, rows, 8 * rows), "y_hi", 0.0 * diagonal[0, 0])
-    square = square + rest_of(gram) * (2.0 * diagonal)
+    twice = 2.0 * diagonal
+    square = sum_pieces(square.reshape(4, rows, 8 * rows), "y_hi", 0.0 * twice[0, 0])
+    square = square + rest_of(gram) * twice
 
     poly = (coef_cubic * gram + coef_quintic * square).astype(jnp.bfloat16)
     poly = lax.all_gather(poly, COL, axis=0, tiled=True)

time: 176 us -> 177 us (level)
  transfers between devices with their start and end apart: 5 -> 5, of which waited for: 2 -> 3; matrix products, arithmetic and copies ran while one was open for 1% -> 1% of each run, Pallas kernels for 0% -> 0%
where the time goes in v32:
time: 177 us; the launch traced here: 176 us
  blocking collectives  123 us (69%)
  starting transfers between devices  25.5 us (14%)
  waiting for transfers between devices  17.2 us (10%)
  matrix products  3.99 us (2%)
  other arithmetic  3.56 us (2%)
  local copies, waits for them, and re-layouts  2.17 us (1%)
    all_to_all x2, blocking collectives, sum_pieces(): lax.all_to_all(jnp.where(mine, zero, pieces).astype(jnp.bfloat16), axis,...  49.4 us
    all_gather x2, blocking collectives, per_device(): by_lo = [lax.all_gather(pair[y], 'x', axis=0, tiled=True) for y in range(2)]  23.9 us
    all_gather x1, blocking collectives, per_device(): left = lax.all_gather(left, 'x', axis=0).reshape(4, 2, rows, 8 * rows)  21.2 us
    all_gather x1, blocking collectives, per_device(): poly = lax.all_gather(poly, COL, axis=0, tiled=True)  18.3 us
    all_to_all x2, starting transfers between devices, spread(): lax.all_to_all(jnp.broadcast_to(block[None], (8,) + block.shape), axis, 0...  15 us
    all_to_all x1, waiting for transfers between devices, sum_pieces(): lax.all_to_all(jnp.where(mine, zero, pieces).astype(jnp.bfloat16), axis,...  8.73 us
    all_to_all x2, waiting for transfers between devices, spread(): lax.all_to_all(jnp.broadcast_to(block[None], (8,) + block.shape), axis, 0...  8.19 us
    ppermute x1, starting transfers between devices, per_device(): right_other = lax.ppermute(right, 'core', [(0, 1), (1, 0)])  6.45 us
  transfers between devices with their start and end apart: 5, of which 3 were waited for; matrix products, arithmetic and copies ran while one was open for 1% of the time, Pallas kernels for 0%

profile of v32, /device:TPU:1, one launch (start us, length us, event | category | flops | bytes accessed | tf_op | source)
XLA Modules:
  0.0 176.0 jit_solution(5224290762142902517)
XLA Ops:
  0.0 1.0 convert_element_type.36
  1.0 1.3 broadcast_in_dim.71
  2.3 10.9 %all-to-all-start = ((bf16[8,64,1536]{2,1,0:T(8,128)(2,1)}), bf16[8,64,1536]{2,1,0:T(8,128)(2,1)S(1)}, u32[]{:S(2)}, u32[]{:S(2)}) async-start(bf16[8,64,1536]{2,1,0:T(8,128)(2,1)} %broadcast_in_dim.71), calls=%async_computation | async-start | bytes 3145728 | tf_op jit(solution)/shard_map/all_to_all | solution.py:32
  13.2 6.1 %all-gather = bf16[128,1536]{1,0:T(8,128)(2,1)S(1)} all-gather(bf16[64,1536]{1,0:T(8,128)(2,1)S(1)} %convert_element_type.36), channel_id=2, replica_groups=mesh['y_lo'=2,'z'=8,'x'=4,'y_hi'=4,'core'=2] {'y_lo'}, dimensions={0}, use_global_device_ids=true | all-gather | bytes 589824 | tf_op jit(solution)/shard_map/all_gather | solution.py:47
  19.3 12.6 %all-gather.5 = bf16[256,1536]{1,0:T(8,128)(2,1)S(1)} all-gather(bf16[64,1536]{1,0:T(8,128)(2,1)S(1)} %get-tuple-element.7), channel_id=7, replica_groups=mesh['y_lo'=2,'z'=8,'x'=4,'y_hi'=4,'core'=2] {'x'}, dimensions={0}, use_global_device_ids=true | all-gather | bytes 983040 | tf_op jit(solution)/shard_map/all_gather | solution.py:48
  32.0 11.3 %all-gather.6 = bf16[256,1536]{1,0:T(8,128)(2,1)S(1)} all-gather(bf16[64,1536]{1,0:T(8,128)(2,1)S(1)} %get-tuple-element.8), channel_id=8, replica_groups=mesh['y_lo'=2,'z'=8,'x'=4,'y_hi'=4,'core'=2] {'x'}, dimensions={0}, use_global_device_ids=true | all-gather | bytes 983040 | tf_op jit(solution)/shard_map/all_gather | solution.py:48
  43.3 8.2 %all-to-all-done = bf16[8,64,1536]{2,1,0:T(8,128)(2,1)S(1)} async-done(((bf16[8,64,1536]{2,1,0:T(8,128)(2,1)}), bf16[8,64,1536]{2,1,0:T(8,128)(2,1)S(1)}, u32[]{:S(2)}, u32[]{:S(2)}) %all-to-all-start) | async-done | bytes 1572896 | tf_op jit(solution)/shard_map/all_to_all | solution.py:32
  51.4 0.6 fusion.11
  52.0 0.6 fusion.10
  52.6 0.1 maximum_multiply_fusion
  52.8 0.2 select_convert_fusion.1
  52.9 25.4 %all_to_all.25 = bf16[8,64,512]{2,1,0:T(8,128)(2,1)S(1)} all-to-all(bf16[8,64,512]{2,1,0:T(8,128)(2,1)S(1)} %select_convert_fusion.1), channel_id=1, replica_groups=mesh['y_lo'=2,'z'=8,'x'=4,'y_hi'=4,'core'=2] {'core','y_hi'}, dimensions={0} | all-to-all | bytes 1048576 | tf_op jit(solution)/shard_map/all_to_all | solution.py:38
  78.4 0.1 convert_reduce_fusion.1
  78.5 0.9 broadcast_in_dim.75
  79.3 4.1 %all-to-all-start.2 = ((bf16[8,64,512]{2,1,0:T(8,128)(2,1)}), bf16[8,64,512]{2,1,0:T(8,128)(2,1)}, u32[]{:S(2)}, u32[]{:S(2)}) async-start(bf16[8,64,512]{2,1,0:T(8,128)(2,1)} %broadcast_in_dim.75), calls=%async_computation.2 | async-start | bytes 1048576 | tf_op jit(solution)/shard_map/all_to_all | solution.py:32
  83.5 0.7 collective-permute-start
  84.2 0.0 collective-permute-done
  84.2 4.3 %all-gather.3 = bf16[128,512]{1,0:T(8,128)(2,1)S(1)} all-gather(bf16[64,512]{1,0:T(8,128)(2,1)S(1)} %collective-permute-done), channel_id=5, replica_groups=mesh['y_lo'=2,'z'=8,'x'=4,'y_hi'=4,'core'=2] {'y_lo'}, dimensions={0}, use_global_device_ids=true | all-gather | bytes 196608 | tf_op jit(solution)/shard_map/all_gather | solution.py:56
  88.5 21.2 %all-gather.4 = bf16[8,64,512]{2,1,0:T(8,128)(2,1)S(1)} all-gather(bf16[2,64,512]{2,1,0:T(8,128)(2,1)S(1)} %bitcast.59), channel_id=6, replica_groups=mesh['y_lo'=2,'z'=8,'x'=4,'y_hi'=4,'core'=2] {'x'}, dimensions={0}, use_global_device_ids=true | all-gather | bytes 655360 | tf_op jit(solution)/shard_map/all_gather | solution.py:57
  109.8 0.1 fusion.5
  109.9 0.0 all-to-all-done.2
  109.9 6.5 %collective-permute-start.1 = (bf16[512,512]{1,0:T(8,128)(2,1)}, bf16[512,512]{1,0:T(8,128)(2,1)S(1)}, u32[]{:S(2)}, u32[]{:S(2)}) collective-permute-start(bf16[512,512]{1,0:T(8,128)(2,1)} %bitcast.8), channel_id=1, source_target_pairs={{0,1},{1,0},{2,3},{3,2},{4,5},{5,4},{6,7},{7,6},{8,9},{9,8},{10,11... | collective-permute-start | bytes 1572872 | tf_op jit(solution)/shard_map/ppermute | solution.py:55
  116.5 1.3 fusion.12
  117.8 0.3 collective-permute-done.1
  118.1 0.3 convolution_add_fusion.1
  118.4 0.8 select_convert_fusion.2
  119.2 3.4 %all-to-all-start.3 = ((bf16[4,64,512]{2,1,0:T(8,128)(2,1)}), bf16[4,64,512]{2,1,0:T(8,128)(2,1)S(1)}, u32[]{:S(2)}, u32[]{:S(2)}) async-start(bf16[4,64,512]{2,1,0:T(8,128)(2,1)} %select_convert_fusion.2), calls=%async_computation.3 | async-start | bytes 524288 | tf_op jit(solution)/shard_map/all_to_all | solution.py:38
  122.6 8.7 %all-to-all-done.3 = bf16[4,64,512]{2,1,0:T(8,128)(2,1)S(1)} async-done(((bf16[4,64,512]{2,1,0:T(8,128)(2,1)}), bf16[4,64,512]{2,1,0:T(8,128)(2,1)S(1)}, u32[]{:S(2)}, u32[]{:S(2)}) %all-to-all-start.3) | async-done | bytes 262176 | tf_op jit(solution)/shard_map/all_to_all | solution.py:38
  131.4 0.0 copy-start
  131.4 0.1 fusion.4
  131.5 18.3 %all_gather.35 = bf16[512,512]{1,0:T(8,128)(2,1)S(1)} all-gather(bf16[64,512]{1,0:T(8,128)(2,1)S(1)} %fusion.4), channel_id=1, replica_groups=mesh['y_lo'=2,'z'=8,'x'=4,'y_hi'=4,'core'=2] {'y_hi','core'}, dimensions={0}, use_global_device_ids=true | all-gather | bytes 589824 | tf_op jit(solution)/shard_map/all_gather | solution.py:74
  149.8 0.0 copy-done
  149.8 1.2 select_convert_fusion
  151.0 24.0 %all_to_all.26 = bf16[8,64,1536]{2,1,0:T(8,128)(2,1)S(1)} all-to-all(bf16[8,64,1536]{2,1,0:T(8,128)(2,1)S(1)} %get-tuple-element.9), channel_id=1, replica_groups=mesh['y_lo'=2,'z'=8,'x'=4,'y_hi'=4,'core'=2] {'x','y_lo'}, dimensions={0} | all-to-all | bytes 3145728 | tf_op jit(solution)/shard_map/all_to_all | solution.py:38
  175.0 0.2 convert_reduce_fusion
  175.2 0.8 bitcast_add_fusion
  (10 shorter events, 0.2 us)
Async XLA Ops:
  2.3 49.1 %all-to-all-start = ((bf16[8,64,1536]{2,1,0:T(8,128)(2,1)}), bf16[8,64,1536]{2,1,0:T(8,128)(2,1)S(1)}, u32[]{:S(2)}, u32[]{:S(2)}) async-start(bf16[8,64,1536]{2,1,0:T(8,128)(2,1)} %broadcast_in_dim.71), calls=%async_computation | async-start | bytes 3145728 | tf_op jit(solution)/shard_map/all_to_all | solution.py:32
  79.3 30.6 %all-to-all-start.2 = ((bf16[8,64,512]{2,1,0:T(8,128)(2,1)}), bf16[8,64,512]{2,1,0:T(8,128)(2,1)}, u32[]{:S(2)}, u32[]{:S(2)}) async-start(bf16[8,64,512]{2,1,0:T(8,128)(2,1)} %broadcast_in_dim.75), calls=%async_computation.2 | async-start | bytes 1048576 | tf_op jit(solution)/shard_map/all_to_all | solution.py:32
  83.5 0.7 collective-permute-start
  109.9 8.2 %collective-permute-start.1 = (bf16[512,512]{1,0:T(8,128)(2,1)}, bf16[512,512]{1,0:T(8,128)(2,1)S(1)}, u32[]{:S(2)}, u32[]{:S(2)}) collective-permute-start(bf16[512,512]{1,0:T(8,128)(2,1)} %bitcast.8), channel_id=1, source_target_pairs={{0,1},{1,0},{2,3},{3,2},{4,5},{5,4},{6,7},{7,6},{8,9},{9,8},{10,11... | collective-permute-start | bytes 1572872 | tf_op jit(solution)/shard_map/ppermute | solution.py:55
  119.2 12.2 %all-to-all-start.3 = ((bf16[4,64,512]{2,1,0:T(8,128)(2,1)}), bf16[4,64,512]{2,1,0:T(8,128)(2,1)S(1)}, u32[]{:S(2)}, u32[]{:S(2)}) async-start(bf16[4,64,512]{2,1,0:T(8,128)(2,1)} %select_convert_fusion.2), calls=%async_computation.3 | async-start | bytes 524288 | tf_op jit(solution)/shard_map/all_to_all | solution.py:38
  131.4 18.4 %copy-start = (f32[64,1536]{1,0:T(8,128)S(1)}, f32[64,1536]{1,0:T(8,128)}, u32[]{:S(2)}) copy-start(f32[64,1536]{1,0:T(8,128)} %param.1) | copy-start | bytes 1179652

commit v33 on v20

--- a/solution.py
+++ b/solution.py
@@ -74,7 +74,9 @@
     poly = (coef_cubic * gram + coef_quintic * square).astype(jnp.bfloat16)
     poly = lax.all_gather(spread(poly, "y_hi"), "core", axis=0).reshape(8 * rows, 8 * rows)
     product = jnp.dot(poly, by_hi, preferred_element_type=jnp.float32)
-    return coef_linear * x_scaled + sum_pieces(product.reshape(8, rows, cols), ("y_lo", "x"))
+    mine = jnp.arange(8)[:, None, None] == lax.axis_index(("y_lo", "x"))
+    linear = coef_linear * jnp.where(mine, x_scaled, 0.0)
+    return sum_pieces(product.reshape(8, rows, cols) + linear, ("y_lo", "x"))
 
 
 def solution(mesh):

time: 174 us -> 174 us (level)
  no operation moved by 1% of the time
where the time goes in v33:
time: 174 us; the launch traced here: 173 us
  blocking collectives  102 us (59%)
  waiting for transfers between devices  36 us (21%)
  starting transfers between devices  24.2 us (14%)
  other arithmetic  4.41 us (3%)
  local copies, waits for them, and re-layouts  3.01 us (2%)
  matrix products  2.96 us (2%)
    all_to_all x2, blocking collectives, sum_pieces(): lax.all_to_all(jnp.where(mine, 0.0, pieces).astype(jnp.bfloat16), axis, 0...  49.8 us
    all_to_all x3, waiting for transfers between devices, spread(): lax.all_to_all(jnp.broadcast_to(block[None], (count,) + block.shape), axi...  29 us
    all_gather x2, blocking collectives, per_device(): by_lo = [lax.all_gather(pair[y], 'x', axis=0, tiled=True) for y in range(2)]  23.9 us
    all_to_all x3, starting transfers between devices, spread(): lax.all_to_all(jnp.broadcast_to(block[None], (count,) + block.shape), axi...  17.8 us
    all_gather x1, blocking collectives, per_device(): left = lax.all_gather(left, 'x', axis=0).reshape(4, 2, rows, 8 * rows)  10.9 us
    all_gather x1, blocking collectives, per_device(): lax.all_gather(spread(poly, 'y_hi'), 'core', axis=0)  7.06 us
    all_to_all x1, waiting for transfers between devices, sum_pieces(): lax.all_to_all(jnp.where(mine, 0.0, pieces).astype(jnp.bfloat16), axis, 0...  7.01 us
    all_gather x1, blocking collectives, per_device(): pair = lax.all_gather(xb, 'y_lo', axis=0)  6.12 us
  transfers between devices with their start and end apart: 6, of which 4 were waited for; matrix products, arithmetic and copies ran while one was open for 1% of the time, Pallas kernels for 0%

profile of v33, /device:TPU:1, one launch (start us, length us, event | category | flops | bytes accessed | tf_op | source)
XLA Modules:
  0.0 172.9 jit_solution(13433538113244617862)
XLA Ops:
  0.0 1.0 convert_element_type.37
  1.0 1.3 broadcast_in_dim.79
  2.3 10.9 %all-to-all-start = ((bf16[8,64,1536]{2,1,0:T(8,128)(2,1)}), bf16[8,64,1536]{2,1,0:T(8,128)(2,1)S(1)}, u32[]{:S(2)}, u32[]{:S(2)}) async-start(bf16[8,64,1536]{2,1,0:T(8,128)(2,1)} %broadcast_in_dim.79), calls=%async_computation | async-start | bytes 3145728 | tf_op jit(solution)/shard_map/all_to_all | solution.py:33
  13.2 6.1 %all-gather = bf16[128,1536]{1,0:T(8,128)(2,1)S(1)} all-gather(bf16[64,1536]{1,0:T(8,128)(2,1)S(1)} %convert_element_type.37), channel_id=2, replica_groups=mesh['y_lo'=2,'z'=8,'x'=4,'y_hi'=4,'core'=2] {'y_lo'}, dimensions={0}, use_global_device_ids=true | all-gather | bytes 589824 | tf_op jit(solution)/shard_map/all_gather | solution.py:48
  19.3 12.6 %all-gather.6 = bf16[256,1536]{1,0:T(8,128)(2,1)S(1)} all-gather(bf16[64,1536]{1,0:T(8,128)(2,1)S(1)} %get-tuple-element.7), channel_id=8, replica_groups=mesh['y_lo'=2,'z'=8,'x'=4,'y_hi'=4,'core'=2] {'x'}, dimensions={0}, use_global_device_ids=true | all-gather | bytes 983040 | tf_op jit(solution)/shard_map/all_gather | solution.py:49
  32.0 11.3 %all-gather.7 = bf16[256,1536]{1,0:T(8,128)(2,1)S(1)} all-gather(bf16[64,1536]{1,0:T(8,128)(2,1)S(1)} %get-tuple-element.8), channel_id=9, replica_groups=mesh['y_lo'=2,'z'=8,'x'=4,'y_hi'=4,'core'=2] {'x'}, dimensions={0}, use_global_device_ids=true | all-gather | bytes 983040 | tf_op jit(solution)/shard_map/all_gather | solution.py:49
  43.3 8.2 %all-to-all-done = bf16[8,64,1536]{2,1,0:T(8,128)(2,1)S(1)} async-done(((bf16[8,64,1536]{2,1,0:T(8,128)(2,1)}), bf16[8,64,1536]{2,1,0:T(8,128)(2,1)S(1)}, u32[]{:S(2)}, u32[]{:S(2)}) %all-to-all-start) | async-done | bytes 1572896 | tf_op jit(solution)/shard_map/all_to_all | solution.py:33
  51.4 0.6 fusion.10
  52.1 0.6 fusion.9
  52.7 0.1 maximum_multiply_fusion
  52.8 0.2 select_convert_fusion.1
  53.0 25.4 %all_to_all.30 = bf16[8,64,512]{2,1,0:T(8,128)(2,1)S(1)} all-to-all(bf16[8,64,512]{2,1,0:T(8,128)(2,1)S(1)} %select_convert_fusion.1), channel_id=1, replica_groups=mesh['y_lo'=2,'z'=8,'x'=4,'y_hi'=4,'core'=2] {'core','y_hi'}, dimensions={0} | all-to-all | bytes 1048576 | tf_op jit(solution)/shard_map/all_to_all | solution.py:39
  78.4 0.1 convert_reduce_fusion.1
  78.5 0.8 broadcast_in_dim.83
  79.3 3.5 %all-to-all-start.2 = ((bf16[8,64,512]{2,1,0:T(8,128)(2,1)}), bf16[8,64,512]{2,1,0:T(8,128)(2,1)S(1)}, u32[]{:S(2)}, u32[]{:S(2)}) async-start(bf16[8,64,512]{2,1,0:T(8,128)(2,1)} %broadcast_in_dim.83), calls=%async_computation.2 | async-start | bytes 1048576 | tf_op jit(solution)/shard_map/all_to_all | solution.py:33
  82.8 0.7 collective-permute-start
  83.5 0.0 collective-permute-done
  83.5 4.3 %all-gather.3 = bf16[128,512]{1,0:T(8,128)(2,1)S(1)} all-gather(bf16[64,512]{1,0:T(8,128)(2,1)S(1)} %collective-permute-done), channel_id=5, replica_groups=mesh['y_lo'=2,'z'=8,'x'=4,'y_hi'=4,'core'=2] {'y_lo'}, dimensions={0}, use_global_device_ids=true | all-gather | bytes 196608 | tf_op jit(solution)/shard_map/all_gather | solution.py:57
  87.9 12.9 %all-to-all-done.2 = bf16[8,64,512]{2,1,0:T(8,128)(2,1)S(1)} async-done(((bf16[8,64,512]{2,1,0:T(8,128)(2,1)}), bf16[8,64,512]{2,1,0:T(8,128)(2,1)S(1)}, u32[]{:S(2)}, u32[]{:S(2)}) %all-to-all-start.2) | async-done | bytes 524320 | tf_op jit(solution)/shard_map/all_to_all | solution.py:33
  100.8 2.3 %collective-permute-start.1 = (bf16[512,512]{1,0:T(8,128)(2,1)S(1)}, bf16[512,512]{1,0:T(8,128)(2,1)S(1)}, u32[]{:S(2)}, u32[]{:S(2)}) collective-permute-start(bf16[512,512]{1,0:T(8,128)(2,1)S(1)} %bitcast.56), channel_id=1, source_target_pairs={{0,1},{1,0},{2,3},{3,2},{4,5},{5,4},{6,7},{7,6},{8,9},{9,8},{10,11... | collective-permute-start | bytes 1572872 | tf_op jit(solution)/shard_map/ppermute | solution.py:56
  103.1 10.9 %all-gather.4 = bf16[8,64,512]{2,1,0:T(8,128)(2,1)S(1)} all-gather(bf16[2,64,512]{2,1,0:T(8,128)(2,1)S(1)} %bitcast.60), channel_id=6, replica_groups=mesh['y_lo'=2,'z'=8,'x'=4,'y_hi'=4,'core'=2] {'x'}, dimensions={0}, use_global_device_ids=true | all-gather | bytes 655360 | tf_op jit(solution)/shard_map/all_gather | solution.py:58
  114.0 0.0 copy-start
  114.1 0.3 fusion.11
  114.4 0.0 collective-permute-done.1
  114.4 0.3 convolution_add_fusion.1
  114.7 0.1 copy-done
  114.8 0.8 select_convert_fusion.2
  115.6 3.4 %all-to-all-start.3 = ((bf16[4,64,512]{2,1,0:T(8,128)(2,1)}), bf16[4,64,512]{2,1,0:T(8,128)(2,1)S(1)}, u32[]{:S(2)}, u32[]{:S(2)}) async-start(bf16[4,64,512]{2,1,0:T(8,128)(2,1)} %select_convert_fusion.2), calls=%async_computation.3 | async-start | bytes 524288 | tf_op jit(solution)/shard_map/all_to_all | solution.py:39
  119.0 1.0 fusion.5
  120.0 7.0 %all-to-all-done.3 = bf16[4,64,512]{2,1,0:T(8,128)(2,1)S(1)} async-done(((bf16[4,64,512]{2,1,0:T(8,128)(2,1)}), bf16[4,64,512]{2,1,0:T(8,128)(2,1)S(1)}, u32[]{:S(2)}, u32[]{:S(2)}) %all-to-all-start.3) | async-done | bytes 262176 | tf_op jit(solution)/shard_map/all_to_all | solution.py:39
  127.1 0.1 fusion.7
  127.2 0.0 copy-start.1
  127.2 0.7 broadcast_in_dim.88
  127.9 3.4 %all-to-all-start.4 = ((bf16[4,64,512]{2,1,0:T(8,128)(2,1)}), bf16[4,64,512]{2,1,0:T(8,128)(2,1)S(1)}, u32[]{:S(2)}, u32[]{:S(2)}) async-start(bf16[4,64,512]{2,1,0:T(8,128)(2,1)} %broadcast_in_dim.88), calls=%async_computation.4 | async-start | bytes 524288 | tf_op jit(solution)/shard_map/all_to_all | solution.py:33
  131.4 7.9 %all-to-all-done.4 = bf16[4,64,512]{2,1,0:T(8,128)(2,1)S(1)} async-done(((bf16[4,64,512]{2,1,0:T(8,128)(2,1)}), bf16[4,64,512]{2,1,0:T(8,128)(2,1)S(1)}, u32[]{:S(2)}, u32[]{:S(2)}) %all-to-all-start.4) | async-done | bytes 262176 | tf_op jit(solution)/shard_map/all_to_all | solution.py:33
  139.2 7.1 %all-gather.5 = bf16[8,64,512]{2,1,0:T(8,128)(2,1)S(1)} all-gather(bf16[4,64,512]{2,1,0:T(8,128)(2,1)S(1)} %all-to-all-done.4), channel_id=7, replica_groups=mesh['y_lo'=2,'z'=8,'x'=4,'y_hi'=4,'core'=2] {'core'}, dimensions={0}, use_global_device_ids=true | all-gather | bytes 786432 | tf_op jit(solution)/shard_map/all_gather | solution.py:75
  146.3 0.0 copy-done.1
  146.3 1.2 select_convert_fusion
  147.5 24.4 %all_to_all.31 = bf16[8,64,1536]{2,1,0:T(8,128)(2,1)S(1)} all-to-all(bf16[8,64,1536]{2,1,0:T(8,128)(2,1)S(1)} %get-tuple-element.9), channel_id=1, replica_groups=mesh['y_lo'=2,'z'=8,'x'=4,'y_hi'=4,'core'=2] {'y_lo','x'}, dimensions={0} | all-to-all | bytes 3145728 | tf_op jit(solution)/shard_map/all_to_all | solution.py:39
  171.9 0.2 convert_reduce_fusion
  172.1 0.8 bitcast_add_fusion
  (10 shorter events, 0.2 us)
Async XLA Ops:
  2.3 49.1 %all-to-all-start = ((bf16[8,64,1536]{2,1,0:T(8,128)(2,1)}), bf16[8,64,1536]{2,1,0:T(8,128)(2,1)S(1)}, u32[]{:S(2)}, u32[]{:S(2)}) async-start(bf16[8,64,1536]{2,1,0:T(8,128)(2,1)} %broadcast_in_dim.79), calls=%async_computation | async-start | bytes 3145728 | tf_op jit(solution)/shard_map/all_to_all | solution.py:33
  79.3 21.5 %all-to-all-start.2 = ((bf16[8,64,512]{2,1,0:T(8,128)(2,1)}), bf16[8,64,512]{2,1,0:T(8,128)(2,1)S(1)}, u32[]{:S(2)}, u32[]{:S(2)}) async-start(bf16[8,64,512]{2,1,0:T(8,128)(2,1)} %broadcast_in_dim.83), calls=%async_computation.2 | async-start | bytes 1048576 | tf_op jit(solution)/shard_map/all_to_all | solution.py:33
  82.8 0.7 collective-permute-start
  100.8 13.6 %collective-permute-start.1 = (bf16[512,512]{1,0:T(8,128)(2,1)S(1)}, bf16[512,512]{1,0:T(8,128)(2,1)S(1)}, u32[]{:S(2)}, u32[]{:S(2)}) collective-permute-start(bf16[512,512]{1,0:T(8,128)(2,1)S(1)} %bitcast.56), channel_id=1, source_target_pairs={{0,1},{1,0},{2,3},{3,2},{4,5},{5,4},{6,7},{7,6},{8,9},{9,8},{10,11... | collective-permute-start | bytes 1572872 | tf_op jit(solution)/shard_map/ppermute | solution.py:56
  114.0 0.8 copy-start
  115.6 11.4 %all-to-all-start.3 = ((bf16[4,64,512]{2,1,0:T(8,128)(2,1)}), bf16[4,64,512]{2,1,0:T(8,128)(2,1)S(1)}, u32[]{:S(2)}, u32[]{:S(2)}) async-start(bf16[4,64,512]{2,1,0:T(8,128)(2,1)} %select_convert_fusion.2), calls=%async_computation.3 | async-start | bytes 524288 | tf_op jit(solution)/shard_map/all_to_all | solution.py:39
  127.2 19.1 %copy-start.1 = (f32[64,1536]{1,0:T(8,128)S(1)}, f32[64,1536]{1,0:T(8,128)}, u32[]{:S(2)}) copy-start(f32[64,1536]{1,0:T(8,128)} %param.1) | copy-start | bytes 1179652
  127.9 11.3 %all-to-all-start.4 = ((bf16[4,64,512]{2,1,0:T(8,128)(2,1)}), bf16[4,64,512]{2,1,0:T(8,128)(2,1)S(1)}, u32[]{:S(2)}, u32[]{:S(2)}) async-start(bf16[4,64,512]{2,1,0:T(8,128)(2,1)} %broadcast_in_dim.88), calls=%async_computation.4 | async-start | bytes 524288 | tf_op jit(solution)/shard_map/all_to_all | solution.py:33
